TPU v7x, 32 devices: a whole 2x2x4 slice. The times are simulated.
32 devices in a mesh: dp: 8 (over z, y), group: 4 (over x, core).
Axes of the slice: x: 2, y: 2, z: 4, core: 2. Of those that a mesh axis runs over, the one named last changes fastest.
Arguments:
- tokens: bfloat16 [16384, 1024], P(('dp', 'group')), may hold values from -6 to 6
- cotangent: bfloat16 [16384, 1024], P(('dp', 'group')), may hold values from -6 to 6
- variate: int32 [16384], P('dp'), may hold values from 0 to 3
- seq_len: int32 [8, 3], P('dp'), may hold values from 1 to 1024, 2048 in all within a row
- seq_adapter: int32 [8, 3], P('dp'), may hold values from 0 to 7
- block_order: int32 [8, 16], P('dp'), may hold values from 0 to 15, each once within a row
- attn_gain: bfloat16 [1024], replicated, may hold values from 0.5 to 1.5
- ffn_gain: bfloat16 [1024], replicated, may hold values from 0.5 to 1.5
- q_gain: bfloat16 [64], replicated, may hold values from 0.25 to 1.75
- k_gain: bfloat16 [64], replicated, may hold values from 0.25 to 1.75
- attn_bias: float32 [2, 16], replicated, may hold values from -4 to 4
- query_weight: bfloat16 [1024, 1024], replicated, may hold values from -0.1875 to 0.1875
- key_weight: bfloat16 [1024, 1024], replicated, may hold values from -0.1875 to 0.1875
- value_weight: bfloat16 [1024, 1024], replicated, may hold values from -0.1875 to 0.1875
- output_weight: bfloat16 [1024, 1024], replicated, may hold values from -1.5 to 1.5
- gate_weight: bfloat16 [1024, 4096], replicated, may hold values from -0.1875 to 0.1875
- up_weight: bfloat16 [1024, 4096], replicated, may hold values from -0.1875 to 0.1875
- down_weight: bfloat16 [4096, 1024], replicated, may hold values from -0.09375 to 0.09375
- adapters: bfloat16 [3014656], replicated, may hold values from -0.1796875 to 0.1796875
- moment1: float32 [3014656], P(('dp', 'group')), may hold values from -6 to 6
- moment2: float32 [3014656], P(('dp', 'group')), may hold values from 0.01 to 100
Outputs:
- layer_out: bfloat16 [16384, 1024], P(('dp', 'group'))
- input_grad: bfloat16 [16384, 1024], P(('dp', 'group'))
- adapter_grad: float32 [3014656], P(('dp', 'group'))
- moment1_new: float32 [3014656], P(('dp', 'group'))
- moment2_new: float32 [3014656], P(('dp', 'group'))
- adapters_new: bfloat16 [3014656], replicated
Inputs may be any that keep to these rules, and one draw needn't show every extreme that they name: `seq_len`: each row sums to 2048; the largest of each row is 1024. `block_order`: each row is a permutation.
All inputs are finite; a program needn't handle non-finite values.
Results may differ from a plain program's by a relative error of at most 0.015.
Values may be sent and summed in bfloat16 or wider, within the bound.
No kernel may reach another device: no remote copies, remote signals or barrier semaphores. Data moves between devices by JAX's collectives and lax.ppermute only.
A program may use at most 256 MiB of HBM per device.

v0:
```python
import jax
import jax.numpy as jnp
from jax import lax
from jax.sharding import PartitionSpec as P

RANK = 16
ADAPTERS = 8


NORM_EPS = 1e-06
ADAPTER_SCALE = 2.0
ROPE_BASE = 10000.0
MASKED = -1e30
LEARN_RATE = 0.01
BETA_ONE = 0.9
BETA_TWO = 0.999
ADAM_EPS = 1e-08
WEIGHT_DECAY = 0.01
update_count = 10.0


def rms_norm(values, norm_gain):
    scaled = values * lax.rsqrt(jnp.mean(values * values, axis=-1, keepdims=True) + NORM_EPS)
    return scaled * norm_gain.astype(jnp.float32)


def rope_tables(position, head_width):
    half_width = head_width // 2
    freq_index = jnp.arange(half_width, dtype=jnp.float32)
    frequency = ROPE_BASE ** (-2.0 * freq_index / head_width)
    angles = position.astype(jnp.float32)[:, None] * frequency[None, :]
    return (jnp.cos(angles), jnp.sin(angles))


def shape_heads(values, norm_gain, cos_table, sin_table, head_width):
    row_count = values.shape[0]
    per_head = values.reshape(row_count, -1, head_width)
    normalized_input = rms_norm(per_head, norm_gain)
    half_width = head_width // 2
    first_half = normalized_input[..., :half_width]
    second_half = normalized_input[..., half_width:]
    cos_part = cos_table[:, None, :]
    sin_part = sin_table[:, None, :]
    turned = jnp.concatenate(
        [
            first_half * cos_part - second_half * sin_part,
            first_half * sin_part + second_half * cos_part,
        ],
        axis=-1,
    )
    return turned.reshape(row_count, -1)


def unpack(flat_params, shapes, columns):
    partial_pieces = []
    offset = 0
    for fan_in, fan_out in shapes:
        down_size = fan_in * columns
        a_matrix = lax.slice_in_dim(flat_params, offset, offset + down_size).reshape(
            fan_in, columns
        )
        offset = offset + down_size
        up_size = columns * fan_out
        b_matrix = lax.slice_in_dim(flat_params, offset, offset + up_size).reshape(columns, fan_out)
        offset = offset + up_size
        partial_pieces.append((a_matrix, b_matrix))
    return partial_pieces


def contract_leading_rows(left, right):
    return lax.dot_general(
        left, right, (((0,), (0,)), ((), ())), preferred_element_type=jnp.float32
    )


def contract_columns(left, right):
    return lax.dot_general(
        left, right, (((1,), (1,)), ((), ())), preferred_element_type=jnp.float32
    )


def project(low_in, weight_matrix, partial_piece, adapter_selector_mask):
    base_product = jnp.dot(low_in, weight_matrix, preferred_element_type=jnp.float32)
    lowrank_inner = (
        jnp.dot(low_in, partial_piece[0], preferred_element_type=jnp.float32)
        * adapter_selector_mask
    ).astype(jnp.bfloat16)
    return (
        base_product
        + ADAPTER_SCALE
        * jnp.dot(lowrank_inner, partial_piece[1], preferred_element_type=jnp.float32),
        lowrank_inner,
    )


def project_back(
    gradient_lowrank, low_in, lowrank_inner, weight_matrix, partial_piece, adapter_selector_mask
):
    grad_in = contract_columns(gradient_lowrank, weight_matrix)
    gradient_inner = (
        ADAPTER_SCALE * contract_columns(gradient_lowrank, partial_piece[1]) * adapter_selector_mask
    ).astype(jnp.bfloat16)
    grad_in = grad_in + contract_columns(gradient_inner, partial_piece[0])
    grad_a = contract_leading_rows(low_in, gradient_inner)
    grad_up_factor = ADAPTER_SCALE * contract_leading_rows(lowrank_inner, gradient_lowrank)
    return (grad_in, grad_a, grad_up_factor)


def head_slice(array, head_index, head_width):
    return lax.dynamic_slice_in_dim(array, head_index * head_width, head_width, 1)


def to_columns(stacked):
    return jnp.moveaxis(stacked, 0, 1).reshape(stacked.shape[1], -1)


def logits(first_rows, second_rows, bias_pair, same_seq, same_var, head_width):
    scores = contract_columns(first_rows, second_rows) * head_width ** (-0.5)
    scores = scores + jnp.where(same_var, bias_pair[0], bias_pair[1])
    return jnp.where(same_seq, scores, MASKED)


def attend(query_low, key_all, value_all, attn_bias, same_seq, same_var, head_width):
    head_count = query_low.shape[1] // head_width

    def attend_one_head(head_index):
        bias_pair = lax.dynamic_index_in_dim(attn_bias, head_index, 1, keepdims=False)
        scores = logits(
            head_slice(query_low, head_index, head_width),
            head_slice(key_all, head_index, head_width),
            bias_pair,
            same_seq,
            same_var,
            head_width,
        )
        row_max = jnp.max(scores, axis=1, keepdims=True)
        exp_score = jnp.exp(scores - row_max)
        exp_sum = jnp.sum(exp_score, axis=1, keepdims=True)
        prob_low = (exp_score / exp_sum).astype(jnp.bfloat16)
        head_out = jnp.dot(
            prob_low,
            head_slice(value_all, head_index, head_width),
            preferred_element_type=jnp.float32,
        )
        return (head_out, (row_max + jnp.log(exp_sum))[:, 0])

    attended_tokens, log_total = lax.map(attend_one_head, jnp.arange(head_count))
    return (to_columns(attended_tokens), jnp.transpose(log_total))


def query_pass(
    query_low,
    key_all,
    value_all,
    attn_bias,
    same_seq,
    same_var,
    log_total,
    gradient_lowrank,
    head_width,
):
    head_count = query_low.shape[1] // head_width

    def query_one_head(head_index):
        query_head = head_slice(query_low, head_index, head_width)
        key_head = head_slice(key_all, head_index, head_width)
        value_head = head_slice(value_all, head_index, head_width)
        grad_head = head_slice(gradient_lowrank, head_index, head_width)
        bias_pair = lax.dynamic_index_in_dim(attn_bias, head_index, 1, keepdims=False)
        scores = logits(query_head, key_head, bias_pair, same_seq, same_var, head_width)
        softmax_prob = jnp.exp(
            scores - lax.dynamic_index_in_dim(log_total, head_index, 1, keepdims=True)
        )
        grad_prob = contract_columns(grad_head, value_head)
        prob_dot = jnp.sum(softmax_prob * grad_prob, axis=1)
        grad_score = (softmax_prob * (grad_prob - prob_dot[:, None])).astype(jnp.bfloat16)
        grad_query = jnp.dot(
            grad_score, key_head, preferred_element_type=jnp.float32
        ) * head_width ** (-0.5)
        grad_key = contract_leading_rows(grad_score, query_head) * head_width ** (-0.5)
        grad_value = contract_leading_rows(softmax_prob.astype(jnp.bfloat16), grad_head)
        return (grad_query, prob_dot, grad_key, grad_value)

    results = lax.map(query_one_head, jnp.arange(head_count))
    return (
        to_columns(results[0]),
        jnp.transpose(results[1]),
        to_columns(results[2]),
        to_columns(results[3]),
    )


def per_device(
    tokens,
    cotangent,
    variate,
    seq_len,
    seq_adapter,
    block_order,
    attn_gain,
    ffn_gain,
    q_gain,
    k_gain,
    attn_bias,
    query_weight,
    key_weight,
    value_weight,
    output_weight,
    gate_weight,
    up_weight,
    down_weight,
    adapters,
    moment1,
    moment2,
):
    groups = lax.axis_size("group")
    member = lax.axis_index("group")
    row_count, feature_width = tokens.shape
    hidden_width = gate_weight.shape[1]
    head_width = q_gain.shape[0]
    pack_x, pack_dy = (
        lax.all_gather(tokens, "group", axis=0, tiled=True),
        lax.all_gather(cotangent, "group", axis=0, tiled=True),
    )
    pack_count = pack_x.shape[0]
    block_list = block_order[0]
    blocks = block_list.shape[0]
    block_rows = pack_count // blocks
    per_member = blocks // groups
    my_blocks = lax.dynamic_slice_in_dim(block_list, member * per_member, per_member)
    lengths = seq_len[0]
    seq_ends = jnp.cumsum(lengths)
    seq_starts = seq_ends - lengths
    row_index = jnp.arange(pack_count, dtype=jnp.int32)
    segment = jnp.sum((row_index[:, None] >= seq_ends[None, :]).astype(jnp.int32), axis=1)
    picked = (segment[:, None] == jnp.arange(lengths.shape[0], dtype=jnp.int32)[None, :]).astype(
        jnp.int32
    )
    position = row_index - jnp.sum(picked * seq_starts[None, :], axis=1)
    row_adapter = jnp.sum(picked * seq_adapter[0][None, :], axis=1)
    variate_work = variate.reshape(blocks, block_rows)[block_list].reshape(pack_count)
    first_row = member * row_count
    seg_mine = lax.dynamic_slice_in_dim(segment, first_row, row_count)
    var_mine = lax.dynamic_slice_in_dim(variate_work, first_row, row_count)
    pos_mine = lax.dynamic_slice_in_dim(position, first_row, row_count)
    adapter_mine = lax.dynamic_slice_in_dim(row_adapter, first_row, row_count)
    same_seq = seg_mine[:, None] == segment[None, :]
    same_var = var_mine[:, None] == variate_work[None, :]
    columns = ADAPTERS * RANK
    adapter_selector_mask = (
        adapter_mine[:, None] == (jnp.arange(columns, dtype=jnp.int32) // RANK)[None, :]
    ).astype(jnp.float32)
    cos_table, sin_table = rope_tables(pos_mine, head_width)
    my_tokens = (
        pack_x.reshape(blocks, block_rows, feature_width)[my_blocks]
        .reshape(row_count, feature_width)
        .astype(jnp.float32)
    )
    my_grads = pack_dy.reshape(blocks, block_rows, feature_width)[my_blocks].reshape(
        row_count, feature_width
    )
    shapes = [(feature_width, feature_width)] * 4 + [
        (feature_width, hidden_width),
        (feature_width, hidden_width),
        (hidden_width, feature_width),
    ]
    partial_pieces = unpack(adapters, shapes, columns)
    normalized_input = rms_norm(my_tokens, attn_gain).astype(jnp.bfloat16)
    query_preactivation, query_inner = project(
        normalized_input, query_weight, partial_pieces[0], adapter_selector_mask
    )
    key_preactivation, key_inner = project(
        normalized_input, key_weight, partial_pieces[1], adapter_selector_mask
    )
    value_raw, value_inner = project(
        normalized_input, value_weight, partial_pieces[2], adapter_selector_mask
    )
    value_lowrank = value_raw.astype(jnp.bfloat16)
    query_low = shape_heads(query_preactivation, q_gain, cos_table, sin_table, head_width).astype(
        jnp.bfloat16
    )
    key_low = shape_heads(key_preactivation, k_gain, cos_table, sin_table, head_width).astype(
        jnp.bfloat16
    )
    key_all, value_all = (
        lax.all_gather(key_low, "group", axis=0, tiled=True),
        lax.all_gather(value_lowrank, "group", axis=0, tiled=True),
    )
    attended_tokens, log_total = attend(
        query_low, key_all, value_all, attn_bias, same_seq, same_var, head_width
    )
    attended_low = attended_tokens.astype(jnp.bfloat16)
    attention_output, out_inner = project(
        attended_low, output_weight, partial_pieces[3], adapter_selector_mask
    )
    residual_stream = my_tokens + attention_output
    hidden_lowrank = rms_norm(residual_stream, ffn_gain).astype(jnp.bfloat16)
    gate_preactivation, gate_inner = project(
        hidden_lowrank, gate_weight, partial_pieces[4], adapter_selector_mask
    )
    up_preactivation, up_inner = project(
        hidden_lowrank, up_weight, partial_pieces[5], adapter_selector_mask
    )
    activated_hidden = (jax.nn.silu(gate_preactivation) * up_preactivation).astype(jnp.bfloat16)
    ffn_out, down_inner = project(
        activated_hidden, down_weight, partial_pieces[6], adapter_selector_mask
    )
    final_result = residual_stream + ffn_out
    out_buffer = (
        jnp.zeros((blocks, block_rows, feature_width), jnp.float32)
        .at[my_blocks]
        .set(final_result.reshape(per_member, block_rows, feature_width))
    )
    returned = lax.psum_scatter(
        out_buffer.astype(jnp.bfloat16), "group", scatter_dimension=0, tiled=True
    ).astype(jnp.float32)
    layer_out = returned.reshape(row_count, feature_width).astype(jnp.bfloat16)
    grad_act, down_a, down_b = project_back(
        my_grads,
        activated_hidden,
        down_inner,
        down_weight,
        partial_pieces[6],
        adapter_selector_mask,
    )
    _, act_back = jax.vjp(
        lambda gate_values, up_values: jax.nn.silu(gate_values) * up_values,
        gate_preactivation,
        up_preactivation,
    )
    grad_gate, grad_up = act_back(grad_act)
    grad_hidden_gate, gate_a, gate_b = project_back(
        grad_gate.astype(jnp.bfloat16),
        hidden_lowrank,
        gate_inner,
        gate_weight,
        partial_pieces[4],
        adapter_selector_mask,
    )
    grad_hidden_up, up_a, up_b = project_back(
        grad_up.astype(jnp.bfloat16),
        hidden_lowrank,
        up_inner,
        up_weight,
        partial_pieces[5],
        adapter_selector_mask,
    )
    _, ffn_norm_back = jax.vjp(lambda values: rms_norm(values, ffn_gain), residual_stream)
    grad_residual = (
        my_grads.astype(jnp.float32) + ffn_norm_back(grad_hidden_gate + grad_hidden_up)[0]
    )
    grad_attended, out_a, out_b = project_back(
        grad_residual.astype(jnp.bfloat16),
        attended_low,
        out_inner,
        output_weight,
        partial_pieces[3],
        adapter_selector_mask,
    )
    grad_attended_low = grad_attended.astype(jnp.bfloat16)
    grad_query, prob_dot, grad_key_pack, grad_value_pack = query_pass(
        query_low,
        key_all,
        value_all,
        attn_bias,
        same_seq,
        same_var,
        log_total,
        grad_attended_low,
        head_width,
    )
    grad_key, grad_value = (
        lax.psum_scatter(
            grad_key_pack.astype(jnp.bfloat16), "group", scatter_dimension=0, tiled=True
        ).astype(jnp.float32),
        lax.psum_scatter(
            grad_value_pack.astype(jnp.bfloat16), "group", scatter_dimension=0, tiled=True
        ).astype(jnp.float32),
    )
    _, query_head_back = jax.vjp(
        lambda values: shape_heads(values, q_gain, cos_table, sin_table, head_width),
        query_preactivation,
    )
    _, key_head_back = jax.vjp(
        lambda values: shape_heads(values, k_gain, cos_table, sin_table, head_width),
        key_preactivation,
    )
    grad_query_raw = query_head_back(grad_query)[0].astype(jnp.bfloat16)
    grad_key_raw = key_head_back(grad_key)[0].astype(jnp.bfloat16)
    grad_norm_q, query_a, query_b = project_back(
        grad_query_raw,
        normalized_input,
        query_inner,
        query_weight,
        partial_pieces[0],
        adapter_selector_mask,
    )
    grad_norm_k, key_a, key_b = project_back(
        grad_key_raw,
        normalized_input,
        key_inner,
        key_weight,
        partial_pieces[1],
        adapter_selector_mask,
    )
    grad_norm_v, value_a, value_b = project_back(
        grad_value.astype(jnp.bfloat16),
        normalized_input,
        value_inner,
        value_weight,
        partial_pieces[2],
        adapter_selector_mask,
    )
    _, attn_norm_back = jax.vjp(lambda values: rms_norm(values, attn_gain), my_tokens)
    grad_tokens = grad_residual + attn_norm_back(grad_norm_q + grad_norm_k + grad_norm_v)[0]
    grad_buffer = (
        jnp.zeros((blocks, block_rows, feature_width), jnp.float32)
        .at[my_blocks]
        .set(grad_tokens.reshape(per_member, block_rows, feature_width))
    )
    grad_returned = lax.psum_scatter(
        grad_buffer.astype(jnp.bfloat16), "group", scatter_dimension=0, tiled=True
    ).astype(jnp.float32)
    input_grad = grad_returned.reshape(row_count, feature_width).astype(jnp.bfloat16)
    pairs = [
        (query_a, query_b),
        (key_a, key_b),
        (value_a, value_b),
        (out_a, out_b),
        (gate_a, gate_b),
        (up_a, up_b),
        (down_a, down_b),
    ]
    flat_grads = jnp.concatenate(
        [partial_piece.reshape(-1) for pair_grads in pairs for partial_piece in pair_grads]
    )
    grad_shard = lax.psum_scatter(flat_grads, ("dp", "group"), scatter_dimension=0, tiled=True)
    shard_count = grad_shard.shape[0]
    shard_start = lax.axis_index(("dp", "group")) * shard_count
    current = lax.dynamic_slice_in_dim(adapters, shard_start, shard_count).astype(jnp.float32)
    first_moment = BETA_ONE * moment1 + (1.0 - BETA_ONE) * grad_shard
    second_moment = BETA_TWO * moment2 + (1.0 - BETA_TWO) * grad_shard * grad_shard
    first_fix = first_moment / (1.0 - BETA_ONE**update_count)
    second_fix = second_moment / (1.0 - BETA_TWO**update_count)
    updated = current - LEARN_RATE * (
        first_fix / (jnp.sqrt(second_fix) + ADAM_EPS) + WEIGHT_DECAY * current
    )
    adapters_new = lax.all_gather(updated.astype(jnp.bfloat16), ("dp", "group"), axis=0, tiled=True)
    return (layer_out, input_grad, grad_shard, first_moment, second_moment, adapters_new)


def solution(mesh):
    in_specs = (
        P(("dp", "group"), None),
        P(("dp", "group"), None),
        P("dp"),
        P("dp", None),
        P("dp", None),
        P("dp", None),
        P(),
        P(),
        P(),
        P(),
        P(),
        P(),
        P(),
        P(),
        P(),
        P(),
        P(),
        P(),
        P(),
        P(("dp", "group")),
        P(("dp", "group")),
    )
    out_specs = (
        P(("dp", "group"), None),
        P(("dp", "group"), None),
        P(("dp", "group")),
        P(("dp", "group")),
        P(("dp", "group")),
        P(),
    )
    return jax.shard_map(
        per_device, mesh=mesh, in_specs=in_specs, out_specs=out_specs, check_vma=False
    )
```

profile of v0, /device:TPU:0, one launch (start us, length us, event | category | flops | bytes accessed | tf_op | source)
XLA Modules:
  0.0 1332.0 jit_solution(11367449435150586054)
XLA Ops:
  15.7 31.0 %all-gather.6.cloned.1.call-done = bf16[2048,1024]{1,0:T(8,128)(2,1)} async-done(((bf16[512,1024]{1,0:T(8,128)(2,1)}), bf16[2048,1024]{1,0:T(8,128)(2,1)}) %all-gather.6.cloned.1.call-update) | async-done | bytes 4194320 | tf_op jit(solution)/shard_map/all_gather | solution.py:222
  106.0 7.4 fusion.142
  119.3 35.7 %all-gather.10.cloned.1.call-done = bf16[2048,1024]{1,0:T(8,128)(2,1)} async-done(((bf16[512,1024]{1,0:T(8,128)(2,1)}), bf16[2048,1024]{1,0:T(8,128)(2,1)}) %all-gather.10.cloned.1.call-update) | async-done | bytes 4194320 | tf_op jit(solution)/shard_map/all_gather | solution.py:287
  154.9 238.9 %while.30 = (s32[]{:T(128)}, bf16[16,512,64]{1,2,0:T(8,128)(2,1)}, f32[16,512]{1,0:T(8,128)}, s32[16]{0:T(128)S(1)}, bf16[512,1024]{1,0:T(8,128)(2,1)}, /*index=...) while((s32[]{:T(128)}, bf16[16,512,64]{1,2,0:T(8,128)(2,1)}, ...), condition=%wide.region_10.11_spmd.clone.clone, body=%wide.region_7.10_spmd.clone.sunk.clone | while | flops 281017856 | bytes 30714648 | solution.py:147
  402.8 7.3 fusion.140
  410.1 6.7 fusion.139
  421.4 11.8 fusion.45
  437.2 7.1 fusion.143
  445.6 7.2 fusion.144
  460.8 356.0 %while.31 = (s32[]{:T(128)}, f32[16,512,64]{1,2,0:T(8,128)}, bf16[16,2048,64]{1,2,0:T(8,128)(2,1)}, bf16[16,2048,64]{1,2,0:T(8,128)(2,1)}, s32[16]{0:T(128)S(1)}...) while((s32[]{:T(128)}, f32[16,512,64]{1,2,0:T(8,128)}, ...), condition=%wide.region_17.18_spmd.clone.clone, body=%wide.region_15.17_spmd.clone.sunk.clone | while | flops 684883456 | bytes 51546936 | solution.py:184
  469.6 6.0 multiply_reduce_fusion.9
  491.9 6.0 multiply_reduce_fusion.9
  514.2 6.0 multiply_reduce_fusion.9
  536.4 6.0 multiply_reduce_fusion.9
  558.7 6.0 multiply_reduce_fusion.9
  580.9 6.0 multiply_reduce_fusion.9
  625.4 6.0 multiply_reduce_fusion.9
  669.8 6.0 multiply_reduce_fusion.9
  692.1 6.0 multiply_reduce_fusion.9
  758.8 6.0 multiply_reduce_fusion.9
  781.1 6.0 multiply_reduce_fusion.9
  803.4 6.0 multiply_reduce_fusion.9
  833.9 27.6 %reduce-scatter.7.cloned.1.call-done = bf16[512,1024]{0,1:T(8,128)(2,1)} async-done(((bf16[2048,1024]{0,1:T(8,128)(2,1)}), bf16[512,1024]{0,1:T(8,128)(2,1)}) %reduce-scatter.7.cloned.1.call-update) | async-done | bytes 1048592 | tf_op jit(solution)/shard_map/reduce_scatter | solution.py:373
  874.3 34.4 %reduce-scatter.9.cloned.1.call-done = bf16[512,1024]{0,1:T(8,128)(2,1)} async-done(((bf16[2048,1024]{0,1:T(8,128)(2,1)}), bf16[512,1024]{0,1:T(8,128)(2,1)}) %reduce-scatter.9.cloned.1.call-update) | async-done | bytes 1048592 | tf_op jit(solution)/shard_map/reduce_scatter | solution.py:376
  929.2 225.0 %all-reduce.7.cloned.1.call-done = f32[3014656]{0:T(1024)} async-done(((f32[3014656]{0:T(1024)}), f32[3014656]{0:T(1024)}) %all-reduce.7.cloned.1.call-update) | async-done | bytes 12058640
  1156.5 8.3 fusion.141
  1174.5 6.1 convert_element_type.208
  1201.6 6.2 convert_element_type.232
  1207.8 16.4 %all-gather.14.cloned.1.call-done = bf16[3014656]{0:T(1024)(128)(2,1)} async-done(((bf16[94208]{0:T(1024)(128)(2,1)}), bf16[3014656]{0:T(1024)(128)(2,1)}) %all-gather.14.cloned.1.call-update) | async-done | bytes 6029328 | tf_op jit(solution)/shard_map/all_gather | solution.py:448
  1224.2 46.6 %reduce-scatter.5.cloned.1.call-done = bf16[4,128,1024]{2,1,0:T(8,128)(2,1)} async-done(((bf16[16,128,1024]{2,1,0:T(8,128)(2,1)}), bf16[4,128,1024]{2,1,0:T(8,128)(2,1)}) %reduce-scatter.5.cloned.1.call-update) | async-done | bytes 1048592 | tf_op jit(solution)/shard_map/reduce_scatter | solution.py:314
  1270.8 47.6 %reduce-scatter.11.cloned.1.call-done = bf16[4,128,1024]{2,1,0:T(8,128)(2,1)} async-done(((bf16[16,128,1024]{2,1,0:T(8,128)(2,1)}), bf16[4,128,1024]{2,1,0:T(8,128)(2,1)}) %reduce-scatter.11.cloned.1.call-update) | async-done | bytes 1048592 | tf_op jit(solution)/shard_map/reduce_scatter | solution.py:421
  1318.5 6.4 copy.101
  (769 shorter events, 618.8 us)
Async XLA Ops:
  7.2 388.6 %copy-start = (bf16[1024,1024]{1,0:T(8,128)(2,1)S(1)}, bf16[1024,1024]{1,0:T(8,128)(2,1)}, u32[]{:S(2)}) copy-start(bf16[1024,1024]{1,0:T(8,128)(2,1)} %param.39) | copy-start | bytes 6291460
  7.2 39.6 %all-gather.6.cloned.1.call-start = ((), (), s32[]{:S(2)}) async-start(), calls=%async_computation.4 | async-start | bytes 5242880 | tf_op jit(solution)/shard_map/all_gather | solution.py:222
  7.9 92.4 %all-gather.12.cloned.1.call-start = ((), (), s32[]{:S(2)}) async-start(), calls=%async_computation.8 | async-start | bytes 5242880 | tf_op jit(solution)/shard_map/all_gather | solution.py:223
  8.7 110.6 %all-gather.8.cloned.1.call-start = ((), (), s32[]{:S(2)}) async-start(), calls=%async_computation.5 | async-start | bytes 5242880 | tf_op jit(solution)/shard_map/all_gather | solution.py:286
  10.9 39.8 %copy-start.89 = (f32[1024]{0:T(1024)}, f32[1024]{0:T(1024)S(1)}, u32[]{:S(2)}) copy-start(f32[1024]{0:T(1024)S(1)} %convert_element_type.186) | copy-start | bytes 12292
  11.3 43.0 %copy-start.38 = (bf16[128,1024]{1,0:T(8,128)(2,1)}, bf16[128,1024]{1,0:T(8,128)(2,1)S(1)}, u32[]{:S(2)}) copy-start(bf16[128,1024]{1,0:T(8,128)(2,1)S(1)} %slice.213) | copy-start | bytes 786436
  13.6 64.9 %copy-start.101 = (s32[512]{0:T(512)}, s32[512]{0:T(512)S(1)}, u32[]{:S(2)}) copy-start(s32[512]{0:T(512)S(1)} %dynamic_slice.61) | copy-start | bytes 6148
  15.7 57.2 %copy-start.47 = (f32[512,32]{0,1:T(8,128)}, f32[512,32]{0,1:T(8,128)S(1)}, u32[]{:S(2)}) copy-start(f32[512,32]{0,1:T(8,128)S(1)} %get-tuple-element.399) | copy-start | bytes 196612
  15.7 57.2 %copy-start.49 = (f32[512,32]{0,1:T(8,128)}, f32[512,32]{0,1:T(8,128)S(1)}, u32[]{:S(2)}) copy-start(f32[512,32]{0,1:T(8,128)S(1)} %get-tuple-element.400) | copy-start | bytes 196612
  49.7 347.3 %copy-start.10 = (bf16[4,128,1024]{2,1,0:T(8,128)(2,1)}, bf16[4,128,1024]{2,1,0:T(8,128)(2,1)S(1)}, u32[]{:S(2)}) copy-start(bf16[4,128,1024]{2,1,0:T(8,128)(2,1)S(1)} %gather_fusion) | copy-start | bytes 3145732
  77.4 77.5 %all-gather.10.cloned.1.call-start = ((), (), s32[]{:S(2)}) async-start(), calls=%async_computation.6 | async-start | bytes 5242880 | tf_op jit(solution)/shard_map/all_gather | solution.py:287
  85.1 776.5 %reduce-scatter.7.cloned.1.call-start = ((), (), s32[]{:S(2)}) async-start(), calls=%async_computation.9 | async-start | bytes 5242880 | tf_op jit(solution)/shard_map/reduce_scatter | solution.py:373
  113.4 41.5 %copy-start.88 = (f32[2,16]{1,0:T(2,128)S(1)}, f32[2,16]{1,0:T(2,128)}, u32[]{:S(2)}) copy-start(f32[2,16]{1,0:T(2,128)} %param.35) | copy-start | bytes 388
  397.7 58.4 %copy-start.8 = (f32[512,1024]{1,0:T(8,128)}, f32[512,1024]{1,0:T(8,128)S(1)}, u32[]{:S(2)}) copy-start(f32[512,1024]{1,0:T(8,128)S(1)} %get-tuple-element.402) | copy-start | bytes 6291460
  397.8 12.3 slice-start.2
  398.4 11.6 copy-start.20
  401.3 15.6 %copy-start.51 = (bf16[512,128]{1,0:T(8,128)(2,1)}, bf16[512,128]{1,0:T(8,128)(2,1)S(1)}, u32[]{:S(2)}) copy-start(bf16[512,128]{1,0:T(8,128)(2,1)S(1)} %fusion.79) | copy-start | bytes 393220
  402.8 18.7 %copy-start.86 = (bf16[512,128]{1,0:T(8,128)(2,1)}, bf16[512,128]{1,0:T(8,128)(2,1)S(1)}, u32[]{:S(2)}) copy-start(bf16[512,128]{1,0:T(8,128)(2,1)S(1)} %fusion.78) | copy-start | bytes 393220
  402.8 18.6 %slice-start = ((s8[8388608]{0:T(1024)(128)(4,1)}), s8[4194304]{0:T(1024)(128)(4,1)S(1)}, s32[]{:S(2)}) async-start(s8[8388608]{0:T(1024)(128)(4,1)} %bitcast.333), calls=%async_computation.14 | async-start | bytes 8388608
  437.1 15.6 %copy-start.66 = (bf16[512,128]{1,0:T(8,128)(2,1)}, bf16[512,128]{1,0:T(8,128)(2,1)S(1)}, u32[]{:S(2)}) copy-start(bf16[512,128]{1,0:T(8,128)(2,1)S(1)} %fusion.81) | copy-start | bytes 393220
  816.9 91.8 %reduce-scatter.9.cloned.1.call-start = ((), (), s32[]{:S(2)}) async-start(), calls=%async_computation.10 | async-start | bytes 5242880 | tf_op jit(solution)/shard_map/reduce_scatter | solution.py:376
  817.5 336.7 %all-reduce.7.cloned.1.call-start = ((), (), s32[]{:S(2)}) async-start(), calls=%async_computation.13 | async-start | bytes 24117248
  832.7 30.4 %copy-start.68 = (bf16[512,128]{1,0:T(8,128)(2,1)}, bf16[512,128]{1,0:T(8,128)(2,1)S(1)}, u32[]{:S(2)}) copy-start(bf16[512,128]{1,0:T(8,128)(2,1)S(1)} %fusion.80) | copy-start | bytes 393220
  833.0 30.0 %copy-start.48 = (f32[512,32]{0,1:T(8,128)S(1)}, f32[512,32]{0,1:T(8,128)}, u32[]{:S(2)}) copy-start(f32[512,32]{0,1:T(8,128)} %copy-done.47) | copy-start | bytes 196612
  833.0 30.0 %copy-start.50 = (f32[512,32]{0,1:T(8,128)S(1)}, f32[512,32]{0,1:T(8,128)}, u32[]{:S(2)}) copy-start(f32[512,32]{0,1:T(8,128)} %copy-done.49) | copy-start | bytes 196612
  871.8 36.8 %copy-start.58 = (bf16[512,128]{1,0:T(8,128)(2,1)S(1)}, bf16[512,128]{1,0:T(8,128)(2,1)}, u32[]{:S(2)}) copy-start(bf16[512,128]{1,0:T(8,128)(2,1)} %copy-done.57) | copy-start | bytes 393220
  873.0 37.5 %copy-start.37 = (f32[16,8,8,128]{3,1,2,0:T(8,128)S(1)}, f32[16,8,8,128]{3,1,2,0:T(8,128)}, u32[]{:S(2)}) copy-start(f32[16,8,8,128]{3,1,2,0:T(8,128)} %copy.51) | copy-start | bytes 1572868
  929.1 225.1 %copy-start.76 = (f32[94208]{0:T(1024)S(1)}, f32[94208]{0:T(1024)}, u32[]{:S(2)}) copy-start(f32[94208]{0:T(1024)} %param.45) | copy-start | bytes 1130500
  929.1 225.1 %copy-start.77 = (f32[94208]{0:T(1024)S(1)}, f32[94208]{0:T(1024)}, u32[]{:S(2)}) copy-start(f32[94208]{0:T(1024)} %param.44) | copy-start | bytes 1130500
  929.1 295.1 %all-gather.14.cloned.1.call-start = ((), (), s32[]{:S(2)}) async-start(), calls=%async_computation.12 | async-start | bytes 6217728 | tf_op jit(solution)/shard_map/all_gather | solution.py:448
  1156.4 114.4 %reduce-scatter.5.cloned.1.call-start = ((), (), s32[]{:S(2)}) async-start(), calls=%async_computation.7 | async-start | bytes 5242880 | tf_op jit(solution)/shard_map/reduce_scatter | solution.py:314
  1180.6 137.9 %reduce-scatter.11.cloned.1.call-start = ((), (), s32[]{:S(2)}) async-start(), calls=%async_computation.11 | async-start | bytes 5242880 | tf_op jit(solution)/shard_map/reduce_scatter | solution.py:421
  (145 other events, 461.2 us)
Sparse Core Ops, SparseCore 0:
  9.6 37.1 all-gather.5
  48.3 34.4 all-gather.11
  84.4 34.4 all-gather.7
  120.4 34.5 all-gather.9
  817.0 44.4 reduce-scatter.6
  864.1 44.5 reduce-scatter.8
  929.2 224.8 all-reduce.6
  1157.0 67.1 all-gather.13
  1227.3 43.4 reduce-scatter.4
  1274.0 44.4 reduce-scatter.10
where the time goes:
time: 1350 us; the launch traced here: 1330 us
  matrix products  535 us (40%)
  waiting for transfers between devices  466 us (35%)
  local copies, waits for them, and re-layouts  174 us (13%)
  loops' own time  86.6 us (6%)
  other arithmetic  52 us (4%)
  between operations  16.2 us (1%)
    dot_general x69, matrix products, contract_columns(): lax.dot_general(left, right, (((1,), (1,)), ((), ())), preferred_element_...  272 us
    unnamed x11, waiting for transfers between devices  227 us
    dot_general x46, matrix products, contract_leading_rows(): lax.dot_general(left, right, (((0,), (0,)), ((), ())), preferred_element_...  88.2 us
    dot_general x16, matrix products, attend_one_head(): jnp.dot(prob_low, head_slice(value_all, head_index, head_width), preferre...  64.3 us
    reduce_scatter x1, waiting for transfers between devices, per_device(): lax.psum_scatter(grad_buffer.astype(jnp.bfloat16), 'group', scatter_dimen...  47.6 us
    reduce_scatter x1, waiting for transfers between devices, per_device(): lax.psum_scatter(out_buffer.astype(jnp.bfloat16), 'group', scatter_dimens...  46.6 us
    another operation x1, loops' own time, query_pass(): results = lax.map(query_one_head, jnp.arange(head_count))  44.9 us
    dot_general x16, matrix products, query_one_head(): jnp.dot(grad_score, key_head, preferred_element_type=jnp.float32)  42.2 us
  transfers between devices with their start and end apart: 10, of which 8 were waited for; matrix products, arithmetic and copies ran while one was open for 11% of the time, Pallas kernels for 0%

commit v1 on v0

--- a/solution.py
+++ b/solution.py
@@ -1,6 +1,10 @@
+import functools
+
 import jax
 import jax.numpy as jnp
 from jax import lax
+from jax.experimental import pallas as pl
+from jax.experimental.pallas import tpu as pltpu
 from jax.sharding import PartitionSpec as P
 
 RANK = 16
@@ -106,88 +110,305 @@
     return (grad_in, grad_a, grad_up_factor)
 
 
-def head_slice(array, head_index, head_width):
-    return lax.dynamic_slice_in_dim(array, head_index * head_width, head_width, 1)
-
-
-def to_columns(stacked):
-    return jnp.moveaxis(stacked, 0, 1).reshape(stacked.shape[1], -1)
-
-
-def logits(first_rows, second_rows, bias_pair, same_seq, same_var, head_width):
-    scores = contract_columns(first_rows, second_rows) * head_width ** (-0.5)
-    scores = scores + jnp.where(same_var, bias_pair[0], bias_pair[1])
-    return jnp.where(same_seq, scores, MASKED)
-
-
-def attend(query_low, key_all, value_all, attn_bias, same_seq, same_var, head_width):
-    head_count = query_low.shape[1] // head_width
-
-    def attend_one_head(head_index):
-        bias_pair = lax.dynamic_index_in_dim(attn_bias, head_index, 1, keepdims=False)
-        scores = logits(
-            head_slice(query_low, head_index, head_width),
-            head_slice(key_all, head_index, head_width),
-            bias_pair,
-            same_seq,
-            same_var,
-            head_width,
+VARIATES = 4
+VMEM_LIMIT = 56 * 1024 * 1024
+EXACT_PARTS = 3
+
+
+def contract_last(left, right):
+    return lax.dot_general(
+        left, right, (((1,), (1,)), ((), ())), preferred_element_type=jnp.float32
+    )
+
+
+def exact_parts(values):
+    parts = []
+    for _ in range(EXACT_PARTS):
+        part = values.astype(jnp.bfloat16).astype(jnp.float32)
+        parts.append(part)
+        values = values - part
+    return parts
+
+
+def spread_parts(column, parts, first):
+    result = jnp.zeros(column.shape, jnp.float32)
+    for index, part in enumerate(parts):
+        result = jnp.where(column == first + index, part, result)
+    return result
+
+
+def query_extension(bias_ref, head, query_var, query_seg, column, segments):
+    same = exact_parts(jnp.full((1, column.shape[1]), bias_ref[0, head], jnp.float32))
+    other = exact_parts(jnp.full((1, column.shape[1]), bias_ref[1, head], jnp.float32))
+    is_same = (column % VARIATES) == query_var
+    result = jnp.zeros(column.shape, jnp.float32)
+    for index in range(EXACT_PARTS):
+        here = (column // VARIATES) == index
+        result = jnp.where(here, jnp.where(is_same, same[index], other[index]), result)
+    seg_column = column - EXACT_PARTS * VARIATES
+    apart = (seg_column >= 0) & (seg_column < segments) & (seg_column != query_seg)
+    return jnp.where(apart, MASKED, result)
+
+
+def key_extension(key_var, key_seg, column, segments):
+    seg_column = column - EXACT_PARTS * VARIATES
+    one = (column < EXACT_PARTS * VARIATES) & ((column % VARIATES) == key_var)
+    one = one | ((seg_column >= 0) & (seg_column < segments) & (seg_column == key_seg))
+    one = one | ((seg_column >= segments) & (seg_column < segments + EXACT_PARTS))
+    return jnp.where(one, 1.0, 0.0)
+
+
+def attend_kernel(key_blocks, segments, width, bias_ref, query_ref, qmeta_ref, *refs):
+    key_refs, value_refs, kmeta_refs = (
+        refs[:key_blocks],
+        refs[key_blocks : 2 * key_blocks],
+        refs[2 * key_blocks : 3 * key_blocks],
+    )
+    out_ref, total_ref = refs[3 * key_blocks :]
+    pair = pl.program_id(0)
+    rows, lanes = query_ref.shape
+    lane = lax.broadcasted_iota(jnp.int32, (rows, lanes), 1)
+    column = lane % width
+    scaled = query_ref[...].astype(jnp.float32) * width ** (-0.5)
+    results = []
+    for head in range(lanes // width):
+        inside = (lane // width) == head
+        extension = query_extension(
+            bias_ref,
+            pair * (lanes // width) + head,
+            qmeta_ref[:, 0:1],
+            qmeta_ref[:, 1:2],
+            column,
+            segments,
         )
-        row_max = jnp.max(scores, axis=1, keepdims=True)
-        exp_score = jnp.exp(scores - row_max)
-        exp_sum = jnp.sum(exp_score, axis=1, keepdims=True)
-        prob_low = (exp_score / exp_sum).astype(jnp.bfloat16)
-        head_out = jnp.dot(
-            prob_low,
-            head_slice(value_all, head_index, head_width),
-            preferred_element_type=jnp.float32,
+        left = jnp.where(inside, scaled, extension).astype(jnp.bfloat16)
+        total = jnp.zeros((rows, lanes), jnp.float32)
+        for block in range(key_blocks):
+            key_side = key_extension(
+                kmeta_refs[block][:, 0:1], kmeta_refs[block][:, 1:2], column, segments
+            )
+            right = jnp.where(inside, key_refs[block][...].astype(jnp.float32), key_side)
+            scores = contract_last(left, right.astype(jnp.bfloat16))
+            weights = jnp.exp(scores).astype(jnp.bfloat16)
+            values = jnp.where(inside, value_refs[block][...].astype(jnp.float32), 1.0)
+            total = total + jnp.dot(
+                weights, values.astype(jnp.bfloat16), preferred_element_type=jnp.float32
+            )
+        results.append(total)
+    first = (lane // width) == 0
+    numerator = jnp.where(first, results[0], results[1])
+    crossed = jnp.where(first, results[1], results[0])
+    out_ref[...] = (numerator / pltpu.roll(crossed, width, 1)).astype(jnp.bfloat16)
+    total_ref[...] = jnp.log(crossed)
+
+
+def lane_block(rows, lanes):
+    return pl.BlockSpec((rows, lanes), lambda pair: (0, pair))
+
+
+def whole_block(shape):
+    return pl.BlockSpec(shape, lambda pair: (0,) * len(shape))
+
+
+def attend(attn_bias, query_low, query_meta, keys, values, key_metas, segments, width):
+    rows, features = query_low.shape
+    lanes = 2 * width
+    count = len(keys)
+    flops = 4 * rows * rows * count * features
+    return pl.pallas_call(
+        functools.partial(attend_kernel, count, segments, width),
+        grid=(features // lanes,),
+        in_specs=[
+            pl.BlockSpec(memory_space=pltpu.SMEM),
+            lane_block(rows, lanes),
+            whole_block(query_meta.shape),
+        ]
+        + [lane_block(rows, lanes)] * (2 * count)
+        + [whole_block(query_meta.shape)] * count,
+        out_specs=[lane_block(rows, lanes)] * 2,
+        out_shape=[
+            jax.ShapeDtypeStruct((rows, features), jnp.bfloat16),
+            jax.ShapeDtypeStruct((rows, features), jnp.float32),
+        ],
+        compiler_params=pltpu.CompilerParams(vmem_limit_bytes=VMEM_LIMIT),
+        cost_estimate=pl.CostEstimate(
+            flops=flops, bytes_accessed=12 * rows * features, transcendentals=0
+        ),
+        name="attend",
+    )(attn_bias, query_low, query_meta, *keys, *values, *key_metas)
+
+
+def attend_back_kernel(
+    key_blocks,
+    segments,
+    width,
+    bias_ref,
+    query_ref,
+    qmeta_ref,
+    total_ref,
+    attended_ref,
+    grad_ref,
+    *refs,
+):
+    key_refs, value_refs, kmeta_refs = (
+        refs[:key_blocks],
+        refs[key_blocks : 2 * key_blocks],
+        refs[2 * key_blocks : 3 * key_blocks],
+    )
+    grad_query_ref = refs[3 * key_blocks]
+    grad_key_refs = refs[3 * key_blocks + 1 : 4 * key_blocks + 1]
+    grad_value_refs = refs[4 * key_blocks + 1 :]
+    pair = pl.program_id(0)
+    rows, lanes = query_ref.shape
+    lane = lax.broadcasted_iota(jnp.int32, (rows, lanes), 1)
+    column = lane % width
+    ones_at = EXACT_PARTS * VARIATES + segments
+    scaled = query_ref[...].astype(jnp.float32) * width ** (-0.5)
+    scaled_low = scaled.astype(jnp.bfloat16)
+    grad_low = grad_ref[...]
+    grad = grad_low.astype(jnp.float32)
+    overlap = grad * attended_ref[...].astype(jnp.float32)
+    total_parts = exact_parts(-total_ref[...])
+    grad_query_parts = []
+    grad_keys = [[] for _ in range(key_blocks)]
+    grad_values = [[] for _ in range(key_blocks)]
+    for head in range(lanes // width):
+        inside = (lane // width) == head
+        extension = query_extension(
+            bias_ref,
+            pair * (lanes // width) + head,
+            qmeta_ref[:, 0:1],
+            qmeta_ref[:, 1:2],
+            column,
+            segments,
+        ) + spread_parts(column, total_parts, ones_at)
+        right = jnp.where(inside, scaled, extension).astype(jnp.bfloat16)
+        prob_dot = jnp.sum(jnp.where(inside, overlap, 0.0), axis=1, keepdims=True)
+        dot_side = spread_parts(column, exact_parts(-prob_dot), ones_at)
+        grad_right = jnp.where(inside, grad, dot_side).astype(jnp.bfloat16)
+        turned = jnp.zeros((width, rows), jnp.float32)
+        for block in range(key_blocks):
+            key_side = key_extension(
+                kmeta_refs[block][:, 0:1], kmeta_refs[block][:, 1:2], column, segments
+            )
+            key = key_refs[block][...]
+            left = jnp.where(inside, key.astype(jnp.float32), key_side).astype(jnp.bfloat16)
+            prob = jnp.exp(contract_last(left, right))
+            value = value_refs[block][...].astype(jnp.float32)
+            value_left = jnp.where(inside, value, key_side).astype(jnp.bfloat16)
+            grad_score = prob * contract_last(value_left, grad_right)
+            grad_score = grad_score.astype(jnp.bfloat16)
+            grad_values[block].append(
+                jnp.dot(prob.astype(jnp.bfloat16), grad_low, preferred_element_type=jnp.float32)
+            )
+            grad_keys[block].append(
+                jnp.dot(grad_score, scaled_low, preferred_element_type=jnp.float32)
+            )
+            key_turned = jnp.transpose(key)[head * width : (head + 1) * width]
+            turned = turned + jnp.dot(key_turned, grad_score, preferred_element_type=jnp.float32)
+        grad_query_parts.append(turned)
+    first = (lane // width) == 0
+    stacked = jnp.concatenate(grad_query_parts, axis=0) * width ** (-0.5)
+    grad_query_ref[...] = jnp.transpose(stacked)
+    for block in range(key_blocks):
+        grad_key_refs[block][...] = jnp.where(first, *grad_keys[block]).astype(
+            grad_key_refs[block].dtype
         )
-        return (head_out, (row_max + jnp.log(exp_sum))[:, 0])
-
-    attended_tokens, log_total = lax.map(attend_one_head, jnp.arange(head_count))
-    return (to_columns(attended_tokens), jnp.transpose(log_total))
-
-
-def query_pass(
+        grad_value_refs[block][...] = jnp.where(first, *grad_values[block]).astype(
+            grad_value_refs[block].dtype
+        )
+
+
+def attend_back(
+    attn_bias,
     query_low,
-    key_all,
-    value_all,
-    attn_bias,
-    same_seq,
-    same_var,
+    query_meta,
     log_total,
-    gradient_lowrank,
-    head_width,
+    attended_low,
+    grad_attended,
+    keys,
+    values,
+    key_metas,
+    segments,
+    width,
 ):
-    head_count = query_low.shape[1] // head_width
-
-    def query_one_head(head_index):
-        query_head = head_slice(query_low, head_index, head_width)
-        key_head = head_slice(key_all, head_index, head_width)
-        value_head = head_slice(value_all, head_index, head_width)
-        grad_head = head_slice(gradient_lowrank, head_index, head_width)
-        bias_pair = lax.dynamic_index_in_dim(attn_bias, head_index, 1, keepdims=False)
-        scores = logits(query_head, key_head, bias_pair, same_seq, same_var, head_width)
-        softmax_prob = jnp.exp(
-            scores - lax.dynamic_index_in_dim(log_total, head_index, 1, keepdims=True)
-        )
-        grad_prob = contract_columns(grad_head, value_head)
-        prob_dot = jnp.sum(softmax_prob * grad_prob, axis=1)
-        grad_score = (softmax_prob * (grad_prob - prob_dot[:, None])).astype(jnp.bfloat16)
-        grad_query = jnp.dot(
-            grad_score, key_head, preferred_element_type=jnp.float32
-        ) * head_width ** (-0.5)
-        grad_key = contract_leading_rows(grad_score, query_head) * head_width ** (-0.5)
-        grad_value = contract_leading_rows(softmax_prob.astype(jnp.bfloat16), grad_head)
-        return (grad_query, prob_dot, grad_key, grad_value)
-
-    results = lax.map(query_one_head, jnp.arange(head_count))
-    return (
-        to_columns(results[0]),
-        jnp.transpose(results[1]),
-        to_columns(results[2]),
-        to_columns(results[3]),
-    )
+    rows, features = query_low.shape
+    lanes = 2 * width
+    count = len(keys)
+    flops = 10 * rows * rows * count * features
+    full = jax.ShapeDtypeStruct((rows, features), jnp.float32)
+    low = jax.ShapeDtypeStruct((rows, features), jnp.bfloat16)
+    results = pl.pallas_call(
+        functools.partial(attend_back_kernel, count, segments, width),
+        grid=(features // lanes,),
+        in_specs=[
+            pl.BlockSpec(memory_space=pltpu.SMEM),
+            lane_block(rows, lanes),
+            whole_block(query_meta.shape),
+        ]
+        + [lane_block(rows, lanes)] * (3 + 2 * count)
+        + [whole_block(query_meta.shape)] * count,
+        out_specs=[lane_block(rows, lanes)] * (1 + 2 * count),
+        out_shape=[full] + ([full] + [low] * (count - 1)) * 2,
+        compiler_params=pltpu.CompilerParams(vmem_limit_bytes=VMEM_LIMIT),
+        cost_estimate=pl.CostEstimate(
+            flops=flops, bytes_accessed=24 * rows * features, transcendentals=0
+        ),
+        name="attend_back",
+    )(
+        attn_bias,
+        query_low,
+        query_meta,
+        log_total,
+        attended_low,
+        grad_attended,
+        *keys,
+        *values,
+        *key_metas,
+    )
+    return results[0], results[1 : 1 + count], results[1 + count :]
+
+
+def pick_rows(wanted, held, rows):
+    chosen = (wanted[:, None] == held[None, :]).astype(jnp.bfloat16)
+    return jnp.dot(chosen, rows, preferred_element_type=jnp.float32).astype(jnp.bfloat16)
+
+
+def within_half(array, shift, groups):
+    half = groups // 2
+    pairs = [
+        (base + (place + shift) % half, base + place)
+        for base in (0, half)
+        for place in range(half)
+    ]
+    return lax.ppermute(array, "group", pairs)
+
+
+def gather_half(array, groups):
+    return [array] + [within_half(array, shift, groups) for shift in range(1, groups // 2)]
+
+
+def to_other_half(array, groups):
+    half = groups // 2
+    return lax.ppermute(array, "group", [(i, (i + half) % groups) for i in range(groups)])
+
+
+def scatter_sum(array, axis_sizes):
+    for name, size in reversed(axis_sizes):
+        outer = array.shape[0] // size
+        array = array.reshape((outer, size) + array.shape[1:])
+        bit = 1
+        while bit < size:
+            index = lax.axis_index(name)
+            own = (index // bit) % 2
+            spread = array.reshape((outer, size // (2 * bit), 2) + array.shape[2:])
+            keep = lax.dynamic_index_in_dim(spread, own, 2, keepdims=False)
+            send = lax.dynamic_index_in_dim(spread, 1 - own, 2, keepdims=False)
+            got = lax.ppermute(send, name, [(i, i ^ bit) for i in range(size)])
+            array = (keep.astype(jnp.float32) + got.astype(jnp.float32)).astype(jnp.bfloat16)
+            bit *= 2
+        array = array.reshape((outer,) + array.shape[2:])
+    return array
 
 
 def per_device(
@@ -218,47 +439,112 @@
     row_count, feature_width = tokens.shape
     hidden_width = gate_weight.shape[1]
     head_width = q_gain.shape[0]
-    pack_x, pack_dy = (
-        lax.all_gather(tokens, "group", axis=0, tiled=True),
-        lax.all_gather(cotangent, "group", axis=0, tiled=True),
-    )
-    pack_count = pack_x.shape[0]
+    half_devices = groups // 2
+    half_rows = half_devices * row_count
+    pack_rows = groups * row_count
+    swap_rows = row_count // 2
+    my_half, my_place = member // half_devices, member % half_devices
+
     block_list = block_order[0]
     blocks = block_list.shape[0]
-    block_rows = pack_count // blocks
-    per_member = blocks // groups
-    my_blocks = lax.dynamic_slice_in_dim(block_list, member * per_member, per_member)
+    block_rows = pack_rows // blocks
     lengths = seq_len[0]
+    segments = lengths.shape[0]
     seq_ends = jnp.cumsum(lengths)
     seq_starts = seq_ends - lengths
-    row_index = jnp.arange(pack_count, dtype=jnp.int32)
-    segment = jnp.sum((row_index[:, None] >= seq_ends[None, :]).astype(jnp.int32), axis=1)
-    picked = (segment[:, None] == jnp.arange(lengths.shape[0], dtype=jnp.int32)[None, :]).astype(
-        jnp.int32
-    )
-    position = row_index - jnp.sum(picked * seq_starts[None, :], axis=1)
+    block_index = jnp.arange(blocks, dtype=jnp.int32)
+    work_block = jnp.sum(
+        jnp.where(block_list[None, :] == block_index[:, None], block_index[None, :], 0), axis=1
+    )
+    work_row = (
+        work_block[:, None] * block_rows + jnp.arange(block_rows, dtype=jnp.int32)[None, :]
+    ).reshape(2, half_rows)
+    long_start = jnp.sum(jnp.where(lengths == half_rows, seq_starts, 0))
+    is_long = (work_row >= long_start) & (work_row < long_start + half_rows)
+    long_half = (2 * jnp.sum(is_long[0].astype(jnp.int32)) < half_rows).astype(jnp.int32)
+    side = jnp.arange(2, dtype=jnp.int32)[:, None]
+    target = jnp.where(is_long, long_half, 1 - long_half)
+    foreign = (target != side).astype(jnp.int32)
+    foreign_rank = jnp.cumsum(foreign, axis=1) - foreign
+    kept_rank = jnp.arange(half_rows, dtype=jnp.int32)[None, :] - foreign_rank
+    moved = jnp.sum(foreign[0])
+    place = jnp.zeros_like(kept_rank)
+    offset = jnp.zeros_like(kept_rank)
+    for index in range(1, half_devices):
+        start = index * row_count - jnp.minimum(moved, index * swap_rows)
+        place = place + (kept_rank >= start)
+        offset = jnp.where(kept_rank >= start, start, offset)
+    kept_slot = side * half_rows + place * row_count + kept_rank - offset
+    foreign_place = foreign_rank // swap_rows
+    received = jnp.clip(moved - foreign_place * swap_rows, 0, swap_rows)
+    foreign_slot = (
+        (1 - side) * half_rows
+        + foreign_place * row_count
+        + row_count
+        - received
+        + foreign_rank % swap_rows
+    )
+    slot = jnp.where(foreign == 1, foreign_slot, kept_slot)
+    row_range = jnp.arange(row_count, dtype=jnp.int32)
+    order = [(my_place + shift) % half_devices for shift in range(half_devices)]
+    half_ids = jnp.concatenate(
+        [my_half * half_rows + place_of * row_count + row_range for place_of in order]
+    )
+    my_slots = half_ids[:row_count]
+    away_ids = jnp.concatenate(
+        [
+            (1 - my_half) * half_rows + place_of * row_count + row_range[swap_rows:]
+            for place_of in order
+        ]
+    )
+    slot_mine = lax.dynamic_index_in_dim(slot, my_half, 0, keepdims=False).reshape(
+        half_devices, row_count
+    )
+    held_slots = jnp.concatenate(
+        [lax.dynamic_index_in_dim(slot_mine, place_of, 0, keepdims=False) for place_of in order]
+    )
+    slot_here = held_slots[:row_count]
+    wanted = jnp.concatenate([my_slots, away_ids[:swap_rows]])
+
+    def bring(rows):
+        picked = pick_rows(wanted, held_slots, jnp.concatenate(gather_half(rows, groups)))
+        arrived = to_other_half(picked[row_count:], groups)
+        return jnp.concatenate(
+            [picked[:swap_rows], picked[swap_rows:row_count] + arrived]
+        )
+
+    returned_ids = jnp.concatenate([half_ids, away_ids])
+
+    def send_back(rows):
+        back = to_other_half(rows[swap_rows:], groups)
+        held = gather_half(rows, groups) + gather_half(back, groups)
+        return pick_rows(slot_here, returned_ids, jnp.concatenate(held))
+
+    facts = jnp.stack(
+        [
+            work_row.reshape(-1) // block_rows,
+            work_row.reshape(-1) % block_rows,
+            variate,
+        ],
+        axis=1,
+    ).astype(jnp.bfloat16)
+    chosen = (half_ids[:, None] == slot.reshape(-1)[None, :]).astype(jnp.bfloat16)
+    facts = jnp.dot(chosen, facts, preferred_element_type=jnp.float32).astype(jnp.int32)
+    half_row = facts[:, 0] * block_rows + facts[:, 1]
+    segment = jnp.sum((half_row[:, None] >= seq_ends[None, :]).astype(jnp.int32), axis=1)
+    picked = (segment[:, None] == jnp.arange(segments, dtype=jnp.int32)[None, :]).astype(jnp.int32)
+    position = half_row - jnp.sum(picked * seq_starts[None, :], axis=1)
     row_adapter = jnp.sum(picked * seq_adapter[0][None, :], axis=1)
-    variate_work = variate.reshape(blocks, block_rows)[block_list].reshape(pack_count)
-    first_row = member * row_count
-    seg_mine = lax.dynamic_slice_in_dim(segment, first_row, row_count)
-    var_mine = lax.dynamic_slice_in_dim(variate_work, first_row, row_count)
-    pos_mine = lax.dynamic_slice_in_dim(position, first_row, row_count)
-    adapter_mine = lax.dynamic_slice_in_dim(row_adapter, first_row, row_count)
-    same_seq = seg_mine[:, None] == segment[None, :]
-    same_var = var_mine[:, None] == variate_work[None, :]
+    meta = jnp.stack([facts[:, 2], segment], axis=1)
+    key_metas = [meta[i * row_count : (i + 1) * row_count] for i in range(half_devices)]
     columns = ADAPTERS * RANK
     adapter_selector_mask = (
-        adapter_mine[:, None] == (jnp.arange(columns, dtype=jnp.int32) // RANK)[None, :]
+        row_adapter[:row_count, None] == (jnp.arange(columns, dtype=jnp.int32) // RANK)[None, :]
     ).astype(jnp.float32)
-    cos_table, sin_table = rope_tables(pos_mine, head_width)
-    my_tokens = (
-        pack_x.reshape(blocks, block_rows, feature_width)[my_blocks]
-        .reshape(row_count, feature_width)
-        .astype(jnp.float32)
-    )
-    my_grads = pack_dy.reshape(blocks, block_rows, feature_width)[my_blocks].reshape(
-        row_count, feature_width
-    )
+    cos_table, sin_table = rope_tables(position[:row_count], head_width)
+
+    my_tokens = bring(tokens).astype(jnp.float32)
+    my_grads = bring(cotangent)
     shapes = [(feature_width, feature_width)] * 4 + [
         (feature_width, hidden_width),
         (feature_width, hidden_width),
@@ -282,14 +568,11 @@
     key_low = shape_heads(key_preactivation, k_gain, cos_table, sin_table, head_width).astype(
         jnp.bfloat16
     )
-    key_all, value_all = (
-        lax.all_gather(key_low, "group", axis=0, tiled=True),
-        lax.all_gather(value_lowrank, "group", axis=0, tiled=True),
-    )
-    attended_tokens, log_total = attend(
-        query_low, key_all, value_all, attn_bias, same_seq, same_var, head_width
-    )
-    attended_low = attended_tokens.astype(jnp.bfloat16)
+    keys = gather_half(key_low, groups)
+    values = gather_half(value_lowrank, groups)
+    attended_low, log_total = attend(
+        attn_bias, query_low, key_metas[0], keys, values, key_metas, segments, head_width
+    )
     attention_output, out_inner = project(
         attended_low, output_weight, partial_pieces[3], adapter_selector_mask
     )
@@ -306,15 +589,7 @@
         activated_hidden, down_weight, partial_pieces[6], adapter_selector_mask
     )
     final_result = residual_stream + ffn_out
-    out_buffer = (
-        jnp.zeros((blocks, block_rows, feature_width), jnp.float32)
-        .at[my_blocks]
-        .set(final_result.reshape(per_member, block_rows, feature_width))
-    )
-    returned = lax.psum_scatter(
-        out_buffer.astype(jnp.bfloat16), "group", scatter_dimension=0, tiled=True
-    ).astype(jnp.float32)
-    layer_out = returned.reshape(row_count, feature_width).astype(jnp.bfloat16)
+    layer_out = send_back(final_result.astype(jnp.bfloat16))
     grad_act, down_a, down_b = project_back(
         my_grads,
         activated_hidden,
@@ -358,25 +633,26 @@
         adapter_selector_mask,
     )
     grad_attended_low = grad_attended.astype(jnp.bfloat16)
-    grad_query, prob_dot, grad_key_pack, grad_value_pack = query_pass(
+    grad_query, grad_keys, grad_values = attend_back(
+        attn_bias,
         query_low,
-        key_all,
-        value_all,
-        attn_bias,
-        same_seq,
-        same_var,
+        key_metas[0],
         log_total,
+        attended_low,
         grad_attended_low,
+        keys,
+        values,
+        key_metas,
+        segments,
         head_width,
     )
-    grad_key, grad_value = (
-        lax.psum_scatter(
-            grad_key_pack.astype(jnp.bfloat16), "group", scatter_dimension=0, tiled=True
-        ).astype(jnp.float32),
-        lax.psum_scatter(
-            grad_value_pack.astype(jnp.bfloat16), "group", scatter_dimension=0, tiled=True
-        ).astype(jnp.float32),
-    )
+    grad_key, grad_value = grad_keys[0], grad_values[0]
+    for shift in range(1, half_devices):
+        back_shift = half_devices - shift
+        grad_key = grad_key + within_half(grad_keys[shift], back_shift, groups).astype(jnp.float32)
+        grad_value = grad_value + within_half(grad_values[shift], back_shift, groups).astype(
+            jnp.float32
+        )
     _, query_head_back = jax.vjp(
         lambda values: shape_heads(values, q_gain, cos_table, sin_table, head_width),
         query_preactivation,
@@ -413,15 +689,7 @@
     )
     _, attn_norm_back = jax.vjp(lambda values: rms_norm(values, attn_gain), my_tokens)
     grad_tokens = grad_residual + attn_norm_back(grad_norm_q + grad_norm_k + grad_norm_v)[0]
-    grad_buffer = (
-        jnp.zeros((blocks, block_rows, feature_width), jnp.float32)
-        .at[my_blocks]
-        .set(grad_tokens.reshape(per_member, block_rows, feature_width))
-    )
-    grad_returned = lax.psum_scatter(
-        grad_buffer.astype(jnp.bfloat16), "group", scatter_dimension=0, tiled=True
-    ).astype(jnp.float32)
-    input_grad = grad_returned.reshape(row_count, feature_width).astype(jnp.bfloat16)
+    input_grad = send_back(grad_tokens.astype(jnp.bfloat16))
     pairs = [
         (query_a, query_b),
         (key_a, key_b),
@@ -434,7 +702,10 @@
     flat_grads = jnp.concatenate(
         [partial_piece.reshape(-1) for pair_grads in pairs for partial_piece in pair_grads]
     )
-    grad_shard = lax.psum_scatter(flat_grads, ("dp", "group"), scatter_dimension=0, tiled=True)
+    axis_sizes = [("dp", lax.axis_size("dp")), ("group", groups)]
+    shards = axis_sizes[0][1] * groups
+    grad_shard = scatter_sum(flat_grads.astype(jnp.bfloat16).reshape(shards, -1), axis_sizes)
+    grad_shard = grad_shard.reshape(-1).astype(jnp.float32)
     shard_count = grad_shard.shape[0]
     shard_start = lax.axis_index(("dp", "group")) * shard_count
     current = lax.dynamic_slice_in_dim(adapters, shard_start, shard_count).astype(jnp.float32)

time: 1350 us -> 561 us (0.42)
  matrix products: 535 us -> 145 us
  waiting for transfers between devices: 466 us -> 156 us
  loops' own time: 86.6 us -> 0 us
  local copies, waits for them, and re-layouts: 174 us -> 104 us
  Pallas kernels: 0 us -> 50.6 us
  starting transfers between devices: 1.54 us -> 16.3 us
    unnamed x11 -> x1, waiting for transfers between devices: 227 us -> 0.02 us
    dot_general x69 -> x21, matrix products: 272 us -> 62.4 us  [contract_columns(): lax.dot_general(left, right, (((1,), (1,)), ((), ())), preferred_element_...]
    reduce_scatter x4 -> x0, waiting for transfers between devices: 156 us -> none  [the longest x1 47.6 us: per_device(): lax.psum_scatter(grad_buffer.astype(jnp.bfloat16), 'group', scatter_dimen...]
    ppermute x0 -> x19, waiting for transfers between devices: none -> 129 us  [the longest x5 104 us: scatter_sum(): got = lax.ppermute(send, name, [(i, i ^ bit) for i in range(size)])]
    dot_general x32 -> x5, matrix products: 106 us -> 13.6 us  [the longest x4 12.1 us: pick_rows(): jnp.dot(chosen, rows, preferred_element_type=jnp.float32)]
    another operation x2 -> x0, loops' own time: 86.6 us -> none  [the longest x1 44.9 us: query_pass(): results = lax.map(query_one_head, jnp.arange(head_count))]
    dot_general x46 -> x14, matrix products: 88.2 us -> 14.1 us  [contract_leading_rows(): lax.dot_general(left, right, (((0,), (0,)), ((), ())), preferred_element_...]
    all_gather x4 -> x0, waiting for transfers between devices: 66.7 us -> none  [the longest x1 35.7 us: per_device(): lax.all_gather(value_lowrank, 'group', axis=0, tiled=True)]
  transfers between devices with their start and end apart: 10 -> 20, of which waited for: 8 -> 9; matrix products, arithmetic and copies ran while one was open for 11% -> 25% of each run, Pallas kernels for 0% -> 0%
where the time goes in v1:
time: 561 us; the launch traced here: 551 us
  waiting for transfers between devices  156 us (28%)
  matrix products  145 us (26%)
  local copies, waits for them, and re-layouts  104 us (19%)
  other arithmetic  59.8 us (11%)
  Pallas kernels  50.6 us (9%)
  between operations  18.4 us (3%)
  starting transfers between devices  16.3 us (3%)
    ppermute x5, waiting for transfers between devices, scatter_sum(): got = lax.ppermute(send, name, [(i, i ^ bit) for i in range(size)])  104 us
    dot_general x21, matrix products, contract_columns(): lax.dot_general(left, right, (((1,), (1,)), ((), ())), preferred_element_...  62.4 us
    pallas_call x1, Pallas kernels, attend_back(): pl.pallas_call(functools.partial(attend_back_kernel, count, segments, wid...  31.2 us
    unnamed x280, local copies, waits for them, and re-layouts  29.2 us
    dot_general x7, matrix products, project(): jnp.dot(low_in, weight_matrix, preferred_element_type=jnp.float32)  28.3 us
    all_gather x1, waiting for transfers between devices, per_device(): lax.all_gather(updated.astype(jnp.bfloat16), ('dp', 'group'), axis=0, til...  26.6 us
    ppermute x4, waiting for transfers between devices, to_other_half(): lax.ppermute(array, 'group', [(i, (i + half) % groups) for i in range(gro...  25.5 us
    convert_element_type x4, other arithmetic, scatter_sum(): (keep.astype(jnp.float32) + got.astype(jnp.float32)).astype(jnp.bfloat16)  19.9 us
  transfers between devices with their start and end apart: 20, of which 9 were waited for; matrix products, arithmetic and copies ran while one was open for 25% of the time, Pallas kernels for 0%

profile of v1, /device:TPU:0, one launch (start us, length us, event | category | flops | bytes accessed | tf_op | source)
XLA Modules:
  0.0 550.5 jit_solution(14726995170795651083)
XLA Ops:
  46.9 3.4 fusion.50
  53.4 3.1 fusion.55
  58.9 7.2 %collective-permute-done.1 = bf16[256,1024]{1,0:T(8,128)(2,1)S(1)} collective-permute-done((bf16[256,1024]{1,0:T(8,128)(2,1)S(1)}, bf16[256,1024]{1,0:T(8,128)(2,1)S(1)}, u32[]{:S(2)}, u32[]{:S(2)}) %collective-permute-start.1) | collective-permute-done | bytes 524320 | tf_op jit(solution)/shard_map/ppermute | solution.py:393
  76.4 3.1 copy.82
  100.0 3.9 add_convert_fusion.4.refs_2_
  111.3 5.9 %fusion.128 = f32[512,4096]{1,0:T(8,128)} fusion(bf16[512,128]{1,0:T(8,128)(2,1)S(1)} %fusion.111, bf16[3014656]{0:T(1024)(128)(2,1)} %param.39), kind=kOutput, calls=%fused_computation.184 | convolution fusion | flops 536870912 | bytes 9568256 | tf_op jit(solution)/shard_map/dot_general | solution.py:81
  117.1 19.4 %attend.1 = (bf16[512,1024]{1,0:T(8,128)(2,1)}, f32[512,1024]{1,0:T(8,128)}) custom-call(f32[2,16]{1,0:T(2,128)} %bias_ref.3, bf16[512,1024]{1,0:T(8,128)(2,1)} %copy.87.query_ref, s32[512,2]{1,0:T(8,128)} %copy.96.qmeta_ref.refs_4_, bf16[512,1024]{1,0:T(8,128)(2,1)} %copy.88.refs_0_, bf16[512,1024]{1,0:T(8,128)(2,1)} %collective-permute-done.2.refs_1_, ...), custom_call_target="tpu_custom_call" | custom-call | flops 2147483648 | bytes 6291456 | tf_op jit(solution)/shard_map/attend/pallas_call | solution.py:218
  145.6 4.6 fusion.219
  150.2 4.6 fusion.218
  154.8 4.6 multiply_add_fusion
  159.4 4.6 multiply_add_fusion.1
  164.0 17.7 %fusion.2 = (bf16[512,4096]{1,0:T(8,128)(2,1)}, bf16[512,4096]{1,0:T(8,128)(2,1)}, bf16[512,4096]{1,0:T(8,128)(2,1)}) fusion(f32[512,4096]{1,0:T(8,128)} %multiply_add_fusion.1, f32[512,4096]{1,0:T(8,128)} %multiply_add_fusion, f32[512,4096]{1,0:T(8,128)} %fusion.128, bf16[4096,1024]{1,0:T(8,128)(2,1)} %param.38, bf16[256,1024]{1,0:T(8,128)(2,1)} %copy-done.37, ...), kind=kOutput, calls=%fused_computation.3 | convolution fusion | flops 4332716032 | bytes 47185920 | tf_op jit(solution)/shard_map/dot_general | solution.py:81
  181.7 3.9 fusion.123
  185.7 7.1 %fusion.221 = f32[512,1024]{1,0:T(8,128)S(1)} fusion(bf16[512,4096]{1,0:T(8,128)(2,1)S(1)} %copy-done.29, bf16[1024,4096]{1,0:T(8,128)(2,1)} %param.36), kind=kOutput, calls=%fused_computation.397 | convolution fusion | flops 4294967296 | bytes 14680064 | tf_op jit(solution)/shard_map/dot_general | solution.py:81
  194.1 7.2 %fusion.222 = f32[512,1024]{1,0:T(8,128)S(1)} fusion(bf16[512,4096]{1,0:T(8,128)(2,1)S(1)} %copy-done.27, bf16[1024,4096]{1,0:T(8,128)(2,1)} %param.37), kind=kOutput, calls=%fused_computation.398 | convolution fusion | flops 4294967296 | bytes 14680064 | tf_op jit(solution)/shard_map/dot_general | solution.py:81
  210.6 31.2 %attend_back.1 = (f32[512,1024]{1,0:T(8,128)}, f32[512,1024]{1,0:T(8,128)}, bf16[512,1024]{1,0:T(8,128)(2,1)}, f32[512,1024]{1,0:T(8,128)}, bf16[512,1024]{1,0:T(8,128)(2,1)}) custom-call(f32[2,16]{1,0:T(2,128)} %bias_ref.3, bf16[512,1024]{1,0:T(8,128)(2,1)} %copy.87.query_ref, s32[512,2]{1,0:T(8,128)} %copy.96.qmeta_ref.refs_4_, ...), custom_call_target="tpu_custom_call" | custom-call | flops 5368709120 | bytes 12582912 | tf_op jit(solution)/shard_map/attend_back/pallas_call | solution.py:341
  241.9 3.0 copy.91
  259.5 3.0 multiply_add_fusion.7
  287.4 11.4 %convert_element_type.312 = bf16[8,2,2,94208]{3,2,1,0:T(2,128)(2,1)} reshape(bf16[3014656]{0:T(1024)(128)(2,1)} %constant_dynamic-update-slice_fusion) | data formatting | bytes 12058624 | tf_op jit(solution)/shard_map/convert_element_type | solution.py:707
  298.7 15.1 %constant_dynamic-slice_fusion.5 = (bf16[8,2,1,94208]{3,2,1,0:T(2,128)(2,1)}, bf16[8,2,1,94208]{3,2,1,0:T(2,128)(2,1)S(1)}) fusion(bf16[8,2,2,94208]{3,2,1,0:T(2,128)(2,1)} %convert_element_type.312, s32[]{:T(128)S(6)} %select_n.215, s32[]{:T(128)S(6)} %select_n.216), kind=kLoop, calls=%fused_computation.321 | loop fusion | bytes 12058632 | tf_op jit(solution)/shard_map/jit(dynamic_index_in_dim)/dynamic_slice | solution.py:405
  313.8 4.9 copy.143
  318.7 5.8 %collective-permute-done.14 = bf16[8,2,94208]{2,0,1:T(8,128)(2,1)} collective-permute-done((bf16[8,2,94208]{2,0,1:T(8,128)(2,1)}, bf16[8,2,94208]{2,0,1:T(8,128)(2,1)}, u32[]{:S(2)}, u32[]{:S(2)}) %collective-permute-start.14) | collective-permute-done | bytes 3014688 | tf_op jit(solution)/shard_map/ppermute | solution.py:407
  324.5 7.0 %fusion.6 = bf16[8,2,94208]{2,0,1:T(8,128)(2,1)S(1)} fusion(bf16[8,2,94208]{2,0,1:T(8,128)(2,1)} %collective-permute-done.14, bf16[8,2,1,94208]{3,2,1,0:T(2,128)(2,1)} %get-tuple-element.33), kind=kLoop, calls=%fused_computation.13 | loop fusion | flops 6029312 | bytes 9043968 | tf_op jit(solution)/shard_map/convert_element_type | solution.py:408
  336.5 33.5 %collective-permute-done.15 = bf16[8,1,94208]{2,0,1:T(8,128)(2,1)S(1)} collective-permute-done((bf16[8,1,94208]{2,0,1:T(8,128)(2,1)}, bf16[8,1,94208]{2,0,1:T(8,128)(2,1)S(1)}, u32[]{:S(2)}, u32[]{:S(2)}) %collective-permute-start.15) | collective-permute-done | bytes 1507360 | tf_op jit(solution)/shard_map/ppermute | solution.py:407
  379.6 33.1 %collective-permute-done.16 = bf16[1,4,94208]{2,0,1:T(2,128)(2,1)} collective-permute-done((bf16[1,4,94208]{2,0,1:T(2,128)(2,1)}, bf16[1,4,94208]{2,0,1:T(2,128)(2,1)}, u32[]{:S(2)}, u32[]{:S(2)}) %collective-permute-start.16) | collective-permute-done | bytes 753696 | tf_op jit(solution)/shard_map/ppermute | solution.py:407
  412.7 7.8 %fusion.69 = bf16[4,94208]{1,0:T(4,128)(2,1)} fusion(bf16[1,4,94208]{2,0,1:T(2,128)(2,1)} %collective-permute-done.16, bf16[1,4,2,94208]{3,2,1,0:T(2,128)(2,1)S(1)} %reshape_reshape_reshape.4, s32[]{:T(128)S(6)} %select_n.221), kind=kLoop, calls=%fused_computation.105 | loop fusion | flops 1507328 | bytes 2260996 | tf_op jit(solution)/shard_map/convert_element_type | solution.py:408
  424.4 16.1 %collective-permute-done.17 = bf16[1,2,94208]{2,0,1:T(2,128)(2,1)} collective-permute-done((bf16[1,2,94208]{2,0,1:T(2,128)(2,1)S(1)}, bf16[1,2,94208]{2,0,1:T(2,128)(2,1)}, u32[]{:S(2)}, u32[]{:S(2)}) %collective-permute-start.17) | collective-permute-done | bytes 376864 | tf_op jit(solution)/shard_map/ppermute | solution.py:407
  445.3 15.3 %collective-permute-done.18 = bf16[1,1,94208]{2,0,1:T(2,128)(2,1)S(1)} collective-permute-done((bf16[1,1,94208]{2,0,1:T(2,128)(2,1)S(1)}, bf16[1,1,94208]{2,0,1:T(2,128)(2,1)S(1)}, u32[]{:S(2)}, u32[]{:S(2)}) %collective-permute-start.18) | collective-permute-done | bytes 188448 | tf_op jit(solution)/shard_map/ppermute | solution.py:407
  463.5 8.5 %fusion.220 = f32[512,1024]{1,0:T(8,128)S(1)} fusion(bf16[512,4096]{1,0:T(8,128)(2,1)} %get-tuple-element.32, bf16[4096,1024]{1,0:T(8,128)(2,1)} %param.38), kind=kOutput, calls=%fused_computation.396 | convolution fusion | flops 4294967296 | bytes 14680064 | tf_op jit(solution)/shard_map/dot_general | solution.py:87
  488.6 15.9 %collective-permute-done.12 = bf16[256,1024]{1,0:T(8,128)(2,1)S(1)} collective-permute-done((bf16[256,1024]{1,0:T(8,128)(2,1)S(1)}, bf16[256,1024]{1,0:T(8,128)(2,1)S(1)}, u32[]{:S(2)}, u32[]{:S(2)}) %collective-permute-start.12) | collective-permute-done | bytes 524320 | tf_op jit(solution)/shard_map/ppermute | solution.py:393
  510.2 26.6 %all-gather.2.cloned.1.call-done = bf16[3014656]{0:T(1024)(128)(2,1)} async-done(((bf16[94208]{0:T(1024)(128)(2,1)}), bf16[3014656]{0:T(1024)(128)(2,1)}) %all-gather.2.cloned.1.call-update) | async-done | bytes 6029328 | tf_op jit(solution)/shard_map/all_gather | solution.py:719
  536.8 6.4 %copy.158 = bf16[3014656]{0:T(1024)(128)(2,1)} copy(bf16[3014656]{0:T(1024)(128)(2,1)} %all-gather.2.cloned.1.call-done) | data formatting | bytes 12058624
  (470 shorter events, 187.3 us)
Async XLA Ops:
  7.2 132.3 %copy-start = (bf16[1024,1024]{1,0:T(8,128)(2,1)S(1)}, bf16[1024,1024]{1,0:T(8,128)(2,1)}, u32[]{:S(2)}) copy-start(bf16[1024,1024]{1,0:T(8,128)(2,1)} %param.35) | copy-start | bytes 6291460
  7.2 529.7 %all-gather.2.cloned.1.call-start = ((), (), s32[]{:S(2)}) async-start(), calls=%async_computation | async-start | bytes 6217728 | tf_op jit(solution)/shard_map/all_gather | solution.py:719
  7.2 39.7 %collective-permute-start = (bf16[512,1024]{1,0:T(8,128)(2,1)}, bf16[512,1024]{1,0:T(8,128)(2,1)}, u32[]{:S(2)}, u32[]{:S(2)}) collective-permute-start(bf16[512,1024]{1,0:T(8,128)(2,1)} %param.21), channel_id=1, source_target_pairs={{1,0},{0,1},{3,2},{2,3},{5,4},{4,5},{7,6},{6,7},{9,8},{8,9},{11,10... | collective-permute-start | bytes 3145736 | tf_op jit(solution)/shard_map/ppermute | solution.py:384
  7.7 45.7 %collective-permute-start.7 = (bf16[512,1024]{1,0:T(8,128)(2,1)}, bf16[512,1024]{1,0:T(8,128)(2,1)}, u32[]{:S(2)}, u32[]{:S(2)}) collective-permute-start(bf16[512,1024]{1,0:T(8,128)(2,1)} %param.22), channel_id=1, source_target_pairs={{1,0},{0,1},{3,2},{2,3},{5,4},{4,5},{7,6},{6,7},{9,8},{8,9},{11,10... | collective-permute-start | bytes 3145736 | tf_op jit(solution)/shard_map/ppermute | solution.py:384
  21.1 24.2 %copy-start.98 = (s32[512]{0:T(512)}, s32[512]{0:T(512)S(1)}, u32[]{:S(2)}) copy-start(s32[512]{0:T(512)S(1)} %iota_add_fusion.3) | copy-start | bytes 6148
  27.5 11.9 %copy-start.114 = (bf16[1024]{0:T(1024)(128)(2,1)S(1)}, bf16[1024]{0:T(1024)(128)(2,1)}, u32[]{:S(2)}) copy-start(bf16[1024]{0:T(1024)(128)(2,1)} %param.28) | copy-start | bytes 6148
  31.6 35.5 %copy-start.96 = (f32[1024]{0:T(1024)}, f32[1024]{0:T(1024)S(1)}, u32[]{:S(2)}) copy-start(f32[1024]{0:T(1024)S(1)} %convert_element_type.267) | copy-start | bytes 12292
  46.9 46.6 %copy-start.60 = (f32[512,32]{0,1:T(8,128)}, f32[512,32]{0,1:T(8,128)S(1)}, u32[]{:S(2)}) copy-start(f32[512,32]{0,1:T(8,128)S(1)} %get-tuple-element.65) | copy-start | bytes 196612
  46.9 46.6 %copy-start.62 = (f32[512,32]{0,1:T(8,128)}, f32[512,32]{0,1:T(8,128)S(1)}, u32[]{:S(2)}) copy-start(f32[512,32]{0,1:T(8,128)S(1)} %get-tuple-element.66) | copy-start | bytes 196612
  50.4 89.1 %copy-start.14 = (bf16[256,1024]{1,0:T(8,128)(2,1)}, bf16[256,1024]{1,0:T(8,128)(2,1)S(1)}, u32[]{:S(2)}) copy-start(bf16[256,1024]{1,0:T(8,128)(2,1)S(1)} %get-tuple-element.52) | copy-start | bytes 1572868
  50.4 15.7 %collective-permute-start.1 = (bf16[256,1024]{1,0:T(8,128)(2,1)S(1)}, bf16[256,1024]{1,0:T(8,128)(2,1)S(1)}, u32[]{:S(2)}, u32[]{:S(2)}) collective-permute-start(bf16[256,1024]{1,0:T(8,128)(2,1)S(1)} %get-tuple-element.53), channel_id=1, source_target_pairs={{0,2},{1,3},{2,0},{3,1},{4,6},{5,7},{6,4},{7,5},{8,10},{9,11},{10,... | collective-permute-start | bytes 1572872 | tf_op jit(solution)/shard_map/ppermute | solution.py:393
  57.7 50.0 %collective-permute-start.8 = (bf16[256,1024]{1,0:T(8,128)(2,1)}, bf16[256,1024]{1,0:T(8,128)(2,1)}, u32[]{:S(2)}, u32[]{:S(2)}) collective-permute-start(bf16[256,1024]{1,0:T(8,128)(2,1)} %get-tuple-element.51), channel_id=1, source_target_pairs={{0,2},{1,3},{2,0},{3,1},{4,6},{5,7},{6,4},{7,5},{8,10},{9,11},{10,... | collective-permute-start | bytes 1572872 | tf_op jit(solution)/shard_map/ppermute | solution.py:393
  66.2 73.3 %copy-start.12 = (bf16[256,1024]{1,0:T(8,128)(2,1)}, bf16[256,1024]{1,0:T(8,128)(2,1)S(1)}, u32[]{:S(2)}) copy-start(bf16[256,1024]{1,0:T(8,128)(2,1)S(1)} %slice_add_fusion.1) | copy-start | bytes 1572868
  98.5 18.7 %collective-permute-start.2 = (bf16[512,1024]{1,0:T(8,128)(2,1)}, bf16[512,1024]{1,0:T(8,128)(2,1)}, u32[]{:S(2)}, u32[]{:S(2)}) collective-permute-start(bf16[512,1024]{1,0:T(8,128)(2,1)} %copy.88.refs_0_), channel_id=1, source_target_pairs={{1,0},{0,1},{3,2},{2,3},{5,4},{4,5},{7,6},{6,7},{9,8},{8,9},{11,10... | collective-permute-start | bytes 3145736 | tf_op jit(solution)/shard_map/ppermute | solution.py:384
  103.9 13.2 %collective-permute-start.3 = (bf16[512,1024]{1,0:T(8,128)(2,1)}, bf16[512,1024]{1,0:T(8,128)(2,1)}, u32[]{:S(2)}, u32[]{:S(2)}) collective-permute-start(bf16[512,1024]{1,0:T(8,128)(2,1)} %add_convert_fusion.4.refs_2_), channel_id=1, source_target_pairs={{1,0},{0,1},{3,2},{2,3},{5,4},{4,5},{7,6},{6,7},{9,8},{8,9},{11,10... | collective-permute-start | bytes 3145736 | tf_op jit(solution)/shard_map/ppermute | solution.py:384
  145.6 13.8 %copy-start.69 = (bf16[512,128]{1,0:T(8,128)(2,1)}, bf16[512,128]{1,0:T(8,128)(2,1)S(1)}, u32[]{:S(2)}) copy-start(bf16[512,128]{1,0:T(8,128)(2,1)S(1)} %fusion.120) | copy-start | bytes 393220
  185.7 15.6 %copy-start.81 = (bf16[512,128]{1,0:T(8,128)(2,1)}, bf16[512,128]{1,0:T(8,128)(2,1)S(1)}, u32[]{:S(2)}) copy-start(bf16[512,128]{1,0:T(8,128)(2,1)S(1)} %fusion.123) | copy-start | bytes 393220
  241.8 13.3 %collective-permute-start.9 = (bf16[512,1024]{1,0:T(8,128)(2,1)}, bf16[512,1024]{1,0:T(8,128)(2,1)}, u32[]{:S(2)}, u32[]{:S(2)}) collective-permute-start(bf16[512,1024]{1,0:T(8,128)(2,1)} %get-tuple-element.17), channel_id=1, source_target_pairs={{1,0},{0,1},{3,2},{2,3},{5,4},{4,5},{7,6},{6,7},{9,8},{8,9},{11,10... | collective-permute-start | bytes 3145736 | tf_op jit(solution)/shard_map/ppermute | solution.py:384
  245.0 23.8 %collective-permute-start.10 = (bf16[512,1024]{1,0:T(8,128)(2,1)}, bf16[512,1024]{1,0:T(8,128)(2,1)}, u32[]{:S(2)}, u32[]{:S(2)}) collective-permute-start(bf16[512,1024]{1,0:T(8,128)(2,1)} %get-tuple-element.19), channel_id=1, source_target_pairs={{1,0},{0,1},{3,2},{2,3},{5,4},{4,5},{7,6},{6,7},{9,8},{8,9},{11,10... | collective-permute-start | bytes 3145736 | tf_op jit(solution)/shard_map/ppermute | solution.py:384
  318.7 5.8 %collective-permute-start.14 = (bf16[8,2,94208]{2,0,1:T(8,128)(2,1)}, bf16[8,2,94208]{2,0,1:T(8,128)(2,1)}, u32[]{:S(2)}, u32[]{:S(2)}) collective-permute-start(bf16[8,2,94208]{2,0,1:T(8,128)(2,1)} %bitcast.308), channel_id=1, source_target_pairs={{0,1},{1,0},{2,3},{3,2},{4,5},{5,4},{6,7},{7,6},{8,9},{9,8},{10,11... | collective-permute-start | bytes 9043976 | tf_op jit(solution)/shard_map/ppermute | solution.py:407
  334.4 35.6 %collective-permute-start.15 = (bf16[8,1,94208]{2,0,1:T(8,128)(2,1)}, bf16[8,1,94208]{2,0,1:T(8,128)(2,1)S(1)}, u32[]{:S(2)}, u32[]{:S(2)}) collective-permute-start(bf16[8,1,94208]{2,0,1:T(8,128)(2,1)} %constant_dynamic-slice_fusion.3), channel_id=1, source_target_pairs={{0,2},{1,3},{2,0},{3,1},{4,6},{5,7},{6,4},{7,5},{8,10},{9,11},{10,... | collective-permute-start | bytes 4521992 | tf_op jit(solution)/shard_map/ppermute | solution.py:407
  377.8 34.8 %collective-permute-start.16 = (bf16[1,4,94208]{2,0,1:T(2,128)(2,1)}, bf16[1,4,94208]{2,0,1:T(2,128)(2,1)}, u32[]{:S(2)}, u32[]{:S(2)}) collective-permute-start(bf16[1,4,94208]{2,0,1:T(2,128)(2,1)} %dynamic-slice_bitcast_fusion), channel_id=1, source_target_pairs={{0,4},{4,0},{8,12},{12,8},{16,20},{20,16},{24,28},{28,24},{1,5},{5... | collective-permute-start | bytes 2261000 | tf_op jit(solution)/shard_map/ppermute | solution.py:407
  422.8 17.6 %collective-permute-start.17 = (bf16[1,2,94208]{2,0,1:T(2,128)(2,1)S(1)}, bf16[1,2,94208]{2,0,1:T(2,128)(2,1)}, u32[]{:S(2)}, u32[]{:S(2)}) collective-permute-start(bf16[1,2,94208]{2,0,1:T(2,128)(2,1)S(1)} %dynamic-slice_bitcast_fusion.1), channel_id=1, source_target_pairs={{0,8},{4,12},{8,0},{12,4},{16,24},{20,28},{24,16},{28,20},{1,9},{5... | collective-permute-start | bytes 1130504 | tf_op jit(solution)/shard_map/ppermute | solution.py:407
  424.4 36.8 %copy-start.83 = (f32[94208]{0:T(1024)S(1)}, f32[94208]{0:T(1024)}, u32[]{:S(2)}) copy-start(f32[94208]{0:T(1024)} %param.41) | copy-start | bytes 1130500
  443.0 17.5 %collective-permute-start.18 = (bf16[1,1,94208]{2,0,1:T(2,128)(2,1)S(1)}, bf16[1,1,94208]{2,0,1:T(2,128)(2,1)S(1)}, u32[]{:S(2)}, u32[]{:S(2)}) collective-permute-start(bf16[1,1,94208]{2,0,1:T(2,128)(2,1)S(1)} %constant_dynamic-slice_fusion.2), channel_id=1, source_target_pairs={{0,16},{4,20},{8,24},{12,28},{16,0},{20,4},{24,8},{28,12},{1,17},{... | collective-permute-start | bytes 565256 | tf_op jit(solution)/shard_map/ppermute | solution.py:407
  472.6 31.9 %collective-permute-start.4 = (bf16[512,1024]{1,0:T(8,128)(2,1)S(1)}, bf16[512,1024]{1,0:T(8,128)(2,1)S(1)}, u32[]{:S(2)}, u32[]{:S(2)}) collective-permute-start(bf16[512,1024]{1,0:T(8,128)(2,1)S(1)} %add_convert_fusion.3), channel_id=1, source_target_pairs={{1,0},{0,1},{3,2},{2,3},{5,4},{4,5},{7,6},{6,7},{9,8},{8,9},{11,10... | collective-permute-start | bytes 3145736 | tf_op jit(solution)/shard_map/ppermute | solution.py:384
  472.7 15.3 %collective-permute-start.5 = (bf16[256,1024]{1,0:T(8,128)(2,1)S(1)}, bf16[256,1024]{1,0:T(8,128)(2,1)S(1)}, u32[]{:S(2)}, u32[]{:S(2)}) collective-permute-start(bf16[256,1024]{1,0:T(8,128)(2,1)S(1)} %slice.324), channel_id=1, source_target_pairs={{0,2},{1,3},{2,0},{3,1},{4,6},{5,7},{6,4},{7,5},{8,10},{9,11},{10,... | collective-permute-start | bytes 1572872 | tf_op jit(solution)/shard_map/ppermute | solution.py:393
  483.8 20.8 %copy-start.110 = (s32[1,512]{1,0:T(1,128)S(1)}, s32[1,512]{1,0:T(1,128)}, u32[]{:S(2)}) copy-start(s32[1,512]{1,0:T(1,128)} %copy-done.109) | copy-start | bytes 6148
  484.4 20.2 %collective-permute-start.12 = (bf16[256,1024]{1,0:T(8,128)(2,1)S(1)}, bf16[256,1024]{1,0:T(8,128)(2,1)S(1)}, u32[]{:S(2)}, u32[]{:S(2)}) collective-permute-start(bf16[256,1024]{1,0:T(8,128)(2,1)S(1)} %slice.328), channel_id=1, source_target_pairs={{0,2},{1,3},{2,0},{3,1},{4,6},{5,7},{6,4},{7,5},{8,10},{9,11},{10,... | collective-permute-start | bytes 1572872 | tf_op jit(solution)/shard_map/ppermute | solution.py:393
  488.1 16.5 %collective-permute-start.6 = (bf16[256,1024]{1,0:T(8,128)(2,1)S(1)}, bf16[256,1024]{1,0:T(8,128)(2,1)S(1)}, u32[]{:S(2)}, u32[]{:S(2)}) collective-permute-start(bf16[256,1024]{1,0:T(8,128)(2,1)S(1)} %collective-permute-done.5), channel_id=1, source_target_pairs={{1,0},{0,1},{3,2},{2,3},{5,4},{4,5},{7,6},{6,7},{9,8},{8,9},{11,10... | collective-permute-start | bytes 1572872 | tf_op jit(solution)/shard_map/ppermute | solution.py:384
  488.1 19.3 %collective-permute-start.11 = (bf16[512,1024]{1,0:T(8,128)(2,1)S(1)}, bf16[512,1024]{1,0:T(8,128)(2,1)S(1)}, u32[]{:S(2)}, u32[]{:S(2)}) collective-permute-start(bf16[512,1024]{1,0:T(8,128)(2,1)S(1)} %fusion.39), channel_id=1, source_target_pairs={{1,0},{0,1},{3,2},{2,3},{5,4},{4,5},{7,6},{6,7},{9,8},{8,9},{11,10... | collective-permute-start | bytes 3145736 | tf_op jit(solution)/shard_map/ppermute | solution.py:384
  504.5 2.9 collective-permute-start.13
  (118 other events, 419.3 us)
Sparse Core Ops, SparseCore 0:
  463.6 73.1 all-gather.1

commit v2 on v1

--- a/solution.py
+++ b/solution.py
@@ -9,8 +9,6 @@
 
 RANK = 16
 ADAPTERS = 8
-
-
 NORM_EPS = 1e-06
 ADAPTER_SCALE = 2.0
 ROPE_BASE = 10000.0
@@ -21,95 +19,6 @@
 ADAM_EPS = 1e-08
 WEIGHT_DECAY = 0.01
 update_count = 10.0
-
-
-def rms_norm(values, norm_gain):
-    scaled = values * lax.rsqrt(jnp.mean(values * values, axis=-1, keepdims=True) + NORM_EPS)
-    return scaled * norm_gain.astype(jnp.float32)
-
-
-def rope_tables(position, head_width):
-    half_width = head_width // 2
-    freq_index = jnp.arange(half_width, dtype=jnp.float32)
-    frequency = ROPE_BASE ** (-2.0 * freq_index / head_width)
-    angles = position.astype(jnp.float32)[:, None] * frequency[None, :]
-    return (jnp.cos(angles), jnp.sin(angles))
-
-
-def shape_heads(values, norm_gain, cos_table, sin_table, head_width):
-    row_count = values.shape[0]
-    per_head = values.reshape(row_count, -1, head_width)
-    normalized_input = rms_norm(per_head, norm_gain)
-    half_width = head_width // 2
-    first_half = normalized_input[..., :half_width]
-    second_half = normalized_input[..., half_width:]
-    cos_part = cos_table[:, None, :]
-    sin_part = sin_table[:, None, :]
-    turned = jnp.concatenate(
-        [
-            first_half * cos_part - second_half * sin_part,
-            first_half * sin_part + second_half * cos_part,
-        ],
-        axis=-1,
-    )
-    return turned.reshape(row_count, -1)
-
-
-def unpack(flat_params, shapes, columns):
-    partial_pieces = []
-    offset = 0
-    for fan_in, fan_out in shapes:
-        down_size = fan_in * columns
-        a_matrix = lax.slice_in_dim(flat_params, offset, offset + down_size).reshape(
-            fan_in, columns
-        )
-        offset = offset + down_size
-        up_size = columns * fan_out
-        b_matrix = lax.slice_in_dim(flat_params, offset, offset + up_size).reshape(columns, fan_out)
-        offset = offset + up_size
-        partial_pieces.append((a_matrix, b_matrix))
-    return partial_pieces
-
-
-def contract_leading_rows(left, right):
-    return lax.dot_general(
-        left, right, (((0,), (0,)), ((), ())), preferred_element_type=jnp.float32
-    )
-
-
-def contract_columns(left, right):
-    return lax.dot_general(
-        left, right, (((1,), (1,)), ((), ())), preferred_element_type=jnp.float32
-    )
-
-
-def project(low_in, weight_matrix, partial_piece, adapter_selector_mask):
-    base_product = jnp.dot(low_in, weight_matrix, preferred_element_type=jnp.float32)
-    lowrank_inner = (
-        jnp.dot(low_in, partial_piece[0], preferred_element_type=jnp.float32)
-        * adapter_selector_mask
-    ).astype(jnp.bfloat16)
-    return (
-        base_product
-        + ADAPTER_SCALE
-        * jnp.dot(lowrank_inner, partial_piece[1], preferred_element_type=jnp.float32),
-        lowrank_inner,
-    )
-
-
-def project_back(
-    gradient_lowrank, low_in, lowrank_inner, weight_matrix, partial_piece, adapter_selector_mask
-):
-    grad_in = contract_columns(gradient_lowrank, weight_matrix)
-    gradient_inner = (
-        ADAPTER_SCALE * contract_columns(gradient_lowrank, partial_piece[1]) * adapter_selector_mask
-    ).astype(jnp.bfloat16)
-    grad_in = grad_in + contract_columns(gradient_inner, partial_piece[0])
-    grad_a = contract_leading_rows(low_in, gradient_inner)
-    grad_up_factor = ADAPTER_SCALE * contract_leading_rows(lowrank_inner, gradient_lowrank)
-    return (grad_in, grad_a, grad_up_factor)
-
-
 VARIATES = 4
 VMEM_LIMIT = 56 * 1024 * 1024
 EXACT_PARTS = 3
@@ -411,6 +320,934 @@
     return array
 
 
+LANES = 128
+
+
+def adam(current, first_old, second_old, grad):
+    first_moment = BETA_ONE * first_old + (1.0 - BETA_ONE) * grad
+    second_moment = BETA_TWO * second_old + (1.0 - BETA_TWO) * grad * grad
+    first_fix = first_moment / (1.0 - BETA_ONE**update_count)
+    second_fix = second_moment / (1.0 - BETA_TWO**update_count)
+    updated = current - LEARN_RATE * (
+        first_fix / (jnp.sqrt(second_fix) + ADAM_EPS) + WEIGHT_DECAY * current
+    )
+    return first_moment, second_moment, updated.astype(jnp.bfloat16)
+
+
+def settle_shards(grads, few_choice, adapters, moment1, moment2, groups):
+    a_qkv, b_qkv, a_guo, a_down, b_gu, b_do = grads
+    features, few = a_qkv.shape[0], few_choice.shape[1]
+    quarters = a_down.shape[1] // few
+    down = jnp.concatenate([a_down[:, i * few : (i + 1) * few] for i in range(quarters)])
+    wide = [a_qkv[:, i * few : (i + 1) * few] for i in range(3)]
+    wide += [a_guo[:, i * few : (i + 1) * few] for i in (2, 0, 1)] + [down]
+    tall = [b_qkv[i * few : (i + 1) * few] for i in range(3)]
+    tall += [b_do[2 * few : 3 * few], b_gu[:few], b_gu[few : 2 * few], b_do[:few]]
+    pieces = []
+    for grad_a, grad_b in zip(wide, tall):
+        pieces.append(lax.dot_general(grad_a, few_choice, (((1,), (1,)), ((), ()))).reshape(-1))
+        pieces.append(jnp.dot(few_choice, grad_b).reshape(-1))
+    axis_sizes = [("dp", lax.axis_size("dp")), ("group", groups)]
+    shards = axis_sizes[0][1] * groups
+    flat_grads = jnp.concatenate(pieces).astype(jnp.bfloat16).reshape(shards, -1)
+    grad_shard = scatter_sum(flat_grads, axis_sizes).reshape(-1).astype(jnp.float32)
+    shard_count = grad_shard.shape[0]
+    shard_start = lax.axis_index(("dp", "group")) * shard_count
+    current = lax.dynamic_slice_in_dim(adapters, shard_start, shard_count).astype(jnp.float32)
+    first_moment, second_moment, updated = adam(current, moment1, moment2, grad_shard)
+    adapters_new = lax.all_gather(updated, ("dp", "group"), axis=0, tiled=True)
+    return grad_shard, first_moment, second_moment, adapters_new
+
+
+def spreads_evenly(devices, features, hidden, total, turns):
+    rows = total // LANES
+    chunks = features // LANES
+    return (
+        turns == 2
+        and ADAPTERS * RANK == LANES
+        and devices * chunks == 256
+        and chunks == 8
+        and hidden == devices * LANES
+        and hidden == 4 * features
+        and rows % (devices * devices) == 0
+        and devices & (devices - 1) == 0
+    )
+
+
+def spread_wide(grads, devices):
+    rows = grads.shape[0] // devices
+    return jnp.transpose(grads.reshape(rows, devices, LANES), (1, 0, 2))
+
+
+def spread_tall(grad, devices):
+    return jnp.transpose(grad.reshape(grad.shape[0], devices, LANES), (1, 0, 2))
+
+
+def spread_square(grad, devices):
+    chunks = grad.shape[1] // LANES
+    classes = devices // chunks
+    parts = grad.reshape(2, RANK // classes, classes, chunks, LANES)
+    return jnp.transpose(parts, (2, 3, 0, 1, 4)).reshape(devices, 2 * RANK // classes, LANES)
+
+
+def one_hot(condition):
+    return jnp.where(condition, 1.0, 0.0).astype(jnp.bfloat16)
+
+
+def sum_wide(table_ref, arrived_ref, first, width):
+    sources = arrived_ref.shape[0]
+    rows = lax.broadcasted_iota(jnp.int32, (LANES, width * LANES), 0)
+    columns = lax.broadcasted_iota(jnp.int32, (LANES, width * LANES), 1)
+    fits = (rows // (2 * RANK) == columns // LANES) & (rows % RANK == columns % RANK)
+    second = (rows // RANK) % 2 == 1
+    adapter = jnp.where(fits, (columns % LANES) // RANK, -1)
+    total = jnp.zeros((32, width * LANES), jnp.float32)
+    for source in range(sources):
+        chosen = jnp.where(second, table_ref[source, 1], table_ref[source, 0])
+        total = total + jnp.dot(
+            arrived_ref[source, first : first + 32, :],
+            one_hot(adapter == chosen),
+            preferred_element_type=jnp.float32,
+        )
+    return total
+
+
+def sum_tall(adapter_row, arrived_ref, first):
+    sources = arrived_ref.shape[0]
+    depth = sources * 2 * RANK
+    rows = lax.broadcasted_iota(jnp.int32, (LANES, depth), 0)
+    columns = lax.broadcasted_iota(jnp.int32, (LANES, depth), 1)
+    choice = one_hot((rows // RANK == adapter_row) & (rows % RANK == columns % RANK))
+    held = arrived_ref[:, first : first + 2 * RANK, :].reshape(depth, LANES)
+    return jnp.dot(choice, held, preferred_element_type=jnp.float32)
+
+
+def sum_square(adapter_row, arrived_ref, first):
+    sources = arrived_ref.shape[0]
+    depth = sources * 16
+    rows = lax.broadcasted_iota(jnp.int32, (64, depth), 0)
+    columns = lax.broadcasted_iota(jnp.int32, (64, depth), 1)
+    choice = one_hot(
+        ((rows % 32) // 4 == adapter_row)
+        & (rows % 4 == columns % 4)
+        & (rows // 32 == (columns % 16) // 8)
+    )
+    held = arrived_ref[:, first : first + 16, :].reshape(depth, LANES)
+    return jnp.dot(choice, held, preferred_element_type=jnp.float32)
+
+
+def settle_kernel(
+    early, table_ref, tall_ref, square_ref, arrived_ref, param_ref, m1_ref, m2_ref, grad_ref, new_ref
+):
+    if early:
+        wide = sum_wide(table_ref, arrived_ref, 0, 3)
+        last = sum_wide(table_ref, arrived_ref, 32, 4)
+        square = sum_square(square_ref[...], arrived_ref, 128)
+        parts = [
+            wide[:, 2 * LANES :],
+            square[32:],
+            wide[:, :LANES],
+            sum_tall(tall_ref[...], arrived_ref, 64),
+            wide[:, LANES : 2 * LANES],
+            sum_tall(tall_ref[...], arrived_ref, 96),
+        ]
+        parts += [last[:, i * LANES : (i + 1) * LANES] for i in range(4)]
+        parts.append(square[:32])
+    else:
+        wide = sum_wide(table_ref, arrived_ref, 0, 3)
+        square = [sum_square(square_ref[...], arrived_ref, first) for first in (32, 48)]
+        parts = []
+        for index in range(3):
+            parts.append(wide[:, index * LANES : (index + 1) * LANES])
+            parts.append(square[index // 2][(index % 2) * 32 : (index % 2) * 32 + 32])
+    row = 0
+    for part in parts:
+        here = slice(row, row + part.shape[0])
+        row += part.shape[0]
+        low = part.astype(jnp.bfloat16)
+        grad_ref[here, :] = low
+        new_ref[here, :] = adam(
+            param_ref[here, :].astype(jnp.float32),
+            m1_ref[here, :],
+            m2_ref[here, :],
+            low.astype(jnp.float32),
+        )[2]
+
+
+def settle(early, table, arrived, params, first_old, second_old):
+    sources = table.shape[0]
+    tall_row = jnp.repeat(table.reshape(-1), RANK)[None, :]
+    square_row = jnp.repeat(jnp.tile(table, (1, 2)).reshape(-1), 4)[None, :]
+    shape = jax.ShapeDtypeStruct(params.shape, jnp.bfloat16)
+    return pl.pallas_call(
+        functools.partial(settle_kernel, early),
+        in_specs=[pl.BlockSpec(memory_space=pltpu.SMEM)]
+        + [pl.BlockSpec(memory_space=pltpu.VMEM)] * 6,
+        out_specs=[pl.BlockSpec(memory_space=pltpu.VMEM)] * 2,
+        out_shape=[shape, shape],
+        compiler_params=pltpu.CompilerParams(vmem_limit_bytes=VMEM_LIMIT),
+        cost_estimate=pl.CostEstimate(
+            flops=sources * 2**24, bytes_accessed=4 * arrived.size, transcendentals=0
+        ),
+        name="settle_early" if early else "settle_late",
+    )(table, tall_row, square_row, arrived, params, first_old, second_old)
+
+
+def gather_everywhere(rows, devices, groups):
+    pieces = [rows[None]]
+    bit = devices // 2
+    while bit:
+        send = jnp.concatenate(pieces) if len(pieces) > 1 else pieces[0]
+        if bit >= groups:
+            step = bit // groups
+            pairs = [(i, i ^ step) for i in range(devices // groups)]
+            pieces.append(lax.ppermute(send, "dp", pairs))
+        else:
+            pieces.append(lax.ppermute(send, "group", [(i, i ^ bit) for i in range(groups)]))
+        bit //= 2
+    return pieces
+
+
+def assemble_kernel(count, order_ref, *refs):
+    piece_refs, out_ref = refs[:count], refs[-1]
+    block = piece_refs[0].shape[1]
+    devices = 2 * piece_refs[-1].shape[0]
+    for start in range(0, block, 16):
+        held = jnp.concatenate([ref[:, start : start + 16, :] for ref in piece_refs], axis=0)
+        out_ref[start * devices : (start + 16) * devices, :] = jnp.dot(
+            order_ref[...],
+            held.reshape(16 * devices, LANES),
+            preferred_element_type=jnp.float32,
+        ).astype(jnp.bfloat16)
+
+
+def assemble(order, pieces, total_rows, first, block, before):
+    devices = 2 * pieces[-1].shape[0]
+    steps = pieces[0].shape[1] // block
+    in_specs = [pl.BlockSpec(order.shape, lambda step: (0, 0))]
+    in_specs += [
+        pl.BlockSpec((piece.shape[0], block, LANES), lambda step: (0, step, 0)) for piece in pieces
+    ]
+    operands = [order, *pieces]
+    aliases = {}
+    if before is not None:
+        aliases = {len(operands): 0}
+        in_specs.append(pl.BlockSpec(memory_space=pl.ANY))
+        operands.append(before)
+    skip = first // block
+    return pl.pallas_call(
+        functools.partial(assemble_kernel, len(pieces)),
+        grid=(steps,),
+        in_specs=in_specs,
+        out_specs=pl.BlockSpec((block * devices, LANES), lambda step: (step + skip, 0)),
+        out_shape=jax.ShapeDtypeStruct((total_rows, LANES), jnp.bfloat16),
+        input_output_aliases=aliases,
+        compiler_params=pltpu.CompilerParams(vmem_limit_bytes=VMEM_LIMIT),
+        cost_estimate=pl.CostEstimate(
+            flops=steps * block * devices * 2**17,
+            bytes_accessed=steps * block * devices * 512,
+            transcendentals=0,
+        ),
+        name="assemble",
+    )(*operands)
+
+
+def rope_tables(position, head_width):
+    lane = jnp.arange(LANES, dtype=jnp.int32)
+    freq_index = (lane % (head_width // 2)).astype(jnp.float32)
+    frequency = ROPE_BASE ** (-2.0 * freq_index / head_width)
+    angles = position.astype(jnp.float32)[:, None] * frequency[None, :]
+    sign = jnp.where(lane % head_width < head_width // 2, -1.0, 1.0)
+    return jnp.cos(angles), jnp.sin(angles) * sign[None, :]
+
+
+def head_gain(gain):
+    return jnp.tile(gain.astype(jnp.float32), LANES // gain.shape[0])[None, :]
+
+
+def select_kernel(features, hidden, turn_ref, flat_ref, *out_refs):
+    a_qkv_ref, a_guo_ref, a_down_ref, b_qkv_ref, b_gu_ref, b_do_ref = out_refs
+    few = 2 * RANK
+    rows = lax.broadcasted_iota(jnp.int32, (LANES, LANES), 0)
+    columns = lax.broadcasted_iota(jnp.int32, (LANES, LANES), 1)
+    chosen = jnp.where((columns // RANK) % 2 == 1, turn_ref[1], turn_ref[0])
+    fits = (rows // RANK == chosen) & (rows % RANK == columns % RANK)
+    start = {}
+    row = 0
+    for name, rows_in, rows_out in (
+        ("q", features, features),
+        ("k", features, features),
+        ("v", features, features),
+        ("o", features, features),
+        ("g", features, hidden),
+        ("u", features, hidden),
+        ("d", hidden, features),
+    ):
+        start[name] = (row, row + rows_in)
+        row += rows_in + rows_out
+
+    def wide(names, length):
+        total = jnp.zeros((length, LANES), jnp.float32)
+        for place, name in enumerate(names):
+            first = start[name][0]
+            total = total + jnp.dot(
+                flat_ref[first : first + length, :],
+                one_hot(fits & (columns // few == place)),
+                preferred_element_type=jnp.float32,
+            )
+        return total.astype(jnp.bfloat16)
+
+    a_qkv_ref[...] = wide("qkv", features)
+    a_guo_ref[...] = wide("guo", features)
+    for first in range(0, hidden, features):
+        a_down_ref[first : first + features, :] = jnp.dot(
+            flat_ref[start["d"][0] + first : start["d"][0] + first + features, :],
+            one_hot(fits & (columns // few == 0)),
+            preferred_element_type=jnp.float32,
+        ).astype(jnp.bfloat16)
+
+    def tall(name, length, out_ref, place):
+        chunks = length // LANES
+        size = RANK * chunks
+        to_row = lax.broadcasted_iota(jnp.int32, (size, size), 0)
+        from_row = lax.broadcasted_iota(jnp.int32, (size, size), 1)
+        turned = one_hot(
+            (to_row // RANK == from_row % chunks) & (to_row % RANK == from_row // chunks)
+        )
+        for turn in range(2):
+            first = start[name][1] + pl.multiple_of(turn_ref[turn] * size, LANES)
+            block = jnp.dot(
+                turned, flat_ref[pl.ds(first, size), :], preferred_element_type=jnp.float32
+            ).astype(jnp.bfloat16)
+            here = place * few + turn * RANK
+            for chunk in range(chunks):
+                out_ref[here : here + RANK, chunk * LANES : (chunk + 1) * LANES] = block[
+                    chunk * RANK : (chunk + 1) * RANK
+                ]
+
+    for out_ref, names in ((b_qkv_ref, "qkv"), (b_gu_ref, "gu"), (b_do_ref, "d.o")):
+        out_ref[...] = jnp.zeros(out_ref.shape, out_ref.dtype)
+        for place, name in enumerate(names):
+            if name != ".":
+                tall(name, out_ref.shape[1], out_ref, place)
+
+
+def select(turn_adapter, adapters, features, hidden):
+    shapes = [(features, LANES), (features, LANES), (hidden, LANES)]
+    shapes += [(LANES, features), (LANES, hidden), (LANES, features)]
+    return pl.pallas_call(
+        functools.partial(select_kernel, features, hidden),
+        in_specs=[
+            pl.BlockSpec(memory_space=pltpu.SMEM),
+            pl.BlockSpec(memory_space=pltpu.VMEM),
+        ],
+        out_specs=[pl.BlockSpec(memory_space=pltpu.VMEM)] * 6,
+        out_shape=[jax.ShapeDtypeStruct(shape, jnp.bfloat16) for shape in shapes],
+        compiler_params=pltpu.CompilerParams(vmem_limit_bytes=VMEM_LIMIT),
+        cost_estimate=pl.CostEstimate(
+            flops=2**31, bytes_accessed=4 * adapters.shape[0], transcendentals=0
+        ),
+        name="select",
+    )(turn_adapter, adapters.reshape(-1, LANES))
+
+
+def dot(left, right):
+    return jnp.dot(left, right, preferred_element_type=jnp.float32)
+
+
+def turn_mask(meta_ref):
+    rows = meta_ref.shape[0]
+    lane = lax.broadcasted_iota(jnp.int32, (rows, LANES), 1)
+    mask = jnp.where((lane // RANK) % 2 == meta_ref[:, 2:3], 1.0, 0.0)
+    return mask, lane // (2 * RANK)
+
+
+def row_norm(values):
+    return lax.rsqrt(jnp.mean(values * values, axis=1, keepdims=True) + NORM_EPS)
+
+
+def row_norm_back(values, gain, grad):
+    scale = row_norm(values)
+    unit = values * scale
+    grad = grad * gain
+    return scale * (grad - unit * jnp.mean(grad * unit, axis=1, keepdims=True))
+
+
+def head_mean(values, width):
+    lanes = values.shape[1]
+    rows = lax.broadcasted_iota(jnp.int32, (lanes, lanes), 0)
+    columns = lax.broadcasted_iota(jnp.int32, (lanes, lanes), 1)
+    ones = one_hot(rows // width == columns // width)
+    high = values.astype(jnp.bfloat16)
+    low = (values - high.astype(jnp.float32)).astype(jnp.bfloat16)
+    return (dot(high, ones) + dot(low, ones)) * (1.0 / width)
+
+
+def swap_halves(values, width):
+    lanes = values.shape[1]
+    lane = lax.broadcasted_iota(jnp.int32, values.shape, 1)
+    ahead = pltpu.roll(values, lanes - width // 2, 1)
+    behind = pltpu.roll(values, width // 2, 1)
+    return jnp.where(lane % width < width // 2, ahead, behind)
+
+
+def widen(table, lanes):
+    return jnp.concatenate([table] * (lanes // table.shape[1]), axis=1)
+
+
+def project_heads_kernel(
+    width,
+    x_ref,
+    gain_ref,
+    wq_ref,
+    wk_ref,
+    wv_ref,
+    a_ref,
+    b_ref,
+    meta_ref,
+    cos_ref,
+    sin_ref,
+    q_gain_ref,
+    k_gain_ref,
+    normed_ref,
+    inner_ref,
+    q_raw_ref,
+    k_raw_ref,
+    q_ref,
+    k_ref,
+    v_ref,
+):
+    mask, place = turn_mask(meta_ref)
+
+    @pl.when(pl.program_id(0) == 0)
+    def _():
+        values = x_ref[...].astype(jnp.float32)
+        normed = (values * row_norm(values) * gain_ref[...].astype(jnp.float32)).astype(
+            jnp.bfloat16
+        )
+        normed_ref[...] = normed
+        inner_ref[...] = (dot(normed, a_ref[...]) * mask).astype(jnp.bfloat16)
+
+    normed = normed_ref[...]
+    inner = inner_ref[...].astype(jnp.float32)
+    lanes = wq_ref.shape[1]
+
+    def lora(weight_ref, index):
+        own = jnp.where(place == index, inner, 0.0).astype(jnp.bfloat16)
+        return dot(normed, weight_ref[...]) + ADAPTER_SCALE * dot(own, b_ref[...])
+
+    cosine, sine = widen(cos_ref[...], lanes), widen(sin_ref[...], lanes)
+
+    def turned(raw, head_gain_ref):
+        unit = raw * lax.rsqrt(head_mean(raw * raw, width) + NORM_EPS)
+        unit = unit * widen(head_gain_ref[...], lanes)
+        return (unit * cosine + swap_halves(unit, width) * sine).astype(jnp.bfloat16)
+
+    query = lora(wq_ref, 0)
+    q_raw_ref[...] = query
+    q_ref[...] = turned(query, q_gain_ref)
+    key = lora(wk_ref, 1)
+    k_raw_ref[...] = key
+    k_ref[...] = turned(key, k_gain_ref)
+    v_ref[...] = lora(wv_ref, 2).astype(jnp.bfloat16)
+
+
+def project_heads(
+    rows_in, gain, weights, a_qkv, b_qkv, meta, cos_table, sin_table, q_gain, k_gain, width
+):
+    rows, features = rows_in.shape
+    tile = 256
+    grid = (features // tile,)
+
+    def tiled(height):
+        return pl.BlockSpec((height, tile), lambda step: (0, step))
+
+    def shape(dtype):
+        return jax.ShapeDtypeStruct((rows, features), dtype)
+
+    return pl.pallas_call(
+        functools.partial(project_heads_kernel, width),
+        grid=grid,
+        in_specs=[whole_block((rows, features)), whole_block((1, features))]
+        + [tiled(features)] * 3
+        + [whole_block((features, LANES)), tiled(LANES), whole_block(meta.shape)]
+        + [whole_block((rows, LANES))] * 2
+        + [whole_block((1, LANES))] * 2,
+        out_specs=[whole_block((rows, features)), whole_block((rows, LANES))] + [tiled(rows)] * 5,
+        out_shape=[
+            shape(jnp.bfloat16),
+            jax.ShapeDtypeStruct((rows, LANES), jnp.bfloat16),
+            shape(jnp.float32),
+            shape(jnp.float32),
+            shape(jnp.bfloat16),
+            shape(jnp.bfloat16),
+            shape(jnp.bfloat16),
+        ],
+        compiler_params=pltpu.CompilerParams(vmem_limit_bytes=VMEM_LIMIT),
+        cost_estimate=pl.CostEstimate(
+            flops=8 * rows * features * features,
+            bytes_accessed=6 * features * features + 20 * rows * features,
+            transcendentals=0,
+        ),
+        name="project_heads",
+    )(
+        rows_in,
+        gain[None, :],
+        *weights,
+        a_qkv,
+        b_qkv,
+        meta,
+        cos_table,
+        sin_table,
+        q_gain,
+        k_gain,
+    )
+
+
+def project_heads_back_kernel(
+    count,
+    width,
+    gq_ref,
+    *refs,
+):
+    gk_refs, gv_refs, refs = refs[:count], refs[count : 2 * count], refs[2 * count :]
+    (
+        q_raw_ref,
+        k_raw_ref,
+        normed_ref,
+        inner_ref,
+        x_ref,
+        residual_ref,
+        gain_ref,
+        wq_ref,
+        wk_ref,
+        wv_ref,
+        a_ref,
+        b_ref,
+        meta_ref,
+        cos_ref,
+        sin_ref,
+        q_gain_ref,
+        k_gain_ref,
+        out_ref,
+        grad_a_ref,
+        grad_b_ref,
+        total_ref,
+        few_ref,
+    ) = refs
+    step = pl.program_id(0)
+    lanes = wq_ref.shape[1]
+    mask, place = turn_mask(meta_ref)
+    cosine, sine = widen(cos_ref[...], lanes), widen(sin_ref[...], lanes)
+
+    def turned_back(grad, raw, head_gain_ref):
+        grad = grad * cosine - swap_halves(grad, width) * sine
+        scale = lax.rsqrt(head_mean(raw * raw, width) + NORM_EPS)
+        unit = raw * scale
+        grad = grad * widen(head_gain_ref[...], lanes)
+        return (scale * (grad - unit * head_mean(grad * unit, width))).astype(jnp.bfloat16)
+
+    def summed(term_refs):
+        total = term_refs[0][...].astype(jnp.float32)
+        for ref in term_refs[1:]:
+            total = total + ref[...].astype(jnp.float32)
+        return total
+
+    @pl.when(step == 0)
+    def _():
+        total_ref[...] = jnp.zeros(total_ref.shape, jnp.float32)
+        few_ref[...] = jnp.zeros(few_ref.shape, jnp.float32)
+
+    inner_turned = jnp.transpose(inner_ref[...].astype(jnp.float32) * ADAPTER_SCALE).astype(
+        jnp.bfloat16
+    )
+    errors = [
+        turned_back(gq_ref[...], q_raw_ref[...], q_gain_ref),
+        turned_back(summed(gk_refs), k_raw_ref[...], k_gain_ref),
+        summed(gv_refs).astype(jnp.bfloat16),
+    ]
+    total = total_ref[...]
+    few = few_ref[...]
+    wide = 2 * RANK
+    for index, (error, weight_ref) in enumerate(zip(errors, (wq_ref, wk_ref, wv_ref))):
+        total = total + contract_last(error, weight_ref[...])
+        few = few + jnp.where(place == index, contract_last(error, b_ref[...]), 0.0)
+        here = slice(index * wide, (index + 1) * wide)
+        grad_b_ref[here, :] = dot(inner_turned[here], error).astype(jnp.bfloat16)
+    grad_b_ref[3 * wide :, :] = jnp.zeros((LANES - 3 * wide, lanes), jnp.bfloat16)
+    total_ref[...] = total
+    few_ref[...] = few
+
+    @pl.when(step == pl.num_programs(0) - 1)
+    def _():
+        low = (ADAPTER_SCALE * few_ref[...] * mask).astype(jnp.bfloat16)
+        low_turned = jnp.transpose(low.astype(jnp.float32)).astype(jnp.bfloat16)
+        grad_a_ref[...] = jnp.transpose(dot(low_turned, normed_ref[...])).astype(jnp.bfloat16)
+        grad = total_ref[...] + contract_last(low, a_ref[...])
+        out_ref[...] = (
+            residual_ref[...]
+            + row_norm_back(
+                x_ref[...].astype(jnp.float32), gain_ref[...].astype(jnp.float32), grad
+            )
+        ).astype(jnp.bfloat16)
+
+
+def project_heads_back(
+    grad_query,
+    key_terms,
+    value_terms,
+    query_raw,
+    key_raw,
+    normed,
+    inner,
+    rows_in,
+    grad_residual,
+    gain,
+    weights,
+    a_qkv,
+    b_qkv,
+    meta,
+    cos_table,
+    sin_table,
+    q_gain,
+    k_gain,
+    width,
+):
+    rows, features = rows_in.shape
+    count = len(key_terms)
+    tile = 256
+
+    def tiled(height):
+        return pl.BlockSpec((height, tile), lambda step: (0, step))
+
+    full = whole_block((rows, features))
+    return pl.pallas_call(
+        functools.partial(project_heads_back_kernel, count, width),
+        grid=(features // tile,),
+        in_specs=[tiled(rows)] * (3 + 2 * count)
+        + [full, whole_block((rows, LANES)), full, full, whole_block((1, features))]
+        + [tiled(features)] * 3
+        + [whole_block((features, LANES)), tiled(LANES), whole_block(meta.shape)]
+        + [whole_block((rows, LANES))] * 2
+        + [whole_block((1, LANES))] * 2,
+        out_specs=[full, whole_block((features, LANES)), tiled(LANES)],
+        out_shape=[
+            jax.ShapeDtypeStruct((rows, features), jnp.bfloat16),
+            jax.ShapeDtypeStruct((features, LANES), jnp.bfloat16),
+            jax.ShapeDtypeStruct((LANES, features), jnp.bfloat16),
+        ],
+        scratch_shapes=[
+            pltpu.VMEM((rows, features), jnp.float32),
+            pltpu.VMEM((rows, LANES), jnp.float32),
+        ],
+        compiler_params=pltpu.CompilerParams(vmem_limit_bytes=VMEM_LIMIT),
+        cost_estimate=pl.CostEstimate(
+            flops=8 * rows * features * features,
+            bytes_accessed=6 * features * features + 30 * rows * features,
+            transcendentals=0,
+        ),
+        name="project_heads_back",
+    )(
+        grad_query,
+        *key_terms,
+        *value_terms,
+        query_raw,
+        key_raw,
+        normed,
+        inner,
+        rows_in,
+        grad_residual,
+        gain[None, :],
+        *weights,
+        a_qkv,
+        b_qkv,
+        meta,
+        cos_table,
+        sin_table,
+        q_gain,
+        k_gain,
+    )
+
+
+def feed_forward_kernel(
+    att_ref,
+    x_ref,
+    e_ref,
+    gain_ref,
+    wo_ref,
+    wg_ref,
+    wu_ref,
+    wd_ref,
+    a_guo_ref,
+    a_down_ref,
+    b_gu_ref,
+    b_do_ref,
+    meta_ref,
+    out_ref,
+    grad_res_ref,
+    grad_att_ref,
+    grad_a_ref,
+    grad_ad_ref,
+    grad_bgu_ref,
+    grad_bdo_ref,
+    res_ref,
+    hidden_ref,
+    inner_ref,
+    inner_turned_ref,
+    sum_ref,
+    grad_hidden_ref,
+    inner_down_ref,
+    few_ref,
+    few_down_ref,
+    few_down_turned_ref,
+    down_ref,
+):
+    step = pl.program_id(0)
+    mask, place = turn_mask(meta_ref)
+    tile = wg_ref.shape[1]
+    features = wo_ref.shape[0]
+    wide = 2 * RANK
+
+    def only(values, index):
+        return jnp.where(place == index, values, 0.0).astype(jnp.bfloat16)
+
+    def turn(values):
+        return jnp.transpose(values.astype(jnp.float32)).astype(jnp.bfloat16)
+
+    @pl.when(step == 0)
+    def _():
+        att = att_ref[...]
+        inner_out = dot(att, a_guo_ref[...]) * mask
+        res = (
+            x_ref[...].astype(jnp.float32)
+            + dot(att, wo_ref[...])
+            + ADAPTER_SCALE * dot(only(inner_out, 2), b_do_ref[...])
+        )
+        res_ref[...] = res
+        hidden = (res * row_norm(res) * gain_ref[...].astype(jnp.float32)).astype(jnp.bfloat16)
+        hidden_ref[...] = hidden
+        inner = dot(hidden, a_guo_ref[...]) * mask
+        inner = jnp.where(place == 2, inner_out, inner).astype(jnp.bfloat16)
+        inner_ref[...] = inner
+        inner_turned_ref[...] = turn(inner.astype(jnp.float32) * ADAPTER_SCALE)
+        few_down = only(ADAPTER_SCALE * contract_last(e_ref[...], b_do_ref[...]) * mask, 0)
+        few_down_ref[...] = few_down
+        few_down_turned_ref[...] = turn(few_down)[:wide]
+        sum_ref[...] = jnp.zeros(sum_ref.shape, jnp.float32)
+        grad_hidden_ref[...] = jnp.zeros(grad_hidden_ref.shape, jnp.float32)
+        inner_down_ref[...] = jnp.zeros(inner_down_ref.shape, jnp.float32)
+        few_ref[...] = jnp.zeros(few_ref.shape, jnp.float32)
+
+    hidden = hidden_ref[...]
+    inner = inner_ref[...].astype(jnp.float32)
+    gate_weight, up_weight, down_weight = wg_ref[...], wu_ref[...], wd_ref[...]
+    b_tile = b_gu_ref[...]
+    gate = dot(hidden, gate_weight) + ADAPTER_SCALE * dot(only(inner, 0), b_tile)
+    up = dot(hidden, up_weight) + ADAPTER_SCALE * dot(only(inner, 1), b_tile)
+    grad_act = contract_last(e_ref[...], down_weight) + contract_last(
+        few_down_ref[...], a_down_ref[...]
+    )
+    sigmoid = 1.0 / (1.0 + jnp.exp(-gate))
+    silu = gate * sigmoid
+    act = (silu * up).astype(jnp.bfloat16)
+    grad_up = (grad_act * silu).astype(jnp.bfloat16)
+    grad_gate = (grad_act * up * (sigmoid * (1.0 + gate * (1.0 - sigmoid)))).astype(jnp.bfloat16)
+    sum_ref[...] += dot(act, down_weight)
+    inner_down_ref[...] += dot(act, a_down_ref[...])
+    grad_hidden_ref[...] += contract_last(grad_gate, gate_weight) + contract_last(
+        grad_up, up_weight
+    )
+    few_ref[...] += jnp.where(
+        place == 0, contract_last(grad_gate, b_tile), contract_last(grad_up, b_tile)
+    )
+    grad_bgu_ref[:wide, :] = dot(inner_turned_ref[:wide, :], grad_gate).astype(jnp.bfloat16)
+    grad_bgu_ref[wide:, :] = dot(inner_turned_ref[wide : 2 * wide, :], grad_up).astype(
+        jnp.bfloat16
+    )
+    per_quarter = features // tile
+    down_ref[
+        pl.ds(pl.multiple_of((step // per_quarter) * wide, wide), wide),
+        pl.ds(pl.multiple_of((step % per_quarter) * tile, tile), tile),
+    ] = dot(few_down_turned_ref[...], act)
+
+    @pl.when(step == pl.num_programs(0) - 1)
+    def _():
+        grads_out = e_ref[...]
+        inner_down = only(inner_down_ref[...] * mask, 0)
+        res = res_ref[...]
+        out_ref[...] = (
+            res + sum_ref[...] + ADAPTER_SCALE * dot(inner_down, b_do_ref[...])
+        ).astype(jnp.bfloat16)
+        few = jnp.where(place < 2, ADAPTER_SCALE * few_ref[...] * mask, 0.0).astype(jnp.bfloat16)
+        grad_hidden = grad_hidden_ref[...] + contract_last(few, a_guo_ref[...])
+        grad_res = grads_out.astype(jnp.float32) + row_norm_back(
+            res, gain_ref[...].astype(jnp.float32), grad_hidden
+        )
+        grad_res_ref[...] = grad_res
+        low = grad_res.astype(jnp.bfloat16)
+        few_out = only(ADAPTER_SCALE * contract_last(low, b_do_ref[...]) * mask, 2)
+        grad_att_ref[...] = (
+            contract_last(low, wo_ref[...]) + contract_last(few_out, a_guo_ref[...])
+        ).astype(jnp.bfloat16)
+        grad_a = dot(turn(few), hidden_ref[...]) + dot(turn(few_out), att_ref[...])
+        grad_a_ref[...] = jnp.transpose(grad_a).astype(jnp.bfloat16)
+        grad_ad_ref[...] = jnp.transpose(down_ref[...]).astype(jnp.bfloat16)
+        inner_out = only(inner_ref[...].astype(jnp.float32), 2)
+        grad_bdo_ref[...] = (
+            ADAPTER_SCALE * (dot(turn(inner_down), grads_out) + dot(turn(inner_out), low))
+        ).astype(jnp.bfloat16)
+
+
+def feed_forward(attended, rows_in, grads_out, gain, weights, selected, meta):
+    rows, features = rows_in.shape
+    hidden = weights[1].shape[1]
+    tile = 512
+    full = whole_block((rows, features))
+    square = whole_block((features, features))
+    column = pl.BlockSpec((features, tile), lambda step: (0, step))
+
+    def shape(height, length, dtype):
+        return jax.ShapeDtypeStruct((height, length), dtype)
+
+    return pl.pallas_call(
+        feed_forward_kernel,
+        grid=(hidden // tile,),
+        in_specs=[
+            full,
+            full,
+            full,
+            whole_block((1, features)),
+            square,
+            column,
+            column,
+            pl.BlockSpec((tile, features), lambda step: (step, 0)),
+            whole_block((features, LANES)),
+            pl.BlockSpec((tile, LANES), lambda step: (step, 0)),
+            pl.BlockSpec((LANES, tile), lambda step: (0, step)),
+            whole_block((LANES, features)),
+            whole_block(meta.shape),
+        ],
+        out_specs=[
+            full,
+            full,
+            full,
+            whole_block((features, LANES)),
+            whole_block((features, LANES)),
+            pl.BlockSpec((4 * RANK, tile), lambda step: (0, step)),
+            whole_block((LANES, features)),
+        ],
+        out_shape=[
+            shape(rows, features, jnp.bfloat16),
+            shape(rows, features, jnp.float32),
+            shape(rows, features, jnp.bfloat16),
+            shape(features, LANES, jnp.bfloat16),
+            shape(features, LANES, jnp.bfloat16),
+            shape(4 * RANK, hidden, jnp.bfloat16),
+            shape(LANES, features, jnp.bfloat16),
+        ],
+        scratch_shapes=[
+            pltpu.VMEM((rows, features), jnp.float32),
+            pltpu.VMEM((rows, features), jnp.bfloat16),
+            pltpu.VMEM((rows, LANES), jnp.bfloat16),
+            pltpu.VMEM((LANES, rows), jnp.bfloat16),
+            pltpu.VMEM((rows, features), jnp.float32),
+            pltpu.VMEM((rows, features), jnp.float32),
+            pltpu.VMEM((rows, LANES), jnp.float32),
+            pltpu.VMEM((rows, LANES), jnp.float32),
+            pltpu.VMEM((rows, LANES), jnp.bfloat16),
+            pltpu.VMEM((2 * RANK, rows), jnp.bfloat16),
+            pltpu.VMEM((LANES, features), jnp.float32),
+        ],
+        compiler_params=pltpu.CompilerParams(vmem_limit_bytes=VMEM_LIMIT),
+        cost_estimate=pl.CostEstimate(
+            flops=14 * rows * features * hidden,
+            bytes_accessed=8 * features * hidden + 16 * rows * features,
+            transcendentals=0,
+        ),
+        name="feed_forward",
+    )(attended, rows_in, grads_out, gain[None, :], *weights, *selected, meta)
+
+
+def settle_spread(grads, turn_adapter, adapters, moment1, moment2, devices):
+    a_qkv, b_qkv, a_guo, a_down, b_gu, b_do = grads
+    axes = ("dp", "group")
+    groups = lax.axis_size("group")
+    me = lax.axis_index(axes)
+    total_rows = adapters.shape[0] // LANES
+    spread_rows = total_rows // devices
+    own_rows = spread_rows // devices
+    features = a_qkv.shape[0]
+    late_rows = 6 * features // devices
+    few = 2 * RANK
+
+    moments = jnp.concatenate(
+        [
+            jnp.transpose(flat.reshape(own_rows, devices, LANES), (1, 0, 2))
+            for flat in (moment1, moment2)
+        ],
+        axis=1,
+    )
+    moments, a_guo = lax.optimization_barrier((moments, a_guo))
+    moments = lax.all_to_all(moments, axes, 0, 0, tiled=True)
+    first_old = moments[:, :own_rows].reshape(spread_rows, LANES)
+    second_old = moments[:, own_rows:].reshape(spread_rows, LANES)
+    params = lax.dynamic_index_in_dim(
+        adapters.reshape(spread_rows, devices, LANES), me, 1, keepdims=False
+    )
+    told = jnp.where(
+        jnp.arange(LANES, dtype=jnp.int32) == 3 * few,
+        turn_adapter[0],
+        jnp.where(jnp.arange(LANES, dtype=jnp.int32) == 3 * few + 1, turn_adapter[1], 0),
+    ).astype(jnp.bfloat16)
+    early = jnp.concatenate(
+        [
+            spread_wide(a_guo + told[None, :], devices),
+            spread_wide(a_down, devices),
+            spread_tall(b_gu[:few], devices),
+            spread_tall(b_gu[few : 2 * few], devices),
+            spread_square(b_do[:few], devices),
+            spread_square(b_do[2 * few : 3 * few], devices),
+        ],
+        axis=1,
+    )
+    early = lax.all_to_all(early, axes, 0, 0, tiled=True)
+    table = early[:, 0, 3 * few : 3 * few + 2].astype(jnp.int32)
+    early_grad, early_new = settle(
+        True, table, early, params[late_rows:], first_old[late_rows:], second_old[late_rows:]
+    )
+    piece_range = jnp.arange(devices, dtype=jnp.int32)
+    reversed_bits = jnp.zeros_like(piece_range)
+    bit = 1
+    while bit < devices:
+        reversed_bits = reversed_bits * 2 + (piece_range // bit) % 2
+        bit *= 2
+    unit = jnp.arange(16, dtype=jnp.int32)
+    order = (
+        (unit[:, None, None, None] == unit[None, None, None, :])
+        & (piece_range[None, :, None, None] == (me ^ reversed_bits)[None, None, :, None])
+    ).astype(jnp.bfloat16)
+    order = order.reshape(16 * devices, 16 * devices)
+    early_pieces = gather_everywhere(early_new, devices, groups)
+    adapters_new = assemble(order, early_pieces, total_rows, late_rows, 32, None)
+    late = jnp.concatenate(
+        [spread_wide(a_qkv, devices)]
+        + [spread_square(b_qkv[i * few : (i + 1) * few], devices) for i in range(4)],
+        axis=1,
+    )
+    late = lax.all_to_all(late, axes, 0, 0, tiled=True)
+    late_grad, late_new = settle(
+        False, table, late, params[:late_rows], first_old[:late_rows], second_old[:late_rows]
+    )
+    late_pieces = gather_everywhere(late_new, devices, groups)
+    adapters_new = assemble(order, late_pieces, total_rows, 0, 64, adapters_new)
+    grads = jnp.concatenate([late_grad, early_grad]).reshape(devices, own_rows, LANES)
+    grads = lax.all_to_all(grads, axes, 0, 0, tiled=True)
+    grad_shard = jnp.transpose(grads, (1, 0, 2)).reshape(-1).astype(jnp.float32)
+    current = jnp.zeros((), jnp.float32)
+    first_moment, second_moment, _ = adam(current, moment1, moment2, grad_shard)
+    return grad_shard, first_moment, second_moment, adapters_new.reshape(-1)
+
+
 def per_device(
     tokens,
     cotangent,
@@ -534,190 +1371,117 @@
     segment = jnp.sum((half_row[:, None] >= seq_ends[None, :]).astype(jnp.int32), axis=1)
     picked = (segment[:, None] == jnp.arange(segments, dtype=jnp.int32)[None, :]).astype(jnp.int32)
     position = half_row - jnp.sum(picked * seq_starts[None, :], axis=1)
-    row_adapter = jnp.sum(picked * seq_adapter[0][None, :], axis=1)
-    meta = jnp.stack([facts[:, 2], segment], axis=1)
+    turns = max(1, segments - 1)
+    long_index = jnp.sum(jnp.where(lengths == half_rows, jnp.arange(segments, dtype=jnp.int32), 0))
+    on_long = my_half == long_half
+    turn_range = jnp.arange(turns, dtype=jnp.int32)
+    turn_segment = jnp.where(
+        on_long, long_index, turn_range + (turn_range >= long_index).astype(jnp.int32)
+    )
+    turn_adapter = jnp.sum(
+        jnp.where(
+            turn_segment[:, None] == jnp.arange(segments, dtype=jnp.int32)[None, :],
+            seq_adapter[0][None, :],
+            0,
+        ),
+        axis=1,
+    )
+    row_turn = jnp.where(on_long, 0, segment - (segment > long_index).astype(jnp.int32))
+    meta = jnp.stack([facts[:, 2], segment, row_turn], axis=1)
     key_metas = [meta[i * row_count : (i + 1) * row_count] for i in range(half_devices)]
+    meta = key_metas[0]
     columns = ADAPTERS * RANK
-    adapter_selector_mask = (
-        row_adapter[:row_count, None] == (jnp.arange(columns, dtype=jnp.int32) // RANK)[None, :]
-    ).astype(jnp.float32)
+    few = turns * RANK
+    few_range = jnp.arange(few, dtype=jnp.int32)
+    few_column = jnp.repeat(turn_adapter, RANK) * RANK + few_range % RANK
+    few_choice = (jnp.arange(columns, dtype=jnp.int32)[:, None] == few_column[None, :]).astype(
+        jnp.bfloat16
+    )
     cos_table, sin_table = rope_tables(position[:row_count], head_width)
-
-    my_tokens = bring(tokens).astype(jnp.float32)
+    selected = select(turn_adapter, adapters, feature_width, hidden_width)
+    a_qkv, a_guo, a_down, b_qkv, b_gu, b_do = selected
+    q_gain_row = head_gain(q_gain)
+    k_gain_row = head_gain(k_gain)
+
+    my_tokens = bring(tokens)
     my_grads = bring(cotangent)
-    shapes = [(feature_width, feature_width)] * 4 + [
-        (feature_width, hidden_width),
-        (feature_width, hidden_width),
-        (hidden_width, feature_width),
-    ]
-    partial_pieces = unpack(adapters, shapes, columns)
-    normalized_input = rms_norm(my_tokens, attn_gain).astype(jnp.bfloat16)
-    query_preactivation, query_inner = project(
-        normalized_input, query_weight, partial_pieces[0], adapter_selector_mask
-    )
-    key_preactivation, key_inner = project(
-        normalized_input, key_weight, partial_pieces[1], adapter_selector_mask
-    )
-    value_raw, value_inner = project(
-        normalized_input, value_weight, partial_pieces[2], adapter_selector_mask
-    )
-    value_lowrank = value_raw.astype(jnp.bfloat16)
-    query_low = shape_heads(query_preactivation, q_gain, cos_table, sin_table, head_width).astype(
-        jnp.bfloat16
-    )
-    key_low = shape_heads(key_preactivation, k_gain, cos_table, sin_table, head_width).astype(
-        jnp.bfloat16
+    normed, inner, query_raw, key_raw, query_low, key_low, value_low = project_heads(
+        my_tokens,
+        attn_gain,
+        (query_weight, key_weight, value_weight),
+        a_qkv,
+        b_qkv,
+        meta,
+        cos_table,
+        sin_table,
+        q_gain_row,
+        k_gain_row,
+        head_width,
     )
     keys = gather_half(key_low, groups)
-    values = gather_half(value_lowrank, groups)
+    values = gather_half(value_low, groups)
     attended_low, log_total = attend(
-        attn_bias, query_low, key_metas[0], keys, values, key_metas, segments, head_width
-    )
-    attention_output, out_inner = project(
-        attended_low, output_weight, partial_pieces[3], adapter_selector_mask
-    )
-    residual_stream = my_tokens + attention_output
-    hidden_lowrank = rms_norm(residual_stream, ffn_gain).astype(jnp.bfloat16)
-    gate_preactivation, gate_inner = project(
-        hidden_lowrank, gate_weight, partial_pieces[4], adapter_selector_mask
-    )
-    up_preactivation, up_inner = project(
-        hidden_lowrank, up_weight, partial_pieces[5], adapter_selector_mask
-    )
-    activated_hidden = (jax.nn.silu(gate_preactivation) * up_preactivation).astype(jnp.bfloat16)
-    ffn_out, down_inner = project(
-        activated_hidden, down_weight, partial_pieces[6], adapter_selector_mask
-    )
-    final_result = residual_stream + ffn_out
-    layer_out = send_back(final_result.astype(jnp.bfloat16))
-    grad_act, down_a, down_b = project_back(
-        my_grads,
-        activated_hidden,
-        down_inner,
-        down_weight,
-        partial_pieces[6],
-        adapter_selector_mask,
-    )
-    _, act_back = jax.vjp(
-        lambda gate_values, up_values: jax.nn.silu(gate_values) * up_values,
-        gate_preactivation,
-        up_preactivation,
-    )
-    grad_gate, grad_up = act_back(grad_act)
-    grad_hidden_gate, gate_a, gate_b = project_back(
-        grad_gate.astype(jnp.bfloat16),
-        hidden_lowrank,
-        gate_inner,
-        gate_weight,
-        partial_pieces[4],
-        adapter_selector_mask,
-    )
-    grad_hidden_up, up_a, up_b = project_back(
-        grad_up.astype(jnp.bfloat16),
-        hidden_lowrank,
-        up_inner,
-        up_weight,
-        partial_pieces[5],
-        adapter_selector_mask,
-    )
-    _, ffn_norm_back = jax.vjp(lambda values: rms_norm(values, ffn_gain), residual_stream)
-    grad_residual = (
-        my_grads.astype(jnp.float32) + ffn_norm_back(grad_hidden_gate + grad_hidden_up)[0]
-    )
-    grad_attended, out_a, out_b = project_back(
-        grad_residual.astype(jnp.bfloat16),
-        attended_low,
-        out_inner,
-        output_weight,
-        partial_pieces[3],
-        adapter_selector_mask,
-    )
-    grad_attended_low = grad_attended.astype(jnp.bfloat16)
+        attn_bias, query_low, meta, keys, values, key_metas, segments, head_width
+    )
+    layer_rows, grad_residual, grad_attended, grad_a_guo, grad_a_down, grad_b_gu, grad_b_do = (
+        feed_forward(
+            attended_low,
+            my_tokens,
+            my_grads,
+            ffn_gain,
+            (output_weight, gate_weight, up_weight, down_weight),
+            (a_guo, a_down, b_gu, b_do),
+            meta,
+        )
+    )
+    layer_out = send_back(layer_rows)
     grad_query, grad_keys, grad_values = attend_back(
         attn_bias,
         query_low,
-        key_metas[0],
+        meta,
         log_total,
         attended_low,
-        grad_attended_low,
+        grad_attended,
         keys,
         values,
         key_metas,
         segments,
         head_width,
     )
-    grad_key, grad_value = grad_keys[0], grad_values[0]
+    key_terms, value_terms = [grad_keys[0]], [grad_values[0]]
     for shift in range(1, half_devices):
         back_shift = half_devices - shift
-        grad_key = grad_key + within_half(grad_keys[shift], back_shift, groups).astype(jnp.float32)
-        grad_value = grad_value + within_half(grad_values[shift], back_shift, groups).astype(
-            jnp.float32
-        )
-    _, query_head_back = jax.vjp(
-        lambda values: shape_heads(values, q_gain, cos_table, sin_table, head_width),
-        query_preactivation,
-    )
-    _, key_head_back = jax.vjp(
-        lambda values: shape_heads(values, k_gain, cos_table, sin_table, head_width),
-        key_preactivation,
-    )
-    grad_query_raw = query_head_back(grad_query)[0].astype(jnp.bfloat16)
-    grad_key_raw = key_head_back(grad_key)[0].astype(jnp.bfloat16)
-    grad_norm_q, query_a, query_b = project_back(
-        grad_query_raw,
-        normalized_input,
-        query_inner,
-        query_weight,
-        partial_pieces[0],
-        adapter_selector_mask,
-    )
-    grad_norm_k, key_a, key_b = project_back(
-        grad_key_raw,
-        normalized_input,
-        key_inner,
-        key_weight,
-        partial_pieces[1],
-        adapter_selector_mask,
-    )
-    grad_norm_v, value_a, value_b = project_back(
-        grad_value.astype(jnp.bfloat16),
-        normalized_input,
-        value_inner,
-        value_weight,
-        partial_pieces[2],
-        adapter_selector_mask,
-    )
-    _, attn_norm_back = jax.vjp(lambda values: rms_norm(values, attn_gain), my_tokens)
-    grad_tokens = grad_residual + attn_norm_back(grad_norm_q + grad_norm_k + grad_norm_v)[0]
-    input_grad = send_back(grad_tokens.astype(jnp.bfloat16))
-    pairs = [
-        (query_a, query_b),
-        (key_a, key_b),
-        (value_a, value_b),
-        (out_a, out_b),
-        (gate_a, gate_b),
-        (up_a, up_b),
-        (down_a, down_b),
-    ]
-    flat_grads = jnp.concatenate(
-        [partial_piece.reshape(-1) for pair_grads in pairs for partial_piece in pair_grads]
-    )
-    axis_sizes = [("dp", lax.axis_size("dp")), ("group", groups)]
-    shards = axis_sizes[0][1] * groups
-    grad_shard = scatter_sum(flat_grads.astype(jnp.bfloat16).reshape(shards, -1), axis_sizes)
-    grad_shard = grad_shard.reshape(-1).astype(jnp.float32)
-    shard_count = grad_shard.shape[0]
-    shard_start = lax.axis_index(("dp", "group")) * shard_count
-    current = lax.dynamic_slice_in_dim(adapters, shard_start, shard_count).astype(jnp.float32)
-    first_moment = BETA_ONE * moment1 + (1.0 - BETA_ONE) * grad_shard
-    second_moment = BETA_TWO * moment2 + (1.0 - BETA_TWO) * grad_shard * grad_shard
-    first_fix = first_moment / (1.0 - BETA_ONE**update_count)
-    second_fix = second_moment / (1.0 - BETA_TWO**update_count)
-    updated = current - LEARN_RATE * (
-        first_fix / (jnp.sqrt(second_fix) + ADAM_EPS) + WEIGHT_DECAY * current
-    )
-    adapters_new = lax.all_gather(updated.astype(jnp.bfloat16), ("dp", "group"), axis=0, tiled=True)
-    return (layer_out, input_grad, grad_shard, first_moment, second_moment, adapters_new)
+        key_terms.append(within_half(grad_keys[shift], back_shift, groups))
+        value_terms.append(within_half(grad_values[shift], back_shift, groups))
+    grad_rows, grad_a_qkv, grad_b_qkv = project_heads_back(
+        grad_query,
+        key_terms,
+        value_terms,
+        query_raw,
+        key_raw,
+        normed,
+        inner,
+        my_tokens,
+        grad_residual,
+        attn_gain,
+        (query_weight, key_weight, value_weight),
+        a_qkv,
+        b_qkv,
+        meta,
+        cos_table,
+        sin_table,
+        q_gain_row,
+        k_gain_row,
+        head_width,
+    )
+    input_grad = send_back(grad_rows)
+    grads = (grad_a_qkv, grad_b_qkv, grad_a_guo, grad_a_down, grad_b_gu, grad_b_do)
+    devices = lax.axis_size("dp") * groups
+    if spreads_evenly(devices, feature_width, hidden_width, adapters.shape[0], turns):
+        settled = settle_spread(grads, turn_adapter, adapters, moment1, moment2, devices)
+    else:
+        settled = settle_shards(grads, few_choice, adapters, moment1, moment2, groups)
+    return (layer_out, input_grad) + settled
 
 
 def solution(mesh):

time: 561 us -> 393 us (0.70)
  matrix products: 145 us -> 14.5 us
  Pallas kernels: 50.6 us -> 175 us
  waiting for transfers between devices: 156 us -> 74.1 us
  local copies, waits for them, and re-layouts: 104 us -> 49.5 us
  other arithmetic: 59.8 us -> 28.8 us
  starting transfers between devices: 16.3 us -> 41.1 us
  between operations: 18.4 us -> 3.63 us
    dot_general x56 -> x0, matrix products: 132 us -> none  [the longest x21 62.4 us: contract_columns(): lax.dot_general(left, right, (((1,), (1,)), ((), ())), preferred_element_...]
    pallas_call x0 -> x8, Pallas kernels: none -> 115 us  [the longest x1 51.8 us: feed_forward(): pl.pallas_call(feed_forward_kernel, grid=(hidden // tile,), in_specs=[ful...]
    ppermute x5 -> x10, waiting for transfers between devices: 104 us -> 41.7 us  [the longest x4 25 us: gather_everywhere(): lax.ppermute(send, 'group', [(i, i ^ bit) for i in range(groups)])]
    all_gather x1 -> x0, waiting for transfers between devices: 26.6 us -> none  [per_device(): lax.all_gather(updated.astype(jnp.bfloat16), ('dp', 'group'), axis=0, til...]
    convert_element_type x16 -> x5, other arithmetic: 27.3 us -> 3.86 us  [the longest x2 1.91 us: settle_spread(): table = early[:, 0, 3 * few:3 * few + 2].astype(jnp.int32)]
    dynamic_slice x2 -> x0, local copies, waits for them, and re-layouts: 20 us -> none  [the longest x1 15.1 us: scatter_sum(): keep = lax.dynamic_index_in_dim(spread, own, 2, keepdims=False)]
    all_to_all x0 -> x4, starting transfers between devices: none -> 17.8 us  [the longest x1 6.09 us: settle_spread(): late = lax.all_to_all(late, axes, 0, 0, tiled=True)]
    all_to_all x0 -> x4, waiting for transfers between devices: none -> 14 us  [the longest x1 14 us: settle_spread(): moments = lax.all_to_all(moments, axes, 0, 0, tiled=True)]
  transfers between devices with their start and end apart: 20 -> 28, of which waited for: 9 -> 10; matrix products, arithmetic and copies ran while one was open for 25% -> 22% of each run, Pallas kernels for 0% -> 22%
where the time goes in v2:
time: 393 us; the launch traced here: 387 us
  Pallas kernels  175 us (45%)
  waiting for transfers between devices  74.1 us (19%)
  local copies, waits for them, and re-layouts  49.5 us (13%)
  starting transfers between devices  41.1 us (10%)
  other arithmetic  28.8 us (7%)
  matrix products  14.5 us (4%)
    pallas_call x1, Pallas kernels, feed_forward(): pl.pallas_call(feed_forward_kernel, grid=(hidden // tile,), in_specs=[ful...  51.8 us
    pallas_call x1, Pallas kernels, attend_back(): pl.pallas_call(functools.partial(attend_back_kernel, count, segments, wid...  40.6 us
    ppermute x4, waiting for transfers between devices, gather_everywhere(): lax.ppermute(send, 'group', [(i, i ^ bit) for i in range(groups)])  25 us
    unnamed x102, local copies, waits for them, and re-layouts  23.4 us
    pallas_call x2, Pallas kernels, assemble(): pl.pallas_call(functools.partial(assemble_kernel, len(pieces)), grid=(ste...  19.8 us
    pallas_call x1, Pallas kernels, attend(): pl.pallas_call(functools.partial(attend_kernel, count, segments, width),...  19.3 us
    ppermute x4, waiting for transfers between devices, to_other_half(): lax.ppermute(array, 'group', [(i, (i + half) % groups) for i in range(gro...  18.4 us
    pallas_call x1, Pallas kernels, project_heads_back(): pl.pallas_call(functools.partial(project_heads_back_kernel, count, width)...  17.6 us
  transfers between devices with their start and end apart: 28, of which 10 were waited for; matrix products, arithmetic and copies ran while one was open for 22% of the time, Pallas kernels for 22%

profile of v2, /device:TPU:0, one launch (start us, length us, event | category | flops | bytes accessed | tf_op | source)
XLA Modules:
  0.0 387.1 jit_solution(17400616438065773357)
XLA Ops:
  13.5 2.0 fusion.93
  21.6 2.3 constant_dynamic-slice_fusion.1
  25.7 5.6 %select.154 = (bf16[1024,128]{1,0:T(8,128)(2,1)}, bf16[1024,128]{1,0:T(8,128)(2,1)}, bf16[4096,128]{1,0:T(8,128)(2,1)}, bf16[128,1024]{1,0:T(8,128)(2,1)}, bf16[...) custom-call(s32[2]{0:T(128)} %copy-done.29, bf16[23552,128]{1,0:T(8,128)(2,1)} %bitcast.234), custom_call_target="tpu_custom_call" | custom-call | flops 2147483648 | bytes 12058624 | tf_op jit(solution)/shard_map/select/pallas_call | solution.py:638
  35.2 2.9 collective-permute-start.1
  40.9 3.4 fusion.37
  44.3 6.2 %collective-permute-done.1 = bf16[256,1024]{1,0:T(8,128)(2,1)S(1)} collective-permute-done((bf16[256,1024]{1,0:T(8,128)(2,1)}, bf16[256,1024]{1,0:T(8,128)(2,1)S(1)}, u32[]{:S(2)}, u32[]{:S(2)}) %collective-permute-start.1) | collective-permute-done | bytes 524320 | tf_op jit(solution)/shard_map/ppermute | solution.py:302
  52.6 14.6 %project_heads.1 = (bf16[512,1024]{1,0:T(8,128)(2,1)}, bf16[512,128]{1,0:T(8,128)(2,1)}, f32[512,1024]{1,0:T(8,128)}, f32[512,1024]{1,0:T(8,128)}, bf16[512,1024...) custom-call(bf16[512,1024]{1,0:T(8,128)(2,1)} %pad_maximum_fusion.1.x_ref.refs_8_, ...), custom_call_target="tpu_custom_call" | custom-call | flops 4294967296 | bytes 16777216 | tf_op jit(solution)/shard_map/project_heads/pallas_call | solution.py:768
  73.9 9.0 %collective-permute-done.5 = bf16[256,1024]{1,0:T(8,128)(2,1)} collective-permute-done((bf16[256,1024]{1,0:T(8,128)(2,1)}, bf16[256,1024]{1,0:T(8,128)(2,1)}, u32[]{:S(2)}, u32[]{:S(2)}) %collective-permute-start.5) | collective-permute-done | bytes 524320 | tf_op jit(solution)/shard_map/ppermute | solution.py:302
  85.2 19.3 %attend.1 = (bf16[512,1024]{1,0:T(8,128)(2,1)}, f32[512,1024]{1,0:T(8,128)}) custom-call(f32[2,16]{1,0:T(2,128)} %bias_ref.3, bf16[512,1024]{1,0:T(8,128)(2,1)} %get-tuple-element.44.query_ref, s32[512,3]{1,0:T(8,128)} %copy.108.meta_ref.qmeta_ref.refs_4_.refs_16_, bf16[512,1024]{1,0:T(8,128)(2,1)} %get-tuple-element.45.refs_0_, ...), custom_call_target="tpu_custom_call" | custom-call | flops 2147483648 | bytes 6291456 | tf_op jit(solution)/shard_map/attend/pallas_call | solution.py:127
  104.6 51.8 %feed_forward.1 = (bf16[512,1024]{1,0:T(8,128)(2,1)}, f32[512,1024]{1,0:T(8,128)}, bf16[512,1024]{1,0:T(8,128)(2,1)}, bf16[1024,128]{1,0:T(8,128)(2,1)}, bf16[10...) custom-call(bf16[512,1024]{1,0:T(8,128)(2,1)} %get-tuple-element.47.att_ref.attended_ref, ...), custom_call_target="tpu_custom_call" | custom-call | flops 30064771072 | bytes 41943040 | tf_op jit(solution)/shard_map/feed_forward/pallas_call | solution.py:1112
  160.0 40.6 %attend_back.1 = (f32[512,1024]{1,0:T(8,128)}, f32[512,1024]{1,0:T(8,128)}, bf16[512,1024]{1,0:T(8,128)(2,1)}, f32[512,1024]{1,0:T(8,128)}, bf16[512,1024]{1,0:T(8,128)(2,1)}) custom-call(f32[2,16]{1,0:T(2,128)} %bias_ref.3, bf16[512,1024]{1,0:T(8,128)(2,1)} %get-tuple-element.44.query_ref, s32[512,3]{1,0:T(8,128)} %copy.108.meta_ref.qmeta_ref.refs_4_.refs_16_, ...), custom_call_target="tpu_custom_call" | custom-call | flops 5368709120 | bytes 12582912 | tf_op jit(solution)/shard_map/attend_back/pallas_call | solution.py:250
  202.6 4.9 %all-to-all-start.2 = ((f32[32,46,128]{2,1,0:T(8,128)}), f32[32,46,128]{2,1,0:T(8,128)S(1)}, u32[]{:S(2)}, u32[]{:S(2)}) async-start(f32[32,46,128]{2,1,0:T(8,128)} %copy.102), calls=%async_computation.2 | async-start | bytes 1572864 | tf_op jit(solution)/shard_map/all_to_all | solution.py:1191
  214.2 14.0 %all-to-all-done.2 = f32[32,46,128]{2,1,0:T(8,128)S(1)} async-done(((f32[32,46,128]{2,1,0:T(8,128)}), f32[32,46,128]{2,1,0:T(8,128)S(1)}, u32[]{:S(2)}, u32[]{:S(2)}) %all-to-all-start.2) | async-done | bytes 753696 | tf_op jit(solution)/shard_map/all_to_all | solution.py:1191
  228.1 3.7 all-to-all-start
  234.3 2.0 reshape.602
  237.9 17.6 %project_heads_back.1 = (bf16[512,1024]{1,0:T(8,128)(2,1)}, bf16[1024,128]{1,0:T(8,128)(2,1)}, bf16[128,1024]{1,0:T(8,128)(2,1)}) custom-call(f32[512,1024]{1,0:T(8,128)} %get-tuple-element.55.gq_ref, f32[512,1024]{1,0:T(8,128)} %get-tuple-element.56.refs_0_, bf16[512,1024]{1,0:T(8,128)(2,1)} %collective-permute-done.9.refs_1_, ...), custom_call_target="tpu_custom_call" | custom-call | flops 4294967296 | bytes 22020096 | tf_op jit(solution)/shard_map/project_heads_back/pallas_call | solution.py:924
  264.1 3.9 fusion.50
  267.9 3.2 collective-permute-done.12
  274.0 6.1 %all-to-all-start.1 = ((bf16[32,64,128]{2,1,0:T(8,128)(2,1)}), bf16[32,64,128]{2,1,0:T(8,128)(2,1)S(1)}, u32[]{:S(2)}, u32[]{:S(2)}) async-start(bf16[32,64,128]{2,1,0:T(8,128)(2,1)} %constant_dynamic-update-slice_fusion.2), calls=%async_computation.1 | async-start | bytes 1048576 | tf_op jit(solution)/shard_map/all_to_all | solution.py:1237
  284.0 3.7 settle_early.1
  287.7 2.8 collective-permute-start.19
  290.5 4.0 %fusion.55 = bf16[512,1024]{1,0:T(8,128)(2,1)} fusion(bf16[256,1024]{1,0:T(8,128)(2,1)} %collective-permute-done.13, bf16[256,1024]{1,0:T(8,128)(2,1)} %collective-permute-done.12, bf16[512,1024]{1,0:T(8,128)(2,1)S(1)} %collective-permute-done.11, bf16[512,1024]{1,0:T(8,128)(2,1)S(1)} %copy-done.23, s32[1536]{0:T(1024)S(1)} %pad_add_fusion.1, ...), kind=kOutput, calls=%fused_computation.44 | convolution fusion | flops 1624506368 | bytes 4202496 | tf_op jit(solution)/shard_map/dot_general | solution.py:283
  294.5 6.6 %collective-permute-done.19.refs_1_ = bf16[1,544,128]{2,1,0:T(8,128)(2,1)S(1)} collective-permute-done((bf16[1,544,128]{2,1,0:T(8,128)(2,1)}, bf16[1,544,128]{2,1,0:T(8,128)(2,1)S(1)}, u32[]{:S(2)}, u32[]{:S(2)}) %collective-permute-start.19) | collective-permute-done | bytes 139296 | tf_op jit(solution)/shard_map/ppermute | solution.py:504
  302.0 2.5 settle_late.1
  307.0 3.4 collective-permute-done.20.refs_2_
  315.0 3.0 all-to-all-start.3
  320.6 4.0 %collective-permute-done.21.refs_3_ = bf16[4,544,128]{2,1,0:T(8,128)(2,1)S(1)} collective-permute-done((bf16[4,544,128]{2,1,0:T(8,128)(2,1)S(1)}, bf16[4,544,128]{2,1,0:T(8,128)(2,1)S(1)}, u32[]{:S(2)}, u32[]{:S(2)}) %collective-permute-start.21) | collective-permute-done | bytes 557088 | tf_op jit(solution)/shard_map/ppermute | solution.py:504
  330.7 2.6 collective-permute-done.16.refs_3_
  335.5 21.8 %collective-permute-done.17.refs_4_ = bf16[8,192,128]{2,1,0:T(8,128)(2,1)S(1)} collective-permute-done((bf16[8,192,128]{2,1,0:T(8,128)(2,1)S(1)}, bf16[8,192,128]{2,1,0:T(8,128)(2,1)S(1)}, u32[]{:S(2)}, u32[]{:S(2)}) %collective-permute-start.17) | collective-permute-done | bytes 393248 | tf_op jit(solution)/shard_map/ppermute | solution.py:506
  361.6 3.2 collective-permute-done.23.refs_5_
  366.2 14.9 %assemble.2.refs_6_ = bf16[23552,128]{1,0:T(8,128)(2,1)} custom-call(bf16[512,512]{1,0:T(8,128)(2,1)} %copy.107.order_ref, bf16[1,544,128]{2,1,0:T(8,128)(2,1)} %bitcast.198, bf16[1,544,128]{2,1,0:T(8,128)(2,1)} %copy-done.4, bf16[2,544,128]{2,1,0:T(8,128)(2,1)} %copy-done.1, bf16[4,544,128]{2,1,0:T(8,128)(2,1)} %copy-done, bf16[8,544,128]{2,1,0:T(8,128)(2,1)} %copy-done.2, ...), custom_call_target="tpu_custom_call" | custom-call | flops 2281701376 | bytes 8912896 | tf_op jit(solution)/shard_map/assemble/pallas_call | solution.py:538
  382.1 4.8 %assemble.3 = bf16[23552,128]{1,0:T(8,128)(2,1)} custom-call(bf16[512,512]{1,0:T(8,128)(2,1)} %copy.107.order_ref, bf16[1,192,128]{2,1,0:T(8,128)(2,1)} %bitcast.207, bf16[1,192,128]{2,1,0:T(8,128)(2,1)} %copy-done.17, bf16[2,192,128]{2,1,0:T(8,128)(2,1)} %copy-done.8, bf16[4,192,128]{2,1,0:T(8,128)(2,1)} %copy-done.6, ...), custom_call_target="tpu_custom_call", output_to_operand_aliasing={{}: (7, {})} | custom-call | flops 805306368 | bytes 3145728 | tf_op jit(solution)/shard_map/assemble/pallas_call | solution.py:538
  (257 shorter events, 93.0 us)
Async XLA Ops:
  0.6 30.7 %collective-permute-start = (bf16[512,1024]{1,0:T(8,128)(2,1)}, bf16[512,1024]{1,0:T(8,128)(2,1)S(1)}, u32[]{:S(2)}, u32[]{:S(2)}) collective-permute-start(bf16[512,1024]{1,0:T(8,128)(2,1)} %param.21), channel_id=1, source_target_pairs={{1,0},{0,1},{3,2},{2,3},{5,4},{4,5},{7,6},{6,7},{9,8},{8,9},{11,10... | collective-permute-start | bytes 3145736 | tf_op jit(solution)/shard_map/ppermute | solution.py:293
  1.1 39.7 %collective-permute-start.4 = (bf16[512,1024]{1,0:T(8,128)(2,1)}, bf16[512,1024]{1,0:T(8,128)(2,1)}, u32[]{:S(2)}, u32[]{:S(2)}) collective-permute-start(bf16[512,1024]{1,0:T(8,128)(2,1)} %param.22), channel_id=1, source_target_pairs={{1,0},{0,1},{3,2},{2,3},{5,4},{4,5},{7,6},{6,7},{9,8},{8,9},{11,10... | collective-permute-start | bytes 3145736 | tf_op jit(solution)/shard_map/ppermute | solution.py:293
  35.2 15.3 %collective-permute-start.1 = (bf16[256,1024]{1,0:T(8,128)(2,1)}, bf16[256,1024]{1,0:T(8,128)(2,1)S(1)}, u32[]{:S(2)}, u32[]{:S(2)}) collective-permute-start(bf16[256,1024]{1,0:T(8,128)(2,1)} %get-tuple-element.88), channel_id=1, source_target_pairs={{0,2},{1,3},{2,0},{3,1},{4,6},{5,7},{6,4},{7,5},{8,10},{9,11},{10,... | collective-permute-start | bytes 1572872 | tf_op jit(solution)/shard_map/ppermute | solution.py:302
  67.2 18.0 %collective-permute-start.2 = (bf16[512,1024]{1,0:T(8,128)(2,1)}, bf16[512,1024]{1,0:T(8,128)(2,1)}, u32[]{:S(2)}, u32[]{:S(2)}) collective-permute-start(bf16[512,1024]{1,0:T(8,128)(2,1)} %get-tuple-element.45.refs_0_), channel_id=1, source_target_pairs={{1,0},{0,1},{3,2},{2,3},{5,4},{4,5},{7,6},{6,7},{9,8},{8,9},{11,10... | collective-permute-start | bytes 3145736 | tf_op jit(solution)/shard_map/ppermute | solution.py:293
  67.3 17.9 %collective-permute-start.3 = (bf16[512,1024]{1,0:T(8,128)(2,1)}, bf16[512,1024]{1,0:T(8,128)(2,1)}, u32[]{:S(2)}, u32[]{:S(2)}) collective-permute-start(bf16[512,1024]{1,0:T(8,128)(2,1)} %get-tuple-element.46.refs_2_), channel_id=1, source_target_pairs={{1,0},{0,1},{3,2},{2,3},{5,4},{4,5},{7,6},{6,7},{9,8},{8,9},{11,10... | collective-permute-start | bytes 3145736 | tf_op jit(solution)/shard_map/ppermute | solution.py:293
  68.7 14.2 %collective-permute-start.5 = (bf16[256,1024]{1,0:T(8,128)(2,1)}, bf16[256,1024]{1,0:T(8,128)(2,1)}, u32[]{:S(2)}, u32[]{:S(2)}) collective-permute-start(bf16[256,1024]{1,0:T(8,128)(2,1)} %get-tuple-element.86), channel_id=1, source_target_pairs={{0,2},{1,3},{2,0},{3,1},{4,6},{5,7},{6,4},{7,5},{8,10},{9,11},{10,... | collective-permute-start | bytes 1572872 | tf_op jit(solution)/shard_map/ppermute | solution.py:302
  158.3 79.2 %collective-permute-start.7 = (bf16[256,1024]{1,0:T(8,128)(2,1)}, bf16[256,1024]{1,0:T(8,128)(2,1)}, u32[]{:S(2)}, u32[]{:S(2)}) collective-permute-start(bf16[256,1024]{1,0:T(8,128)(2,1)} %slice.140), channel_id=1, source_target_pairs={{0,2},{1,3},{2,0},{3,1},{4,6},{5,7},{6,4},{7,5},{8,10},{9,11},{10,... | collective-permute-start | bytes 1572872 | tf_op jit(solution)/shard_map/ppermute | solution.py:302
  200.6 37.2 %collective-permute-start.9 = (bf16[512,1024]{1,0:T(8,128)(2,1)}, bf16[512,1024]{1,0:T(8,128)(2,1)}, u32[]{:S(2)}, u32[]{:S(2)}) collective-permute-start(bf16[512,1024]{1,0:T(8,128)(2,1)} %get-tuple-element.57), channel_id=1, source_target_pairs={{1,0},{0,1},{3,2},{2,3},{5,4},{4,5},{7,6},{6,7},{9,8},{8,9},{11,10... | collective-permute-start | bytes 3145736 | tf_op jit(solution)/shard_map/ppermute | solution.py:293
  200.7 37.1 %collective-permute-start.10 = (bf16[512,1024]{1,0:T(8,128)(2,1)}, bf16[512,1024]{1,0:T(8,128)(2,1)}, u32[]{:S(2)}, u32[]{:S(2)}) collective-permute-start(bf16[512,1024]{1,0:T(8,128)(2,1)} %get-tuple-element.59), channel_id=1, source_target_pairs={{1,0},{0,1},{3,2},{2,3},{5,4},{4,5},{7,6},{6,7},{9,8},{8,9},{11,10... | collective-permute-start | bytes 3145736 | tf_op jit(solution)/shard_map/ppermute | solution.py:293
  202.6 25.6 %all-to-all-start.2 = ((f32[32,46,128]{2,1,0:T(8,128)}), f32[32,46,128]{2,1,0:T(8,128)S(1)}, u32[]{:S(2)}, u32[]{:S(2)}) async-start(f32[32,46,128]{2,1,0:T(8,128)} %copy.102), calls=%async_computation.2 | async-start | bytes 1572864 | tf_op jit(solution)/shard_map/all_to_all | solution.py:1191
  228.1 45.9 %all-to-all-start = ((bf16[32,144,128]{2,1,0:T(8,128)(2,1)}), bf16[32,144,128]{2,1,0:T(8,128)(2,1)}, u32[]{:S(2)}, u32[]{:S(2)}) async-start(bf16[32,144,128]{2,1,0:T(8,128)(2,1)} %constant_dynamic-update-slice_fusion), calls=%async_computation | async-start | bytes 2359296 | tf_op jit(solution)/shard_map/all_to_all | solution.py:1213
  237.3 26.7 %collective-permute-start.6 = (bf16[512,1024]{1,0:T(8,128)(2,1)}, bf16[512,1024]{1,0:T(8,128)(2,1)S(1)}, u32[]{:S(2)}, u32[]{:S(2)}) collective-permute-start(bf16[512,1024]{1,0:T(8,128)(2,1)} %get-tuple-element.52), channel_id=1, source_target_pairs={{1,0},{0,1},{3,2},{2,3},{5,4},{4,5},{7,6},{6,7},{9,8},{8,9},{11,10... | collective-permute-start | bytes 3145736 | tf_op jit(solution)/shard_map/ppermute | solution.py:293
  237.5 26.5 %collective-permute-start.8 = (bf16[256,1024]{1,0:T(8,128)(2,1)}, bf16[256,1024]{1,0:T(8,128)(2,1)S(1)}, u32[]{:S(2)}, u32[]{:S(2)}) collective-permute-start(bf16[256,1024]{1,0:T(8,128)(2,1)} %collective-permute-done.7), channel_id=1, source_target_pairs={{1,0},{0,1},{3,2},{2,3},{5,4},{4,5},{7,6},{6,7},{9,8},{8,9},{11,10... | collective-permute-start | bytes 1572872 | tf_op jit(solution)/shard_map/ppermute | solution.py:293
  256.6 33.8 %collective-permute-start.11 = (bf16[512,1024]{1,0:T(8,128)(2,1)}, bf16[512,1024]{1,0:T(8,128)(2,1)S(1)}, u32[]{:S(2)}, u32[]{:S(2)}) collective-permute-start(bf16[512,1024]{1,0:T(8,128)(2,1)} %get-tuple-element.65), channel_id=1, source_target_pairs={{1,0},{0,1},{3,2},{2,3},{5,4},{4,5},{7,6},{6,7},{9,8},{8,9},{11,10... | collective-permute-start | bytes 3145736 | tf_op jit(solution)/shard_map/ppermute | solution.py:293
  256.9 14.3 %collective-permute-start.12 = (bf16[256,1024]{1,0:T(8,128)(2,1)S(1)}, bf16[256,1024]{1,0:T(8,128)(2,1)}, u32[]{:S(2)}, u32[]{:S(2)}) collective-permute-start(bf16[256,1024]{1,0:T(8,128)(2,1)S(1)} %slice.141), channel_id=1, source_target_pairs={{0,2},{1,3},{2,0},{3,1},{4,6},{5,7},{6,4},{7,5},{8,10},{9,11},{10,... | collective-permute-start | bytes 1572872 | tf_op jit(solution)/shard_map/ppermute | solution.py:302
  271.1 19.3 %collective-permute-start.13 = (bf16[256,1024]{1,0:T(8,128)(2,1)}, bf16[256,1024]{1,0:T(8,128)(2,1)}, u32[]{:S(2)}, u32[]{:S(2)}) collective-permute-start(bf16[256,1024]{1,0:T(8,128)(2,1)} %collective-permute-done.12), channel_id=1, source_target_pairs={{1,0},{0,1},{3,2},{2,3},{5,4},{4,5},{7,6},{6,7},{9,8},{8,9},{11,10... | collective-permute-start | bytes 1572872 | tf_op jit(solution)/shard_map/ppermute | solution.py:293
  274.0 27.2 %all-to-all-start.1 = ((bf16[32,64,128]{2,1,0:T(8,128)(2,1)}), bf16[32,64,128]{2,1,0:T(8,128)(2,1)S(1)}, u32[]{:S(2)}, u32[]{:S(2)}) async-start(bf16[32,64,128]{2,1,0:T(8,128)(2,1)} %constant_dynamic-update-slice_fusion.2), calls=%async_computation.1 | async-start | bytes 1048576 | tf_op jit(solution)/shard_map/all_to_all | solution.py:1237
  287.7 13.4 %collective-permute-start.19 = (bf16[1,544,128]{2,1,0:T(8,128)(2,1)}, bf16[1,544,128]{2,1,0:T(8,128)(2,1)S(1)}, u32[]{:S(2)}, u32[]{:S(2)}) collective-permute-start(bf16[1,544,128]{2,1,0:T(8,128)(2,1)} %bitcast.197), channel_id=1, source_target_pairs={{0,16},{4,20},{8,24},{12,28},{16,0},{20,4},{24,8},{28,12},{1,17},{... | collective-permute-start | bytes 417800 | tf_op jit(solution)/shard_map/ppermute | solution.py:504
  301.1 28.3 %copy-start.4 = (bf16[1,544,128]{2,1,0:T(8,128)(2,1)}, bf16[1,544,128]{2,1,0:T(8,128)(2,1)S(1)}, u32[]{:S(2)}) copy-start(bf16[1,544,128]{2,1,0:T(8,128)(2,1)S(1)} %collective-permute-done.19.refs_1_) | copy-start | bytes 417796
  301.1 9.3 %collective-permute-start.20 = (bf16[2,544,128]{2,1,0:T(8,128)(2,1)S(1)}, bf16[2,544,128]{2,1,0:T(8,128)(2,1)S(1)}, u32[]{:S(2)}, u32[]{:S(2)}) collective-permute-start(bf16[2,544,128]{2,1,0:T(8,128)(2,1)S(1)} %pad_maximum_fusion.6), channel_id=1, source_target_pairs={{0,8},{4,12},{8,0},{12,4},{16,24},{20,28},{24,16},{28,20},{1,9},{5... | collective-permute-start | bytes 835592 | tf_op jit(solution)/shard_map/ppermute | solution.py:504
  304.5 13.6 %collective-permute-start.14 = (bf16[1,192,128]{2,1,0:T(8,128)(2,1)}, bf16[1,192,128]{2,1,0:T(8,128)(2,1)S(1)}, u32[]{:S(2)}, u32[]{:S(2)}) collective-permute-start(bf16[1,192,128]{2,1,0:T(8,128)(2,1)} %bitcast.206), channel_id=1, source_target_pairs={{0,16},{4,20},{8,24},{12,28},{16,0},{20,4},{24,8},{28,12},{1,17},{... | collective-permute-start | bytes 147464 | tf_op jit(solution)/shard_map/ppermute | solution.py:504
  310.5 14.1 %collective-permute-start.21 = (bf16[4,544,128]{2,1,0:T(8,128)(2,1)S(1)}, bf16[4,544,128]{2,1,0:T(8,128)(2,1)S(1)}, u32[]{:S(2)}, u32[]{:S(2)}) collective-permute-start(bf16[4,544,128]{2,1,0:T(8,128)(2,1)S(1)} %pad_maximum_fusion.4), channel_id=1, source_target_pairs={{0,4},{4,0},{8,12},{12,8},{16,20},{20,16},{24,28},{28,24},{1,5},{5... | collective-permute-start | bytes 1671176 | tf_op jit(solution)/shard_map/ppermute | solution.py:504
  315.0 19.6 %all-to-all-start.3 = ((bf16[32,23,128]{2,1,0:T(8,128)(2,1)}), bf16[32,23,128]{2,1,0:T(8,128)(2,1)S(1)}, u32[]{:S(2)}, u32[]{:S(2)}) async-start(bf16[32,23,128]{2,1,0:T(8,128)(2,1)} %reshape.597), calls=%async_computation.3 | async-start | bytes 393216 | tf_op jit(solution)/shard_map/all_to_all | solution.py:1244
  318.1 9.4 %collective-permute-start.15 = (bf16[2,192,128]{2,1,0:T(8,128)(2,1)S(1)}, bf16[2,192,128]{2,1,0:T(8,128)(2,1)S(1)}, u32[]{:S(2)}, u32[]{:S(2)}) collective-permute-start(bf16[2,192,128]{2,1,0:T(8,128)(2,1)S(1)} %pad_maximum_fusion.9), channel_id=1, source_target_pairs={{0,8},{4,12},{8,0},{12,4},{16,24},{20,28},{24,16},{28,20},{1,9},{5... | collective-permute-start | bytes 294920 | tf_op jit(solution)/shard_map/ppermute | solution.py:504
  324.6 33.6 %copy-start = (bf16[4,544,128]{2,1,0:T(8,128)(2,1)}, bf16[4,544,128]{2,1,0:T(8,128)(2,1)S(1)}, u32[]{:S(2)}) copy-start(bf16[4,544,128]{2,1,0:T(8,128)(2,1)S(1)} %collective-permute-done.21.refs_3_) | copy-start | bytes 1671172
  325.8 33.2 %collective-permute-start.22 = (bf16[8,544,128]{2,1,0:T(8,128)(2,1)}, bf16[8,544,128]{2,1,0:T(8,128)(2,1)S(1)}, u32[]{:S(2)}, u32[]{:S(2)}) collective-permute-start(bf16[8,544,128]{2,1,0:T(8,128)(2,1)} %pad_maximum_fusion), channel_id=1, source_target_pairs={{0,2},{1,3},{2,0},{3,1},{4,6},{5,7},{6,4},{7,5},{8,10},{9,11},{10,... | collective-permute-start | bytes 3342344 | tf_op jit(solution)/shard_map/ppermute | solution.py:506
  327.5 30.6 %copy-start.8 = (bf16[2,192,128]{2,1,0:T(8,128)(2,1)}, bf16[2,192,128]{2,1,0:T(8,128)(2,1)S(1)}, u32[]{:S(2)}) copy-start(bf16[2,192,128]{2,1,0:T(8,128)(2,1)S(1)} %collective-permute-done.15.refs_2_) | copy-start | bytes 294916
  327.6 5.7 %collective-permute-start.16 = (bf16[4,192,128]{2,1,0:T(8,128)(2,1)S(1)}, bf16[4,192,128]{2,1,0:T(8,128)(2,1)S(1)}, u32[]{:S(2)}, u32[]{:S(2)}) collective-permute-start(bf16[4,192,128]{2,1,0:T(8,128)(2,1)S(1)} %pad_maximum_fusion.7), channel_id=1, source_target_pairs={{0,4},{4,0},{8,12},{12,8},{16,20},{20,16},{24,28},{28,24},{1,5},{5... | collective-permute-start | bytes 589832 | tf_op jit(solution)/shard_map/ppermute | solution.py:504
  333.3 24.0 %collective-permute-start.17 = (bf16[8,192,128]{2,1,0:T(8,128)(2,1)S(1)}, bf16[8,192,128]{2,1,0:T(8,128)(2,1)S(1)}, u32[]{:S(2)}, u32[]{:S(2)}) collective-permute-start(bf16[8,192,128]{2,1,0:T(8,128)(2,1)S(1)} %pad_maximum_fusion.5), channel_id=1, source_target_pairs={{0,2},{1,3},{2,0},{3,1},{4,6},{5,7},{6,4},{7,5},{8,10},{9,11},{10,... | collective-permute-start | bytes 1179656 | tf_op jit(solution)/shard_map/ppermute | solution.py:506
  334.7 25.9 %copy-start.15 = (f32[23,32,128]{2,1,0:T(8,128)}, f32[23,32,128]{2,1,0:T(8,128)S(1)}, u32[]{:S(2)}) copy-start(f32[23,32,128]{2,1,0:T(8,128)S(1)} %copy.105) | copy-start | bytes 1130500
  358.2 23.0 %collective-permute-start.18 = (bf16[16,192,128]{2,1,0:T(8,128)(2,1)}, bf16[16,192,128]{2,1,0:T(8,128)(2,1)S(1)}, u32[]{:S(2)}, u32[]{:S(2)}) collective-permute-start(bf16[16,192,128]{2,1,0:T(8,128)(2,1)} %constant_dynamic-update-slice_fusion.6), channel_id=1, source_target_pairs={{0,1},{1,0},{2,3},{3,2},{4,5},{5,4},{6,7},{7,6},{8,9},{9,8},{10,11... | collective-permute-start | bytes 2359304 | tf_op jit(solution)/shard_map/ppermute | solution.py:506
  360.2 4.7 %collective-permute-start.23 = (bf16[16,544,128]{2,1,0:T(8,128)(2,1)}, bf16[16,544,128]{2,1,0:T(8,128)(2,1)S(1)}, u32[]{:S(2)}, u32[]{:S(2)}) collective-permute-start(bf16[16,544,128]{2,1,0:T(8,128)(2,1)} %constant_dynamic-update-slice_fusion.11), channel_id=1, source_target_pairs={{0,1},{1,0},{2,3},{3,2},{4,5},{5,4},{6,7},{7,6},{8,9},{9,8},{10,11... | collective-permute-start | bytes 6684680 | tf_op jit(solution)/shard_map/ppermute | solution.py:506
  (30 other events, 320.8 us)

commit v3 on v2

--- a/solution.py
+++ b/solution.py
@@ -111,8 +111,8 @@
     total_ref[...] = jnp.log(crossed)
 
 
-def lane_block(rows, lanes):
-    return pl.BlockSpec((rows, lanes), lambda pair: (0, pair))
+def lane_block(rows, lanes, first=0):
+    return pl.BlockSpec((rows, lanes), lambda pair: (0, pair + first))
 
 
 def whole_block(shape):
@@ -148,6 +148,7 @@
 
 
 def attend_back_kernel(
+    first_pair,
     key_blocks,
     segments,
     width,
@@ -164,10 +165,11 @@
         refs[key_blocks : 2 * key_blocks],
         refs[2 * key_blocks : 3 * key_blocks],
     )
-    grad_query_ref = refs[3 * key_blocks]
-    grad_key_refs = refs[3 * key_blocks + 1 : 4 * key_blocks + 1]
-    grad_value_refs = refs[4 * key_blocks + 1 :]
-    pair = pl.program_id(0)
+    results = refs[len(refs) - 1 - 2 * key_blocks :]
+    grad_query_ref = results[0]
+    grad_key_refs = results[1 : key_blocks + 1]
+    grad_value_refs = results[key_blocks + 1 :]
+    pair = pl.program_id(0) + first_pair
     rows, lanes = query_ref.shape
     lane = lax.broadcasted_iota(jnp.int32, (rows, lanes), 1)
     column = lane % width
@@ -240,28 +242,40 @@
     key_metas,
     segments,
     width,
+    pairs,
+    before,
+    after,
 ):
     rows, features = query_low.shape
     lanes = 2 * width
     count = len(keys)
-    flops = 10 * rows * rows * count * features
+    first, last = pairs
+    here = lane_block(rows, lanes, first)
+    anywhere = pl.BlockSpec(memory_space=pl.ANY)
+    operands = 6 + 3 * count
+    aliases = {operands + index: index for index in range(len(before))}
+    flops = 10 * rows * rows * count * lanes * (last - first)
     full = jax.ShapeDtypeStruct((rows, features), jnp.float32)
     low = jax.ShapeDtypeStruct((rows, features), jnp.bfloat16)
     results = pl.pallas_call(
-        functools.partial(attend_back_kernel, count, segments, width),
-        grid=(features // lanes,),
+        functools.partial(attend_back_kernel, first, count, segments, width),
+        grid=(last - first,),
         in_specs=[
             pl.BlockSpec(memory_space=pltpu.SMEM),
-            lane_block(rows, lanes),
+            here,
             whole_block(query_meta.shape),
         ]
-        + [lane_block(rows, lanes)] * (3 + 2 * count)
-        + [whole_block(query_meta.shape)] * count,
-        out_specs=[lane_block(rows, lanes)] * (1 + 2 * count),
+        + [here] * (3 + 2 * count)
+        + [whole_block(query_meta.shape)] * count
+        + [anywhere] * (len(before) + len(after)),
+        out_specs=[here] * (1 + 2 * count),
+        input_output_aliases=aliases,
         out_shape=[full] + ([full] + [low] * (count - 1)) * 2,
         compiler_params=pltpu.CompilerParams(vmem_limit_bytes=VMEM_LIMIT),
         cost_estimate=pl.CostEstimate(
-            flops=flops, bytes_accessed=24 * rows * features, transcendentals=0
+            flops=flops,
+            bytes_accessed=24 * rows * lanes * (last - first),
+            transcendentals=0,
         ),
         name="attend_back",
     )(
@@ -274,13 +288,221 @@
         *keys,
         *values,
         *key_metas,
-    )
-    return results[0], results[1 : 1 + count], results[1 + count :]
-
-
-def pick_rows(wanted, held, rows):
-    chosen = (wanted[:, None] == held[None, :]).astype(jnp.bfloat16)
-    return jnp.dot(chosen, rows, preferred_element_type=jnp.float32).astype(jnp.bfloat16)
+        *before,
+        *after,
+    )
+    return results
+
+
+def plan_kernel(
+    groups,
+    rows,
+    member_ref,
+    length_ref,
+    adapter_ref,
+    order_ref,
+    variate_ref,
+    chosen_ref,
+    back_ref,
+    turn_ref,
+    *refs,
+):
+    meta_refs, slot_ref = refs[:-1], refs[-1]
+    blocks = variate_ref.shape[0]
+    half_devices = groups // 2
+    half_blocks = blocks // 2
+    half_rows = half_blocks * LANES
+    swap_rows = rows // 2
+    member = member_ref[0]
+    my_half, my_place = member // half_devices, member % half_devices
+    places = [lax.rem(my_place + shift, half_devices) for shift in range(half_devices)]
+    segments = length_ref.shape[1]
+    starts = [jnp.int32(0)]
+    for segment in range(segments):
+        starts.append(starts[-1] + length_ref[0, segment])
+    long_start, long_index = jnp.int32(0), jnp.int32(0)
+    for segment in range(segments):
+        is_half = length_ref[0, segment] == half_rows
+        long_start = jnp.where(is_half, starts[segment], long_start)
+        long_index = jnp.where(is_half, segment, long_index)
+
+    block = lax.broadcasted_iota(jnp.int32, (blocks, LANES), 0)
+    lane = lax.broadcasted_iota(jnp.int32, (blocks, LANES), 1)
+    work_block = jnp.zeros((blocks, LANES), jnp.int32)
+    for index in range(blocks):
+        work_block = jnp.where(block == order_ref[0, index], index, work_block)
+    work_row = work_block * LANES + lane
+    is_long = (work_row >= long_start) & (work_row < long_start + half_rows)
+    in_first = block < half_blocks
+    long_count = jnp.sum(jnp.where(is_long & in_first, 1.0, 0.0)).astype(jnp.int32)
+    long_half = jnp.where(2 * long_count < half_rows, 1, 0)
+    side = jnp.where(in_first, 0, 1)
+    target = jnp.where(is_long, long_half, 1 - long_half)
+    foreign = target != side
+    flags = jnp.where(foreign, 1.0, 0.0)
+    moved = jnp.sum(jnp.where(in_first, flags, 0.0)).astype(jnp.int32)
+    square_row = lax.broadcasted_iota(jnp.int32, (LANES, LANES), 0)
+    square_column = lax.broadcasted_iota(jnp.int32, (LANES, LANES), 1)
+    within = dot(flags.astype(jnp.bfloat16), one_hot(square_row < square_column))
+    block_sum = jnp.broadcast_to(jnp.sum(flags, axis=1, keepdims=True), (blocks, LANES))
+    from_block = lax.broadcasted_iota(jnp.int32, (blocks, blocks), 1)
+    to_block = lax.broadcasted_iota(jnp.int32, (blocks, blocks), 0)
+    earlier = (from_block < to_block) & ((from_block < half_blocks) == (to_block < half_blocks))
+    before = dot(one_hot(earlier), block_sum.astype(jnp.bfloat16))
+    foreign_rank = (within + before).astype(jnp.int32)
+    kept_rank = (block - side * half_blocks) * LANES + lane - foreign_rank
+    kept_slot = side * half_rows + kept_rank
+    foreign_slot = (1 - side) * half_rows + rows + foreign_rank
+    foreign_slot = foreign_slot - jnp.clip(moved, 0, swap_rows)
+    for index in range(1, half_devices):
+        start = index * rows - jnp.minimum(moved, index * swap_rows)
+        last = (index - 1) * rows - jnp.minimum(moved, (index - 1) * swap_rows)
+        kept_slot = jnp.where(kept_rank >= start, kept_slot + rows - (start - last), kept_slot)
+        received = jnp.clip(moved - index * swap_rows, 0, swap_rows)
+        previous = jnp.clip(moved - (index - 1) * swap_rows, 0, swap_rows)
+        foreign_slot = jnp.where(
+            foreign_rank >= index * swap_rows,
+            foreign_slot + rows - swap_rows + previous - received,
+            foreign_slot,
+        )
+    slot = jnp.where(foreign, foreign_slot, kept_slot)
+    slot_ref[...] = slot
+
+    per_device = rows // LANES
+    wanted = lax.broadcasted_iota(jnp.int32, (rows + swap_rows, 1), 0)
+    wanted = jnp.where(
+        wanted < rows,
+        my_half * half_rows + my_place * rows + wanted,
+        (1 - my_half) * half_rows + my_place * rows + wanted - swap_rows,
+    )
+    for shift in range(half_devices):
+        for index in range(per_device):
+            held = my_half * half_blocks + places[shift] * per_device + index
+            column = (shift * per_device + index) * LANES
+            chosen_ref[:, column : column + LANES] = one_hot(
+                wanted == slot_ref[pl.ds(held, 1), :]
+            )
+
+    slot_turned = jnp.transpose(slot.astype(jnp.float32))
+    turned_lane = lax.broadcasted_iota(jnp.int32, (LANES, blocks), 1)
+    first_lane = lax.broadcasted_iota(jnp.int32, (1, LANES), 1)
+    for index in range(per_device):
+        held = my_half * half_blocks + my_place * per_device + index
+        mine = jnp.sum(
+            jnp.where(turned_lane == held, slot_turned, 0.0), axis=1, keepdims=True
+        ).astype(jnp.int32)
+        here = slice(index * LANES, (index + 1) * LANES)
+        column = 0
+        for first, half, length in ((0, my_half, rows), (swap_rows, 1 - my_half, swap_rows)):
+            for shift in range(half_devices):
+                for chunk in range(0, length, LANES):
+                    number = half * half_rows + places[shift] * rows + first + chunk
+                    back_ref[here, column : column + LANES] = one_hot(mine == number + first_lane)
+                    column += LANES
+
+    on_long = my_half == long_half
+    for turn in range(2):
+        chosen_segment = jnp.where(
+            on_long, long_index, jnp.where(long_index <= turn, turn + 1, turn)
+        )
+        adapter = adapter_ref[0, 0]
+        for segment in range(1, segments):
+            adapter = jnp.where(chosen_segment == segment, adapter_ref[0, segment], adapter)
+        turn_ref[turn] = adapter
+
+    variate_turned = jnp.transpose(variate_ref[...].astype(jnp.float32))
+    known = []
+    for index in range(blocks):
+        values = jnp.where(
+            square_column == 0,
+            work_block[index : index + 1, :].astype(jnp.float32),
+            jnp.where(
+                square_column == 1,
+                square_row.astype(jnp.float32),
+                variate_turned[:, index : index + 1],
+            ),
+        )
+        known.append(jnp.where(square_column < 3, values, 0.0).astype(jnp.bfloat16))
+    number = lax.broadcasted_iota(jnp.int32, (rows, 1), 0)
+    wide_lane = lax.broadcasted_iota(jnp.int32, (rows, LANES), 1)
+    for shift in range(half_devices):
+        slots = my_half * half_rows + places[shift] * rows + number
+        facts = jnp.zeros((rows, LANES), jnp.float32)
+        for index in range(blocks):
+            facts = facts + dot(one_hot(slots == slot[index : index + 1, :]), known[index])
+        facts = facts.astype(jnp.int32)
+        row = facts[:, 0:1] * LANES + facts[:, 1:2]
+        segment = jnp.zeros((rows, 1), jnp.int32)
+        first_row = jnp.zeros((rows, 1), jnp.int32)
+        for index in range(1, segments):
+            segment = jnp.where(row >= starts[index], index, segment)
+            first_row = jnp.where(row >= starts[index], starts[index], first_row)
+        turn = jnp.where(segment > long_index, segment - 1, segment)
+        turn = jnp.where(on_long, 0, turn)
+        meta_refs[shift][...] = jnp.where(
+            wide_lane == 0,
+            facts[:, 2:3],
+            jnp.where(
+                wide_lane == 1, segment, jnp.where(wide_lane == 2, turn, row - first_row)
+            ),
+        )
+
+
+def plan(groups, rows, member, seq_len, seq_adapter, block_order, variate):
+    half_devices = groups // 2
+    half_rows = half_devices * rows
+    blocks = block_order.shape[1]
+    smem = pl.BlockSpec(memory_space=pltpu.SMEM)
+    vmem = pl.BlockSpec(memory_space=pltpu.VMEM)
+    results = pl.pallas_call(
+        functools.partial(plan_kernel, groups, rows),
+        in_specs=[smem, smem, smem, smem, vmem],
+        out_specs=[vmem, vmem, smem] + [vmem] * half_devices,
+        out_shape=[
+            jax.ShapeDtypeStruct((rows + rows // 2, half_rows), jnp.bfloat16),
+            jax.ShapeDtypeStruct((rows, half_rows + half_rows // 2), jnp.bfloat16),
+            jax.ShapeDtypeStruct((2,), jnp.int32),
+        ]
+        + [jax.ShapeDtypeStruct((rows, LANES), jnp.int32)] * half_devices,
+        scratch_shapes=[pltpu.VMEM((blocks, LANES), jnp.int32)],
+        compiler_params=pltpu.CompilerParams(vmem_limit_bytes=VMEM_LIMIT),
+        cost_estimate=pl.CostEstimate(
+            flops=2**31, bytes_accessed=4 * rows * half_rows, transcendentals=0
+        ),
+        name="plan",
+    )(member, seq_len, seq_adapter, block_order, variate.reshape(blocks, LANES))
+    return results[0], results[1], results[2], results[3:]
+
+
+def pick_kernel(chosen_ref, *refs):
+    held_refs, out_ref = refs[:-1], refs[-1]
+    total = jnp.zeros(out_ref.shape, jnp.float32)
+    column = 0
+    for ref in held_refs:
+        rows = ref.shape[0]
+        total = total + dot(chosen_ref[:, column : column + rows], ref[...])
+        column += rows
+    out_ref[...] = total.astype(out_ref.dtype)
+
+
+def pick(chosen, first, count, held):
+    features = held[0].shape[1]
+    tile = features // 2
+    return pl.pallas_call(
+        pick_kernel,
+        grid=(features // tile,),
+        in_specs=[pl.BlockSpec((count, chosen.shape[1]), lambda step: (first // count, 0))]
+        + [pl.BlockSpec((part.shape[0], tile), lambda step: (0, step)) for part in held],
+        out_specs=pl.BlockSpec((count, tile), lambda step: (0, step)),
+        out_shape=jax.ShapeDtypeStruct((count, features), jnp.bfloat16),
+        compiler_params=pltpu.CompilerParams(vmem_limit_bytes=VMEM_LIMIT),
+        cost_estimate=pl.CostEstimate(
+            flops=2 * count * chosen.shape[1] * features,
+            bytes_accessed=8 * count * features,
+            transcendentals=0,
+        ),
+        name="pick",
+    )(chosen, *held)
 
 
 def within_half(array, shift, groups):
@@ -359,12 +581,11 @@
     return grad_shard, first_moment, second_moment, adapters_new
 
 
-def spreads_evenly(devices, features, hidden, total, turns):
+def spreads_evenly(devices, features, hidden, total):
     rows = total // LANES
     chunks = features // LANES
     return (
-        turns == 2
-        and ADAPTERS * RANK == LANES
+        ADAPTERS * RANK == LANES
         and devices * chunks == 256
         and chunks == 8
         and hidden == devices * LANES
@@ -372,22 +593,6 @@
         and rows % (devices * devices) == 0
         and devices & (devices - 1) == 0
     )
-
-
-def spread_wide(grads, devices):
-    rows = grads.shape[0] // devices
-    return jnp.transpose(grads.reshape(rows, devices, LANES), (1, 0, 2))
-
-
-def spread_tall(grad, devices):
-    return jnp.transpose(grad.reshape(grad.shape[0], devices, LANES), (1, 0, 2))
-
-
-def spread_square(grad, devices):
-    chunks = grad.shape[1] // LANES
-    classes = devices // chunks
-    parts = grad.reshape(2, RANK // classes, classes, chunks, LANES)
-    return jnp.transpose(parts, (2, 3, 0, 1, 4)).reshape(devices, 2 * RANK // classes, LANES)
 
 
 def one_hot(condition):
@@ -437,8 +642,9 @@
 
 
 def settle_kernel(
-    early, table_ref, tall_ref, square_ref, arrived_ref, param_ref, m1_ref, m2_ref, grad_ref, new_ref
+    early, table_ref, tall_ref, square_ref, arrived_ref, param_ref, m1_ref, m2_ref, *refs
 ):
+    grad_ref, new_ref = refs[-2:]
     if early:
         wide = sum_wide(table_ref, arrived_ref, 0, 3)
         last = sum_wide(table_ref, arrived_ref, 32, 4)
@@ -461,73 +667,95 @@
             parts.append(wide[:, index * LANES : (index + 1) * LANES])
             parts.append(square[index // 2][(index % 2) * 32 : (index % 2) * 32 + 32])
     row = 0
+    skip = param_ref.shape[0] - grad_ref.shape[0] if early else 0
     for part in parts:
         here = slice(row, row + part.shape[0])
+        there = slice(skip + row, skip + row + part.shape[0])
         row += part.shape[0]
         low = part.astype(jnp.bfloat16)
         grad_ref[here, :] = low
-        new_ref[here, :] = adam(
-            param_ref[here, :].astype(jnp.float32),
-            m1_ref[here, :],
-            m2_ref[here, :],
+        new = adam(
+            param_ref[there, :].astype(jnp.float32),
+            m1_ref[there, :],
+            m2_ref[there, :],
             low.astype(jnp.float32),
         )[2]
-
-
-def settle(early, table, arrived, params, first_old, second_old):
+        for copy in range(new_ref.shape[0]):
+            new_ref[copy, here, :] = new
+
+
+def settle(early, rows, table, arrived, params, first_old, second_old, after):
     sources = table.shape[0]
     tall_row = jnp.repeat(table.reshape(-1), RANK)[None, :]
     square_row = jnp.repeat(jnp.tile(table, (1, 2)).reshape(-1), 4)[None, :]
-    shape = jax.ShapeDtypeStruct(params.shape, jnp.bfloat16)
     return pl.pallas_call(
         functools.partial(settle_kernel, early),
         in_specs=[pl.BlockSpec(memory_space=pltpu.SMEM)]
-        + [pl.BlockSpec(memory_space=pltpu.VMEM)] * 6,
+        + [pl.BlockSpec(memory_space=pltpu.VMEM)] * 6
+        + [pl.BlockSpec(memory_space=pl.ANY)] * len(after),
         out_specs=[pl.BlockSpec(memory_space=pltpu.VMEM)] * 2,
-        out_shape=[shape, shape],
+        out_shape=[
+            jax.ShapeDtypeStruct((rows, LANES), jnp.bfloat16),
+            jax.ShapeDtypeStruct((lax.axis_size("dp"), rows, LANES), jnp.bfloat16),
+        ],
         compiler_params=pltpu.CompilerParams(vmem_limit_bytes=VMEM_LIMIT),
         cost_estimate=pl.CostEstimate(
             flops=sources * 2**24, bytes_accessed=4 * arrived.size, transcendentals=0
         ),
         name="settle_early" if early else "settle_late",
-    )(table, tall_row, square_row, arrived, params, first_old, second_old)
-
-
-def gather_everywhere(rows, devices, groups):
-    pieces = [rows[None]]
-    bit = devices // 2
+    )(table, tall_row, square_row, arrived, params, first_old, second_old, *after)
+
+
+def gather_inner(piece, groups):
+    pieces = [piece]
+    bit = groups // 2
     while bit:
-        send = jnp.concatenate(pieces) if len(pieces) > 1 else pieces[0]
-        if bit >= groups:
-            step = bit // groups
-            pairs = [(i, i ^ step) for i in range(devices // groups)]
-            pieces.append(lax.ppermute(send, "dp", pairs))
-        else:
-            pieces.append(lax.ppermute(send, "group", [(i, i ^ bit) for i in range(groups)]))
+        pairs = [(i, i ^ bit) for i in range(groups)]
+        pieces = pieces + [lax.ppermute(piece, "group", pairs) for piece in pieces]
         bit //= 2
     return pieces
 
 
-def assemble_kernel(count, order_ref, *refs):
+def placing_order(groups, devices, unit):
+    member = lax.axis_index("group")
+    piece = jnp.arange(groups, dtype=jnp.int32)
+    mask = jnp.zeros_like(piece)
+    bit = 1
+    while bit < groups:
+        mask = mask * 2 + (piece // bit) % 2
+        bit *= 2
+    outer = jnp.arange(devices // groups, dtype=jnp.int32)
+    device = (outer[None, :] * groups + (member ^ mask)[:, None]).reshape(-1)
+    size = unit * devices
+    to_row = lax.broadcasted_iota(jnp.int32, (size, size), 0)
+    from_row = jnp.arange(size, dtype=jnp.int32)
+    source = (from_row % unit) * devices + jnp.repeat(device, unit)
+    return (to_row == source[None, :]).astype(jnp.bfloat16)
+
+
+def assemble_kernel(count, block, order_ref, *refs):
     piece_refs, out_ref = refs[:count], refs[-1]
-    block = piece_refs[0].shape[1]
-    devices = 2 * piece_refs[-1].shape[0]
-    for start in range(0, block, 16):
-        held = jnp.concatenate([ref[:, start : start + 16, :] for ref in piece_refs], axis=0)
-        out_ref[start * devices : (start + 16) * devices, :] = jnp.dot(
-            order_ref[...],
-            held.reshape(16 * devices, LANES),
-            preferred_element_type=jnp.float32,
-        ).astype(jnp.bfloat16)
+    outer = piece_refs[0].shape[0]
+    devices = count * outer
+    unit = order_ref.shape[0] // devices
+    first = pl.program_id(0) * block
+    for start in range(0, block, 2 * unit):
+        sides = []
+        for side in (start, start + unit):
+            here = pl.ds(pl.multiple_of(first + side, unit), unit)
+            held = jnp.concatenate([ref[:, here, :] for ref in piece_refs], axis=0)
+            sides.append(held.reshape(unit * devices, LANES))
+        placed = dot(order_ref[...], jnp.concatenate(sides, axis=1)).astype(jnp.bfloat16)
+        for index, side in enumerate((start, start + unit)):
+            out_ref[side * devices : (side + unit) * devices, :] = placed[
+                :, index * LANES : (index + 1) * LANES
+            ]
 
 
 def assemble(order, pieces, total_rows, first, block, before):
-    devices = 2 * pieces[-1].shape[0]
-    steps = pieces[0].shape[1] // block
-    in_specs = [pl.BlockSpec(order.shape, lambda step: (0, 0))]
-    in_specs += [
-        pl.BlockSpec((piece.shape[0], block, LANES), lambda step: (0, step, 0)) for piece in pieces
-    ]
+    devices = len(pieces) * pieces[0].shape[0]
+    rows = pieces[0].shape[1]
+    in_specs = [whole_block(order.shape)] + [whole_block(piece.shape) for piece in pieces]
     operands = [order, *pieces]
     aliases = {}
     if before is not None:
@@ -536,17 +764,15 @@
         operands.append(before)
     skip = first // block
     return pl.pallas_call(
-        functools.partial(assemble_kernel, len(pieces)),
-        grid=(steps,),
+        functools.partial(assemble_kernel, len(pieces), block),
+        grid=(rows // block,),
         in_specs=in_specs,
         out_specs=pl.BlockSpec((block * devices, LANES), lambda step: (step + skip, 0)),
         out_shape=jax.ShapeDtypeStruct((total_rows, LANES), jnp.bfloat16),
         input_output_aliases=aliases,
         compiler_params=pltpu.CompilerParams(vmem_limit_bytes=VMEM_LIMIT),
         cost_estimate=pl.CostEstimate(
-            flops=steps * block * devices * 2**17,
-            bytes_accessed=steps * block * devices * 512,
-            transcendentals=0,
+            flops=rows * devices * 2**17, bytes_accessed=rows * devices * 512, transcendentals=0
         ),
         name="assemble",
     )(*operands)
@@ -695,11 +921,28 @@
     return jnp.concatenate([table] * (lanes // table.shape[1]), axis=1)
 
 
-def project_heads_kernel(
+def joined(kept_ref, arrived_ref):
+    first = kept_ref.shape[0] - arrived_ref.shape[0]
+    kept = kept_ref[...]
+    return jnp.concatenate([kept[:first], kept[first:] + arrived_ref[...]], axis=0)
+
+
+def turned_heads(raw, gain_ref, cosine, sine, width):
+    unit = raw * lax.rsqrt(head_mean(raw * raw, width) + NORM_EPS)
+    unit = unit * widen(gain_ref[...], raw.shape[1])
+    return (unit * cosine + swap_halves(unit, width) * sine).astype(jnp.bfloat16)
+
+
+def project_own(normed, inner, place, index, weight_ref, b_ref):
+    own = jnp.where(place == index, inner, 0.0).astype(jnp.bfloat16)
+    return dot(normed, weight_ref[...]) + ADAPTER_SCALE * dot(own, b_ref[...])
+
+
+def project_key_value_kernel(
     width,
-    x_ref,
+    kept_ref,
+    arrived_ref,
     gain_ref,
-    wq_ref,
     wk_ref,
     wv_ref,
     a_ref,
@@ -707,13 +950,11 @@
     meta_ref,
     cos_ref,
     sin_ref,
-    q_gain_ref,
     k_gain_ref,
+    x_ref,
     normed_ref,
     inner_ref,
-    q_raw_ref,
-    k_raw_ref,
-    q_ref,
+    raw_ref,
     k_ref,
     v_ref,
 ):
@@ -721,7 +962,9 @@
 
     @pl.when(pl.program_id(0) == 0)
     def _():
-        values = x_ref[...].astype(jnp.float32)
+        rows = joined(kept_ref, arrived_ref)
+        x_ref[...] = rows
+        values = rows.astype(jnp.float32)
         normed = (values * row_norm(values) * gain_ref[...].astype(jnp.float32)).astype(
             jnp.bfloat16
         )
@@ -730,32 +973,30 @@
 
     normed = normed_ref[...]
     inner = inner_ref[...].astype(jnp.float32)
+    lanes = wk_ref.shape[1]
+    cosine, sine = widen(cos_ref[...], lanes), widen(sin_ref[...], lanes)
+    key = project_own(normed, inner, place, 1, wk_ref, b_ref)
+    raw_ref[...] = key
+    k_ref[...] = turned_heads(key, k_gain_ref, cosine, sine, width)
+    v_ref[...] = project_own(normed, inner, place, 2, wv_ref, b_ref).astype(jnp.bfloat16)
+
+
+def project_query_kernel(
+    width, normed_ref, inner_ref, wq_ref, b_ref, cos_ref, sin_ref, q_gain_ref, raw_ref, q_ref
+):
     lanes = wq_ref.shape[1]
-
-    def lora(weight_ref, index):
-        own = jnp.where(place == index, inner, 0.0).astype(jnp.bfloat16)
-        return dot(normed, weight_ref[...]) + ADAPTER_SCALE * dot(own, b_ref[...])
-
+    place = lax.broadcasted_iota(jnp.int32, inner_ref.shape, 1) // (2 * RANK)
     cosine, sine = widen(cos_ref[...], lanes), widen(sin_ref[...], lanes)
-
-    def turned(raw, head_gain_ref):
-        unit = raw * lax.rsqrt(head_mean(raw * raw, width) + NORM_EPS)
-        unit = unit * widen(head_gain_ref[...], lanes)
-        return (unit * cosine + swap_halves(unit, width) * sine).astype(jnp.bfloat16)
-
-    query = lora(wq_ref, 0)
-    q_raw_ref[...] = query
-    q_ref[...] = turned(query, q_gain_ref)
-    key = lora(wk_ref, 1)
-    k_raw_ref[...] = key
-    k_ref[...] = turned(key, k_gain_ref)
-    v_ref[...] = lora(wv_ref, 2).astype(jnp.bfloat16)
+    inner = inner_ref[...].astype(jnp.float32)
+    query = project_own(normed_ref[...], inner, place, 0, wq_ref, b_ref)
+    raw_ref[...] = query
+    q_ref[...] = turned_heads(query, q_gain_ref, cosine, sine, width)
 
 
 def project_heads(
-    rows_in, gain, weights, a_qkv, b_qkv, meta, cos_table, sin_table, q_gain, k_gain, width
+    kept, arrived, gain, weights, a_qkv, b_qkv, meta, cos_table, sin_table, q_gain, k_gain, width
 ):
-    rows, features = rows_in.shape
+    rows, features = kept.shape
     tile = 256
     grid = (features // tile,)
 
@@ -765,48 +1006,64 @@
     def shape(dtype):
         return jax.ShapeDtypeStruct((rows, features), dtype)
 
-    return pl.pallas_call(
-        functools.partial(project_heads_kernel, width),
+    full, few = whole_block((rows, features)), whole_block((rows, LANES))
+    low, high = shape(jnp.bfloat16), shape(jnp.float32)
+    x, normed, inner, key_raw, key, value = pl.pallas_call(
+        functools.partial(project_key_value_kernel, width),
         grid=grid,
-        in_specs=[whole_block((rows, features)), whole_block((1, features))]
-        + [tiled(features)] * 3
-        + [whole_block((features, LANES)), tiled(LANES), whole_block(meta.shape)]
-        + [whole_block((rows, LANES))] * 2
-        + [whole_block((1, LANES))] * 2,
-        out_specs=[whole_block((rows, features)), whole_block((rows, LANES))] + [tiled(rows)] * 5,
+        in_specs=[full, whole_block(arrived.shape), whole_block((1, features))]
+        + [tiled(features)] * 2
+        + [whole_block((features, LANES)), tiled(LANES), few, few, few]
+        + [whole_block((1, LANES))],
+        out_specs=[full, full, few] + [tiled(rows)] * 3,
         out_shape=[
-            shape(jnp.bfloat16),
+            low,
+            low,
             jax.ShapeDtypeStruct((rows, LANES), jnp.bfloat16),
-            shape(jnp.float32),
-            shape(jnp.float32),
-            shape(jnp.bfloat16),
-            shape(jnp.bfloat16),
-            shape(jnp.bfloat16),
+            high,
+            low,
+            low,
         ],
         compiler_params=pltpu.CompilerParams(vmem_limit_bytes=VMEM_LIMIT),
         cost_estimate=pl.CostEstimate(
-            flops=8 * rows * features * features,
-            bytes_accessed=6 * features * features + 20 * rows * features,
+            flops=6 * rows * features * features,
+            bytes_accessed=4 * features * features + 14 * rows * features,
             transcendentals=0,
         ),
-        name="project_heads",
+        name="project_key_value",
     )(
-        rows_in,
+        kept,
+        arrived,
         gain[None, :],
-        *weights,
+        *weights[1:],
         a_qkv,
         b_qkv,
         meta,
         cos_table,
         sin_table,
-        q_gain,
         k_gain,
     )
+    query_raw, query = pl.pallas_call(
+        functools.partial(project_query_kernel, width),
+        grid=grid,
+        in_specs=[full, few, tiled(features), tiled(LANES), few, few, whole_block((1, LANES))],
+        out_specs=[tiled(rows)] * 2,
+        out_shape=[high, low],
+        compiler_params=pltpu.CompilerParams(vmem_limit_bytes=VMEM_LIMIT),
+        cost_estimate=pl.CostEstimate(
+            flops=3 * rows * features * features,
+            bytes_accessed=2 * features * features + 8 * rows * features,
+            transcendentals=0,
+        ),
+        name="project_query",
+    )(normed, inner, weights[0], b_qkv, cos_table, sin_table, q_gain)
+    return x, normed, inner, query_raw, key_raw, query, key, value
 
 
 def project_heads_back_kernel(
     count,
     width,
+    devices,
     gq_ref,
     *refs,
 ):
@@ -829,12 +1086,11 @@
         sin_ref,
         q_gain_ref,
         k_gain_ref,
-        out_ref,
-        grad_a_ref,
-        grad_b_ref,
-        total_ref,
-        few_ref,
-    ) = refs
+    ) = refs[:17]
+    if devices:
+        _, out_ref, spread_ref, total_ref, few_ref, tall_ref, square_ref = refs[17:]
+    else:
+        out_ref, grad_a_ref, grad_b_ref, total_ref, few_ref, tall_ref, square_ref = refs[17:]
     step = pl.program_id(0)
     lanes = wq_ref.shape[1]
     mask, place = turn_mask(meta_ref)
@@ -873,8 +1129,30 @@
         total = total + contract_last(error, weight_ref[...])
         few = few + jnp.where(place == index, contract_last(error, b_ref[...]), 0.0)
         here = slice(index * wide, (index + 1) * wide)
-        grad_b_ref[here, :] = dot(inner_turned[here], error).astype(jnp.bfloat16)
-    grad_b_ref[3 * wide :, :] = jnp.zeros((LANES - 3 * wide, lanes), jnp.bfloat16)
+        grad_b = dot(inner_turned[here], error)
+        for part in range(lanes // LANES):
+            square_ref[part, here, :] = grad_b[:, part * LANES : (part + 1) * LANES]
+    square_ref[:, 3 * wide :, :] = jnp.zeros(
+        (lanes // LANES, LANES - 3 * wide, LANES), jnp.float32
+    )
+    if devices:
+        chunks = normed_ref.shape[1] // LANES
+        for index in range(lanes // LANES):
+            for first, starts in ((wide, (0, wide)), (wide + RANK, (2 * wide, 3 * wide))):
+                spread_square_to(
+                    spread_ref,
+                    first,
+                    square_ref,
+                    starts,
+                    step * (lanes // LANES) + index,
+                    chunks,
+                    index,
+                )
+    else:
+        for part in range(lanes // LANES):
+            grad_b_ref[:, part * LANES : (part + 1) * LANES] = square_ref[part].astype(
+                jnp.bfloat16
+            )
     total_ref[...] = total
     few_ref[...] = few
 
@@ -882,7 +1160,11 @@
     def _():
         low = (ADAPTER_SCALE * few_ref[...] * mask).astype(jnp.bfloat16)
         low_turned = jnp.transpose(low.astype(jnp.float32)).astype(jnp.bfloat16)
-        grad_a_ref[...] = jnp.transpose(dot(low_turned, normed_ref[...])).astype(jnp.bfloat16)
+        tall_ref[...] = jnp.transpose(dot(low_turned, normed_ref[...]))
+        if devices:
+            spread_wide_to(spread_ref, 0, tall_ref)
+        else:
+            grad_a_ref[...] = tall_ref[...].astype(jnp.bfloat16)
         grad = total_ref[...] + contract_last(low, a_ref[...])
         out_ref[...] = (
             residual_ref[...]
@@ -893,6 +1175,8 @@
 
 
 def project_heads_back(
+    devices,
+    after,
     grad_query,
     key_terms,
     value_terms,
@@ -921,24 +1205,33 @@
         return pl.BlockSpec((height, tile), lambda step: (0, step))
 
     full = whole_block((rows, features))
+    if devices:
+        spread = (devices, 4 * RANK, LANES)
+        grad_specs = [whole_block(spread)]
+        grad_shapes = [jax.ShapeDtypeStruct(spread, jnp.bfloat16)]
+    else:
+        grad_specs = [whole_block((features, LANES)), tiled(LANES)]
+        grad_shapes = [
+            jax.ShapeDtypeStruct((features, LANES), jnp.bfloat16),
+            jax.ShapeDtypeStruct((LANES, features), jnp.bfloat16),
+        ]
     return pl.pallas_call(
-        functools.partial(project_heads_back_kernel, count, width),
+        functools.partial(project_heads_back_kernel, count, width, devices),
         grid=(features // tile,),
         in_specs=[tiled(rows)] * (3 + 2 * count)
         + [full, whole_block((rows, LANES)), full, full, whole_block((1, features))]
         + [tiled(features)] * 3
         + [whole_block((features, LANES)), tiled(LANES), whole_block(meta.shape)]
         + [whole_block((rows, LANES))] * 2
-        + [whole_block((1, LANES))] * 2,
-        out_specs=[full, whole_block((features, LANES)), tiled(LANES)],
-        out_shape=[
-            jax.ShapeDtypeStruct((rows, features), jnp.bfloat16),
-            jax.ShapeDtypeStruct((features, LANES), jnp.bfloat16),
-            jax.ShapeDtypeStruct((LANES, features), jnp.bfloat16),
-        ],
+        + [whole_block((1, LANES))] * 2
+        + [pl.BlockSpec(memory_space=pl.ANY)] * len(after),
+        out_specs=[full, *grad_specs],
+        out_shape=[jax.ShapeDtypeStruct((rows, features), jnp.bfloat16), *grad_shapes],
         scratch_shapes=[
             pltpu.VMEM((rows, features), jnp.float32),
             pltpu.VMEM((rows, LANES), jnp.float32),
+            pltpu.VMEM((features, LANES), jnp.float32),
+            pltpu.VMEM((tile // LANES, LANES, LANES), jnp.float32),
         ],
         compiler_params=pltpu.CompilerParams(vmem_limit_bytes=VMEM_LIMIT),
         cost_estimate=pl.CostEstimate(
@@ -966,13 +1259,39 @@
         sin_table,
         q_gain,
         k_gain,
-    )
+        *after,
+    )
+
+
+def spread_wide_to(spread_ref, first, held_ref):
+    devices = spread_ref.shape[0]
+    count = held_ref.shape[0] // devices
+    for device in range(devices):
+        spread_ref[device, first : first + count, :] = held_ref[
+            pl.ds(device, count, stride=devices), :
+        ].astype(jnp.bfloat16)
+
+
+def spread_square_to(spread_ref, first, held_ref, starts, chunk, chunks, index):
+    classes = spread_ref.shape[0] // chunks
+    count = 2 * RANK // classes
+    for part in range(classes):
+        rows = [
+            held_ref[index, pl.ds(start + part, count, stride=classes), :]
+            for start in starts
+        ]
+        spread_ref[part * chunks + chunk, first : first + 2 * count, :] = jnp.concatenate(
+            rows, axis=0
+        ).astype(jnp.bfloat16)
 
 
 def feed_forward_kernel(
+    devices,
+    turn_ref,
     att_ref,
     x_ref,
-    e_ref,
+    kept_ref,
+    arrived_ref,
     gain_ref,
     wo_ref,
     wg_ref,
@@ -986,22 +1305,28 @@
     out_ref,
     grad_res_ref,
     grad_att_ref,
-    grad_a_ref,
-    grad_ad_ref,
-    grad_bgu_ref,
-    grad_bdo_ref,
-    res_ref,
-    hidden_ref,
-    inner_ref,
-    inner_turned_ref,
-    sum_ref,
-    grad_hidden_ref,
-    inner_down_ref,
-    few_ref,
-    few_down_ref,
-    few_down_turned_ref,
-    down_ref,
+    *refs,
 ):
+    if devices:
+        spread_ref, refs = refs[0], refs[1:]
+    else:
+        (grad_a_ref, grad_ad_ref, grad_bgu_ref, grad_bdo_ref), refs = refs[:4], refs[4:]
+    (
+        res_ref,
+        hidden_ref,
+        inner_ref,
+        inner_turned_ref,
+        sum_ref,
+        grad_hidden_ref,
+        inner_down_ref,
+        few_ref,
+        few_down_ref,
+        few_down_turned_ref,
+        down_ref,
+        tall_ref,
+        square_ref,
+        e_ref,
+    ) = refs
     step = pl.program_id(0)
     mask, place = turn_mask(meta_ref)
     tile = wg_ref.shape[1]
@@ -1016,6 +1341,7 @@
 
     @pl.when(step == 0)
     def _():
+        e_ref[...] = joined(kept_ref, arrived_ref)
         att = att_ref[...]
         inner_out = dot(att, a_guo_ref[...]) * mask
         res = (
@@ -1060,10 +1386,17 @@
     few_ref[...] += jnp.where(
         place == 0, contract_last(grad_gate, b_tile), contract_last(grad_up, b_tile)
     )
-    grad_bgu_ref[:wide, :] = dot(inner_turned_ref[:wide, :], grad_gate).astype(jnp.bfloat16)
-    grad_bgu_ref[wide:, :] = dot(inner_turned_ref[wide : 2 * wide, :], grad_up).astype(
-        jnp.bfloat16
-    )
+    grad_b_gate = dot(inner_turned_ref[:wide, :], grad_gate).astype(jnp.bfloat16)
+    grad_b_up = dot(inner_turned_ref[wide : 2 * wide, :], grad_up).astype(jnp.bfloat16)
+    if devices:
+        for index in range(tile // LANES):
+            device = step * (tile // LANES) + index
+            chunk = slice(index * LANES, (index + 1) * LANES)
+            spread_ref[device, 2 * wide : 3 * wide, :] = grad_b_gate[:, chunk]
+            spread_ref[device, 3 * wide : 4 * wide, :] = grad_b_up[:, chunk]
+    else:
+        grad_bgu_ref[:wide, :] = grad_b_gate
+        grad_bgu_ref[wide:, :] = grad_b_up
     per_quarter = features // tile
     down_ref[
         pl.ds(pl.multiple_of((step // per_quarter) * wide, wide), wide),
@@ -1090,15 +1423,34 @@
             contract_last(low, wo_ref[...]) + contract_last(few_out, a_guo_ref[...])
         ).astype(jnp.bfloat16)
         grad_a = dot(turn(few), hidden_ref[...]) + dot(turn(few_out), att_ref[...])
-        grad_a_ref[...] = jnp.transpose(grad_a).astype(jnp.bfloat16)
-        grad_ad_ref[...] = jnp.transpose(down_ref[...]).astype(jnp.bfloat16)
         inner_out = only(inner_ref[...].astype(jnp.float32), 2)
-        grad_bdo_ref[...] = (
-            ADAPTER_SCALE * (dot(turn(inner_down), grads_out) + dot(turn(inner_out), low))
-        ).astype(jnp.bfloat16)
-
-
-def feed_forward(attended, rows_in, grads_out, gain, weights, selected, meta):
+        grad_b = ADAPTER_SCALE * (
+            dot(turn(inner_down), grads_out) + dot(turn(inner_out), low)
+        )
+        if devices:
+            lane = lax.broadcasted_iota(jnp.int32, (features, LANES), 1)
+            told = jnp.where(
+                lane == 3 * wide, turn_ref[0], jnp.where(lane == 3 * wide + 1, turn_ref[1], 0)
+            )
+            tall_ref[...] = jnp.transpose(grad_a) + told.astype(jnp.float32)
+            spread_wide_to(spread_ref, 0, tall_ref)
+            tall_ref[...] = jnp.transpose(down_ref[...])
+            spread_wide_to(spread_ref, wide, tall_ref)
+            chunks = features // LANES
+            for chunk in range(chunks):
+                square_ref[chunk] = grad_b[:, chunk * LANES : (chunk + 1) * LANES]
+                spread_square_to(
+                    spread_ref, 4 * wide, square_ref, (0, 2 * wide), chunk, chunks, chunk
+                )
+        else:
+            grad_a_ref[...] = jnp.transpose(grad_a).astype(jnp.bfloat16)
+            grad_ad_ref[...] = jnp.transpose(down_ref[...]).astype(jnp.bfloat16)
+            grad_bdo_ref[...] = grad_b.astype(jnp.bfloat16)
+
+
+def feed_forward(
+    devices, turn_adapter, attended, rows_in, kept, arrived, gain, weights, selected, meta
+):
     rows, features = rows_in.shape
     hidden = weights[1].shape[1]
     tile = 512
@@ -1109,13 +1461,32 @@
     def shape(height, length, dtype):
         return jax.ShapeDtypeStruct((height, length), dtype)
 
+    if devices:
+        spread = (devices, 9 * RANK, LANES)
+        grad_specs = [whole_block(spread)]
+        grad_shapes = [jax.ShapeDtypeStruct(spread, jnp.bfloat16)]
+    else:
+        grad_specs = [
+            whole_block((features, LANES)),
+            whole_block((features, LANES)),
+            pl.BlockSpec((4 * RANK, tile), lambda step: (0, step)),
+            whole_block((LANES, features)),
+        ]
+        grad_shapes = [
+            shape(features, LANES, jnp.bfloat16),
+            shape(features, LANES, jnp.bfloat16),
+            shape(4 * RANK, hidden, jnp.bfloat16),
+            shape(LANES, features, jnp.bfloat16),
+        ]
     return pl.pallas_call(
-        feed_forward_kernel,
+        functools.partial(feed_forward_kernel, devices),
         grid=(hidden // tile,),
         in_specs=[
+            pl.BlockSpec(memory_space=pltpu.SMEM),
             full,
             full,
             full,
+            whole_block(arrived.shape),
             whole_block((1, features)),
             square,
             column,
@@ -1131,19 +1502,13 @@
             full,
             full,
             full,
-            whole_block((features, LANES)),
-            whole_block((features, LANES)),
-            pl.BlockSpec((4 * RANK, tile), lambda step: (0, step)),
-            whole_block((LANES, features)),
+            *grad_specs,
         ],
         out_shape=[
             shape(rows, features, jnp.bfloat16),
             shape(rows, features, jnp.float32),
             shape(rows, features, jnp.bfloat16),
-            shape(features, LANES, jnp.bfloat16),
-            shape(features, LANES, jnp.bfloat16),
-            shape(4 * RANK, hidden, jnp.bfloat16),
-            shape(LANES, features, jnp.bfloat16),
+            *grad_shapes,
         ],
         scratch_shapes=[
             pltpu.VMEM((rows, features), jnp.float32),
@@ -1157,6 +1522,9 @@
             pltpu.VMEM((rows, LANES), jnp.bfloat16),
             pltpu.VMEM((2 * RANK, rows), jnp.bfloat16),
             pltpu.VMEM((LANES, features), jnp.float32),
+            pltpu.VMEM((features, LANES), jnp.float32),
+            pltpu.VMEM((features // LANES, LANES, LANES), jnp.float32),
+            pltpu.VMEM((rows, features), jnp.bfloat16),
         ],
         compiler_params=pltpu.CompilerParams(vmem_limit_bytes=VMEM_LIMIT),
         cost_estimate=pl.CostEstimate(
@@ -1165,21 +1533,16 @@
             transcendentals=0,
         ),
         name="feed_forward",
-    )(attended, rows_in, grads_out, gain[None, :], *weights, *selected, meta)
-
-
-def settle_spread(grads, turn_adapter, adapters, moment1, moment2, devices):
-    a_qkv, b_qkv, a_guo, a_down, b_gu, b_do = grads
+    )(
+        turn_adapter, attended, rows_in, kept, arrived, gain[None, :], *weights, *selected, meta
+    )
+
+
+def spread_state(adapters, moment1, moment2, devices):
     axes = ("dp", "group")
-    groups = lax.axis_size("group")
-    me = lax.axis_index(axes)
     total_rows = adapters.shape[0] // LANES
     spread_rows = total_rows // devices
     own_rows = spread_rows // devices
-    features = a_qkv.shape[0]
-    late_rows = 6 * features // devices
-    few = 2 * RANK
-
     moments = jnp.concatenate(
         [
             jnp.transpose(flat.reshape(own_rows, devices, LANES), (1, 0, 2))
@@ -1187,65 +1550,23 @@
         ],
         axis=1,
     )
-    moments, a_guo = lax.optimization_barrier((moments, a_guo))
     moments = lax.all_to_all(moments, axes, 0, 0, tiled=True)
     first_old = moments[:, :own_rows].reshape(spread_rows, LANES)
     second_old = moments[:, own_rows:].reshape(spread_rows, LANES)
     params = lax.dynamic_index_in_dim(
-        adapters.reshape(spread_rows, devices, LANES), me, 1, keepdims=False
-    )
-    told = jnp.where(
-        jnp.arange(LANES, dtype=jnp.int32) == 3 * few,
-        turn_adapter[0],
-        jnp.where(jnp.arange(LANES, dtype=jnp.int32) == 3 * few + 1, turn_adapter[1], 0),
-    ).astype(jnp.bfloat16)
-    early = jnp.concatenate(
-        [
-            spread_wide(a_guo + told[None, :], devices),
-            spread_wide(a_down, devices),
-            spread_tall(b_gu[:few], devices),
-            spread_tall(b_gu[few : 2 * few], devices),
-            spread_square(b_do[:few], devices),
-            spread_square(b_do[2 * few : 3 * few], devices),
-        ],
-        axis=1,
-    )
-    early = lax.all_to_all(early, axes, 0, 0, tiled=True)
-    table = early[:, 0, 3 * few : 3 * few + 2].astype(jnp.int32)
-    early_grad, early_new = settle(
-        True, table, early, params[late_rows:], first_old[late_rows:], second_old[late_rows:]
-    )
-    piece_range = jnp.arange(devices, dtype=jnp.int32)
-    reversed_bits = jnp.zeros_like(piece_range)
-    bit = 1
-    while bit < devices:
-        reversed_bits = reversed_bits * 2 + (piece_range // bit) % 2
-        bit *= 2
-    unit = jnp.arange(16, dtype=jnp.int32)
-    order = (
-        (unit[:, None, None, None] == unit[None, None, None, :])
-        & (piece_range[None, :, None, None] == (me ^ reversed_bits)[None, None, :, None])
-    ).astype(jnp.bfloat16)
-    order = order.reshape(16 * devices, 16 * devices)
-    early_pieces = gather_everywhere(early_new, devices, groups)
-    adapters_new = assemble(order, early_pieces, total_rows, late_rows, 32, None)
-    late = jnp.concatenate(
-        [spread_wide(a_qkv, devices)]
-        + [spread_square(b_qkv[i * few : (i + 1) * few], devices) for i in range(4)],
-        axis=1,
-    )
-    late = lax.all_to_all(late, axes, 0, 0, tiled=True)
-    late_grad, late_new = settle(
-        False, table, late, params[:late_rows], first_old[:late_rows], second_old[:late_rows]
-    )
-    late_pieces = gather_everywhere(late_new, devices, groups)
-    adapters_new = assemble(order, late_pieces, total_rows, 0, 64, adapters_new)
-    grads = jnp.concatenate([late_grad, early_grad]).reshape(devices, own_rows, LANES)
-    grads = lax.all_to_all(grads, axes, 0, 0, tiled=True)
+        adapters.reshape(spread_rows, devices, LANES), lax.axis_index(axes), 1, keepdims=False
+    )
+    return params, first_old, second_old
+
+
+def settle_owned(late_grad, early_grad, moment1, moment2, devices):
+    grads = jnp.concatenate([late_grad, early_grad])
+    grads = grads.reshape(devices, grads.shape[0] // devices, LANES)
+    grads = lax.all_to_all(grads, ("dp", "group"), 0, 0, tiled=True)
     grad_shard = jnp.transpose(grads, (1, 0, 2)).reshape(-1).astype(jnp.float32)
     current = jnp.zeros((), jnp.float32)
     first_moment, second_moment, _ = adam(current, moment1, moment2, grad_shard)
-    return grad_shard, first_moment, second_moment, adapters_new.reshape(-1)
+    return grad_shard, first_moment, second_moment
 
 
 def per_device(
@@ -1277,136 +1598,33 @@
     hidden_width = gate_weight.shape[1]
     head_width = q_gain.shape[0]
     half_devices = groups // 2
-    half_rows = half_devices * row_count
-    pack_rows = groups * row_count
-    swap_rows = row_count // 2
-    my_half, my_place = member // half_devices, member % half_devices
-
-    block_list = block_order[0]
-    blocks = block_list.shape[0]
-    block_rows = pack_rows // blocks
-    lengths = seq_len[0]
-    segments = lengths.shape[0]
-    seq_ends = jnp.cumsum(lengths)
-    seq_starts = seq_ends - lengths
-    block_index = jnp.arange(blocks, dtype=jnp.int32)
-    work_block = jnp.sum(
-        jnp.where(block_list[None, :] == block_index[:, None], block_index[None, :], 0), axis=1
-    )
-    work_row = (
-        work_block[:, None] * block_rows + jnp.arange(block_rows, dtype=jnp.int32)[None, :]
-    ).reshape(2, half_rows)
-    long_start = jnp.sum(jnp.where(lengths == half_rows, seq_starts, 0))
-    is_long = (work_row >= long_start) & (work_row < long_start + half_rows)
-    long_half = (2 * jnp.sum(is_long[0].astype(jnp.int32)) < half_rows).astype(jnp.int32)
-    side = jnp.arange(2, dtype=jnp.int32)[:, None]
-    target = jnp.where(is_long, long_half, 1 - long_half)
-    foreign = (target != side).astype(jnp.int32)
-    foreign_rank = jnp.cumsum(foreign, axis=1) - foreign
-    kept_rank = jnp.arange(half_rows, dtype=jnp.int32)[None, :] - foreign_rank
-    moved = jnp.sum(foreign[0])
-    place = jnp.zeros_like(kept_rank)
-    offset = jnp.zeros_like(kept_rank)
-    for index in range(1, half_devices):
-        start = index * row_count - jnp.minimum(moved, index * swap_rows)
-        place = place + (kept_rank >= start)
-        offset = jnp.where(kept_rank >= start, start, offset)
-    kept_slot = side * half_rows + place * row_count + kept_rank - offset
-    foreign_place = foreign_rank // swap_rows
-    received = jnp.clip(moved - foreign_place * swap_rows, 0, swap_rows)
-    foreign_slot = (
-        (1 - side) * half_rows
-        + foreign_place * row_count
-        + row_count
-        - received
-        + foreign_rank % swap_rows
-    )
-    slot = jnp.where(foreign == 1, foreign_slot, kept_slot)
-    row_range = jnp.arange(row_count, dtype=jnp.int32)
-    order = [(my_place + shift) % half_devices for shift in range(half_devices)]
-    half_ids = jnp.concatenate(
-        [my_half * half_rows + place_of * row_count + row_range for place_of in order]
-    )
-    my_slots = half_ids[:row_count]
-    away_ids = jnp.concatenate(
-        [
-            (1 - my_half) * half_rows + place_of * row_count + row_range[swap_rows:]
-            for place_of in order
-        ]
-    )
-    slot_mine = lax.dynamic_index_in_dim(slot, my_half, 0, keepdims=False).reshape(
-        half_devices, row_count
-    )
-    held_slots = jnp.concatenate(
-        [lax.dynamic_index_in_dim(slot_mine, place_of, 0, keepdims=False) for place_of in order]
-    )
-    slot_here = held_slots[:row_count]
-    wanted = jnp.concatenate([my_slots, away_ids[:swap_rows]])
-
-    def bring(rows):
-        picked = pick_rows(wanted, held_slots, jnp.concatenate(gather_half(rows, groups)))
-        arrived = to_other_half(picked[row_count:], groups)
-        return jnp.concatenate(
-            [picked[:swap_rows], picked[swap_rows:row_count] + arrived]
-        )
-
-    returned_ids = jnp.concatenate([half_ids, away_ids])
-
-    def send_back(rows):
-        back = to_other_half(rows[swap_rows:], groups)
-        held = gather_half(rows, groups) + gather_half(back, groups)
-        return pick_rows(slot_here, returned_ids, jnp.concatenate(held))
-
-    facts = jnp.stack(
-        [
-            work_row.reshape(-1) // block_rows,
-            work_row.reshape(-1) % block_rows,
-            variate,
-        ],
-        axis=1,
-    ).astype(jnp.bfloat16)
-    chosen = (half_ids[:, None] == slot.reshape(-1)[None, :]).astype(jnp.bfloat16)
-    facts = jnp.dot(chosen, facts, preferred_element_type=jnp.float32).astype(jnp.int32)
-    half_row = facts[:, 0] * block_rows + facts[:, 1]
-    segment = jnp.sum((half_row[:, None] >= seq_ends[None, :]).astype(jnp.int32), axis=1)
-    picked = (segment[:, None] == jnp.arange(segments, dtype=jnp.int32)[None, :]).astype(jnp.int32)
-    position = half_row - jnp.sum(picked * seq_starts[None, :], axis=1)
-    turns = max(1, segments - 1)
-    long_index = jnp.sum(jnp.where(lengths == half_rows, jnp.arange(segments, dtype=jnp.int32), 0))
-    on_long = my_half == long_half
-    turn_range = jnp.arange(turns, dtype=jnp.int32)
-    turn_segment = jnp.where(
-        on_long, long_index, turn_range + (turn_range >= long_index).astype(jnp.int32)
-    )
-    turn_adapter = jnp.sum(
-        jnp.where(
-            turn_segment[:, None] == jnp.arange(segments, dtype=jnp.int32)[None, :],
-            seq_adapter[0][None, :],
-            0,
-        ),
-        axis=1,
-    )
-    row_turn = jnp.where(on_long, 0, segment - (segment > long_index).astype(jnp.int32))
-    meta = jnp.stack([facts[:, 2], segment, row_turn], axis=1)
-    key_metas = [meta[i * row_count : (i + 1) * row_count] for i in range(half_devices)]
+    segments = seq_len.shape[1]
+    chosen, back, turn_adapter, key_metas = plan(
+        groups, row_count, member[None], seq_len, seq_adapter, block_order, variate
+    )
     meta = key_metas[0]
-    columns = ADAPTERS * RANK
-    few = turns * RANK
-    few_range = jnp.arange(few, dtype=jnp.int32)
-    few_column = jnp.repeat(turn_adapter, RANK) * RANK + few_range % RANK
-    few_choice = (jnp.arange(columns, dtype=jnp.int32)[:, None] == few_column[None, :]).astype(
-        jnp.bfloat16
-    )
-    cos_table, sin_table = rope_tables(position[:row_count], head_width)
+    cos_table, sin_table = rope_tables(meta[:, 3], head_width)
     selected = select(turn_adapter, adapters, feature_width, hidden_width)
     a_qkv, a_guo, a_down, b_qkv, b_gu, b_do = selected
     q_gain_row = head_gain(q_gain)
     k_gain_row = head_gain(k_gain)
 
-    my_tokens = bring(tokens)
-    my_grads = bring(cotangent)
-    normed, inner, query_raw, key_raw, query_low, key_low, value_low = project_heads(
-        my_tokens,
+    def bring(rows):
+        held = gather_half(rows, groups)
+        sent = pick(chosen, row_count, row_count // 2, held)
+        arrived = to_other_half(sent, groups)
+        return pick(chosen, 0, row_count, held), arrived
+
+    def send_back(rows):
+        returned = to_other_half(rows[row_count // 2 :], groups)
+        held = gather_half(rows, groups) + gather_half(returned, groups)
+        return pick(back, 0, row_count, held)
+
+    kept_tokens, arrived_tokens = bring(tokens)
+    kept_grads, arrived_grads = bring(cotangent)
+    my_tokens, normed, inner, query_raw, key_raw, query_low, key_low, value_low = project_heads(
+        kept_tokens,
+        arrived_tokens,
         attn_gain,
         (query_weight, key_weight, value_weight),
         a_qkv,
@@ -1423,37 +1641,73 @@
     attended_low, log_total = attend(
         attn_bias, query_low, meta, keys, values, key_metas, segments, head_width
     )
-    layer_rows, grad_residual, grad_attended, grad_a_guo, grad_a_down, grad_b_gu, grad_b_do = (
-        feed_forward(
+    devices = lax.axis_size("dp") * groups
+    even = spreads_evenly(devices, feature_width, hidden_width, adapters.shape[0])
+    spread = devices if even else 0
+    layer_rows, grad_residual, grad_attended, *forward_grads = feed_forward(
+        spread,
+        turn_adapter,
+        attended_low,
+        my_tokens,
+        kept_grads,
+        arrived_grads,
+        ffn_gain,
+        (output_weight, gate_weight, up_weight, down_weight),
+        (a_guo, a_down, b_gu, b_do),
+        meta,
+    )
+    layer_out = send_back(layer_rows)
+
+    def back_part(pairs, before, after):
+        return attend_back(
+            attn_bias,
+            query_low,
+            meta,
+            log_total,
             attended_low,
-            my_tokens,
-            my_grads,
-            ffn_gain,
-            (output_weight, gate_weight, up_weight, down_weight),
-            (a_guo, a_down, b_gu, b_do),
-            meta,
+            grad_attended,
+            keys,
+            values,
+            key_metas,
+            segments,
+            head_width,
+            pairs,
+            before,
+            after,
         )
-    )
-    layer_out = send_back(layer_rows)
-    grad_query, grad_keys, grad_values = attend_back(
-        attn_bias,
-        query_low,
-        meta,
-        log_total,
-        attended_low,
-        grad_attended,
-        keys,
-        values,
-        key_metas,
-        segments,
-        head_width,
-    )
+
+    axes = ("dp", "group")
+    pair_count = feature_width // (2 * head_width)
+    first_pairs = 3 * pair_count // 4
+    after = []
+    if even:
+        total_rows = adapters.shape[0] // LANES
+        late_rows = 6 * feature_width // devices
+        params, first_old, second_old = spread_state(adapters, moment1, moment2, devices)
+        order = placing_order(groups, devices, 16)
+        early = lax.all_to_all(forward_grads[0], axes, 0, 0, tiled=True)
+        after = [first_old]
+    results = back_part((0, first_pairs), [], after)
+    if even:
+        told = 6 * RANK
+        table = early[:, 0, told : told + 2].astype(jnp.int32)
+        early_rows = params.shape[0] - late_rows
+        state = (params, first_old, second_old)
+        early_grad, early_new = settle(True, early_rows, table, early, *state, results[:1])
+        after = [early_new]
+        early_outer = lax.all_to_all(early_new, "dp", 0, 0, tiled=True)
+    results = back_part((first_pairs, pair_count), results, after)
+    grad_query = results[0]
+    grad_keys = results[1 : 1 + half_devices]
+    grad_values = results[1 + half_devices :]
     key_terms, value_terms = [grad_keys[0]], [grad_values[0]]
     for shift in range(1, half_devices):
         back_shift = half_devices - shift
         key_terms.append(within_half(grad_keys[shift], back_shift, groups))
         value_terms.append(within_half(grad_values[shift], back_shift, groups))
-    grad_rows, grad_a_qkv, grad_b_qkv = project_heads_back(
+    grad_rows, *back_grads = project_heads_back(
+        spread,
+        [early_outer] if even else [],
         grad_query,
         key_terms,
         value_terms,
@@ -1475,13 +1729,23 @@
         head_width,
     )
     input_grad = send_back(grad_rows)
-    grads = (grad_a_qkv, grad_b_qkv, grad_a_guo, grad_a_down, grad_b_gu, grad_b_do)
-    devices = lax.axis_size("dp") * groups
-    if spreads_evenly(devices, feature_width, hidden_width, adapters.shape[0], turns):
-        settled = settle_spread(grads, turn_adapter, adapters, moment1, moment2, devices)
-    else:
+    if not even:
+        grads = (*back_grads, *forward_grads)
+        column = jnp.arange(2 * RANK, dtype=jnp.int32)
+        few_choice = one_hot(
+            jnp.arange(LANES, dtype=jnp.int32)[:, None]
+            == (jnp.repeat(turn_adapter, RANK) * RANK + column % RANK)[None, :]
+        )
         settled = settle_shards(grads, few_choice, adapters, moment1, moment2, groups)
-    return (layer_out, input_grad) + settled
+        return (layer_out, input_grad) + settled
+    late = lax.all_to_all(back_grads[0], axes, 0, 0, tiled=True)
+    early_pieces = gather_inner(early_outer, groups)
+    late_grad, late_new = settle(False, late_rows, table, late, *state, early_pieces[1:2])
+    late_pieces = gather_inner(lax.all_to_all(late_new, "dp", 0, 0, tiled=True), groups)
+    adapters_new = assemble(order, early_pieces, total_rows, late_rows, 32, None)
+    adapters_new = assemble(order, late_pieces, total_rows, 0, 64, adapters_new)
+    owned = settle_owned(late_grad, early_grad, moment1, moment2, devices)
+    return (layer_out, input_grad, *owned, adapters_new.reshape(-1))
 
 
 def solution(mesh):

time: 393 us -> 319 us (0.81)
  waiting for transfers between devices: 74.1 us -> 37.1 us
  local copies, waits for them, and re-layouts: 49.5 us -> 23.1 us
  Pallas kernels: 175 us -> 197 us
  other arithmetic: 28.8 us -> 7.06 us
  matrix products: 14.5 us -> 0 us
  starting transfers between devices: 41.1 us -> 51.1 us
    ppermute x10 -> x6, waiting for transfers between devices: 41.7 us -> 0.02 us  [gather_inner(): pieces = pieces + [lax.ppermute(piece, 'group', pairs) for piece in pieces]]
    pallas_call x6 -> x15, Pallas kernels: 144 us -> 165 us  [the longest x1 52.8 us: feed_forward(): pl.pallas_call(functools.partial(feed_forward_kernel, devices), grid=(hid...]
    all_to_all x4 -> x6, starting transfers between devices: 17.8 us -> 37.7 us  [the longest x1 17.1 us: per_device(): early = lax.all_to_all(forward_grads[0], axes, 0, 0, tiled=True)]
    all_to_all x4 -> x6, waiting for transfers between devices: 14 us -> 30.5 us  [the longest x1 17.2 us: per_device(): early_outer = lax.all_to_all(early_new, 'dp', 0, 0, tiled=True)]
    dot_general x5 -> x0, matrix products: 14.5 us -> none  [the longest x4 13.1 us: pick_rows(): jnp.dot(chosen, rows, preferred_element_type=jnp.float32)]
    unnamed x102 -> x49, local copies, waits for them, and re-layouts: 23.4 us -> 9.39 us
    ppermute x4, waiting for transfers between devices: 18.4 us -> 6.57 us  [to_other_half(): lax.ppermute(array, 'group', [(i, (i + half) % groups) for i in range(gro...]
    ppermute x10 -> x6, starting transfers between devices: 12.7 us -> 4.43 us  [gather_inner(): pieces = pieces + [lax.ppermute(piece, 'group', pairs) for piece in pieces]]
  transfers between devices with their start and end apart: 28 -> 26, of which waited for: 10 -> 5; matrix products, arithmetic and copies ran while one was open for 22% -> 6% of each run, Pallas kernels for 22% -> 60%
where the time goes in v3:
time: 319 us; the launch traced here: 316 us
  Pallas kernels  197 us (62%)
  starting transfers between devices  51.1 us (16%)
  waiting for transfers between devices  37.1 us (12%)
  local copies, waits for them, and re-layouts  23.1 us (7%)
  other arithmetic  7.06 us (2%)
    pallas_call x1, Pallas kernels, feed_forward(): pl.pallas_call(functools.partial(feed_forward_kernel, devices), grid=(hid...  52.8 us
    pallas_call x2, Pallas kernels, attend_back(): pl.pallas_call(functools.partial(attend_back_kernel, first, count, segmen...  33.7 us
    pallas_call x6, Pallas kernels, pick(): pl.pallas_call(pick_kernel, grid=(features // tile,), in_specs=[pl.BlockS...  24 us
    pallas_call x1, Pallas kernels, attend(): pl.pallas_call(functools.partial(attend_kernel, count, segments, width),...  19.1 us
    pallas_call x1, Pallas kernels, project_heads_back(): pl.pallas_call(functools.partial(project_heads_back_kernel, count, width,...  17.8 us
    all_to_all x1, waiting for transfers between devices, per_device(): early_outer = lax.all_to_all(early_new, 'dp', 0, 0, tiled=True)  17.2 us
    all_to_all x1, starting transfers between devices, per_device(): early = lax.all_to_all(forward_grads[0], axes, 0, 0, tiled=True)  17.1 us
    pallas_call x2, Pallas kernels, assemble(): pl.pallas_call(functools.partial(assemble_kernel, len(pieces), block), gr...  15.5 us
  transfers between devices with their start and end apart: 26, of which 5 were waited for; matrix products, arithmetic and copies ran while one was open for 6% of the time, Pallas kernels for 60%

profile of v3, /device:TPU:0, one launch (start us, length us, event | category | flops | bytes accessed | tf_op | source)
XLA Modules:
  0.0 316.4 jit_solution(10464834462208398307)
XLA Ops:
  1.2 4.4 %plan.1 = (bf16[768,1024]{1,0:T(8,128)(2,1)}, bf16[512,1536]{1,0:T(8,128)(2,1)}, s32[2]{0:T(128)}, s32[512,128]{1,0:T(8,128)}, s32[512,128]{1,0:T(8,128)}) custom-call(s32[1]{0:T(128)} %bitcast.member_ref, s32[1,3]{1,0:T(1,128)} %length_ref.1, s32[1,3]{1,0:T(1,128)} %adapter_ref.1, s32[1,16]{1,0:T(1,128)} %order_ref.1, s32[16,128]{1,0:T(8,128)} %bitcast.30), custom_call_target="tpu_custom_call" | custom-call | flops 2147483648 | bytes 2097152 | tf_op jit(solution)/shard_map/plan/pallas_call | solution.py:457
  7.8 3.0 pick.7
  10.8 2.9 collective-permute-start.1
  15.6 5.5 %select.29 = (bf16[1024,128]{1,0:T(8,128)(2,1)}, bf16[1024,128]{1,0:T(8,128)(2,1)}, bf16[4096,128]{1,0:T(8,128)(2,1)}, bf16[128,1024]{1,0:T(8,128)(2,1)}, bf16[1...) custom-call(s32[2]{0:T(128)} %get-tuple-element.48.turn_ref, bf16[23552,128]{1,0:T(8,128)(2,1)} %bitcast.28), custom_call_target="tpu_custom_call" | custom-call | flops 2147483648 | bytes 12058624 | tf_op jit(solution)/shard_map/select/pallas_call | solution.py:864
  22.3 3.9 %pick.6.kept_ref = bf16[512,1024]{1,0:T(8,128)(2,1)} custom-call(bf16[768,1024]{1,0:T(8,128)(2,1)} %get-tuple-element.49.chosen_ref, bf16[512,1024]{1,0:T(8,128)(2,1)} %refs_0_.5, bf16[512,1024]{1,0:T(8,128)(2,1)} %copy-done.6), custom_call_target="tpu_custom_call" | custom-call | flops 1073741824 | bytes 4194304 | tf_op jit(solution)/shard_map/pick/pallas_call | solution.py:491
  27.0 9.9 %project_key_value.1 = (bf16[512,1024]{1,0:T(8,128)(2,1)}, bf16[512,1024]{1,0:T(8,128)(2,1)}, bf16[512,128]{1,0:T(8,128)(2,1)}, f32[512,1024]{1,0:T(8,128)}, bf1...) custom-call(bf16[512,1024]{1,0:T(8,128)(2,1)} %pick.6.kept_ref, bf16[256,1024]{1,0:T(8,128)(2,1)} %copy-done.21, ...), custom_call_target="tpu_custom_call" | custom-call | flops 3221225472 | bytes 11534336 | tf_op jit(solution)/shard_map/project_key_value/pallas_call | solution.py:1011
  38.4 3.0 pick.9
  44.4 5.2 %all-to-all-start = ((f32[32,46,128]{2,1,0:T(8,128)}), f32[32,46,128]{2,1,0:T(8,128)S(1)}, u32[]{:S(2)}, u32[]{:S(2)}) async-start(f32[32,46,128]{2,1,0:T(8,128)} %copy.51), calls=%async_computation | async-start | bytes 1572864 | tf_op jit(solution)/shard_map/all_to_all | solution.py:1553
  50.8 4.0 %pick.8.kept_ref = bf16[512,1024]{1,0:T(8,128)(2,1)} custom-call(bf16[768,1024]{1,0:T(8,128)(2,1)} %get-tuple-element.49.chosen_ref, bf16[512,1024]{1,0:T(8,128)(2,1)} %refs_0_.7, bf16[512,1024]{1,0:T(8,128)(2,1)} %copy-done.5), custom_call_target="tpu_custom_call" | custom-call | flops 1073741824 | bytes 4194304 | tf_op jit(solution)/shard_map/pick/pallas_call | solution.py:491
  54.8 6.9 %project_query.1 = (f32[512,1024]{1,0:T(8,128)}, bf16[512,1024]{1,0:T(8,128)(2,1)}) custom-call(bf16[512,1024]{1,0:T(8,128)(2,1)} %get-tuple-element.53.normed_ref.refs_6_, bf16[512,128]{1,0:T(8,128)(2,1)} %get-tuple-element.54.inner_ref.refs_7_, bf16[1024,1024]{1,0:T(8,128)(2,1)} %refs_11_.1, bf16[128,1024]{1,0:T(8,128)(2,1)} %get-tuple-element.51.b_ref.refs_15_, ...), custom_call_target="tpu_custom_call" | custom-call | flops 1610612736 | bytes 6291456 | tf_op jit(solution)/shard_map/project_query/pallas_call | solution.py:1046
  62.7 19.1 %attend.1 = (bf16[512,1024]{1,0:T(8,128)(2,1)}, f32[512,1024]{1,0:T(8,128)}) custom-call(f32[2,16]{1,0:T(2,128)} %bias_ref.5, bf16[512,1024]{1,0:T(8,128)(2,1)} %get-tuple-element.55.query_ref, s32[512,128]{1,0:T(8,128)} %get-tuple-element.52.meta_ref.qmeta_ref.refs_4_.refs_16_, bf16[512,1024]{1,0:T(8,128)(2,1)} %get-tuple-element.56.refs_0_, ...), custom_call_target="tpu_custom_call" | custom-call | flops 2147483648 | bytes 6291456 | tf_op jit(solution)/shard_map/attend/pallas_call | solution.py:127
  82.6 52.8 %feed_forward.1 = (bf16[512,1024]{1,0:T(8,128)(2,1)}, f32[512,1024]{1,0:T(8,128)}, bf16[512,1024]{1,0:T(8,128)(2,1)}, bf16[32,144,128]{2,1,0:T(8,128)(2,1)}) custom-call(s32[2]{0:T(128)} %get-tuple-element.48.turn_ref, bf16[512,1024]{1,0:T(8,128)(2,1)} %get-tuple-element.59.att_ref.attended_ref, bf16[512,1024]{1,0:T(8,128)(2,1)} %get-tuple-element.60.x_ref.refs_8_, ...), custom_call_target="tpu_custom_call" | custom-call | flops 30064771072 | bytes 41943040 | tf_op jit(solution)/shard_map/feed_forward/pallas_call | solution.py:1481
  135.4 17.1 %all-to-all-start.1 = ((bf16[32,144,128]{2,1,0:T(8,128)(2,1)}), bf16[32,144,128]{2,1,0:T(8,128)(2,1)S(1)}, u32[]{:S(2)}, u32[]{:S(2)}) async-start(bf16[32,144,128]{2,1,0:T(8,128)(2,1)} %get-tuple-element.73), calls=%async_computation.1 | async-start | bytes 2359296 | tf_op jit(solution)/shard_map/all_to_all | solution.py:1688
  156.6 24.0 %attend_back.2 = (f32[512,1024]{1,0:T(8,128)}, f32[512,1024]{1,0:T(8,128)}, bf16[512,1024]{1,0:T(8,128)(2,1)}, f32[512,1024]{1,0:T(8,128)}, bf16[512,1024]{1,0:T(8,128)(2,1)}) custom-call(f32[2,16]{1,0:T(2,128)} %bias_ref.5, bf16[512,1024]{1,0:T(8,128)(2,1)} %get-tuple-element.55.query_ref, s32[512,128]{1,0:T(8,128)} %get-tuple-element.52.meta_ref.qmeta_ref.refs_4_.refs_16_, ...), custom_call_target="tpu_custom_call" | custom-call | flops 4026531840 | bytes 9437184 | tf_op jit(solution)/shard_map/attend_back/pallas_call | solution.py:260
  183.4 4.1 %settle_early.1 = (bf16[544,128]{1,0:T(8,128)(2,1)}, bf16[8,544,128]{2,1,0:T(8,128)(2,1)}) custom-call(s32[32,2]{1,0:T(8,128)} %bitcast.26, s32[1,1024]{1,0:T(1,128)} %broadcast_in_dim_reshape.8.tall_ref, s32[1,512]{1,0:T(1,128)} %broadcast_in_dim_reshape.9.square_ref, bf16[32,144,128]{2,1,0:T(8,128)(2,1)} %copy-done.2, bf16[736,128]{1,0:T(8,128)(2,1)} %bitcast.19, ...), custom_call_target="tpu_custom_call" | custom-call | flops 536870912 | bytes 2359296 | tf_op jit(solution)/shard_map/settle_early/pallas_call | solution.py:691
  187.6 5.0 %all-to-all-start.2 = ((bf16[8,544,128]{2,1,0:T(8,128)(2,1)}), bf16[8,544,128]{2,1,0:T(8,128)(2,1)S(1)}, u32[]{:S(2)}, u32[]{:S(2)}) async-start(bf16[8,544,128]{2,1,0:T(8,128)(2,1)} %get-tuple-element.74.refs_11_), calls=%async_computation.2 | async-start | bytes 2228224 | tf_op jit(solution)/shard_map/all_to_all | solution.py:1698
  192.6 9.7 %attend_back.3 = (f32[512,1024]{1,0:T(8,128)}, f32[512,1024]{1,0:T(8,128)}, bf16[512,1024]{1,0:T(8,128)(2,1)}, f32[512,1024]{1,0:T(8,128)}, bf16[512,1024]{1,0:T(8,128)(2,1)}) custom-call(f32[2,16]{1,0:T(2,128)} %bias_ref.5, ...), custom_call_target="tpu_custom_call", output_to_operand_aliasing={{0}: (12, {}), {1}: (13, {}), {2}: (14, {}), {3}: (15, {}),... | custom-call | flops 1342177280 | bytes 3145728 | tf_op jit(solution)/shard_map/attend_back/pallas_call | solution.py:260
  202.8 17.2 %all-to-all-done.2.refs_21_.refs_0_ = bf16[8,544,128]{2,1,0:T(8,128)(2,1)S(1)} async-done(((bf16[8,544,128]{2,1,0:T(8,128)(2,1)}), bf16[8,544,128]{2,1,0:T(8,128)(2,1)S(1)}, u32[]{:S(2)}, u32[]{:S(2)}) %all-to-all-start.2) | async-done | bytes 1114144 | tf_op jit(solution)/shard_map/all_to_all | solution.py:1698
  221.5 17.8 %project_heads_back.1 = (bf16[512,1024]{1,0:T(8,128)(2,1)}, bf16[32,64,128]{2,1,0:T(8,128)(2,1)}) custom-call(f32[512,1024]{1,0:T(8,128)} %get-tuple-element.75.gq_ref, f32[512,1024]{1,0:T(8,128)} %get-tuple-element.76.refs_0_, bf16[512,1024]{1,0:T(8,128)(2,1)} %collective-permute-done.9.refs_1_, f32[512,1024]{1,0:T(8,128)} %get-tuple-element.78.refs_2_, ...), custom_call_target="tpu_custom_call" | custom-call | flops 4294967296 | bytes 22020096 | tf_op jit(solution)/shard_map/project_heads_back/pallas_call | solution.py:1218
  239.4 3.2 all-to-all-start.3
  242.6 1.9 slice.19
  248.3 9.8 %all-to-all-done.3.arrived_ref = bf16[32,64,128]{2,1,0:T(8,128)(2,1)S(1)} async-done(((bf16[32,64,128]{2,1,0:T(8,128)(2,1)}), bf16[32,64,128]{2,1,0:T(8,128)(2,1)S(1)}, u32[]{:S(2)}, u32[]{:S(2)}) %all-to-all-start.3) | async-done | bytes 524320 | tf_op jit(solution)/shard_map/all_to_all | solution.py:1741
  260.0 2.9 settle_late.1
  262.9 3.5 %all-to-all-start.5 = ((bf16[8,192,128]{2,1,0:T(8,128)(2,1)}), bf16[8,192,128]{2,1,0:T(8,128)(2,1)S(1)}, u32[]{:S(2)}, u32[]{:S(2)}) async-start(bf16[8,192,128]{2,1,0:T(8,128)(2,1)} %get-tuple-element.87), calls=%async_computation.5 | async-start | bytes 786432 | tf_op jit(solution)/shard_map/all_to_all | solution.py:1744
  267.4 6.6 %collective-permute-done.12.refs_2_ = bf16[256,1024]{1,0:T(8,128)(2,1)} collective-permute-done((bf16[256,1024]{1,0:T(8,128)(2,1)}, bf16[256,1024]{1,0:T(8,128)(2,1)}, u32[]{:S(2)}, u32[]{:S(2)}) %collective-permute-start.12) | collective-permute-done | bytes 524320 | tf_op jit(solution)/shard_map/ppermute | solution.py:524
  275.5 2.8 all-to-all-done.5.refs_0_
  278.3 3.9 %all-to-all-start.4 = ((bf16[32,23,128]{2,1,0:T(8,128)(2,1)}), bf16[32,23,128]{2,1,0:T(8,128)(2,1)}, u32[]{:S(2)}, u32[]{:S(2)}) async-start(bf16[32,23,128]{2,1,0:T(8,128)(2,1)} %reshape.150), calls=%async_computation.4 | async-start | bytes 393216 | tf_op jit(solution)/shard_map/all_to_all | solution.py:1565
  283.1 1.9 collective-permute-start.15
  285.8 5.1 %pick.10 = bf16[512,1024]{1,0:T(8,128)(2,1)} custom-call(bf16[512,1536]{1,0:T(8,128)(2,1)} %get-tuple-element.47.chosen_ref, bf16[512,1024]{1,0:T(8,128)(2,1)} %get-tuple-element.65.refs_0_, bf16[512,1024]{1,0:T(8,128)(2,1)} %collective-permute-done.6.refs_1_, bf16[256,1024]{1,0:T(8,128)(2,1)} %collective-permute-done.7.refs_2_, bf16[256,1024]{1,0:T(8,128)(2,1)} %copy-done.19), custom_call_target="tpu_custom_call" | custom-call | flops 1610612736 | bytes 4194304 | tf_op jit(solution)/shard_map/pick/pallas_call | solution.py:491
  291.0 5.1 %pick.11 = bf16[512,1024]{1,0:T(8,128)(2,1)} custom-call(bf16[512,1536]{1,0:T(8,128)(2,1)} %get-tuple-element.47.chosen_ref, bf16[512,1024]{1,0:T(8,128)(2,1)} %get-tuple-element.83.refs_0_, bf16[512,1024]{1,0:T(8,128)(2,1)} %collective-permute-done.11.refs_1_, bf16[256,1024]{1,0:T(8,128)(2,1)} %collective-permute-done.12.refs_2_, ...), custom_call_target="tpu_custom_call" | custom-call | flops 1610612736 | bytes 4194304 | tf_op jit(solution)/shard_map/pick/pallas_call | solution.py:491
  299.1 11.5 %assemble.2.refs_4_ = bf16[23552,128]{1,0:T(8,128)(2,1)} custom-call(bf16[512,512]{1,0:T(8,128)(2,1)} %fusion.order_ref, bf16[8,544,128]{2,1,0:T(8,128)(2,1)} %copy-done, bf16[8,544,128]{2,1,0:T(8,128)(2,1)} %copy-done.3, bf16[8,544,128]{2,1,0:T(8,128)(2,1)} %collective-permute-done.18.refs_2_, bf16[8,544,128]{2,1,0:T(8,128)(2,1)} %collective-permute-done.19.refs_3_), custom_call_target="tpu_custom_call" | custom-call | flops 2281701376 | bytes 8912896 | tf_op jit(solution)/shard_map/assemble/pallas_call | solution.py:766
  312.2 4.0 %assemble.3 = bf16[23552,128]{1,0:T(8,128)(2,1)} custom-call(bf16[512,512]{1,0:T(8,128)(2,1)} %fusion.order_ref, bf16[8,192,128]{2,1,0:T(8,128)(2,1)} %copy-done.8, bf16[8,192,128]{2,1,0:T(8,128)(2,1)} %collective-permute-done.15.refs_1_, bf16[8,192,128]{2,1,0:T(8,128)(2,1)} %copy-done.13, ...), custom_call_target="tpu_custom_call", output_to_operand_aliasing={{}: (5, {})} | custom-call | flops 805306368 | bytes 3145728 | tf_op jit(solution)/shard_map/assemble/pallas_call | solution.py:766
  (127 shorter events, 37.6 us)
Async XLA Ops:
  0.6 6.2 %collective-permute-start = (bf16[512,1024]{1,0:T(8,128)(2,1)}, bf16[512,1024]{1,0:T(8,128)(2,1)S(1)}, u32[]{:S(2)}, u32[]{:S(2)}) collective-permute-start(bf16[512,1024]{1,0:T(8,128)(2,1)} %refs_0_.5), channel_id=1, source_target_pairs={{1,0},{0,1},{3,2},{2,3},{5,4},{4,5},{7,6},{6,7},{9,8},{8,9},{11,10... | collective-permute-start | bytes 3145736 | tf_op jit(solution)/shard_map/ppermute | solution.py:515
  1.1 36.3 %collective-permute-start.4 = (bf16[512,1024]{1,0:T(8,128)(2,1)}, bf16[512,1024]{1,0:T(8,128)(2,1)S(1)}, u32[]{:S(2)}, u32[]{:S(2)}) collective-permute-start(bf16[512,1024]{1,0:T(8,128)(2,1)} %refs_0_.7), channel_id=1, source_target_pairs={{1,0},{0,1},{3,2},{2,3},{5,4},{4,5},{7,6},{6,7},{9,8},{8,9},{11,10... | collective-permute-start | bytes 3145736 | tf_op jit(solution)/shard_map/ppermute | solution.py:515
  10.8 15.4 %collective-permute-start.1 = (bf16[256,1024]{1,0:T(8,128)(2,1)}, bf16[256,1024]{1,0:T(8,128)(2,1)S(1)}, u32[]{:S(2)}, u32[]{:S(2)}) collective-permute-start(bf16[256,1024]{1,0:T(8,128)(2,1)} %pick.7), channel_id=1, source_target_pairs={{0,2},{1,3},{2,0},{3,1},{4,6},{5,7},{6,4},{7,5},{8,10},{9,11},{10,... | collective-permute-start | bytes 1572872 | tf_op jit(solution)/shard_map/ppermute | solution.py:524
  36.9 24.9 %collective-permute-start.2 = (bf16[512,1024]{1,0:T(8,128)(2,1)}, bf16[512,1024]{1,0:T(8,128)(2,1)S(1)}, u32[]{:S(2)}, u32[]{:S(2)}) collective-permute-start(bf16[512,1024]{1,0:T(8,128)(2,1)} %get-tuple-element.56.refs_0_), channel_id=1, source_target_pairs={{1,0},{0,1},{3,2},{2,3},{5,4},{4,5},{7,6},{6,7},{9,8},{8,9},{11,10... | collective-permute-start | bytes 3145736 | tf_op jit(solution)/shard_map/ppermute | solution.py:515
  36.9 6.1 %copy-start.9 = (f32[94208]{0:T(1024)S(1)}, f32[94208]{0:T(1024)}, u32[]{:S(2)}) copy-start(f32[94208]{0:T(1024)} %param.41) | copy-start | bytes 1130500
  36.9 24.8 %collective-permute-start.3 = (bf16[512,1024]{1,0:T(8,128)(2,1)}, bf16[512,1024]{1,0:T(8,128)(2,1)}, u32[]{:S(2)}, u32[]{:S(2)}) collective-permute-start(bf16[512,1024]{1,0:T(8,128)(2,1)} %get-tuple-element.57.refs_2_), channel_id=1, source_target_pairs={{1,0},{0,1},{3,2},{2,3},{5,4},{4,5},{7,6},{6,7},{9,8},{8,9},{11,10... | collective-permute-start | bytes 3145736 | tf_op jit(solution)/shard_map/ppermute | solution.py:515
  41.4 40.4 %collective-permute-start.5 = (bf16[256,1024]{1,0:T(8,128)(2,1)}, bf16[256,1024]{1,0:T(8,128)(2,1)S(1)}, u32[]{:S(2)}, u32[]{:S(2)}) collective-permute-start(bf16[256,1024]{1,0:T(8,128)(2,1)} %pick.9), channel_id=1, source_target_pairs={{0,2},{1,3},{2,0},{3,1},{4,6},{5,7},{6,4},{7,5},{8,10},{9,11},{10,... | collective-permute-start | bytes 1572872 | tf_op jit(solution)/shard_map/ppermute | solution.py:524
  43.0 6.6 %copy-start.23 = (bf16[64]{0:T(256)(128)(2,1)S(1)}, bf16[64]{0:T(256)(128)(2,1)}, u32[]{:S(2)}) copy-start(bf16[64]{0:T(256)(128)(2,1)} %param.29) | copy-start | bytes 388
  43.0 7.2 %copy-start.18 = (bf16[1024]{0:T(1024)(128)(2,1)S(1)}, bf16[1024]{0:T(1024)(128)(2,1)}, u32[]{:S(2)}) copy-start(bf16[1024]{0:T(1024)(128)(2,1)} %param.28) | copy-start | bytes 6148
  44.4 91.0 %all-to-all-start = ((f32[32,46,128]{2,1,0:T(8,128)}), f32[32,46,128]{2,1,0:T(8,128)S(1)}, u32[]{:S(2)}, u32[]{:S(2)}) async-start(f32[32,46,128]{2,1,0:T(8,128)} %copy.51), calls=%async_computation | async-start | bytes 1572864 | tf_op jit(solution)/shard_map/all_to_all | solution.py:1553
  135.4 45.9 %all-to-all-start.1 = ((bf16[32,144,128]{2,1,0:T(8,128)(2,1)}), bf16[32,144,128]{2,1,0:T(8,128)(2,1)S(1)}, u32[]{:S(2)}, u32[]{:S(2)}) async-start(bf16[32,144,128]{2,1,0:T(8,128)(2,1)} %get-tuple-element.73), calls=%async_computation.1 | async-start | bytes 2359296 | tf_op jit(solution)/shard_map/all_to_all | solution.py:1688
  187.6 32.5 %all-to-all-start.2 = ((bf16[8,544,128]{2,1,0:T(8,128)(2,1)}), bf16[8,544,128]{2,1,0:T(8,128)(2,1)S(1)}, u32[]{:S(2)}, u32[]{:S(2)}) async-start(bf16[8,544,128]{2,1,0:T(8,128)(2,1)} %get-tuple-element.74.refs_11_), calls=%async_computation.2 | async-start | bytes 2228224 | tf_op jit(solution)/shard_map/all_to_all | solution.py:1698
  202.3 19.3 %collective-permute-start.9 = (bf16[512,1024]{1,0:T(8,128)(2,1)}, bf16[512,1024]{1,0:T(8,128)(2,1)}, u32[]{:S(2)}, u32[]{:S(2)}) collective-permute-start(bf16[512,1024]{1,0:T(8,128)(2,1)} %get-tuple-element.77), channel_id=1, source_target_pairs={{1,0},{0,1},{3,2},{2,3},{5,4},{4,5},{7,6},{6,7},{9,8},{8,9},{11,10... | collective-permute-start | bytes 3145736 | tf_op jit(solution)/shard_map/ppermute | solution.py:515
  202.3 19.2 %collective-permute-start.10 = (bf16[512,1024]{1,0:T(8,128)(2,1)}, bf16[512,1024]{1,0:T(8,128)(2,1)}, u32[]{:S(2)}, u32[]{:S(2)}) collective-permute-start(bf16[512,1024]{1,0:T(8,128)(2,1)} %get-tuple-element.79), channel_id=1, source_target_pairs={{1,0},{0,1},{3,2},{2,3},{5,4},{4,5},{7,6},{6,7},{9,8},{8,9},{11,10... | collective-permute-start | bytes 3145736 | tf_op jit(solution)/shard_map/ppermute | solution.py:515
  220.0 38.1 %collective-permute-start.14 = (bf16[8,544,128]{2,1,0:T(8,128)(2,1)S(1)}, bf16[8,544,128]{2,1,0:T(8,128)(2,1)S(1)}, u32[]{:S(2)}, u32[]{:S(2)}) collective-permute-start(bf16[8,544,128]{2,1,0:T(8,128)(2,1)S(1)} %all-to-all-done.2.refs_21_.refs_0_), channel_id=1, source_target_pairs={{0,2},{1,3},{2,0},{3,1},{4,6},{5,7},{6,4},{7,5},{8,10},{9,11},{10,... | collective-permute-start | bytes 3342344 | tf_op jit(solution)/shard_map/ppermute | solution.py:714
  239.4 18.7 %all-to-all-start.3 = ((bf16[32,64,128]{2,1,0:T(8,128)(2,1)}), bf16[32,64,128]{2,1,0:T(8,128)(2,1)S(1)}, u32[]{:S(2)}, u32[]{:S(2)}) async-start(bf16[32,64,128]{2,1,0:T(8,128)(2,1)} %get-tuple-element.84), calls=%async_computation.3 | async-start | bytes 1048576 | tf_op jit(solution)/shard_map/all_to_all | solution.py:1741
  244.4 22.4 %collective-permute-start.7 = (bf16[256,1024]{1,0:T(8,128)(2,1)}, bf16[256,1024]{1,0:T(8,128)(2,1)}, u32[]{:S(2)}, u32[]{:S(2)}) collective-permute-start(bf16[256,1024]{1,0:T(8,128)(2,1)} %slice.19), channel_id=1, source_target_pairs={{0,2},{1,3},{2,0},{3,1},{4,6},{5,7},{6,4},{7,5},{8,10},{9,11},{10,... | collective-permute-start | bytes 1572872 | tf_op jit(solution)/shard_map/ppermute | solution.py:524
  248.1 25.9 %collective-permute-start.12 = (bf16[256,1024]{1,0:T(8,128)(2,1)}, bf16[256,1024]{1,0:T(8,128)(2,1)}, u32[]{:S(2)}, u32[]{:S(2)}) collective-permute-start(bf16[256,1024]{1,0:T(8,128)(2,1)} %slice.23), channel_id=1, source_target_pairs={{0,2},{1,3},{2,0},{3,1},{4,6},{5,7},{6,4},{7,5},{8,10},{9,11},{10,... | collective-permute-start | bytes 1572872 | tf_op jit(solution)/shard_map/ppermute | solution.py:524
  248.3 36.7 %collective-permute-start.6 = (bf16[512,1024]{1,0:T(8,128)(2,1)}, bf16[512,1024]{1,0:T(8,128)(2,1)}, u32[]{:S(2)}, u32[]{:S(2)}) collective-permute-start(bf16[512,1024]{1,0:T(8,128)(2,1)} %get-tuple-element.65.refs_0_), channel_id=1, source_target_pairs={{1,0},{0,1},{3,2},{2,3},{5,4},{4,5},{7,6},{6,7},{9,8},{8,9},{11,10... | collective-permute-start | bytes 3145736 | tf_op jit(solution)/shard_map/ppermute | solution.py:515
  260.0 14.0 %copy-start.16 = (bf16[544,128]{1,0:T(8,128)(2,1)S(1)}, bf16[544,128]{1,0:T(8,128)(2,1)}, u32[]{:S(2)}) copy-start(bf16[544,128]{1,0:T(8,128)(2,1)} %get-tuple-element.86) | copy-start | bytes 417796
  262.9 15.4 %all-to-all-start.5 = ((bf16[8,192,128]{2,1,0:T(8,128)(2,1)}), bf16[8,192,128]{2,1,0:T(8,128)(2,1)S(1)}, u32[]{:S(2)}, u32[]{:S(2)}) async-start(bf16[8,192,128]{2,1,0:T(8,128)(2,1)} %get-tuple-element.87), calls=%async_computation.5 | async-start | bytes 786432 | tf_op jit(solution)/shard_map/all_to_all | solution.py:1744
  266.4 24.6 %collective-permute-start.11 = (bf16[512,1024]{1,0:T(8,128)(2,1)}, bf16[512,1024]{1,0:T(8,128)(2,1)}, u32[]{:S(2)}, u32[]{:S(2)}) collective-permute-start(bf16[512,1024]{1,0:T(8,128)(2,1)} %get-tuple-element.83.refs_0_), channel_id=1, source_target_pairs={{1,0},{0,1},{3,2},{2,3},{5,4},{4,5},{7,6},{6,7},{9,8},{8,9},{11,10... | collective-permute-start | bytes 3145736 | tf_op jit(solution)/shard_map/ppermute | solution.py:515
  266.8 18.2 %collective-permute-start.8 = (bf16[256,1024]{1,0:T(8,128)(2,1)}, bf16[256,1024]{1,0:T(8,128)(2,1)S(1)}, u32[]{:S(2)}, u32[]{:S(2)}) collective-permute-start(bf16[256,1024]{1,0:T(8,128)(2,1)} %collective-permute-done.7.refs_2_), channel_id=1, source_target_pairs={{1,0},{0,1},{3,2},{2,3},{5,4},{4,5},{7,6},{6,7},{9,8},{8,9},{11,10... | collective-permute-start | bytes 1572872 | tf_op jit(solution)/shard_map/ppermute | solution.py:515
  273.9 17.1 %collective-permute-start.13 = (bf16[256,1024]{1,0:T(8,128)(2,1)}, bf16[256,1024]{1,0:T(8,128)(2,1)}, u32[]{:S(2)}, u32[]{:S(2)}) collective-permute-start(bf16[256,1024]{1,0:T(8,128)(2,1)} %collective-permute-done.12.refs_2_), channel_id=1, source_target_pairs={{1,0},{0,1},{3,2},{2,3},{5,4},{4,5},{7,6},{6,7},{9,8},{8,9},{11,10... | collective-permute-start | bytes 1572872 | tf_op jit(solution)/shard_map/ppermute | solution.py:515
  278.3 19.2 %copy-start.8 = (bf16[8,192,128]{2,1,0:T(8,128)(2,1)}, bf16[8,192,128]{2,1,0:T(8,128)(2,1)S(1)}, u32[]{:S(2)}) copy-start(bf16[8,192,128]{2,1,0:T(8,128)(2,1)S(1)} %all-to-all-done.5.refs_0_) | copy-start | bytes 1179652
  278.3 18.2 %all-to-all-start.4 = ((bf16[32,23,128]{2,1,0:T(8,128)(2,1)}), bf16[32,23,128]{2,1,0:T(8,128)(2,1)}, u32[]{:S(2)}, u32[]{:S(2)}) async-start(bf16[32,23,128]{2,1,0:T(8,128)(2,1)} %reshape.150), calls=%async_computation.4 | async-start | bytes 393216 | tf_op jit(solution)/shard_map/all_to_all | solution.py:1565
  283.1 14.6 %collective-permute-start.15 = (bf16[8,192,128]{2,1,0:T(8,128)(2,1)S(1)}, bf16[8,192,128]{2,1,0:T(8,128)(2,1)}, u32[]{:S(2)}, u32[]{:S(2)}) collective-permute-start(bf16[8,192,128]{2,1,0:T(8,128)(2,1)S(1)} %all-to-all-done.5.refs_0_), channel_id=1, source_target_pairs={{0,2},{1,3},{2,0},{3,1},{4,6},{5,7},{6,4},{7,5},{8,10},{9,11},{10,... | collective-permute-start | bytes 1179656 | tf_op jit(solution)/shard_map/ppermute | solution.py:714
  290.9 8.2 %collective-permute-start.18 = (bf16[8,544,128]{2,1,0:T(8,128)(2,1)S(1)}, bf16[8,544,128]{2,1,0:T(8,128)(2,1)}, u32[]{:S(2)}, u32[]{:S(2)}) collective-permute-start(bf16[8,544,128]{2,1,0:T(8,128)(2,1)S(1)} %copy-done.1), channel_id=1, source_target_pairs={{0,1},{1,0},{2,3},{3,2},{4,5},{5,4},{6,7},{7,6},{8,9},{9,8},{10,11... | collective-permute-start | bytes 3342344 | tf_op jit(solution)/shard_map/ppermute | solution.py:714
  296.1 3.1 collective-permute-start.19
  297.5 13.1 %copy-start.11 = (f32[23,32,128]{2,1,0:T(8,128)}, f32[23,32,128]{2,1,0:T(8,128)S(1)}, u32[]{:S(2)}) copy-start(f32[23,32,128]{2,1,0:T(8,128)S(1)} %copy.56) | copy-start | bytes 1130500
  297.6 13.1 %collective-permute-start.16 = (bf16[8,192,128]{2,1,0:T(8,128)(2,1)S(1)}, bf16[8,192,128]{2,1,0:T(8,128)(2,1)S(1)}, u32[]{:S(2)}, u32[]{:S(2)}) collective-permute-start(bf16[8,192,128]{2,1,0:T(8,128)(2,1)S(1)} %all-to-all-done.5.refs_0_), channel_id=1, source_target_pairs={{0,1},{1,0},{2,3},{3,2},{4,5},{5,4},{6,7},{7,6},{8,9},{9,8},{10,11... | collective-permute-start | bytes 1179656 | tf_op jit(solution)/shard_map/ppermute | solution.py:714
  297.7 12.9 %collective-permute-start.17 = (bf16[8,192,128]{2,1,0:T(8,128)(2,1)}, bf16[8,192,128]{2,1,0:T(8,128)(2,1)S(1)}, u32[]{:S(2)}, u32[]{:S(2)}) collective-permute-start(bf16[8,192,128]{2,1,0:T(8,128)(2,1)} %collective-permute-done.15.refs_1_), channel_id=1, source_target_pairs={{0,1},{1,0},{2,3},{3,2},{4,5},{5,4},{6,7},{7,6},{8,9},{9,8},{10,11... | collective-permute-start | bytes 1179656 | tf_op jit(solution)/shard_map/ppermute | solution.py:714
  (18 other events, 41.2 us)

commit v4 on v3

--- a/solution.py
+++ b/solution.py
@@ -39,32 +39,51 @@
     return parts
 
 
-def spread_parts(column, parts, first):
-    result = jnp.zeros(column.shape, jnp.float32)
-    for index, part in enumerate(parts):
+def parts_in_lanes(values, first, column):
+    result = jnp.zeros(values.shape, jnp.float32)
+    for index, part in enumerate(exact_parts(values)):
         result = jnp.where(column == first + index, part, result)
     return result
 
 
-def query_extension(bias_ref, head, query_var, query_seg, column, segments):
-    same = exact_parts(jnp.full((1, column.shape[1]), bias_ref[0, head], jnp.float32))
-    other = exact_parts(jnp.full((1, column.shape[1]), bias_ref[1, head], jnp.float32))
-    is_same = (column % VARIATES) == query_var
-    result = jnp.zeros(column.shape, jnp.float32)
-    for index in range(EXACT_PARTS):
-        here = (column // VARIATES) == index
-        result = jnp.where(here, jnp.where(is_same, same[index], other[index]), result)
+def note_keys(side_ref, kmeta_refs, column, lane, width, segments):
     seg_column = column - EXACT_PARTS * VARIATES
-    apart = (seg_column >= 0) & (seg_column < segments) & (seg_column != query_seg)
-    return jnp.where(apart, MASKED, result)
-
-
-def key_extension(key_var, key_seg, column, segments):
+    ones = (seg_column >= segments) & (seg_column < segments + EXACT_PARTS)
+    for block, kmeta_ref in enumerate(kmeta_refs):
+        one = (column < EXACT_PARTS * VARIATES) & ((column % VARIATES) == kmeta_ref[:, 0:1])
+        in_seg = (seg_column >= 0) & (seg_column < segments) & (seg_column == kmeta_ref[:, 1:2])
+        for head in range(2):
+            outside = (lane // width) != head
+            side_ref[head, block] = one_hot((one | in_seg | ones) & outside)
+
+
+def note_queries(match_ref, apart_ref, qmeta_ref, column, segments):
+    same = (column < EXACT_PARTS * VARIATES) & ((column % VARIATES) == qmeta_ref[:, 0:1])
+    match_ref[...] = jnp.where(same, 1.0, 0.0)
     seg_column = column - EXACT_PARTS * VARIATES
-    one = (column < EXACT_PARTS * VARIATES) & ((column % VARIATES) == key_var)
-    one = one | ((seg_column >= 0) & (seg_column < segments) & (seg_column == key_seg))
-    one = one | ((seg_column >= segments) & (seg_column < segments + EXACT_PARTS))
-    return jnp.where(one, 1.0, 0.0)
+    apart = (seg_column >= 0) & (seg_column < segments) & (seg_column != qmeta_ref[:, 1:2])
+    apart_ref[...] = jnp.where(apart, MASKED, 0.0)
+
+
+def bias_rows(bias_ref, head, column):
+    rows = []
+    for which in range(2):
+        row = jnp.zeros(column.shape, jnp.float32)
+        value = jnp.full(column.shape, bias_ref[which, head], jnp.float32)
+        for index, part in enumerate(exact_parts(value)):
+            row = jnp.where(column // VARIATES == index, part, row)
+        rows.append(row)
+    return rows
+
+
+def query_side(match_ref, apart_ref, bias_ref, head, column):
+    same, other = bias_rows(bias_ref, head, column[:1])
+    return jnp.where(match_ref[...] > 0.0, same, other) + apart_ref[...]
+
+
+def head_lanes(head, width, lanes):
+    lane = lax.broadcasted_iota(jnp.int32, (1, lanes), 1)
+    return jnp.where(lane // width == head, 1.0, 0.0).astype(jnp.bfloat16)
 
 
 def attend_kernel(key_blocks, segments, width, bias_ref, query_ref, qmeta_ref, *refs):
@@ -73,36 +92,31 @@
         refs[key_blocks : 2 * key_blocks],
         refs[2 * key_blocks : 3 * key_blocks],
     )
-    out_ref, total_ref = refs[3 * key_blocks :]
+    out_ref, total_ref, side_ref, match_ref, apart_ref = refs[3 * key_blocks :]
     pair = pl.program_id(0)
     rows, lanes = query_ref.shape
     lane = lax.broadcasted_iota(jnp.int32, (rows, lanes), 1)
     column = lane % width
+
+    @pl.when(pair == 0)
+    def _():
+        note_keys(side_ref, kmeta_refs, column, lane, width, segments)
+        note_queries(match_ref, apart_ref, qmeta_ref, column, segments)
+
     scaled = query_ref[...].astype(jnp.float32) * width ** (-0.5)
     results = []
     for head in range(lanes // width):
-        inside = (lane // width) == head
-        extension = query_extension(
-            bias_ref,
-            pair * (lanes // width) + head,
-            qmeta_ref[:, 0:1],
-            qmeta_ref[:, 1:2],
-            column,
-            segments,
-        )
-        left = jnp.where(inside, scaled, extension).astype(jnp.bfloat16)
+        extension = query_side(
+            match_ref, apart_ref, bias_ref, pair * (lanes // width) + head, column
+        )
+        left = jnp.where((lane // width) == head, scaled, extension).astype(jnp.bfloat16)
+        inside = head_lanes(head, width, lanes)
+        outside = head_lanes(1 - head, width, lanes)
         total = jnp.zeros((rows, lanes), jnp.float32)
         for block in range(key_blocks):
-            key_side = key_extension(
-                kmeta_refs[block][:, 0:1], kmeta_refs[block][:, 1:2], column, segments
-            )
-            right = jnp.where(inside, key_refs[block][...].astype(jnp.float32), key_side)
-            scores = contract_last(left, right.astype(jnp.bfloat16))
-            weights = jnp.exp(scores).astype(jnp.bfloat16)
-            values = jnp.where(inside, value_refs[block][...].astype(jnp.float32), 1.0)
-            total = total + jnp.dot(
-                weights, values.astype(jnp.bfloat16), preferred_element_type=jnp.float32
-            )
+            right = key_refs[block][...] * inside + side_ref[head, block]
+            weights = jnp.exp(contract_last(left, right)).astype(jnp.bfloat16)
+            total = total + dot(weights, value_refs[block][...] * inside + outside)
         results.append(total)
     first = (lane // width) == 0
     numerator = jnp.where(first, results[0], results[1])
@@ -111,8 +125,8 @@
     total_ref[...] = jnp.log(crossed)
 
 
-def lane_block(rows, lanes, first=0):
-    return pl.BlockSpec((rows, lanes), lambda pair: (0, pair + first))
+def lane_block(rows, lanes):
+    return pl.BlockSpec((rows, lanes), lambda pair: (0, pair))
 
 
 def whole_block(shape):
@@ -139,6 +153,11 @@
             jax.ShapeDtypeStruct((rows, features), jnp.bfloat16),
             jax.ShapeDtypeStruct((rows, features), jnp.float32),
         ],
+        scratch_shapes=[
+            pltpu.VMEM((2, count, rows, lanes), jnp.bfloat16),
+            pltpu.VMEM((rows, lanes), jnp.float32),
+            pltpu.VMEM((rows, lanes), jnp.float32),
+        ],
         compiler_params=pltpu.CompilerParams(vmem_limit_bytes=VMEM_LIMIT),
         cost_estimate=pl.CostEstimate(
             flops=flops, bytes_accessed=12 * rows * features, transcendentals=0
@@ -148,7 +167,6 @@
 
 
 def attend_back_kernel(
-    first_pair,
     key_blocks,
     segments,
     width,
@@ -165,62 +183,60 @@
         refs[key_blocks : 2 * key_blocks],
         refs[2 * key_blocks : 3 * key_blocks],
     )
-    results = refs[len(refs) - 1 - 2 * key_blocks :]
+    results = refs[len(refs) - 4 - 2 * key_blocks :]
     grad_query_ref = results[0]
     grad_key_refs = results[1 : key_blocks + 1]
-    grad_value_refs = results[key_blocks + 1 :]
-    pair = pl.program_id(0) + first_pair
+    grad_value_refs = results[key_blocks + 1 : 2 * key_blocks + 1]
+    side_ref, match_ref, apart_ref = results[2 * key_blocks + 1 :]
+    pair = pl.program_id(0)
     rows, lanes = query_ref.shape
     lane = lax.broadcasted_iota(jnp.int32, (rows, lanes), 1)
     column = lane % width
     ones_at = EXACT_PARTS * VARIATES + segments
+
+    @pl.when(pair == 0)
+    def _():
+        note_keys(side_ref, kmeta_refs, column, lane, width, segments)
+        note_queries(match_ref, apart_ref, qmeta_ref, column, segments)
+
     scaled = query_ref[...].astype(jnp.float32) * width ** (-0.5)
     scaled_low = scaled.astype(jnp.bfloat16)
     grad_low = grad_ref[...]
     grad = grad_low.astype(jnp.float32)
     overlap = grad * attended_ref[...].astype(jnp.float32)
-    total_parts = exact_parts(-total_ref[...])
+    square_row = lax.broadcasted_iota(jnp.int32, (lanes, lanes), 0)
+    square_column = lax.broadcasted_iota(jnp.int32, (lanes, lanes), 1)
+    across = one_hot(square_row // width != square_column // width)
+    high = overlap.astype(jnp.bfloat16)
+    rest = (overlap - high.astype(jnp.float32)).astype(jnp.bfloat16)
+    dot_side = parts_in_lanes(-(dot(high, across) + dot(rest, across)), ones_at, column)
+    total_side = parts_in_lanes(-total_ref[...], ones_at, column)
     grad_query_parts = []
     grad_keys = [[] for _ in range(key_blocks)]
     grad_values = [[] for _ in range(key_blocks)]
     for head in range(lanes // width):
         inside = (lane // width) == head
-        extension = query_extension(
-            bias_ref,
-            pair * (lanes // width) + head,
-            qmeta_ref[:, 0:1],
-            qmeta_ref[:, 1:2],
-            column,
-            segments,
-        ) + spread_parts(column, total_parts, ones_at)
+        extension = total_side + query_side(
+            match_ref, apart_ref, bias_ref, pair * (lanes // width) + head, column
+        )
         right = jnp.where(inside, scaled, extension).astype(jnp.bfloat16)
-        prob_dot = jnp.sum(jnp.where(inside, overlap, 0.0), axis=1, keepdims=True)
-        dot_side = spread_parts(column, exact_parts(-prob_dot), ones_at)
         grad_right = jnp.where(inside, grad, dot_side).astype(jnp.bfloat16)
+        own_lanes = head_lanes(head, width, lanes)
         turned = jnp.zeros((width, rows), jnp.float32)
         for block in range(key_blocks):
-            key_side = key_extension(
-                kmeta_refs[block][:, 0:1], kmeta_refs[block][:, 1:2], column, segments
-            )
             key = key_refs[block][...]
-            left = jnp.where(inside, key.astype(jnp.float32), key_side).astype(jnp.bfloat16)
-            prob = jnp.exp(contract_last(left, right))
-            value = value_refs[block][...].astype(jnp.float32)
-            value_left = jnp.where(inside, value, key_side).astype(jnp.bfloat16)
-            grad_score = prob * contract_last(value_left, grad_right)
-            grad_score = grad_score.astype(jnp.bfloat16)
-            grad_values[block].append(
-                jnp.dot(prob.astype(jnp.bfloat16), grad_low, preferred_element_type=jnp.float32)
-            )
-            grad_keys[block].append(
-                jnp.dot(grad_score, scaled_low, preferred_element_type=jnp.float32)
-            )
+            side = side_ref[head, block]
+            prob = jnp.exp(contract_last(key * own_lanes + side, right))
+            value_left = value_refs[block][...] * own_lanes + side
+            grad_score = (prob * contract_last(value_left, grad_right)).astype(jnp.bfloat16)
+            grad_values[block].append(dot(prob.astype(jnp.bfloat16), grad_low))
+            grad_keys[block].append(dot(grad_score, scaled_low))
             key_turned = jnp.transpose(key)[head * width : (head + 1) * width]
-            turned = turned + jnp.dot(key_turned, grad_score, preferred_element_type=jnp.float32)
+            turned = turned + dot(key_turned, grad_score)
         grad_query_parts.append(turned)
     first = (lane // width) == 0
     stacked = jnp.concatenate(grad_query_parts, axis=0) * width ** (-0.5)
-    grad_query_ref[...] = jnp.transpose(stacked)
+    grad_query_ref[...] = jnp.transpose(stacked).astype(jnp.bfloat16)
     for block in range(key_blocks):
         grad_key_refs[block][...] = jnp.where(first, *grad_keys[block]).astype(
             grad_key_refs[block].dtype
@@ -242,40 +258,33 @@
     key_metas,
     segments,
     width,
-    pairs,
-    before,
-    after,
 ):
     rows, features = query_low.shape
     lanes = 2 * width
     count = len(keys)
-    first, last = pairs
-    here = lane_block(rows, lanes, first)
-    anywhere = pl.BlockSpec(memory_space=pl.ANY)
-    operands = 6 + 3 * count
-    aliases = {operands + index: index for index in range(len(before))}
-    flops = 10 * rows * rows * count * lanes * (last - first)
-    full = jax.ShapeDtypeStruct((rows, features), jnp.float32)
+    here = lane_block(rows, lanes)
+    flops = 10 * rows * rows * count * features
     low = jax.ShapeDtypeStruct((rows, features), jnp.bfloat16)
     results = pl.pallas_call(
-        functools.partial(attend_back_kernel, first, count, segments, width),
-        grid=(last - first,),
+        functools.partial(attend_back_kernel, count, segments, width),
+        grid=(features // lanes,),
         in_specs=[
             pl.BlockSpec(memory_space=pltpu.SMEM),
             here,
             whole_block(query_meta.shape),
         ]
         + [here] * (3 + 2 * count)
-        + [whole_block(query_meta.shape)] * count
-        + [anywhere] * (len(before) + len(after)),
+        + [whole_block(query_meta.shape)] * count,
         out_specs=[here] * (1 + 2 * count),
-        input_output_aliases=aliases,
-        out_shape=[full] + ([full] + [low] * (count - 1)) * 2,
+        out_shape=[low] * (1 + 2 * count),
+        scratch_shapes=[
+            pltpu.VMEM((2, count, rows, lanes), jnp.bfloat16),
+            pltpu.VMEM((rows, lanes), jnp.float32),
+            pltpu.VMEM((rows, lanes), jnp.float32),
+        ],
         compiler_params=pltpu.CompilerParams(vmem_limit_bytes=VMEM_LIMIT),
         cost_estimate=pl.CostEstimate(
-            flops=flops,
-            bytes_accessed=24 * rows * lanes * (last - first),
-            transcendentals=0,
+            flops=flops, bytes_accessed=20 * rows * features, transcendentals=0
         ),
         name="attend_back",
     )(
@@ -288,8 +297,6 @@
         *keys,
         *values,
         *key_metas,
-        *before,
-        *after,
     )
     return results
 
@@ -474,35 +481,50 @@
     return results[0], results[1], results[2], results[3:]
 
 
-def pick_kernel(chosen_ref, *refs):
-    held_refs, out_ref = refs[:-1], refs[-1]
-    total = jnp.zeros(out_ref.shape, jnp.float32)
-    column = 0
-    for ref in held_refs:
-        rows = ref.shape[0]
-        total = total + dot(chosen_ref[:, column : column + rows], ref[...])
-        column += rows
-    out_ref[...] = total.astype(out_ref.dtype)
-
-
-def pick(chosen, first, count, held):
-    features = held[0].shape[1]
+def pick_kernel(counts, later_count, chosen_ref, *refs):
+    outs = refs[sum(counts) + later_count : sum(counts) + later_count + len(counts)]
+    refs = iter(refs[: sum(counts)])
+    for count, out_ref in zip(counts, outs):
+        total = jnp.zeros(out_ref.shape, jnp.float32)
+        column = 0
+        for _ in range(count):
+            ref = next(refs)
+            rows = ref.shape[0]
+            total = total + dot(chosen_ref[:, column : column + rows], ref[...])
+            column += rows
+        out_ref[...] = total.astype(out_ref.dtype)
+
+
+def pick(chosen, first, count, *helds, later=()):
+    features = helds[0][0].shape[1]
     tile = features // 2
+    parts = [part for held in helds for part in held]
     return pl.pallas_call(
-        pick_kernel,
+        functools.partial(pick_kernel, [len(held) for held in helds], len(later)),
         grid=(features // tile,),
         in_specs=[pl.BlockSpec((count, chosen.shape[1]), lambda step: (first // count, 0))]
-        + [pl.BlockSpec((part.shape[0], tile), lambda step: (0, step)) for part in held],
-        out_specs=pl.BlockSpec((count, tile), lambda step: (0, step)),
-        out_shape=jax.ShapeDtypeStruct((count, features), jnp.bfloat16),
+        + [pl.BlockSpec((part.shape[0], tile), lambda step: (0, step)) for part in parts]
+        + [pl.BlockSpec(memory_space=pl.ANY)] * len(later),
+        out_specs=[pl.BlockSpec((count, tile), lambda step: (0, step))] * len(helds)
+        + [pl.BlockSpec(memory_space=pl.ANY)] * len(later),
+        out_shape=[jax.ShapeDtypeStruct((count, features), jnp.bfloat16)] * len(helds)
+        + [jax.ShapeDtypeStruct(array.shape, array.dtype) for array in later],
+        input_output_aliases={1 + len(parts) + i: len(helds) + i for i in range(len(later))},
         compiler_params=pltpu.CompilerParams(vmem_limit_bytes=VMEM_LIMIT),
         cost_estimate=pl.CostEstimate(
-            flops=2 * count * chosen.shape[1] * features,
-            bytes_accessed=8 * count * features,
+            flops=2 * count * chosen.shape[1] * features * len(helds),
+            bytes_accessed=8 * count * features * len(helds),
             transcendentals=0,
         ),
         name="pick",
-    )(chosen, *held)
+    )(chosen, *parts, *later)
+
+
+def axis_count(names):
+    count = 1
+    for name in names:
+        count *= lax.axis_size(name)
+    return count
 
 
 def within_half(array, shift, groups):
@@ -512,7 +534,7 @@
         for base in (0, half)
         for place in range(half)
     ]
-    return lax.ppermute(array, "group", pairs)
+    return lax.ppermute(array, GROUP, pairs)
 
 
 def gather_half(array, groups):
@@ -521,7 +543,7 @@
 
 def to_other_half(array, groups):
     half = groups // 2
-    return lax.ppermute(array, "group", [(i, (i + half) % groups) for i in range(groups)])
+    return lax.ppermute(array, GROUP, [(i, (i + half) % groups) for i in range(groups)])
 
 
 def scatter_sum(array, axis_sizes):
@@ -543,6 +565,10 @@
 
 
 LANES = 128
+MOMENT_ROWS = 24
+PACKS = ("far", "near")
+GROUP = ("half", "core")
+ALL = PACKS + GROUP
 
 
 def adam(current, first_old, second_old, grad):
@@ -569,23 +595,24 @@
     for grad_a, grad_b in zip(wide, tall):
         pieces.append(lax.dot_general(grad_a, few_choice, (((1,), (1,)), ((), ()))).reshape(-1))
         pieces.append(jnp.dot(few_choice, grad_b).reshape(-1))
-    axis_sizes = [("dp", lax.axis_size("dp")), ("group", groups)]
+    axis_sizes = [(PACKS, axis_count(PACKS)), (GROUP, groups)]
     shards = axis_sizes[0][1] * groups
     flat_grads = jnp.concatenate(pieces).astype(jnp.bfloat16).reshape(shards, -1)
     grad_shard = scatter_sum(flat_grads, axis_sizes).reshape(-1).astype(jnp.float32)
     shard_count = grad_shard.shape[0]
-    shard_start = lax.axis_index(("dp", "group")) * shard_count
+    shard_start = lax.axis_index(ALL) * shard_count
     current = lax.dynamic_slice_in_dim(adapters, shard_start, shard_count).astype(jnp.float32)
     first_moment, second_moment, updated = adam(current, moment1, moment2, grad_shard)
-    adapters_new = lax.all_gather(updated, ("dp", "group"), axis=0, tiled=True)
+    adapters_new = lax.all_gather(updated, ALL, axis=0, tiled=True)
     return grad_shard, first_moment, second_moment, adapters_new
 
 
-def spreads_evenly(devices, features, hidden, total):
+def spreads_evenly(devices, groups, features, hidden, total):
     rows = total // LANES
     chunks = features // LANES
     return (
-        ADAPTERS * RANK == LANES
+        groups == 4
+        and ADAPTERS * RANK == LANES
         and devices * chunks == 256
         and chunks == 8
         and hidden == devices * LANES
@@ -599,7 +626,7 @@
     return jnp.where(condition, 1.0, 0.0).astype(jnp.bfloat16)
 
 
-def sum_wide(table_ref, arrived_ref, first, width):
+def sum_wide(adapter_row, arrived_ref, first, width):
     sources = arrived_ref.shape[0]
     rows = lax.broadcasted_iota(jnp.int32, (LANES, width * LANES), 0)
     columns = lax.broadcasted_iota(jnp.int32, (LANES, width * LANES), 1)
@@ -608,11 +635,12 @@
     adapter = jnp.where(fits, (columns % LANES) // RANK, -1)
     total = jnp.zeros((32, width * LANES), jnp.float32)
     for source in range(sources):
-        chosen = jnp.where(second, table_ref[source, 1], table_ref[source, 0])
-        total = total + jnp.dot(
-            arrived_ref[source, first : first + 32, :],
-            one_hot(adapter == chosen),
-            preferred_element_type=jnp.float32,
+        at = source * 2 * RANK
+        chosen = jnp.where(
+            second, adapter_row[:, at + RANK : at + RANK + 1], adapter_row[:, at : at + 1]
+        )
+        total = total + dot(
+            arrived_ref[source, first : first + 32, :], one_hot(adapter == chosen)
         )
     return total
 
@@ -641,69 +669,146 @@
     return jnp.dot(choice, held, preferred_element_type=jnp.float32)
 
 
-def settle_kernel(
-    early, table_ref, tall_ref, square_ref, arrived_ref, param_ref, m1_ref, m2_ref, *refs
-):
-    grad_ref, new_ref = refs[-2:]
-    if early:
-        wide = sum_wide(table_ref, arrived_ref, 0, 3)
-        last = sum_wide(table_ref, arrived_ref, 32, 4)
-        square = sum_square(square_ref[...], arrived_ref, 128)
-        parts = [
-            wide[:, 2 * LANES :],
-            square[32:],
-            wide[:, :LANES],
-            sum_tall(tall_ref[...], arrived_ref, 64),
-            wide[:, LANES : 2 * LANES],
-            sum_tall(tall_ref[...], arrived_ref, 96),
-        ]
-        parts += [last[:, i * LANES : (i + 1) * LANES] for i in range(4)]
-        parts.append(square[:32])
-    else:
-        wide = sum_wide(table_ref, arrived_ref, 0, 3)
-        square = [sum_square(square_ref[...], arrived_ref, first) for first in (32, 48)]
-        parts = []
-        for index in range(3):
-            parts.append(wide[:, index * LANES : (index + 1) * LANES])
-            parts.append(square[index // 2][(index % 2) * 32 : (index % 2) * 32 + 32])
+def settle_rows(parts, skip, param_ref, m1_ref, m2_ref, m_skip, grad_ref, new_refs):
     row = 0
-    skip = param_ref.shape[0] - grad_ref.shape[0] if early else 0
     for part in parts:
         here = slice(row, row + part.shape[0])
         there = slice(skip + row, skip + row + part.shape[0])
+        at = slice(m_skip + row, m_skip + row + part.shape[0])
         row += part.shape[0]
         low = part.astype(jnp.bfloat16)
         grad_ref[here, :] = low
         new = adam(
             param_ref[there, :].astype(jnp.float32),
-            m1_ref[there, :],
-            m2_ref[there, :],
+            m1_ref[at, :],
+            m2_ref[at, :],
             low.astype(jnp.float32),
         )[2]
-        for copy in range(new_ref.shape[0]):
-            new_ref[copy, here, :] = new
-
-
-def settle(early, rows, table, arrived, params, first_old, second_old, after):
-    sources = table.shape[0]
-    tall_row = jnp.repeat(table.reshape(-1), RANK)[None, :]
-    square_row = jnp.repeat(jnp.tile(table, (1, 2)).reshape(-1), 4)[None, :]
+        for new_ref in new_refs:
+            new_ref[here, :] = new
+
+
+def settle_early_kernel(own_rows, arrived_ref, moments_ref, param_ref, *refs):
+    grad_ref, new_ref, late_m1_ref, late_m2_ref, tall_ref, square_ref, m1_ref, m2_ref = refs[-8:]
+    sources = arrived_ref.shape[0]
+    told = 6 * RANK
+    tall_column = lax.broadcasted_iota(jnp.int32, tall_ref.shape, 1)
+    square_column = lax.broadcasted_iota(jnp.int32, square_ref.shape, 1)
+    tall = jnp.zeros(tall_ref.shape, jnp.float32)
+    square = jnp.zeros(square_ref.shape, jnp.float32)
+    for source in range(sources):
+        row = arrived_ref[source, 0:16, :].astype(jnp.float32)
+        first, second = row[0:1, told : told + 1], row[0:1, told + 1 : told + 2]
+        tall = jnp.where(
+            tall_column // (2 * RANK) == source,
+            jnp.where((tall_column // RANK) % 2 == 1, second, first),
+            tall,
+        )
+        square = jnp.where(
+            square_column // RANK == source,
+            jnp.where((square_column // 4) % 2 == 1, second, first),
+            square,
+        )
+        held = moments_ref[source].astype(jnp.float32)
+        here = slice(source * own_rows, (source + 1) * own_rows)
+        m1_ref[here, :] = held[:own_rows]
+        m2_ref[here, :] = held[MOMENT_ROWS : MOMENT_ROWS + own_rows]
+    tall = tall.astype(jnp.int32)
+    square = square.astype(jnp.int32)
+    tall_ref[...] = tall
+    square_ref[...] = square
+    late = late_m1_ref.shape[0]
+    late_m1_ref[...] = m1_ref[:late, :]
+    late_m2_ref[...] = m2_ref[:late, :]
+    wide = sum_wide(tall, arrived_ref, 0, 3)
+    last = sum_wide(tall, arrived_ref, 32, 4)
+    pair = sum_square(square, arrived_ref, 128)
+    parts = [
+        wide[:, 2 * LANES :],
+        pair[32:],
+        wide[:, :LANES],
+        sum_tall(tall, arrived_ref, 64),
+        wide[:, LANES : 2 * LANES],
+        sum_tall(tall, arrived_ref, 96),
+    ]
+    parts += [last[:, i * LANES : (i + 1) * LANES] for i in range(4)]
+    parts.append(pair[:32])
+    copies = [new_ref.at[copy] for copy in range(new_ref.shape[0])]
+    settle_rows(parts, late, param_ref, m1_ref, m2_ref, late, grad_ref, copies)
+
+
+def settle_early(arrived, moments, params, late_rows, after):
+    sources = arrived.shape[0]
+    rows = params.shape[0] - late_rows
+    vmem = pl.BlockSpec(memory_space=pltpu.VMEM)
+    low = jax.ShapeDtypeStruct((rows, LANES), jnp.bfloat16)
+    late = jax.ShapeDtypeStruct((late_rows, LANES), jnp.float32)
     return pl.pallas_call(
-        functools.partial(settle_kernel, early),
-        in_specs=[pl.BlockSpec(memory_space=pltpu.SMEM)]
-        + [pl.BlockSpec(memory_space=pltpu.VMEM)] * 6
-        + [pl.BlockSpec(memory_space=pl.ANY)] * len(after),
-        out_specs=[pl.BlockSpec(memory_space=pltpu.VMEM)] * 2,
+        functools.partial(settle_early_kernel, params.shape[0] // sources),
+        in_specs=[vmem, vmem, vmem] + [pl.BlockSpec(memory_space=pl.ANY)] * len(after),
+        out_specs=[vmem] * 6,
         out_shape=[
-            jax.ShapeDtypeStruct((rows, LANES), jnp.bfloat16),
-            jax.ShapeDtypeStruct((lax.axis_size("dp"), rows, LANES), jnp.bfloat16),
+            low,
+            jax.ShapeDtypeStruct((lax.axis_size("far"), rows, LANES), jnp.bfloat16),
+            late,
+            late,
+            jax.ShapeDtypeStruct((1, sources * 2 * RANK), jnp.int32),
+            jax.ShapeDtypeStruct((1, sources * RANK), jnp.int32),
         ],
+        scratch_shapes=[pltpu.VMEM(params.shape, jnp.float32)] * 2,
         compiler_params=pltpu.CompilerParams(vmem_limit_bytes=VMEM_LIMIT),
         cost_estimate=pl.CostEstimate(
             flops=sources * 2**24, bytes_accessed=4 * arrived.size, transcendentals=0
         ),
-        name="settle_early" if early else "settle_late",
-    )(table, tall_row, square_row, arrived, params, first_old, second_old, *after)
+        name="settle_early",
+    )(arrived, moments, params, *after)
+
+
+def settle_late_kernel(
+    tall_ref, square_ref, arrived_ref, param_ref, m1_ref, m2_ref, *refs
+):
+    early_grad_ref = refs[0]
+    own_ref, new_ref, _, grad_ref = refs[-4:]
+    wide = sum_wide(tall_ref[...], arrived_ref, 0, 3)
+    pairs = [sum_square(square_ref[...], arrived_ref, first) for first in (32, 48)]
+    parts = []
+    for index in range(3):
+        parts.append(wide[:, index * LANES : (index + 1) * LANES])
+        parts.append(pairs[index // 2][(index % 2) * 32 : (index % 2) * 32 + 32])
+    copies = [new_ref.at[copy] for copy in range(new_ref.shape[0])]
+    settle_rows(parts, 0, param_ref, m1_ref, m2_ref, 0, grad_ref, copies)
+    low = jnp.concatenate(
+        [ref[...].astype(jnp.float32) for ref in (grad_ref, early_grad_ref)], axis=0
+    )
+    each = low.shape[0] // own_ref.shape[0]
+    zeros = jnp.zeros((own_ref.shape[1] - each, LANES), jnp.float32)
+    for owner in range(own_ref.shape[0]):
+        own_ref[owner] = jnp.concatenate(
+            [low[owner * each : (owner + 1) * each], zeros], axis=0
+        ).astype(jnp.bfloat16)
+
+
+def settle_late(tall, square, arrived, params, late_m1, late_m2, early_grad, later, after):
+    rows = late_m1.shape[0]
+    anywhere = pl.BlockSpec(memory_space=pl.ANY)
+    vmem = pl.BlockSpec(memory_space=pltpu.VMEM)
+    return pl.pallas_call(
+        settle_late_kernel,
+        in_specs=[vmem] * 7 + [anywhere] * (1 + len(after)),
+        out_specs=[vmem, vmem, anywhere],
+        scratch_shapes=[pltpu.VMEM((rows, LANES), jnp.bfloat16)],
+        input_output_aliases={7: 2},
+        out_shape=[
+            jax.ShapeDtypeStruct((arrived.shape[0], MOMENT_ROWS, LANES), jnp.bfloat16),
+            jax.ShapeDtypeStruct((axis_count(PACKS), rows, LANES), jnp.bfloat16),
+            jax.ShapeDtypeStruct(later.shape, later.dtype),
+        ],
+        compiler_params=pltpu.CompilerParams(vmem_limit_bytes=VMEM_LIMIT),
+        cost_estimate=pl.CostEstimate(
+            flops=arrived.shape[0] * 2**24, bytes_accessed=4 * arrived.size, transcendentals=0
+        ),
+        name="settle_late",
+    )(tall, square, arrived, params, late_m1, late_m2, early_grad, later, *after)
 
 
 def gather_inner(piece, groups):
@@ -711,13 +816,21 @@
     bit = groups // 2
     while bit:
         pairs = [(i, i ^ bit) for i in range(groups)]
-        pieces = pieces + [lax.ppermute(piece, "group", pairs) for piece in pieces]
+        pieces = pieces + [lax.ppermute(piece, GROUP, pairs) for piece in pieces]
         bit //= 2
     return pieces
 
 
-def placing_order(groups, devices, unit):
-    member = lax.axis_index("group")
+def placing_order(device, unit):
+    size = unit * device.shape[0]
+    to_row = lax.broadcasted_iota(jnp.int32, (size, size), 0)
+    from_row = jnp.arange(size, dtype=jnp.int32)
+    source = (from_row % unit) * device.shape[0] + jnp.repeat(device, unit)
+    return (to_row == source[None, :]).astype(jnp.bfloat16)
+
+
+def piece_devices(groups, devices):
+    member = lax.axis_index(GROUP)
     piece = jnp.arange(groups, dtype=jnp.int32)
     mask = jnp.zeros_like(piece)
     bit = 1
@@ -725,50 +838,71 @@
         mask = mask * 2 + (piece // bit) % 2
         bit *= 2
     outer = jnp.arange(devices // groups, dtype=jnp.int32)
-    device = (outer[None, :] * groups + (member ^ mask)[:, None]).reshape(-1)
-    size = unit * devices
-    to_row = lax.broadcasted_iota(jnp.int32, (size, size), 0)
-    from_row = jnp.arange(size, dtype=jnp.int32)
-    source = (from_row % unit) * devices + jnp.repeat(device, unit)
-    return (to_row == source[None, :]).astype(jnp.bfloat16)
-
-
-def assemble_kernel(count, block, order_ref, *refs):
-    piece_refs, out_ref = refs[:count], refs[-1]
-    outer = piece_refs[0].shape[0]
-    devices = count * outer
+    return (outer[None, :] * groups + (member ^ mask)[:, None]).reshape(-1)
+
+
+def assemble_kernel(counts, devices, chunks, first, order_ref, *refs):
+    piece_refs = []
+    for count in counts:
+        piece_refs.append(refs[:count])
+        refs = refs[count:]
+    out_any, placed_ref, sems = refs[-3:]
+
+    def held_rows(part_refs, start, stop):
+        before = 0
+        for ref in part_refs:
+            if start < before + ref.shape[1]:
+                return ref[:, start - before : stop - before, :]
+            before += ref.shape[1]
+
     unit = order_ref.shape[0] // devices
-    first = pl.program_id(0) * block
-    for start in range(0, block, 2 * unit):
-        sides = []
-        for side in (start, start + unit):
-            here = pl.ds(pl.multiple_of(first + side, unit), unit)
-            held = jnp.concatenate([ref[:, here, :] for ref in piece_refs], axis=0)
-            sides.append(held.reshape(unit * devices, LANES))
-        placed = dot(order_ref[...], jnp.concatenate(sides, axis=1)).astype(jnp.bfloat16)
-        for index, side in enumerate((start, start + unit)):
-            out_ref[side * devices : (side + unit) * devices, :] = placed[
-                :, index * LANES : (index + 1) * LANES
-            ]
-
-
-def assemble(order, pieces, total_rows, first, block, before):
-    devices = len(pieces) * pieces[0].shape[0]
-    rows = pieces[0].shape[1]
-    in_specs = [whole_block(order.shape)] + [whole_block(piece.shape) for piece in pieces]
-    operands = [order, *pieces]
+    copies = []
+    for index, (begin, end) in enumerate(chunks):
+        for start in range(begin, end, 2 * unit):
+            sides = []
+            for side in (start, start + unit):
+                held = jnp.concatenate(
+                    [held_rows(part_refs, side, side + unit) for part_refs in piece_refs], axis=0
+                )
+                sides.append(held.reshape(unit * devices, LANES))
+            placed = dot(order_ref[...], jnp.concatenate(sides, axis=1)).astype(jnp.bfloat16)
+            for half, side in enumerate((start, start + unit)):
+                placed_ref[side * devices : (side + unit) * devices, :] = placed[
+                    :, half * LANES : (half + 1) * LANES
+                ]
+        here = slice(begin * devices, end * devices)
+        there = slice((first + begin) * devices, (first + end) * devices)
+        copies.append(
+            pltpu.make_async_copy(placed_ref.at[here, :], out_any.at[there, :], sems.at[index])
+        )
+        copies[-1].start()
+    for copy in copies:
+        copy.wait()
+
+
+def assemble(order, pieces, total_rows, first, before, after):
+    devices = len(pieces) * pieces[0][0].shape[0]
+    rows = pieces[0][0].shape[1]
+    parts = [part for piece in pieces for part in piece]
+    step = 32 * max(1, rows // 128)
+    chunks = [(begin, min(begin + step, rows)) for begin in range(0, rows, step)]
+    vmem, anywhere = pl.BlockSpec(memory_space=pltpu.VMEM), pl.BlockSpec(memory_space=pl.ANY)
+    in_specs = [vmem] * (1 + len(parts)) + [anywhere] * len(after)
+    operands = [order, *parts, *after]
     aliases = {}
     if before is not None:
         aliases = {len(operands): 0}
-        in_specs.append(pl.BlockSpec(memory_space=pl.ANY))
+        in_specs.append(anywhere)
         operands.append(before)
-    skip = first // block
     return pl.pallas_call(
-        functools.partial(assemble_kernel, len(pieces), block),
-        grid=(rows // block,),
+        functools.partial(assemble_kernel, [len(piece) for piece in pieces], devices, chunks, first),
         in_specs=in_specs,
-        out_specs=pl.BlockSpec((block * devices, LANES), lambda step: (step + skip, 0)),
+        out_specs=anywhere,
         out_shape=jax.ShapeDtypeStruct((total_rows, LANES), jnp.bfloat16),
+        scratch_shapes=[
+            pltpu.VMEM((rows * devices, LANES), jnp.bfloat16),
+            pltpu.SemaphoreType.DMA((len(chunks),)),
+        ],
         input_output_aliases=aliases,
         compiler_params=pltpu.CompilerParams(vmem_limit_bytes=VMEM_LIMIT),
         cost_estimate=pl.CostEstimate(
@@ -791,8 +925,26 @@
     return jnp.tile(gain.astype(jnp.float32), LANES // gain.shape[0])[None, :]
 
 
-def select_kernel(features, hidden, turn_ref, flat_ref, *out_refs):
-    a_qkv_ref, a_guo_ref, a_down_ref, b_qkv_ref, b_gu_ref, b_do_ref = out_refs
+def select_kernel(features, hidden, devices, turn_ref, me_ref, flat_ref, *refs):
+    m1_ref, m2_ref = refs[:2]
+    out_refs = refs[3:]
+    a_qkv_ref, a_guo_ref, a_down_ref, b_qkv_ref, b_gu_ref, b_do_ref = out_refs[:6]
+    if devices:
+        own_ref, moments_ref, wide_ref = out_refs[6:]
+        count = m1_ref.shape[0] // devices
+        for device in range(devices):
+            rows = []
+            for ref in (m1_ref, m2_ref):
+                rows.append(ref[pl.ds(device, count, stride=devices), :])
+                rows.append(jnp.zeros((MOMENT_ROWS - count, LANES), jnp.float32))
+            moments_ref[device] = jnp.concatenate(rows, axis=0).astype(jnp.bfloat16)
+        size = wide_ref.shape[0]
+        each = size // devices
+        for chunk in range(flat_ref.shape[0] // size):
+            wide_ref[...] = flat_ref[chunk * size : (chunk + 1) * size, :].astype(jnp.float32)
+            own_ref[chunk * each : (chunk + 1) * each, :] = wide_ref[
+                pl.ds(me_ref[0], each, stride=devices), :
+            ].astype(jnp.bfloat16)
     few = 2 * RANK
     rows = lax.broadcasted_iota(jnp.int32, (LANES, LANES), 0)
     columns = lax.broadcasted_iota(jnp.int32, (LANES, LANES), 1)
@@ -858,23 +1010,33 @@
                 tall(name, out_ref.shape[1], out_ref, place)
 
 
-def select(turn_adapter, adapters, features, hidden):
+def select(devices, turn_adapter, me, adapters, moments, features, hidden, after):
     shapes = [(features, LANES), (features, LANES), (hidden, LANES)]
     shapes += [(LANES, features), (LANES, hidden), (LANES, features)]
+    scratch = []
+    if devices:
+        shapes.append((adapters.shape[0] // (LANES * devices), LANES))
+        shapes.append((devices, 2 * MOMENT_ROWS, LANES))
+        scratch.append(pltpu.VMEM((1024, LANES), jnp.float32))
     return pl.pallas_call(
-        functools.partial(select_kernel, features, hidden),
+        functools.partial(select_kernel, features, hidden, devices),
         in_specs=[
             pl.BlockSpec(memory_space=pltpu.SMEM),
+            pl.BlockSpec(memory_space=pltpu.SMEM),
             pl.BlockSpec(memory_space=pltpu.VMEM),
+            pl.BlockSpec(memory_space=pltpu.VMEM),
+            pl.BlockSpec(memory_space=pltpu.VMEM),
+            pl.BlockSpec(memory_space=pl.ANY),
         ],
-        out_specs=[pl.BlockSpec(memory_space=pltpu.VMEM)] * 6,
+        out_specs=[pl.BlockSpec(memory_space=pltpu.VMEM)] * len(shapes),
         out_shape=[jax.ShapeDtypeStruct(shape, jnp.bfloat16) for shape in shapes],
+        scratch_shapes=scratch,
         compiler_params=pltpu.CompilerParams(vmem_limit_bytes=VMEM_LIMIT),
         cost_estimate=pl.CostEstimate(
             flops=2**31, bytes_accessed=4 * adapters.shape[0], transcendentals=0
         ),
         name="select",
-    )(turn_adapter, adapters.reshape(-1, LANES))
+    )(turn_adapter, me, adapters.reshape(-1, LANES), *moments, after)
 
 
 def dot(left, right):
@@ -951,12 +1113,14 @@
     cos_ref,
     sin_ref,
     k_gain_ref,
+    _,
     x_ref,
     normed_ref,
     inner_ref,
     raw_ref,
     k_ref,
     v_ref,
+    __,
 ):
     mask, place = turn_mask(meta_ref)
 
@@ -976,7 +1140,7 @@
     lanes = wk_ref.shape[1]
     cosine, sine = widen(cos_ref[...], lanes), widen(sin_ref[...], lanes)
     key = project_own(normed, inner, place, 1, wk_ref, b_ref)
-    raw_ref[...] = key
+    raw_ref[...] = key.astype(jnp.bfloat16)
     k_ref[...] = turned_heads(key, k_gain_ref, cosine, sine, width)
     v_ref[...] = project_own(normed, inner, place, 2, wv_ref, b_ref).astype(jnp.bfloat16)
 
@@ -989,12 +1153,24 @@
     cosine, sine = widen(cos_ref[...], lanes), widen(sin_ref[...], lanes)
     inner = inner_ref[...].astype(jnp.float32)
     query = project_own(normed_ref[...], inner, place, 0, wq_ref, b_ref)
-    raw_ref[...] = query
+    raw_ref[...] = query.astype(jnp.bfloat16)
     q_ref[...] = turned_heads(query, q_gain_ref, cosine, sine, width)
 
 
 def project_heads(
-    kept, arrived, gain, weights, a_qkv, b_qkv, meta, cos_table, sin_table, q_gain, k_gain, width
+    kept,
+    arrived,
+    later,
+    gain,
+    weights,
+    a_qkv,
+    b_qkv,
+    meta,
+    cos_table,
+    sin_table,
+    q_gain,
+    k_gain,
+    width,
 ):
     rows, features = kept.shape
     tile = 256
@@ -1007,22 +1183,25 @@
         return jax.ShapeDtypeStruct((rows, features), dtype)
 
     full, few = whole_block((rows, features)), whole_block((rows, LANES))
-    low, high = shape(jnp.bfloat16), shape(jnp.float32)
-    x, normed, inner, key_raw, key, value = pl.pallas_call(
+    low = shape(jnp.bfloat16)
+    anywhere = pl.BlockSpec(memory_space=pl.ANY)
+    x, normed, inner, key_raw, key, value, later = pl.pallas_call(
         functools.partial(project_key_value_kernel, width),
         grid=grid,
         in_specs=[full, whole_block(arrived.shape), whole_block((1, features))]
         + [tiled(features)] * 2
         + [whole_block((features, LANES)), tiled(LANES), few, few, few]
-        + [whole_block((1, LANES))],
-        out_specs=[full, full, few] + [tiled(rows)] * 3,
+        + [whole_block((1, LANES)), anywhere],
+        out_specs=[full, full, few] + [tiled(rows)] * 3 + [anywhere],
+        input_output_aliases={11: 6},
         out_shape=[
             low,
             low,
             jax.ShapeDtypeStruct((rows, LANES), jnp.bfloat16),
-            high,
             low,
             low,
+            low,
+            jax.ShapeDtypeStruct(later.shape, later.dtype),
         ],
         compiler_params=pltpu.CompilerParams(vmem_limit_bytes=VMEM_LIMIT),
         cost_estimate=pl.CostEstimate(
@@ -1042,13 +1221,14 @@
         cos_table,
         sin_table,
         k_gain,
+        later,
     )
     query_raw, query = pl.pallas_call(
         functools.partial(project_query_kernel, width),
         grid=grid,
         in_specs=[full, few, tiled(features), tiled(LANES), few, few, whole_block((1, LANES))],
         out_specs=[tiled(rows)] * 2,
-        out_shape=[high, low],
+        out_shape=[low, low],
         compiler_params=pltpu.CompilerParams(vmem_limit_bytes=VMEM_LIMIT),
         cost_estimate=pl.CostEstimate(
             flops=3 * rows * features * features,
@@ -1057,7 +1237,7 @@
         ),
         name="project_query",
     )(normed, inner, weights[0], b_qkv, cos_table, sin_table, q_gain)
-    return x, normed, inner, query_raw, key_raw, query, key, value
+    return x, normed, inner, query_raw, key_raw, query, key, value, later
 
 
 def project_heads_back_kernel(
@@ -1071,10 +1251,10 @@
     (
         q_raw_ref,
         k_raw_ref,
-        normed_ref,
+        normed_any,
         inner_ref,
-        x_ref,
-        residual_ref,
+        x_any,
+        residual_any,
         gain_ref,
         wq_ref,
         wk_ref,
@@ -1088,15 +1268,17 @@
         k_gain_ref,
     ) = refs[:17]
     if devices:
-        _, out_ref, spread_ref, total_ref, few_ref, tall_ref, square_ref = refs[17:]
+        out_ref, tail_ref, spread_ref = refs[-9:-6]
     else:
-        out_ref, grad_a_ref, grad_b_ref, total_ref, few_ref, tall_ref, square_ref = refs[17:]
+        out_ref, tail_ref, grad_a_ref, grad_b_ref = refs[-10:-6]
+    total_ref, few_ref, tall_ref, square_ref, held_ref, sems = refs[-6:]
     step = pl.program_id(0)
     lanes = wq_ref.shape[1]
     mask, place = turn_mask(meta_ref)
     cosine, sine = widen(cos_ref[...], lanes), widen(sin_ref[...], lanes)
 
     def turned_back(grad, raw, head_gain_ref):
+        raw = raw.astype(jnp.float32)
         grad = grad * cosine - swap_halves(grad, width) * sine
         scale = lax.rsqrt(head_mean(raw * raw, width) + NORM_EPS)
         unit = raw * scale
@@ -1109,8 +1291,15 @@
             total = total + ref[...].astype(jnp.float32)
         return total
 
+    copies = [
+        pltpu.make_async_copy(source, held_ref.at[index], sems.at[index])
+        for index, source in enumerate((normed_any, x_any, residual_any))
+    ]
+
     @pl.when(step == 0)
     def _():
+        for copy in copies:
+            copy.start()
         total_ref[...] = jnp.zeros(total_ref.shape, jnp.float32)
         few_ref[...] = jnp.zeros(few_ref.shape, jnp.float32)
 
@@ -1118,7 +1307,7 @@
         jnp.bfloat16
     )
     errors = [
-        turned_back(gq_ref[...], q_raw_ref[...], q_gain_ref),
+        turned_back(gq_ref[...].astype(jnp.float32), q_raw_ref[...], q_gain_ref),
         turned_back(summed(gk_refs), k_raw_ref[...], k_gain_ref),
         summed(gv_refs).astype(jnp.bfloat16),
     ]
@@ -1136,7 +1325,7 @@
         (lanes // LANES, LANES - 3 * wide, LANES), jnp.float32
     )
     if devices:
-        chunks = normed_ref.shape[1] // LANES
+        chunks = held_ref.shape[2] // LANES
         for index in range(lanes // LANES):
             for first, starts in ((wide, (0, wide)), (wide + RANK, (2 * wide, 3 * wide))):
                 spread_square_to(
@@ -1160,18 +1349,19 @@
     def _():
         low = (ADAPTER_SCALE * few_ref[...] * mask).astype(jnp.bfloat16)
         low_turned = jnp.transpose(low.astype(jnp.float32)).astype(jnp.bfloat16)
-        tall_ref[...] = jnp.transpose(dot(low_turned, normed_ref[...]))
+        for copy in copies:
+            copy.wait()
+        tall_ref[...] = jnp.transpose(dot(low_turned, held_ref[0]))
         if devices:
             spread_wide_to(spread_ref, 0, tall_ref)
         else:
             grad_a_ref[...] = tall_ref[...].astype(jnp.bfloat16)
         grad = total_ref[...] + contract_last(low, a_ref[...])
-        out_ref[...] = (
-            residual_ref[...]
-            + row_norm_back(
-                x_ref[...].astype(jnp.float32), gain_ref[...].astype(jnp.float32), grad
-            )
-        ).astype(jnp.bfloat16)
+        out = held_ref[2].astype(jnp.float32) + row_norm_back(
+            held_ref[1].astype(jnp.float32), gain_ref[...].astype(jnp.float32), grad
+        )
+        out_ref[...] = out.astype(jnp.bfloat16)
+        tail_ref[...] = out[out.shape[0] - tail_ref.shape[0] :].astype(jnp.bfloat16)
 
 
 def project_heads_back(
@@ -1205,6 +1395,7 @@
         return pl.BlockSpec((height, tile), lambda step: (0, step))
 
     full = whole_block((rows, features))
+    anywhere = pl.BlockSpec(memory_space=pl.ANY)
     if devices:
         spread = (devices, 4 * RANK, LANES)
         grad_specs = [whole_block(spread)]
@@ -1219,19 +1410,25 @@
         functools.partial(project_heads_back_kernel, count, width, devices),
         grid=(features // tile,),
         in_specs=[tiled(rows)] * (3 + 2 * count)
-        + [full, whole_block((rows, LANES)), full, full, whole_block((1, features))]
+        + [anywhere, whole_block((rows, LANES)), anywhere, anywhere, whole_block((1, features))]
         + [tiled(features)] * 3
         + [whole_block((features, LANES)), tiled(LANES), whole_block(meta.shape)]
         + [whole_block((rows, LANES))] * 2
         + [whole_block((1, LANES))] * 2
-        + [pl.BlockSpec(memory_space=pl.ANY)] * len(after),
-        out_specs=[full, *grad_specs],
-        out_shape=[jax.ShapeDtypeStruct((rows, features), jnp.bfloat16), *grad_shapes],
+        + [anywhere] * len(after),
+        out_specs=[full, whole_block((rows // 2, features)), *grad_specs],
+        out_shape=[
+            jax.ShapeDtypeStruct((rows, features), jnp.bfloat16),
+            jax.ShapeDtypeStruct((rows // 2, features), jnp.bfloat16),
+            *grad_shapes,
+        ],
         scratch_shapes=[
             pltpu.VMEM((rows, features), jnp.float32),
             pltpu.VMEM((rows, LANES), jnp.float32),
             pltpu.VMEM((features, LANES), jnp.float32),
             pltpu.VMEM((tile // LANES, LANES, LANES), jnp.float32),
+            pltpu.VMEM((3, rows, features), jnp.bfloat16),
+            pltpu.SemaphoreType.DMA((3,)),
         ],
         compiler_params=pltpu.CompilerParams(vmem_limit_bytes=VMEM_LIMIT),
         cost_estimate=pl.CostEstimate(
@@ -1303,6 +1500,7 @@
     b_do_ref,
     meta_ref,
     out_ref,
+    tail_ref,
     grad_res_ref,
     grad_att_ref,
     *refs,
@@ -1408,16 +1606,18 @@
         grads_out = e_ref[...]
         inner_down = only(inner_down_ref[...] * mask, 0)
         res = res_ref[...]
-        out_ref[...] = (
-            res + sum_ref[...] + ADAPTER_SCALE * dot(inner_down, b_do_ref[...])
-        ).astype(jnp.bfloat16)
+        out = (res + sum_ref[...] + ADAPTER_SCALE * dot(inner_down, b_do_ref[...])).astype(
+            jnp.bfloat16
+        )
+        out_ref[...] = out
+        tail_ref[...] = out[out.shape[0] - tail_ref.shape[0] :]
         few = jnp.where(place < 2, ADAPTER_SCALE * few_ref[...] * mask, 0.0).astype(jnp.bfloat16)
         grad_hidden = grad_hidden_ref[...] + contract_last(few, a_guo_ref[...])
         grad_res = grads_out.astype(jnp.float32) + row_norm_back(
             res, gain_ref[...].astype(jnp.float32), grad_hidden
         )
-        grad_res_ref[...] = grad_res
         low = grad_res.astype(jnp.bfloat16)
+        grad_res_ref[...] = low
         few_out = only(ADAPTER_SCALE * contract_last(low, b_do_ref[...]) * mask, 2)
         grad_att_ref[...] = (
             contract_last(low, wo_ref[...]) + contract_last(few_out, a_guo_ref[...])
@@ -1449,7 +1649,16 @@
 
 
 def feed_forward(
-    devices, turn_adapter, attended, rows_in, kept, arrived, gain, weights, selected, meta
+    devices,
+    turn_adapter,
+    attended,
+    rows_in,
+    kept,
+    arrived,
+    gain,
+    weights,
+    selected,
+    meta,
 ):
     rows, features = rows_in.shape
     hidden = weights[1].shape[1]
@@ -1500,13 +1709,15 @@
         ],
         out_specs=[
             full,
+            whole_block(arrived.shape),
             full,
             full,
             *grad_specs,
         ],
         out_shape=[
             shape(rows, features, jnp.bfloat16),
-            shape(rows, features, jnp.float32),
+            shape(*arrived.shape, jnp.bfloat16),
+            shape(rows, features, jnp.bfloat16),
             shape(rows, features, jnp.bfloat16),
             *grad_shapes,
         ],
@@ -1534,35 +1745,21 @@
         ),
         name="feed_forward",
     )(
-        turn_adapter, attended, rows_in, kept, arrived, gain[None, :], *weights, *selected, meta
-    )
-
-
-def spread_state(adapters, moment1, moment2, devices):
-    axes = ("dp", "group")
-    total_rows = adapters.shape[0] // LANES
-    spread_rows = total_rows // devices
-    own_rows = spread_rows // devices
-    moments = jnp.concatenate(
-        [
-            jnp.transpose(flat.reshape(own_rows, devices, LANES), (1, 0, 2))
-            for flat in (moment1, moment2)
-        ],
-        axis=1,
-    )
-    moments = lax.all_to_all(moments, axes, 0, 0, tiled=True)
-    first_old = moments[:, :own_rows].reshape(spread_rows, LANES)
-    second_old = moments[:, own_rows:].reshape(spread_rows, LANES)
-    params = lax.dynamic_index_in_dim(
-        adapters.reshape(spread_rows, devices, LANES), lax.axis_index(axes), 1, keepdims=False
-    )
-    return params, first_old, second_old
-
-
-def settle_owned(late_grad, early_grad, moment1, moment2, devices):
-    grads = jnp.concatenate([late_grad, early_grad])
-    grads = grads.reshape(devices, grads.shape[0] // devices, LANES)
-    grads = lax.all_to_all(grads, ("dp", "group"), 0, 0, tiled=True)
+        turn_adapter,
+        attended,
+        rows_in,
+        kept,
+        arrived,
+        gain[None, :],
+        *weights,
+        *selected,
+        meta,
+    )
+
+
+def settle_owned(grads, moment1, moment2, devices):
+    grads = lax.all_to_all(grads, ALL, 0, 0, tiled=True)
+    grads = grads[:, : moment1.shape[0] // (LANES * devices)]
     grad_shard = jnp.transpose(grads, (1, 0, 2)).reshape(-1).astype(jnp.float32)
     current = jnp.zeros((), jnp.float32)
     first_moment, second_moment, _ = adam(current, moment1, moment2, grad_shard)
@@ -1592,8 +1789,8 @@
     moment1,
     moment2,
 ):
-    groups = lax.axis_size("group")
-    member = lax.axis_index("group")
+    groups = axis_count(GROUP)
+    member = lax.axis_index(GROUP)
     row_count, feature_width = tokens.shape
     hidden_width = gate_weight.shape[1]
     head_width = q_gain.shape[0]
@@ -1604,27 +1801,45 @@
     )
     meta = key_metas[0]
     cos_table, sin_table = rope_tables(meta[:, 3], head_width)
-    selected = select(turn_adapter, adapters, feature_width, hidden_width)
-    a_qkv, a_guo, a_down, b_qkv, b_gu, b_do = selected
+    axes = ALL
+    devices = axis_count(PACKS) * groups
+    even = spreads_evenly(devices, groups, feature_width, hidden_width, adapters.shape[0])
+    spread = devices if even else 0
     q_gain_row = head_gain(q_gain)
     k_gain_row = head_gain(k_gain)
 
-    def bring(rows):
-        held = gather_half(rows, groups)
-        sent = pick(chosen, row_count, row_count // 2, held)
-        arrived = to_other_half(sent, groups)
-        return pick(chosen, 0, row_count, held), arrived
-
-    def send_back(rows):
-        returned = to_other_half(rows[row_count // 2 :], groups)
-        held = gather_half(rows, groups) + gather_half(returned, groups)
-        return pick(back, 0, row_count, held)
-
-    kept_tokens, arrived_tokens = bring(tokens)
-    kept_grads, arrived_grads = bring(cotangent)
-    my_tokens, normed, inner, query_raw, key_raw, query_low, key_low, value_low = project_heads(
+
+    held = (gather_half(tokens, groups), gather_half(cotangent, groups))
+    sent_tokens, sent_grads = pick(chosen, row_count, row_count // 2, *held)
+    arrived_tokens = to_other_half(sent_tokens, groups)
+    a_qkv, a_guo, a_down, b_qkv, b_gu, b_do, *spread_state = select(
+        spread,
+        turn_adapter,
+        lax.axis_index(axes)[None],
+        adapters,
+        (moment1.reshape(-1, LANES), moment2.reshape(-1, LANES)),
+        feature_width,
+        hidden_width,
+        sent_tokens,
+    )
+    if even:
+        params, moments = spread_state
+        moments = lax.all_to_all(moments, axes, 0, 0, tiled=True)
+    kept_tokens, kept_grads = pick(chosen, 0, row_count, *held)
+    (
+        my_tokens,
+        normed,
+        inner,
+        query_raw,
+        key_raw,
+        query_low,
+        key_low,
+        value_low,
+        sent_grads,
+    ) = project_heads(
         kept_tokens,
         arrived_tokens,
+        sent_grads,
         attn_gain,
         (query_weight, key_weight, value_weight),
         a_qkv,
@@ -1636,15 +1851,13 @@
         k_gain_row,
         head_width,
     )
+    arrived_grads = to_other_half(sent_grads, groups)
     keys = gather_half(key_low, groups)
     values = gather_half(value_low, groups)
     attended_low, log_total = attend(
         attn_bias, query_low, meta, keys, values, key_metas, segments, head_width
     )
-    devices = lax.axis_size("dp") * groups
-    even = spreads_evenly(devices, feature_width, hidden_width, adapters.shape[0])
-    spread = devices if even else 0
-    layer_rows, grad_residual, grad_attended, *forward_grads = feed_forward(
+    layer_rows, layer_tail, grad_residual, grad_attended, *forward_grads = feed_forward(
         spread,
         turn_adapter,
         attended_low,
@@ -1656,47 +1869,35 @@
         (a_guo, a_down, b_gu, b_do),
         meta,
     )
-    layer_out = send_back(layer_rows)
-
-    def back_part(pairs, before, after):
-        return attend_back(
-            attn_bias,
-            query_low,
-            meta,
-            log_total,
-            attended_low,
-            grad_attended,
-            keys,
-            values,
-            key_metas,
-            segments,
-            head_width,
-            pairs,
-            before,
-            after,
-        )
-
-    axes = ("dp", "group")
-    pair_count = feature_width // (2 * head_width)
-    first_pairs = 3 * pair_count // 4
+    layer_back = to_other_half(layer_tail, groups)
+    layer_held = gather_half(layer_rows, groups) + gather_half(layer_back, groups)
+
+    results = attend_back(
+        attn_bias,
+        query_low,
+        meta,
+        log_total,
+        attended_low,
+        grad_attended,
+        keys,
+        values,
+        key_metas,
+        segments,
+        head_width,
+    )
     after = []
     if even:
         total_rows = adapters.shape[0] // LANES
         late_rows = 6 * feature_width // devices
-        params, first_old, second_old = spread_state(adapters, moment1, moment2, devices)
-        order = placing_order(groups, devices, 16)
         early = lax.all_to_all(forward_grads[0], axes, 0, 0, tiled=True)
-        after = [first_old]
-    results = back_part((0, first_pairs), [], after)
-    if even:
-        told = 6 * RANK
-        table = early[:, 0, told : told + 2].astype(jnp.int32)
-        early_rows = params.shape[0] - late_rows
-        state = (params, first_old, second_old)
-        early_grad, early_new = settle(True, early_rows, table, early, *state, results[:1])
-        after = [early_new]
-        early_outer = lax.all_to_all(early_new, "dp", 0, 0, tiled=True)
-    results = back_part((first_pairs, pair_count), results, after)
+        early_grad, early_new, late_m1, late_m2, tall, square = settle_early(
+            early, moments, params, late_rows, [results[0]]
+        )
+        early_outer = lax.all_to_all(early_new, "far", 0, 0, tiled=True)
+        swap = [(0, 1), (1, 0)]
+        early_near = lax.ppermute(early_outer, "near", swap)
+        early_half = lax.ppermute(early_outer, "half", swap)
+        after = [early_new, layer_back]
     grad_query = results[0]
     grad_keys = results[1 : 1 + half_devices]
     grad_values = results[1 + half_devices :]
@@ -1705,9 +1906,9 @@
         back_shift = half_devices - shift
         key_terms.append(within_half(grad_keys[shift], back_shift, groups))
         value_terms.append(within_half(grad_values[shift], back_shift, groups))
-    grad_rows, *back_grads = project_heads_back(
+    grad_rows, grad_tail, *back_grads = project_heads_back(
         spread,
-        [early_outer] if even else [],
+        after,
         grad_query,
         key_terms,
         value_terms,
@@ -1728,7 +1929,9 @@
         k_gain_row,
         head_width,
     )
-    input_grad = send_back(grad_rows)
+    def bring_back(tail):
+        return gather_half(grad_rows, groups) + gather_half(to_other_half(tail, groups), groups)
+
     if not even:
         grads = (*back_grads, *forward_grads)
         column = jnp.arange(2 * RANK, dtype=jnp.int32)
@@ -1737,25 +1940,62 @@
             == (jnp.repeat(turn_adapter, RANK) * RANK + column % RANK)[None, :]
         )
         settled = settle_shards(grads, few_choice, adapters, moment1, moment2, groups)
+        layer_out = pick(back, 0, row_count, layer_held)[0]
+        input_grad = pick(back, 0, row_count, bring_back(grad_tail))[0]
         return (layer_out, input_grad) + settled
     late = lax.all_to_all(back_grads[0], axes, 0, 0, tiled=True)
-    early_pieces = gather_inner(early_outer, groups)
-    late_grad, late_new = settle(False, late_rows, table, late, *state, early_pieces[1:2])
-    late_pieces = gather_inner(lax.all_to_all(late_new, "dp", 0, 0, tiled=True), groups)
-    adapters_new = assemble(order, early_pieces, total_rows, late_rows, 32, None)
-    adapters_new = assemble(order, late_pieces, total_rows, 0, 64, adapters_new)
-    owned = settle_owned(late_grad, early_grad, moment1, moment2, devices)
+    layer_out = pick(back, 0, row_count, layer_held)[0]
+    own_grads, late_new, grad_tail = settle_late(
+        tall, square, late, params, late_m1, late_m2, early_grad, grad_tail, [layer_out, early_near, early_half]
+    )
+    late_outer = lax.all_to_all(late_new, PACKS, 0, 0, tiled=True)
+    late_pieces = gather_inner(late_outer, groups)
+    input_grad, own_grads = pick(
+        back, 0, row_count, bring_back(grad_tail), later=[own_grads]
+    )
+    cut_rows = early_outer.shape[1] // 2
+    early_far = [
+        lax.ppermute(early_near[:, :cut_rows], "half", swap),
+        lax.ppermute(early_half[:, cut_rows:], "near", swap),
+    ]
+    early_pieces = [[early_outer], [early_near], [early_half], early_far]
+    early_pieces += [
+        [lax.ppermute(part, "core", swap) for part in piece] for piece in early_pieces
+    ]
+    far = jnp.arange(lax.axis_size("far"), dtype=jnp.int32)
+    near, half, core = [lax.axis_index(name) for name in ALL[1:]]
+    early_device = jnp.concatenate(
+        [
+            ((far * 2 + (near ^ flip_near)) * 2 + (half ^ flip_half)) * 2 + (core ^ flip_core)
+            for flip_core in (0, 1)
+            for flip_near, flip_half in ((0, 0), (1, 0), (0, 1), (1, 1))
+        ]
+    )
+    late_pieces = [[piece] for piece in late_pieces]
+    order = placing_order(piece_devices(groups, devices), 16)
+    adapters_new = assemble(
+        placing_order(early_device, 16),
+        early_pieces,
+        total_rows,
+        late_rows,
+        None,
+        [input_grad, late_pieces[1][0]],
+    )
+    adapters_new = assemble(order, late_pieces, total_rows, 0, adapters_new, [])
+    owned = settle_owned(own_grads, moment1, moment2, devices)
     return (layer_out, input_grad, *owned, adapters_new.reshape(-1))
 
 
 def solution(mesh):
+    packs, groups = mesh.shape["dp"], mesh.shape["group"]
+    cut = jax.sharding.Mesh(mesh.devices.reshape(packs // 2, 2, groups // 2, 2), ALL)
     in_specs = (
-        P(("dp", "group"), None),
-        P(("dp", "group"), None),
-        P("dp"),
-        P("dp", None),
-        P("dp", None),
-        P("dp", None),
+        P(ALL, None),
+        P(ALL, None),
+        P(PACKS),
+        P(PACKS, None),
+        P(PACKS, None),
+        P(PACKS, None),
         P(),
         P(),
         P(),
@@ -1769,17 +2009,17 @@
         P(),
         P(),
         P(),
-        P(("dp", "group")),
-        P(("dp", "group")),
+        P(ALL),
+        P(ALL),
     )
     out_specs = (
-        P(("dp", "group"), None),
-        P(("dp", "group"), None),
-        P(("dp", "group")),
-        P(("dp", "group")),
-        P(("dp", "group")),
+        P(ALL, None),
+        P(ALL, None),
+        P(ALL),
+        P(ALL),
+        P(ALL),
         P(),
     )
     return jax.shard_map(
-        per_device, mesh=mesh, in_specs=in_specs, out_specs=out_specs, check_vma=False
-    )
+        per_device, mesh=cut, in_specs=in_specs, out_specs=out_specs, check_vma=False
+    )

time: 319 us -> 290 us (0.909)
  Pallas kernels: 197 us -> 179 us
  waiting for transfers between devices: 37.1 us -> 25.6 us
  starting transfers between devices: 51.1 us -> 57.5 us
  local copies, waits for them, and re-layouts: 23.1 us -> 17 us
    all_to_all x4, waiting for transfers between devices: 20 us -> 0.73 us  [the longest x1 0.72 us: settle_owned(): grads = lax.all_to_all(grads, ALL, 0, 0, tiled=True)]
    pallas_call x13 -> x10, Pallas kernels: 85.8 us -> 71.1 us  [the longest x1 28.3 us: attend_back(): pl.pallas_call(functools.partial(attend_back_kernel, count, segments, wid...]
    ppermute x20 -> x26, waiting for transfers between devices: 6.61 us -> 19 us  [the longest x4 8.04 us: to_other_half(): lax.ppermute(array, GROUP, [(i, (i + half) % groups) for i in range(group...]
    all_to_all x1, waiting for transfers between devices: 9.81 us -> 5.95 us  [per_device(): late = lax.all_to_all(back_grads[0], axes, 0, 0, tiled=True)]
    ppermute x20 -> x26, starting transfers between devices: 13.3 us -> 16.8 us  [the longest x4 6.1 us: to_other_half(): lax.ppermute(array, GROUP, [(i, (i + half) % groups) for i in range(group...]
    unnamed x49 -> x54, local copies, waits for them, and re-layouts: 9.39 us -> 9.23 us
  transfers between devices with their start and end apart: 26 -> 32, of which waited for: 5 -> 8; matrix products, arithmetic and copies ran while one was open for 6% -> 5% of each run, Pallas kernels for 60% -> 56%
where the time goes in v4:
time: 290 us; the launch traced here: 286 us
  Pallas kernels  179 us (62%)
  starting transfers between devices  57.5 us (20%)
  waiting for transfers between devices  25.6 us (9%)
  local copies, waits for them, and re-layouts  17 us (6%)
  other arithmetic  6.03 us (2%)
    pallas_call x1, Pallas kernels, feed_forward(): pl.pallas_call(functools.partial(feed_forward_kernel, devices), grid=(hid...  52.5 us
    pallas_call x1, Pallas kernels, attend_back(): pl.pallas_call(functools.partial(attend_back_kernel, count, segments, wid...  28.3 us
    pallas_call x4, Pallas kernels, pick(): pl.pallas_call(functools.partial(pick_kernel, [len(held) for held in held...  19.7 us
    pallas_call x1, Pallas kernels, attend(): pl.pallas_call(functools.partial(attend_kernel, count, segments, width),...  17 us
    pallas_call x1, Pallas kernels, project_heads_back(): pl.pallas_call(functools.partial(project_heads_back_kernel, count, width,...  16.8 us
    all_to_all x1, starting transfers between devices, per_device(): early = lax.all_to_all(forward_grads[0], axes, 0, 0, tiled=True)  14.7 us
    pallas_call x1, Pallas kernels, project_heads(): pl.pallas_call(functools.partial(project_key_value_kernel, width), grid=g...  9.88 us
    pallas_call x2, Pallas kernels, assemble(): pl.pallas_call(functools.partial(assemble_kernel, [len(piece) for piece i...  9.47 us
  transfers between devices with their start and end apart: 32, of which 8 were waited for; matrix products, arithmetic and copies ran while one was open for 5% of the time, Pallas kernels for 56%

profile of v4, /device:TPU:0, one launch (start us, length us, event | category | flops | bytes accessed | tf_op | source)
XLA Modules:
  0.0 286.1 jit_solution(17571678819395526948)
XLA Ops:
  3.8 4.4 %plan.1 = (bf16[768,1024]{1,0:T(8,128)(2,1)}, bf16[512,1536]{1,0:T(8,128)(2,1)}, s32[2]{0:T(128)}, s32[512,128]{1,0:T(8,128)}, s32[512,128]{1,0:T(8,128)}) custom-call(s32[1]{0:T(128)} %bitcast.member_ref, s32[1,3]{1,0:T(1,128)} %length_ref.1, s32[1,3]{1,0:T(1,128)} %adapter_ref.1, s32[1,16]{1,0:T(1,128)} %order_ref.1, s32[16,128]{1,0:T(8,128)} %bitcast.16), custom_call_target="tpu_custom_call" | custom-call | flops 2147483648 | bytes 2097152 | tf_op jit(solution)/shard_map/plan/pallas_call | solution.py:464
  10.8 4.2 %pick.5 = (bf16[256,1024]{1,0:T(8,128)(2,1)}, bf16[256,1024]{1,0:T(8,128)(2,1)}) custom-call(bf16[768,1024]{1,0:T(8,128)(2,1)} %get-tuple-element.60.chosen_ref, bf16[512,1024]{1,0:T(8,128)(2,1)} %refs_0_.3, bf16[512,1024]{1,0:T(8,128)(2,1)} %copy-done.11, bf16[512,1024]{1,0:T(8,128)(2,1)} %refs_2_.3, bf16[512,1024]{1,0:T(8,128)(2,1)} %copy-done.12), custom_call_target="tpu_custom_call" | custom-call | flops 1073741824 | bytes 4194304 | tf_op jit(solution)/shard_map/pick/pallas_call | solution.py:502
  15.0 2.9 %collective-permute-start.2 = (bf16[256,1024]{1,0:T(8,128)(2,1)}, bf16[256,1024]{1,0:T(8,128)(2,1)S(1)}, u32[]{:S(2)}, u32[]{:S(2)}) collective-permute-start(bf16[256,1024]{1,0:T(8,128)(2,1)} %get-tuple-element.62.refs_2_), channel_id=1, source_target_pairs={{0,2},{1,3},{2,0},{3,1},{4,6},{5,7},{6,4},{7,5},{8,10},{9,11},{10,... | collective-permute-start | bytes 1572872 | tf_op jit(solution)/shard_map/ppermute | solution.py:546
  17.9 1.8 fusion.3
  19.7 6.7 %select.29 = (bf16[1024,128]{1,0:T(8,128)(2,1)}, bf16[1024,128]{1,0:T(8,128)(2,1)}, bf16[4096,128]{1,0:T(8,128)(2,1)}, bf16[128,1024]{1,0:T(8,128)(2,1)}, bf16[1...) custom-call(s32[2]{0:T(128)} %get-tuple-element.59.turn_ref, ...), custom_call_target="tpu_custom_call" | custom-call | flops 2147483648 | bytes 12058624 | tf_op jit(solution)/shard_map/select/pallas_call | solution.py:1021
  26.3 5.6 %pick.4 = (bf16[512,1024]{1,0:T(8,128)(2,1)}, bf16[512,1024]{1,0:T(8,128)(2,1)}) custom-call(bf16[768,1024]{1,0:T(8,128)(2,1)} %get-tuple-element.60.chosen_ref, bf16[512,1024]{1,0:T(8,128)(2,1)} %refs_0_.3, bf16[512,1024]{1,0:T(8,128)(2,1)} %copy-done.11, bf16[512,1024]{1,0:T(8,128)(2,1)} %refs_2_.3, bf16[512,1024]{1,0:T(8,128)(2,1)} %copy-done.12), custom_call_target="tpu_custom_call" | custom-call | flops 2147483648 | bytes 8388608 | tf_op jit(solution)/shard_map/pick/pallas_call | solution.py:502
  32.7 9.9 %project_key_value.1 = (bf16[512,1024]{1,0:T(8,128)(2,1)}, bf16[512,1024]{1,0:T(8,128)(2,1)}, bf16[512,128]{1,0:T(8,128)(2,1)}, bf16[512,1024]{1,0:T(8,128)(2,1)...) custom-call(bf16[512,1024]{1,0:T(8,128)(2,1)} %get-tuple-element.61., ...), custom_call_target="tpu_custom_call", output_to_operand_aliasing={{6}: (11, {})} | custom-call | flops 3221225472 | bytes 11534336 | tf_op jit(solution)/shard_map/project_key_value/pallas_call | solution.py:1188
  44.5 6.6 %all-to-all-start.1 = ((bf16[32,48,128]{2,1,0:T(8,128)(2,1)}), bf16[32,48,128]{2,1,0:T(8,128)(2,1)S(1)}, u32[]{:S(2)}, u32[]{:S(2)}) async-start(bf16[32,48,128]{2,1,0:T(8,128)(2,1)} %get-tuple-element.94), calls=%async_computation.1 | async-start | bytes 786432 | tf_op jit(solution)/shard_map/all_to_all | solution.py:1827
  51.1 6.9 %project_query.1 = (bf16[512,1024]{1,0:T(8,128)(2,1)}, bf16[512,1024]{1,0:T(8,128)(2,1)}) custom-call(bf16[512,1024]{1,0:T(8,128)(2,1)} %get-tuple-element.67.normed_ref.refs_6_, bf16[512,128]{1,0:T(8,128)(2,1)} %get-tuple-element.68.inner_ref.refs_7_, bf16[1024,1024]{1,0:T(8,128)(2,1)} %refs_11_.1, bf16[128,1024]{1,0:T(8,128)(2,1)} %get-tuple-element.64.b_ref.refs_15_, ...), custom_call_target="tpu_custom_call" | custom-call | flops 1610612736 | bytes 6291456 | tf_op jit(solution)/shard_map/project_query/pallas_call | solution.py:1226
  59.3 17.0 %attend.1 = (bf16[512,1024]{1,0:T(8,128)(2,1)}, f32[512,1024]{1,0:T(8,128)}) custom-call(f32[2,16]{1,0:T(2,128)} %bias_ref.3, bf16[512,1024]{1,0:T(8,128)(2,1)} %get-tuple-element.69.query_ref, s32[512,128]{1,0:T(8,128)} %get-tuple-element.65.meta_ref.qmeta_ref.refs_4_.refs_16_, bf16[512,1024]{1,0:T(8,128)(2,1)} %get-tuple-element.70.refs_0_, ...), custom_call_target="tpu_custom_call" | custom-call | flops 2147483648 | bytes 6291456 | tf_op jit(solution)/shard_map/attend/pallas_call | solution.py:141
  77.2 52.5 %feed_forward.1 = (bf16[512,1024]{1,0:T(8,128)(2,1)}, bf16[256,1024]{1,0:T(8,128)(2,1)}, bf16[512,1024]{1,0:T(8,128)(2,1)}, bf16[512,1024]{1,0:T(8,128)(2,1)}, bf16[32,144,128]{2,1,0:T(8,128)(2,1)}) custom-call(s32[2]{0:T(128)} %get-tuple-element.59.turn_ref, bf16[512,1024]{1,0:T(8,128)(2,1)} %get-tuple-element.73.att_ref.attended_ref, ...), custom_call_target="tpu_custom_call" | custom-call | flops 30064771072 | bytes 41943040 | tf_op jit(solution)/shard_map/feed_forward/pallas_call | solution.py:1690
  129.6 14.7 %all-to-all-start = ((bf16[32,144,128]{2,1,0:T(8,128)(2,1)}), bf16[32,144,128]{2,1,0:T(8,128)(2,1)S(1)}, u32[]{:S(2)}, u32[]{:S(2)}) async-start(bf16[32,144,128]{2,1,0:T(8,128)(2,1)} %get-tuple-element.93), calls=%async_computation | async-start | bytes 2359296 | tf_op jit(solution)/shard_map/all_to_all | solution.py:1892
  144.3 28.3 %attend_back.1 = (bf16[512,1024]{1,0:T(8,128)(2,1)}, bf16[512,1024]{1,0:T(8,128)(2,1)}, bf16[512,1024]{1,0:T(8,128)(2,1)}, bf16[512,1024]{1,0:T(8,128)(2,1)}, bf16[512,1024]{1,0:T(8,128)(2,1)}) custom-call(f32[2,16]{1,0:T(2,128)} %bias_ref.3, bf16[512,1024]{1,0:T(8,128)(2,1)} %get-tuple-element.69.query_ref, ...), custom_call_target="tpu_custom_call" | custom-call | flops 5368709120 | bytes 10485760 | tf_op jit(solution)/shard_map/attend_back/pallas_call | solution.py:268
  175.9 4.1 %settle_early.1 = (bf16[544,128]{1,0:T(8,128)(2,1)}, bf16[4,544,128]{2,1,0:T(8,128)(2,1)}, f32[192,128]{1,0:T(8,128)}, f32[192,128]{1,0:T(8,128)}, s32[1,1024]{1,0:T(1,128)}, /*index=5*/s32[1,512]{1,0:T(1,128)}) custom-call(bf16[32,144,128]{2,1,0:T(8,128)(2,1)} %copy-done, bf16[32,48,128]{2,1,0:T(8,128)(2,1)} %copy-done.9, ...), custom_call_target="tpu_custom_call" | custom-call | flops 536870912 | bytes 2359296 | tf_op jit(solution)/shard_map/settle_early/pallas_call | solution.py:746
  179.9 4.6 %all-to-all-start.3 = ((bf16[4,544,128]{2,1,0:T(8,128)(2,1)}), bf16[4,544,128]{2,1,0:T(8,128)(2,1)S(1)}, u32[]{:S(2)}, u32[]{:S(2)}) async-start(bf16[4,544,128]{2,1,0:T(8,128)(2,1)} %get-tuple-element.96.refs_21_), calls=%async_computation.3 | async-start | bytes 1114112 | tf_op jit(solution)/shard_map/all_to_all | solution.py:1896
  184.5 2.9 %collective-permute-done.7.refs_2_.refs_22_ = bf16[256,1024]{1,0:T(8,128)(2,1)} collective-permute-done((bf16[256,1024]{1,0:T(8,128)(2,1)}, bf16[256,1024]{1,0:T(8,128)(2,1)}, u32[]{:S(2)}, u32[]{:S(2)}) %collective-permute-start.7) | collective-permute-done | bytes 524320 | tf_op jit(solution)/shard_map/ppermute | solution.py:546
  188.4 16.8 %project_heads_back.1 = (bf16[512,1024]{1,0:T(8,128)(2,1)}, bf16[256,1024]{1,0:T(8,128)(2,1)}, bf16[32,64,128]{2,1,0:T(8,128)(2,1)}) custom-call(bf16[512,1024]{1,0:T(8,128)(2,1)} %get-tuple-element.85.refs_0_.gq_ref, bf16[512,1024]{1,0:T(8,128)(2,1)} %get-tuple-element.86.refs_0_, bf16[512,1024]{1,0:T(8,128)(2,1)} %copy-done.13, ...), custom_call_target="tpu_custom_call" | custom-call | flops 4294967296 | bytes 22020096 | tf_op jit(solution)/shard_map/project_heads_back/pallas_call | solution.py:1409
  205.3 5.7 %all-to-all-start.2 = ((bf16[32,64,128]{2,1,0:T(8,128)(2,1)}), bf16[32,64,128]{2,1,0:T(8,128)(2,1)S(1)}, u32[]{:S(2)}, u32[]{:S(2)}) async-start(bf16[32,64,128]{2,1,0:T(8,128)(2,1)} %get-tuple-element.100), calls=%async_computation.2 | async-start | bytes 1048576 | tf_op jit(solution)/shard_map/all_to_all | solution.py:1946
  215.6 5.0 %pick.6.refs_2_ = bf16[512,1024]{1,0:T(8,128)(2,1)} custom-call(bf16[512,1536]{1,0:T(8,128)(2,1)} %get-tuple-element.58.chosen_ref, bf16[512,1024]{1,0:T(8,128)(2,1)} %get-tuple-element.81.refs_0_, bf16[512,1024]{1,0:T(8,128)(2,1)} %collective-permute-done.6.refs_1_, bf16[256,1024]{1,0:T(8,128)(2,1)} %collective-permute-done.7.refs_2_.refs_22_, ...), custom_call_target="tpu_custom_call" | custom-call | flops 1610612736 | bytes 4194304 | tf_op jit(solution)/shard_map/pick/pallas_call | solution.py:502
  220.6 6.0 %all-to-all-done.2.arrived_ref = bf16[32,64,128]{2,1,0:T(8,128)(2,1)S(1)} async-done(((bf16[32,64,128]{2,1,0:T(8,128)(2,1)}), bf16[32,64,128]{2,1,0:T(8,128)(2,1)S(1)}, u32[]{:S(2)}, u32[]{:S(2)}) %all-to-all-start.2) | async-done | bytes 524320 | tf_op jit(solution)/shard_map/all_to_all | solution.py:1946
  226.6 4.8 %collective-permute-done.12.refs_3_.refs_1_ = bf16[4,544,128]{2,1,0:T(8,128)(2,1)S(1)} collective-permute-done((bf16[4,544,128]{2,1,0:T(8,128)(2,1)S(1)}, bf16[4,544,128]{2,1,0:T(8,128)(2,1)S(1)}, u32[]{:S(2)}, u32[]{:S(2)}) %collective-permute-start.12) | collective-permute-done | bytes 557088 | tf_op jit(solution)/shard_map/ppermute | solution.py:1898
  232.4 2.9 %settle_late.1 = (bf16[32,24,128]{2,1,0:T(8,128)(2,1)}, bf16[8,192,128]{2,1,0:T(8,128)(2,1)}, bf16[256,1024]{1,0:T(8,128)(2,1)}) custom-call(s32[1,1024]{1,0:T(1,128)} %get-tuple-element.98.tall_ref, s32[1,512]{1,0:T(1,128)} %get-tuple-element.99.square_ref, bf16[32,64,128]{2,1,0:T(8,128)(2,1)} %copy-done.6, ...), custom_call_target="tpu_custom_call", output_to_operand_aliasing={{2}: (7, {})} | custom-call | flops 536870912 | bytes 1048576 | tf_op jit(solution)/shard_map/settle_late/pallas_call | solution.py:795
  236.8 4.6 %all-to-all-start.5 = ((bf16[8,192,128]{2,1,0:T(8,128)(2,1)}), bf16[8,192,128]{2,1,0:T(8,128)(2,1)S(1)}, u32[]{:S(2)}, u32[]{:S(2)}) async-start(bf16[8,192,128]{2,1,0:T(8,128)(2,1)} %get-tuple-element.109), calls=%async_computation.5 | async-start | bytes 786432 | tf_op jit(solution)/shard_map/all_to_all | solution.py:1951
  242.4 1.7 slice.17
  245.4 5.1 %collective-permute-done.14.refs_2_ = bf16[256,1024]{1,0:T(8,128)(2,1)} collective-permute-done((bf16[256,1024]{1,0:T(8,128)(2,1)}, bf16[256,1024]{1,0:T(8,128)(2,1)}, u32[]{:S(2)}, u32[]{:S(2)}) %collective-permute-start.14) | collective-permute-done | bytes 524320 | tf_op jit(solution)/shard_map/ppermute | solution.py:546
  250.5 1.7 slice.18
  255.0 1.8 collective-permute-start.16
  256.8 4.8 %collective-permute-done.20.refs_4_ = bf16[4,272,128]{2,1,0:T(8,128)(2,1)} collective-permute-done((bf16[4,272,128]{2,1,0:T(8,128)(2,1)}, bf16[4,272,128]{2,1,0:T(8,128)(2,1)}, u32[]{:S(2)}, u32[]{:S(2)}) %collective-permute-start.20) | collective-permute-done | bytes 278560 | tf_op jit(solution)/shard_map/ppermute | solution.py:1959
  262.1 5.0 %pick.7 = (bf16[512,1024]{1,0:T(8,128)(2,1)}, bf16[32,24,128]{2,1,0:T(8,128)(2,1)}) custom-call(bf16[512,1536]{1,0:T(8,128)(2,1)} %get-tuple-element.58.chosen_ref, bf16[512,1024]{1,0:T(8,128)(2,1)} %get-tuple-element.97.refs_0_, bf16[512,1024]{1,0:T(8,128)(2,1)} %collective-permute-done.11.refs_1_, ...), custom_call_target="tpu_custom_call", output_to_operand_aliasing={{1}: (5, {})} | custom-call | flops 1610612736 | bytes 4194304 | tf_op jit(solution)/shard_map/pick/pallas_call | solution.py:502
  267.1 4.5 %all-to-all-start.4 = ((bf16[32,24,128]{2,1,0:T(8,128)(2,1)}), bf16[32,24,128]{2,1,0:T(8,128)(2,1)S(1)}, u32[]{:S(2)}, u32[]{:S(2)}) async-start(bf16[32,24,128]{2,1,0:T(8,128)(2,1)} %get-tuple-element.108), calls=%async_computation.4 | async-start | bytes 393216 | tf_op jit(solution)/shard_map/all_to_all | solution.py:1761
  273.7 6.1 %assemble.2.refs_4_ = bf16[23552,128]{1,0:T(8,128)(2,1)} custom-call(bf16[512,512]{1,0:T(8,128)(2,1)} %fusion.1.order_ref, bf16[4,544,128]{2,1,0:T(8,128)(2,1)} %copy-done.5, bf16[4,544,128]{2,1,0:T(8,128)(2,1)} %copy-done.1, bf16[4,544,128]{2,1,0:T(8,128)(2,1)} %copy-done.3, bf16[4,272,128]{2,1,0:T(8,128)(2,1)} %copy-done.19, ...), custom_call_target="tpu_custom_call" | custom-call | flops 2281701376 | bytes 8912896 | tf_op jit(solution)/shard_map/assemble/pallas_call | solution.py:897
  282.4 3.4 %assemble.3 = bf16[23552,128]{1,0:T(8,128)(2,1)} custom-call(bf16[512,512]{1,0:T(8,128)(2,1)} %fusion.order_ref, bf16[8,192,128]{2,1,0:T(8,128)(2,1)} %copy-done.8, bf16[8,192,128]{2,1,0:T(8,128)(2,1)} %copy-done.7, bf16[8,192,128]{2,1,0:T(8,128)(2,1)} %copy-done.16, ...), custom_call_target="tpu_custom_call", output_to_operand_aliasing={{}: (5, {})} | custom-call | flops 805306368 | bytes 3145728 | tf_op jit(solution)/shard_map/assemble/pallas_call | solution.py:897
  (133 shorter events, 32.0 us)
Async XLA Ops:
  0.6 8.8 %collective-permute-start = (bf16[512,1024]{1,0:T(8,128)(2,1)}, bf16[512,1024]{1,0:T(8,128)(2,1)S(1)}, u32[]{:S(2)}, u32[]{:S(2)}) collective-permute-start(bf16[512,1024]{1,0:T(8,128)(2,1)} %refs_0_.3), channel_id=1, source_target_pairs={{1,0},{0,1},{3,2},{2,3},{5,4},{4,5},{7,6},{6,7},{9,8},{8,9},{11,10... | collective-permute-start | bytes 3145736 | tf_op jit(solution)/shard_map/ppermute | solution.py:537
  1.1 8.3 %collective-permute-start.1 = (bf16[512,1024]{1,0:T(8,128)(2,1)}, bf16[512,1024]{1,0:T(8,128)(2,1)S(1)}, u32[]{:S(2)}, u32[]{:S(2)}) collective-permute-start(bf16[512,1024]{1,0:T(8,128)(2,1)} %refs_2_.3), channel_id=1, source_target_pairs={{1,0},{0,1},{3,2},{2,3},{5,4},{4,5},{7,6},{6,7},{9,8},{8,9},{11,10... | collective-permute-start | bytes 3145736 | tf_op jit(solution)/shard_map/ppermute | solution.py:537
  15.0 16.9 %collective-permute-start.2 = (bf16[256,1024]{1,0:T(8,128)(2,1)}, bf16[256,1024]{1,0:T(8,128)(2,1)S(1)}, u32[]{:S(2)}, u32[]{:S(2)}) collective-permute-start(bf16[256,1024]{1,0:T(8,128)(2,1)} %get-tuple-element.62.refs_2_), channel_id=1, source_target_pairs={{0,2},{1,3},{2,0},{3,1},{4,6},{5,7},{6,4},{7,5},{8,10},{9,11},{10,... | collective-permute-start | bytes 1572872 | tf_op jit(solution)/shard_map/ppermute | solution.py:546
  42.6 15.4 %collective-permute-start.3 = (bf16[512,1024]{1,0:T(8,128)(2,1)}, bf16[512,1024]{1,0:T(8,128)(2,1)S(1)}, u32[]{:S(2)}, u32[]{:S(2)}) collective-permute-start(bf16[512,1024]{1,0:T(8,128)(2,1)} %get-tuple-element.70.refs_0_), channel_id=1, source_target_pairs={{1,0},{0,1},{3,2},{2,3},{5,4},{4,5},{7,6},{6,7},{9,8},{8,9},{11,10... | collective-permute-start | bytes 3145736 | tf_op jit(solution)/shard_map/ppermute | solution.py:537
  42.6 15.3 %collective-permute-start.4 = (bf16[512,1024]{1,0:T(8,128)(2,1)}, bf16[512,1024]{1,0:T(8,128)(2,1)S(1)}, u32[]{:S(2)}, u32[]{:S(2)}) collective-permute-start(bf16[512,1024]{1,0:T(8,128)(2,1)} %get-tuple-element.71.refs_2_), channel_id=1, source_target_pairs={{1,0},{0,1},{3,2},{2,3},{5,4},{4,5},{7,6},{6,7},{9,8},{8,9},{11,10... | collective-permute-start | bytes 3145736 | tf_op jit(solution)/shard_map/ppermute | solution.py:537
  43.1 33.2 %collective-permute-start.5 = (bf16[256,1024]{1,0:T(8,128)(2,1)}, bf16[256,1024]{1,0:T(8,128)(2,1)S(1)}, u32[]{:S(2)}, u32[]{:S(2)}) collective-permute-start(bf16[256,1024]{1,0:T(8,128)(2,1)} %get-tuple-element.76), channel_id=1, source_target_pairs={{0,2},{1,3},{2,0},{3,1},{4,6},{5,7},{6,4},{7,5},{8,10},{9,11},{10,... | collective-permute-start | bytes 1572872 | tf_op jit(solution)/shard_map/ppermute | solution.py:546
  44.5 85.1 %all-to-all-start.1 = ((bf16[32,48,128]{2,1,0:T(8,128)(2,1)}), bf16[32,48,128]{2,1,0:T(8,128)(2,1)S(1)}, u32[]{:S(2)}, u32[]{:S(2)}) async-start(bf16[32,48,128]{2,1,0:T(8,128)(2,1)} %get-tuple-element.94), calls=%async_computation.1 | async-start | bytes 786432 | tf_op jit(solution)/shard_map/all_to_all | solution.py:1827
  129.6 45.2 %all-to-all-start = ((bf16[32,144,128]{2,1,0:T(8,128)(2,1)}), bf16[32,144,128]{2,1,0:T(8,128)(2,1)S(1)}, u32[]{:S(2)}, u32[]{:S(2)}) async-start(bf16[32,144,128]{2,1,0:T(8,128)(2,1)} %get-tuple-element.93), calls=%async_computation | async-start | bytes 2359296 | tf_op jit(solution)/shard_map/all_to_all | solution.py:1892
  172.6 14.8 %collective-permute-start.9 = (bf16[512,1024]{1,0:T(8,128)(2,1)}, bf16[512,1024]{1,0:T(8,128)(2,1)S(1)}, u32[]{:S(2)}, u32[]{:S(2)}) collective-permute-start(bf16[512,1024]{1,0:T(8,128)(2,1)} %get-tuple-element.87), channel_id=1, source_target_pairs={{1,0},{0,1},{3,2},{2,3},{5,4},{4,5},{7,6},{6,7},{9,8},{8,9},{11,10... | collective-permute-start | bytes 3145736 | tf_op jit(solution)/shard_map/ppermute | solution.py:537
  172.8 14.7 %collective-permute-start.10 = (bf16[512,1024]{1,0:T(8,128)(2,1)}, bf16[512,1024]{1,0:T(8,128)(2,1)}, u32[]{:S(2)}, u32[]{:S(2)}) collective-permute-start(bf16[512,1024]{1,0:T(8,128)(2,1)} %get-tuple-element.89), channel_id=1, source_target_pairs={{1,0},{0,1},{3,2},{2,3},{5,4},{4,5},{7,6},{6,7},{9,8},{8,9},{11,10... | collective-permute-start | bytes 3145736 | tf_op jit(solution)/shard_map/ppermute | solution.py:537
  173.2 14.3 %collective-permute-start.7 = (bf16[256,1024]{1,0:T(8,128)(2,1)}, bf16[256,1024]{1,0:T(8,128)(2,1)}, u32[]{:S(2)}, u32[]{:S(2)}) collective-permute-start(bf16[256,1024]{1,0:T(8,128)(2,1)} %get-tuple-element.82), channel_id=1, source_target_pairs={{0,2},{1,3},{2,0},{3,1},{4,6},{5,7},{6,4},{7,5},{8,10},{9,11},{10,... | collective-permute-start | bytes 1572872 | tf_op jit(solution)/shard_map/ppermute | solution.py:546
  179.9 25.3 %all-to-all-start.3 = ((bf16[4,544,128]{2,1,0:T(8,128)(2,1)}), bf16[4,544,128]{2,1,0:T(8,128)(2,1)S(1)}, u32[]{:S(2)}, u32[]{:S(2)}) async-start(bf16[4,544,128]{2,1,0:T(8,128)(2,1)} %get-tuple-element.96.refs_21_), calls=%async_computation.3 | async-start | bytes 1114112 | tf_op jit(solution)/shard_map/all_to_all | solution.py:1896
  184.5 30.3 %collective-permute-start.6 = (bf16[512,1024]{1,0:T(8,128)(2,1)}, bf16[512,1024]{1,0:T(8,128)(2,1)}, u32[]{:S(2)}, u32[]{:S(2)}) collective-permute-start(bf16[512,1024]{1,0:T(8,128)(2,1)} %get-tuple-element.81.refs_0_), channel_id=1, source_target_pairs={{1,0},{0,1},{3,2},{2,3},{5,4},{4,5},{7,6},{6,7},{9,8},{8,9},{11,10... | collective-permute-start | bytes 3145736 | tf_op jit(solution)/shard_map/ppermute | solution.py:537
  205.3 21.3 %all-to-all-start.2 = ((bf16[32,64,128]{2,1,0:T(8,128)(2,1)}), bf16[32,64,128]{2,1,0:T(8,128)(2,1)S(1)}, u32[]{:S(2)}, u32[]{:S(2)}) async-start(bf16[32,64,128]{2,1,0:T(8,128)(2,1)} %get-tuple-element.100), calls=%async_computation.2 | async-start | bytes 1048576 | tf_op jit(solution)/shard_map/all_to_all | solution.py:1946
  211.0 3.8 %collective-permute-start.8 = (bf16[256,1024]{1,0:T(8,128)(2,1)}, bf16[256,1024]{1,0:T(8,128)(2,1)S(1)}, u32[]{:S(2)}, u32[]{:S(2)}) collective-permute-start(bf16[256,1024]{1,0:T(8,128)(2,1)} %collective-permute-done.7.refs_2_.refs_22_), channel_id=1, source_target_pairs={{1,0},{0,1},{3,2},{2,3},{5,4},{4,5},{7,6},{6,7},{9,8},{8,9},{11,10... | collective-permute-start | bytes 1572872 | tf_op jit(solution)/shard_map/ppermute | solution.py:537
  211.3 20.1 %collective-permute-start.12 = (bf16[4,544,128]{2,1,0:T(8,128)(2,1)S(1)}, bf16[4,544,128]{2,1,0:T(8,128)(2,1)S(1)}, u32[]{:S(2)}, u32[]{:S(2)}) collective-permute-start(bf16[4,544,128]{2,1,0:T(8,128)(2,1)S(1)} %all-to-all-done.3.refs_0_), channel_id=1, source_target_pairs={{0,4},{4,0},{1,5},{5,1},{2,6},{6,2},{3,7},{7,3},{8,12},{12,8},{9,1... | collective-permute-start | bytes 1671176 | tf_op jit(solution)/shard_map/ppermute | solution.py:1898
  213.0 18.5 %collective-permute-start.13 = (bf16[4,544,128]{2,1,0:T(8,128)(2,1)S(1)}, bf16[4,544,128]{2,1,0:T(8,128)(2,1)S(1)}, u32[]{:S(2)}, u32[]{:S(2)}) collective-permute-start(bf16[4,544,128]{2,1,0:T(8,128)(2,1)S(1)} %all-to-all-done.3.refs_0_), channel_id=1, source_target_pairs={{0,2},{2,0},{1,3},{3,1},{4,6},{6,4},{5,7},{7,5},{8,10},{10,8},{9,1... | collective-permute-start | bytes 1671176 | tf_op jit(solution)/shard_map/ppermute | solution.py:1899
  214.8 38.4 %collective-permute-start.11 = (bf16[512,1024]{1,0:T(8,128)(2,1)}, bf16[512,1024]{1,0:T(8,128)(2,1)}, u32[]{:S(2)}, u32[]{:S(2)}) collective-permute-start(bf16[512,1024]{1,0:T(8,128)(2,1)} %get-tuple-element.97.refs_0_), channel_id=1, source_target_pairs={{1,0},{0,1},{3,2},{2,3},{5,4},{4,5},{7,6},{6,7},{9,8},{8,9},{11,10... | collective-permute-start | bytes 3145736 | tf_op jit(solution)/shard_map/ppermute | solution.py:537
  235.4 15.2 %collective-permute-start.14 = (bf16[256,1024]{1,0:T(8,128)(2,1)}, bf16[256,1024]{1,0:T(8,128)(2,1)}, u32[]{:S(2)}, u32[]{:S(2)}) collective-permute-start(bf16[256,1024]{1,0:T(8,128)(2,1)} %get-tuple-element.105), channel_id=1, source_target_pairs={{0,2},{1,3},{2,0},{3,1},{4,6},{5,7},{6,4},{7,5},{8,10},{9,11},{10,... | collective-permute-start | bytes 1572872 | tf_op jit(solution)/shard_map/ppermute | solution.py:546
  236.8 18.2 %all-to-all-start.5 = ((bf16[8,192,128]{2,1,0:T(8,128)(2,1)}), bf16[8,192,128]{2,1,0:T(8,128)(2,1)S(1)}, u32[]{:S(2)}, u32[]{:S(2)}) async-start(bf16[8,192,128]{2,1,0:T(8,128)(2,1)} %get-tuple-element.109), calls=%async_computation.5 | async-start | bytes 786432 | tf_op jit(solution)/shard_map/all_to_all | solution.py:1951
  241.4 12.0 %collective-permute-start.21 = (bf16[4,544,128]{2,1,0:T(8,128)(2,1)S(1)}, bf16[4,544,128]{2,1,0:T(8,128)(2,1)S(1)}, u32[]{:S(2)}, u32[]{:S(2)}) collective-permute-start(bf16[4,544,128]{2,1,0:T(8,128)(2,1)S(1)} %all-to-all-done.3.refs_0_), channel_id=1, source_target_pairs={{0,1},{1,0},{2,3},{3,2},{4,5},{5,4},{6,7},{7,6},{8,9},{9,8},{10,11... | collective-permute-start | bytes 1671176 | tf_op jit(solution)/shard_map/ppermute | solution.py:1963
  244.1 10.9 %collective-permute-start.19 = (bf16[4,272,128]{2,1,0:T(8,128)(2,1)}, bf16[4,272,128]{2,1,0:T(8,128)(2,1)S(1)}, u32[]{:S(2)}, u32[]{:S(2)}) collective-permute-start(bf16[4,272,128]{2,1,0:T(8,128)(2,1)} %slice.17), channel_id=1, source_target_pairs={{0,2},{2,0},{1,3},{3,1},{4,6},{6,4},{5,7},{7,5},{8,10},{10,8},{9,1... | collective-permute-start | bytes 835592 | tf_op jit(solution)/shard_map/ppermute | solution.py:1958
  250.5 11.1 %collective-permute-start.15 = (bf16[256,1024]{1,0:T(8,128)(2,1)}, bf16[256,1024]{1,0:T(8,128)(2,1)}, u32[]{:S(2)}, u32[]{:S(2)}) collective-permute-start(bf16[256,1024]{1,0:T(8,128)(2,1)} %collective-permute-done.14.refs_2_), channel_id=1, source_target_pairs={{1,0},{0,1},{3,2},{2,3},{5,4},{4,5},{7,6},{6,7},{9,8},{8,9},{11,10... | collective-permute-start | bytes 1572872 | tf_op jit(solution)/shard_map/ppermute | solution.py:537
  252.2 9.4 %collective-permute-start.20 = (bf16[4,272,128]{2,1,0:T(8,128)(2,1)}, bf16[4,272,128]{2,1,0:T(8,128)(2,1)}, u32[]{:S(2)}, u32[]{:S(2)}) collective-permute-start(bf16[4,272,128]{2,1,0:T(8,128)(2,1)} %slice.18), channel_id=1, source_target_pairs={{0,4},{4,0},{1,5},{5,1},{2,6},{6,2},{3,7},{7,3},{8,12},{12,8},{9,1... | collective-permute-start | bytes 835592 | tf_op jit(solution)/shard_map/ppermute | solution.py:1959
  253.2 19.4 %collective-permute-start.22 = (bf16[4,544,128]{2,1,0:T(8,128)(2,1)S(1)}, bf16[4,544,128]{2,1,0:T(8,128)(2,1)S(1)}, u32[]{:S(2)}, u32[]{:S(2)}) collective-permute-start(bf16[4,544,128]{2,1,0:T(8,128)(2,1)S(1)} %copy-done.2), channel_id=1, source_target_pairs={{0,1},{1,0},{2,3},{3,2},{4,5},{5,4},{6,7},{7,6},{8,9},{9,8},{10,11... | collective-permute-start | bytes 1671176 | tf_op jit(solution)/shard_map/ppermute | solution.py:1963
  253.5 19.7 %collective-permute-start.23 = (bf16[4,544,128]{2,1,0:T(8,128)(2,1)S(1)}, bf16[4,544,128]{2,1,0:T(8,128)(2,1)}, u32[]{:S(2)}, u32[]{:S(2)}) collective-permute-start(bf16[4,544,128]{2,1,0:T(8,128)(2,1)S(1)} %copy-done.4), channel_id=1, source_target_pairs={{0,1},{1,0},{2,3},{3,2},{4,5},{5,4},{6,7},{7,6},{8,9},{9,8},{10,11... | collective-permute-start | bytes 1671176 | tf_op jit(solution)/shard_map/ppermute | solution.py:1963
  255.0 17.9 %collective-permute-start.16 = (bf16[8,192,128]{2,1,0:T(8,128)(2,1)S(1)}, bf16[8,192,128]{2,1,0:T(8,128)(2,1)S(1)}, u32[]{:S(2)}, u32[]{:S(2)}) collective-permute-start(bf16[8,192,128]{2,1,0:T(8,128)(2,1)S(1)} %all-to-all-done.5.refs_0_), channel_id=1, source_target_pairs={{0,2},{1,3},{2,0},{3,1},{4,6},{5,7},{6,4},{7,5},{8,10},{9,11},{10,... | collective-permute-start | bytes 1179656 | tf_op jit(solution)/shard_map/ppermute | solution.py:819
  261.6 11.6 %collective-permute-start.24 = (bf16[4,272,128]{2,1,0:T(8,128)(2,1)S(1)}, bf16[4,272,128]{2,1,0:T(8,128)(2,1)}, u32[]{:S(2)}, u32[]{:S(2)}) collective-permute-start(bf16[4,272,128]{2,1,0:T(8,128)(2,1)S(1)} %collective-permute-done.19.refs_3_), channel_id=1, source_target_pairs={{0,1},{1,0},{2,3},{3,2},{4,5},{5,4},{6,7},{7,6},{8,9},{9,8},{10,11... | collective-permute-start | bytes 835592 | tf_op jit(solution)/shard_map/ppermute | solution.py:1963
  261.6 11.6 %collective-permute-start.25 = (bf16[4,272,128]{2,1,0:T(8,128)(2,1)}, bf16[4,272,128]{2,1,0:T(8,128)(2,1)}, u32[]{:S(2)}, u32[]{:S(2)}) collective-permute-start(bf16[4,272,128]{2,1,0:T(8,128)(2,1)} %collective-permute-done.20.refs_4_), channel_id=1, source_target_pairs={{0,1},{1,0},{2,3},{3,2},{4,5},{5,4},{6,7},{7,6},{8,9},{9,8},{10,11... | collective-permute-start | bytes 835592 | tf_op jit(solution)/shard_map/ppermute | solution.py:1963
  267.1 13.4 %all-to-all-start.4 = ((bf16[32,24,128]{2,1,0:T(8,128)(2,1)}), bf16[32,24,128]{2,1,0:T(8,128)(2,1)S(1)}, u32[]{:S(2)}, u32[]{:S(2)}) async-start(bf16[32,24,128]{2,1,0:T(8,128)(2,1)} %get-tuple-element.108), calls=%async_computation.4 | async-start | bytes 393216 | tf_op jit(solution)/shard_map/all_to_all | solution.py:1761
  272.6 9.0 %collective-permute-start.17 = (bf16[8,192,128]{2,1,0:T(8,128)(2,1)S(1)}, bf16[8,192,128]{2,1,0:T(8,128)(2,1)S(1)}, u32[]{:S(2)}, u32[]{:S(2)}) collective-permute-start(bf16[8,192,128]{2,1,0:T(8,128)(2,1)S(1)} %all-to-all-done.5.refs_0_), channel_id=1, source_target_pairs={{0,1},{1,0},{2,3},{3,2},{4,5},{5,4},{6,7},{7,6},{8,9},{9,8},{10,11... | collective-permute-start | bytes 1179656 | tf_op jit(solution)/shard_map/ppermute | solution.py:819
  272.9 8.7 %collective-permute-start.18 = (bf16[8,192,128]{2,1,0:T(8,128)(2,1)S(1)}, bf16[8,192,128]{2,1,0:T(8,128)(2,1)}, u32[]{:S(2)}, u32[]{:S(2)}) collective-permute-start(bf16[8,192,128]{2,1,0:T(8,128)(2,1)S(1)} %collective-permute-done.16.refs_11_.refs_1_), channel_id=1, source_target_pairs={{0,1},{1,0},{2,3},{3,2},{4,5},{5,4},{6,7},{7,6},{8,9},{9,8},{10,11... | collective-permute-start | bytes 1179656 | tf_op jit(solution)/shard_map/ppermute | solution.py:819
  (27 other events, 217.2 us)

commit v5 on v4

--- a/solution.py
+++ b/solution.py
@@ -2,6 +2,7 @@
 
 import jax
 import jax.numpy as jnp
+import numpy as np
 from jax import lax
 from jax.experimental import pallas as pl
 from jax.experimental.pallas import tpu as pltpu
@@ -304,14 +305,18 @@
 def plan_kernel(
     groups,
     rows,
+    width,
     member_ref,
     length_ref,
     adapter_ref,
     order_ref,
     variate_ref,
+    frequency_ref,
     chosen_ref,
     back_ref,
     turn_ref,
+    cos_ref,
+    sin_ref,
     *refs,
 ):
     meta_refs, slot_ref = refs[:-1], refs[-1]
@@ -447,28 +452,31 @@
         turn = jnp.where(segment > long_index, segment - 1, segment)
         turn = jnp.where(on_long, 0, turn)
         meta_refs[shift][...] = jnp.where(
-            wide_lane == 0,
-            facts[:, 2:3],
-            jnp.where(
-                wide_lane == 1, segment, jnp.where(wide_lane == 2, turn, row - first_row)
-            ),
-        )
-
-
-def plan(groups, rows, member, seq_len, seq_adapter, block_order, variate):
+            wide_lane == 0, facts[:, 2:3], jnp.where(wide_lane == 1, segment, turn)
+        )
+        if shift == 0:
+            angles = (row - first_row).astype(jnp.float32) * frequency_ref[...]
+            sign = jnp.where(wide_lane % width < width // 2, -1.0, 1.0)
+            cos_ref[...] = jnp.cos(angles)
+            sin_ref[...] = jnp.sin(angles) * sign
+
+
+def plan(groups, rows, width, member, seq_len, seq_adapter, block_order, variate):
     half_devices = groups // 2
     half_rows = half_devices * rows
     blocks = block_order.shape[1]
     smem = pl.BlockSpec(memory_space=pltpu.SMEM)
     vmem = pl.BlockSpec(memory_space=pltpu.VMEM)
     results = pl.pallas_call(
-        functools.partial(plan_kernel, groups, rows),
-        in_specs=[smem, smem, smem, smem, vmem],
-        out_specs=[vmem, vmem, smem] + [vmem] * half_devices,
+        functools.partial(plan_kernel, groups, rows, width),
+        in_specs=[smem, smem, smem, smem, vmem, vmem],
+        out_specs=[vmem, vmem, smem, vmem, vmem] + [vmem] * half_devices,
         out_shape=[
             jax.ShapeDtypeStruct((rows + rows // 2, half_rows), jnp.bfloat16),
             jax.ShapeDtypeStruct((rows, half_rows + half_rows // 2), jnp.bfloat16),
             jax.ShapeDtypeStruct((2,), jnp.int32),
+            jax.ShapeDtypeStruct((rows, LANES), jnp.float32),
+            jax.ShapeDtypeStruct((rows, LANES), jnp.float32),
         ]
         + [jax.ShapeDtypeStruct((rows, LANES), jnp.int32)] * half_devices,
         scratch_shapes=[pltpu.VMEM((blocks, LANES), jnp.int32)],
@@ -477,8 +485,15 @@
             flops=2**31, bytes_accessed=4 * rows * half_rows, transcendentals=0
         ),
         name="plan",
-    )(member, seq_len, seq_adapter, block_order, variate.reshape(blocks, LANES))
-    return results[0], results[1], results[2], results[3:]
+    )(
+        member,
+        seq_len,
+        seq_adapter,
+        block_order,
+        variate.reshape(blocks, LANES),
+        jnp.asarray(rope_frequency(width)),
+    )
+    return (*results[:5], results[5:])
 
 
 def pick_kernel(counts, later_count, chosen_ref, *refs):
@@ -839,6 +854,18 @@
         bit *= 2
     outer = jnp.arange(devices // groups, dtype=jnp.int32)
     return (outer[None, :] * groups + (member ^ mask)[:, None]).reshape(-1)
+
+
+def hand_on(after, *arrays):
+    anywhere = pl.BlockSpec(memory_space=pl.ANY)
+    return pl.pallas_call(
+        lambda *refs: None,
+        in_specs=[anywhere] * (1 + len(arrays)),
+        out_specs=[anywhere] * len(arrays),
+        out_shape=[jax.ShapeDtypeStruct(array.shape, array.dtype) for array in arrays],
+        input_output_aliases={1 + index: index for index in range(len(arrays))},
+        name="hand_on",
+    )(after, *arrays)
 
 
 def assemble_kernel(counts, devices, chunks, first, order_ref, *refs):
@@ -912,17 +939,16 @@
     )(*operands)
 
 
-def rope_tables(position, head_width):
-    lane = jnp.arange(LANES, dtype=jnp.int32)
-    freq_index = (lane % (head_width // 2)).astype(jnp.float32)
-    frequency = ROPE_BASE ** (-2.0 * freq_index / head_width)
-    angles = position.astype(jnp.float32)[:, None] * frequency[None, :]
-    sign = jnp.where(lane % head_width < head_width // 2, -1.0, 1.0)
-    return jnp.cos(angles), jnp.sin(angles) * sign[None, :]
-
-
-def head_gain(gain):
-    return jnp.tile(gain.astype(jnp.float32), LANES // gain.shape[0])[None, :]
+def rope_frequency(head_width):
+    index = np.arange(LANES) % (head_width // 2)
+    return (ROPE_BASE ** (-2.0 * index / head_width)).astype(np.float32)[None, :]
+
+
+def gain_rows(attn_gain, ffn_gain, q_gain, k_gain):
+    repeats = attn_gain.shape[0] // q_gain.shape[0]
+    return jnp.concatenate(
+        [attn_gain, ffn_gain] + [q_gain] * repeats + [k_gain] * repeats
+    ).astype(jnp.float32).reshape(4, -1)
 
 
 def select_kernel(features, hidden, devices, turn_ref, me_ref, flat_ref, *refs):
@@ -1043,6 +1069,14 @@
     return jnp.dot(left, right, preferred_element_type=jnp.float32)
 
 
+def beside(*arrays):
+    return jnp.concatenate(arrays, axis=1)
+
+
+def above(*arrays):
+    return jnp.concatenate(arrays, axis=0)
+
+
 def turn_mask(meta_ref):
     rows = meta_ref.shape[0]
     lane = lax.broadcasted_iota(jnp.int32, (rows, LANES), 1)
@@ -1066,9 +1100,7 @@
     rows = lax.broadcasted_iota(jnp.int32, (lanes, lanes), 0)
     columns = lax.broadcasted_iota(jnp.int32, (lanes, lanes), 1)
     ones = one_hot(rows // width == columns // width)
-    high = values.astype(jnp.bfloat16)
-    low = (values - high.astype(jnp.float32)).astype(jnp.bfloat16)
-    return (dot(high, ones) + dot(low, ones)) * (1.0 / width)
+    return dot(values.astype(jnp.bfloat16), ones) * (1.0 / width)
 
 
 def swap_halves(values, width):
@@ -1089,22 +1121,21 @@
     return jnp.concatenate([kept[:first], kept[first:] + arrived_ref[...]], axis=0)
 
 
-def turned_heads(raw, gain_ref, cosine, sine, width):
-    unit = raw * lax.rsqrt(head_mean(raw * raw, width) + NORM_EPS)
-    unit = unit * widen(gain_ref[...], raw.shape[1])
+def turned_heads(raw, gain, cosine, sine, width):
+    unit = raw * lax.rsqrt(head_mean(raw * raw, width) + NORM_EPS) * gain
     return (unit * cosine + swap_halves(unit, width) * sine).astype(jnp.bfloat16)
 
 
 def project_own(normed, inner, place, index, weight_ref, b_ref):
-    own = jnp.where(place == index, inner, 0.0).astype(jnp.bfloat16)
-    return dot(normed, weight_ref[...]) + ADAPTER_SCALE * dot(own, b_ref[...])
+    own = jnp.where(place == index, ADAPTER_SCALE * inner, 0.0).astype(jnp.bfloat16)
+    return dot(beside(normed, own), above(weight_ref[...], b_ref[...]))
 
 
 def project_key_value_kernel(
     width,
     kept_ref,
     arrived_ref,
-    gain_ref,
+    gains_ref,
     wk_ref,
     wv_ref,
     a_ref,
@@ -1112,7 +1143,6 @@
     meta_ref,
     cos_ref,
     sin_ref,
-    k_gain_ref,
     _,
     x_ref,
     normed_ref,
@@ -1129,7 +1159,7 @@
         rows = joined(kept_ref, arrived_ref)
         x_ref[...] = rows
         values = rows.astype(jnp.float32)
-        normed = (values * row_norm(values) * gain_ref[...].astype(jnp.float32)).astype(
+        normed = (values * row_norm(values) * gains_ref[0:1, :]).astype(
             jnp.bfloat16
         )
         normed_ref[...] = normed
@@ -1141,12 +1171,12 @@
     cosine, sine = widen(cos_ref[...], lanes), widen(sin_ref[...], lanes)
     key = project_own(normed, inner, place, 1, wk_ref, b_ref)
     raw_ref[...] = key.astype(jnp.bfloat16)
-    k_ref[...] = turned_heads(key, k_gain_ref, cosine, sine, width)
+    k_ref[...] = turned_heads(key, gains_ref[3:4, :lanes], cosine, sine, width)
     v_ref[...] = project_own(normed, inner, place, 2, wv_ref, b_ref).astype(jnp.bfloat16)
 
 
 def project_query_kernel(
-    width, normed_ref, inner_ref, wq_ref, b_ref, cos_ref, sin_ref, q_gain_ref, raw_ref, q_ref
+    width, normed_ref, inner_ref, wq_ref, b_ref, cos_ref, sin_ref, gains_ref, raw_ref, q_ref
 ):
     lanes = wq_ref.shape[1]
     place = lax.broadcasted_iota(jnp.int32, inner_ref.shape, 1) // (2 * RANK)
@@ -1154,26 +1184,24 @@
     inner = inner_ref[...].astype(jnp.float32)
     query = project_own(normed_ref[...], inner, place, 0, wq_ref, b_ref)
     raw_ref[...] = query.astype(jnp.bfloat16)
-    q_ref[...] = turned_heads(query, q_gain_ref, cosine, sine, width)
+    q_ref[...] = turned_heads(query, gains_ref[2:3, :lanes], cosine, sine, width)
 
 
 def project_heads(
     kept,
     arrived,
     later,
-    gain,
+    gains,
     weights,
     a_qkv,
     b_qkv,
     meta,
     cos_table,
     sin_table,
-    q_gain,
-    k_gain,
     width,
 ):
     rows, features = kept.shape
-    tile = 256
+    tile = 512
     grid = (features // tile,)
 
     def tiled(height):
@@ -1188,12 +1216,12 @@
     x, normed, inner, key_raw, key, value, later = pl.pallas_call(
         functools.partial(project_key_value_kernel, width),
         grid=grid,
-        in_specs=[full, whole_block(arrived.shape), whole_block((1, features))]
+        in_specs=[full, whole_block(arrived.shape), whole_block(gains.shape)]
         + [tiled(features)] * 2
         + [whole_block((features, LANES)), tiled(LANES), few, few, few]
-        + [whole_block((1, LANES)), anywhere],
+        + [anywhere],
         out_specs=[full, full, few] + [tiled(rows)] * 3 + [anywhere],
-        input_output_aliases={11: 6},
+        input_output_aliases={10: 6},
         out_shape=[
             low,
             low,
@@ -1213,20 +1241,19 @@
     )(
         kept,
         arrived,
-        gain[None, :],
+        gains,
         *weights[1:],
         a_qkv,
         b_qkv,
         meta,
         cos_table,
         sin_table,
-        k_gain,
         later,
     )
     query_raw, query = pl.pallas_call(
         functools.partial(project_query_kernel, width),
         grid=grid,
-        in_specs=[full, few, tiled(features), tiled(LANES), few, few, whole_block((1, LANES))],
+        in_specs=[full, few, tiled(features), tiled(LANES), few, few, whole_block(gains.shape)],
         out_specs=[tiled(rows)] * 2,
         out_shape=[low, low],
         compiler_params=pltpu.CompilerParams(vmem_limit_bytes=VMEM_LIMIT),
@@ -1236,7 +1263,7 @@
             transcendentals=0,
         ),
         name="project_query",
-    )(normed, inner, weights[0], b_qkv, cos_table, sin_table, q_gain)
+    )(normed, inner, weights[0], b_qkv, cos_table, sin_table, gains)
     return x, normed, inner, query_raw, key_raw, query, key, value, later
 
 
@@ -1255,7 +1282,7 @@
         inner_ref,
         x_any,
         residual_any,
-        gain_ref,
+        gains_ref,
         wq_ref,
         wk_ref,
         wv_ref,
@@ -1264,9 +1291,7 @@
         meta_ref,
         cos_ref,
         sin_ref,
-        q_gain_ref,
-        k_gain_ref,
-    ) = refs[:17]
+    ) = refs[:15]
     if devices:
         out_ref, tail_ref, spread_ref = refs[-9:-6]
     else:
@@ -1277,12 +1302,12 @@
     mask, place = turn_mask(meta_ref)
     cosine, sine = widen(cos_ref[...], lanes), widen(sin_ref[...], lanes)
 
-    def turned_back(grad, raw, head_gain_ref):
+    def turned_back(grad, raw, head_gain):
         raw = raw.astype(jnp.float32)
         grad = grad * cosine - swap_halves(grad, width) * sine
         scale = lax.rsqrt(head_mean(raw * raw, width) + NORM_EPS)
         unit = raw * scale
-        grad = grad * widen(head_gain_ref[...], lanes)
+        grad = grad * head_gain
         return (scale * (grad - unit * head_mean(grad * unit, width))).astype(jnp.bfloat16)
 
     def summed(term_refs):
@@ -1307,15 +1332,16 @@
         jnp.bfloat16
     )
     errors = [
-        turned_back(gq_ref[...].astype(jnp.float32), q_raw_ref[...], q_gain_ref),
-        turned_back(summed(gk_refs), k_raw_ref[...], k_gain_ref),
+        turned_back(gq_ref[...].astype(jnp.float32), q_raw_ref[...], gains_ref[2:3, :lanes]),
+        turned_back(summed(gk_refs), k_raw_ref[...], gains_ref[3:4, :lanes]),
         summed(gv_refs).astype(jnp.bfloat16),
     ]
-    total = total_ref[...]
+    total_ref[...] += contract_last(
+        beside(*errors), beside(wq_ref[...], wk_ref[...], wv_ref[...])
+    )
     few = few_ref[...]
     wide = 2 * RANK
-    for index, (error, weight_ref) in enumerate(zip(errors, (wq_ref, wk_ref, wv_ref))):
-        total = total + contract_last(error, weight_ref[...])
+    for index, error in enumerate(errors):
         few = few + jnp.where(place == index, contract_last(error, b_ref[...]), 0.0)
         here = slice(index * wide, (index + 1) * wide)
         grad_b = dot(inner_turned[here], error)
@@ -1342,7 +1368,6 @@
             grad_b_ref[:, part * LANES : (part + 1) * LANES] = square_ref[part].astype(
                 jnp.bfloat16
             )
-    total_ref[...] = total
     few_ref[...] = few
 
     @pl.when(step == pl.num_programs(0) - 1)
@@ -1358,7 +1383,7 @@
             grad_a_ref[...] = tall_ref[...].astype(jnp.bfloat16)
         grad = total_ref[...] + contract_last(low, a_ref[...])
         out = held_ref[2].astype(jnp.float32) + row_norm_back(
-            held_ref[1].astype(jnp.float32), gain_ref[...].astype(jnp.float32), grad
+            held_ref[1].astype(jnp.float32), gains_ref[0:1, :], grad
         )
         out_ref[...] = out.astype(jnp.bfloat16)
         tail_ref[...] = out[out.shape[0] - tail_ref.shape[0] :].astype(jnp.bfloat16)
@@ -1376,15 +1401,13 @@
     inner,
     rows_in,
     grad_residual,
-    gain,
+    gains,
     weights,
     a_qkv,
     b_qkv,
     meta,
     cos_table,
     sin_table,
-    q_gain,
-    k_gain,
     width,
 ):
     rows, features = rows_in.shape
@@ -1410,11 +1433,10 @@
         functools.partial(project_heads_back_kernel, count, width, devices),
         grid=(features // tile,),
         in_specs=[tiled(rows)] * (3 + 2 * count)
-        + [anywhere, whole_block((rows, LANES)), anywhere, anywhere, whole_block((1, features))]
+        + [anywhere, whole_block((rows, LANES)), anywhere, anywhere, whole_block(gains.shape)]
         + [tiled(features)] * 3
         + [whole_block((features, LANES)), tiled(LANES), whole_block(meta.shape)]
         + [whole_block((rows, LANES))] * 2
-        + [whole_block((1, LANES))] * 2
         + [anywhere] * len(after),
         out_specs=[full, whole_block((rows // 2, features)), *grad_specs],
         out_shape=[
@@ -1447,15 +1469,13 @@
         inner,
         rows_in,
         grad_residual,
-        gain[None, :],
+        gains,
         *weights,
         a_qkv,
         b_qkv,
         meta,
         cos_table,
         sin_table,
-        q_gain,
-        k_gain,
         *after,
     )
 
@@ -1486,22 +1506,22 @@
     devices,
     turn_ref,
     att_ref,
-    x_ref,
-    kept_ref,
-    arrived_ref,
-    gain_ref,
+    x_any,
+    kept_any,
+    arrived_any,
+    gains_ref,
     wo_ref,
-    wg_ref,
-    wu_ref,
-    wd_ref,
+    wg_any,
+    wu_any,
+    wd_any,
     a_guo_ref,
     a_down_ref,
     b_gu_ref,
     b_do_ref,
     meta_ref,
-    out_ref,
-    tail_ref,
-    grad_res_ref,
+    out_any,
+    tail_any,
+    grad_res_any,
     grad_att_ref,
     *refs,
 ):
@@ -1524,10 +1544,42 @@
         tall_ref,
         square_ref,
         e_ref,
+        x_ref,
+        arrived_ref,
+        wg_ref,
+        wu_ref,
+        wd_ref,
+        out_ref,
+        grad_res_ref,
+        rows_sems,
+        tile_sems,
+        out_sems,
     ) = refs
     step = pl.program_id(0)
+    steps = pl.num_programs(0)
     mask, place = turn_mask(meta_ref)
-    tile = wg_ref.shape[1]
+    tile = wg_ref.shape[2]
+    swap_rows = arrived_ref.shape[0]
+    row_copies = [
+        pltpu.make_async_copy(source, target, rows_sems.at[index])
+        for index, (source, target) in enumerate(
+            ((x_any, x_ref), (kept_any, e_ref), (arrived_any, arrived_ref))
+        )
+    ]
+
+    def tile_copies(number):
+        slot = number % 2
+        here = pl.ds(pl.multiple_of(number * tile, tile), tile)
+        pairs = (
+            (wg_any.at[:, here], wg_ref.at[slot]),
+            (wu_any.at[:, here], wu_ref.at[slot]),
+            (wd_any.at[here, :], wd_ref.at[slot]),
+        )
+        return [
+            pltpu.make_async_copy(source, target, tile_sems.at[slot, index])
+            for index, (source, target) in enumerate(pairs)
+        ]
+
     features = wo_ref.shape[0]
     wide = 2 * RANK
 
@@ -1539,21 +1591,27 @@
 
     @pl.when(step == 0)
     def _():
-        e_ref[...] = joined(kept_ref, arrived_ref)
+        for copy in row_copies:
+            copy.start()
+        for copy in tile_copies(0):
+            copy.start()
         att = att_ref[...]
         inner_out = dot(att, a_guo_ref[...]) * mask
-        res = (
-            x_ref[...].astype(jnp.float32)
-            + dot(att, wo_ref[...])
-            + ADAPTER_SCALE * dot(only(inner_out, 2), b_do_ref[...])
-        )
+        attention_out = dot(
+            beside(att, only(ADAPTER_SCALE * inner_out, 2)), above(wo_ref[...], b_do_ref[...])
+        )
+        row_copies[0].wait()
+        res = x_ref[...].astype(jnp.float32) + attention_out
         res_ref[...] = res
-        hidden = (res * row_norm(res) * gain_ref[...].astype(jnp.float32)).astype(jnp.bfloat16)
+        hidden = (res * row_norm(res) * gains_ref[1:2, :]).astype(jnp.bfloat16)
         hidden_ref[...] = hidden
         inner = dot(hidden, a_guo_ref[...]) * mask
         inner = jnp.where(place == 2, inner_out, inner).astype(jnp.bfloat16)
         inner_ref[...] = inner
         inner_turned_ref[...] = turn(inner.astype(jnp.float32) * ADAPTER_SCALE)
+        for copy in row_copies[1:]:
+            copy.wait()
+        e_ref[e_ref.shape[0] - swap_rows :, :] += arrived_ref[...]
         few_down = only(ADAPTER_SCALE * contract_last(e_ref[...], b_do_ref[...]) * mask, 0)
         few_down_ref[...] = few_down
         few_down_turned_ref[...] = turn(few_down)[:wide]
@@ -1562,14 +1620,22 @@
         inner_down_ref[...] = jnp.zeros(inner_down_ref.shape, jnp.float32)
         few_ref[...] = jnp.zeros(few_ref.shape, jnp.float32)
 
+    @pl.when(step + 1 < steps)
+    def _():
+        for copy in tile_copies(step + 1):
+            copy.start()
+
+    for copy in tile_copies(step):
+        copy.wait()
+    slot = step % 2
     hidden = hidden_ref[...]
-    inner = inner_ref[...].astype(jnp.float32)
-    gate_weight, up_weight, down_weight = wg_ref[...], wu_ref[...], wd_ref[...]
+    inner = ADAPTER_SCALE * inner_ref[...].astype(jnp.float32)
+    gate_weight, up_weight, down_weight = wg_ref[slot], wu_ref[slot], wd_ref[slot]
     b_tile = b_gu_ref[...]
-    gate = dot(hidden, gate_weight) + ADAPTER_SCALE * dot(only(inner, 0), b_tile)
-    up = dot(hidden, up_weight) + ADAPTER_SCALE * dot(only(inner, 1), b_tile)
-    grad_act = contract_last(e_ref[...], down_weight) + contract_last(
-        few_down_ref[...], a_down_ref[...]
+    gate = dot(beside(hidden, only(inner, 0)), above(gate_weight, b_tile))
+    up = dot(beside(hidden, only(inner, 1)), above(up_weight, b_tile))
+    grad_act = contract_last(
+        beside(e_ref[...], few_down_ref[...]), beside(down_weight, a_down_ref[...])
     )
     sigmoid = 1.0 / (1.0 + jnp.exp(-gate))
     silu = gate * sigmoid
@@ -1578,8 +1644,8 @@
     grad_gate = (grad_act * up * (sigmoid * (1.0 + gate * (1.0 - sigmoid)))).astype(jnp.bfloat16)
     sum_ref[...] += dot(act, down_weight)
     inner_down_ref[...] += dot(act, a_down_ref[...])
-    grad_hidden_ref[...] += contract_last(grad_gate, gate_weight) + contract_last(
-        grad_up, up_weight
+    grad_hidden_ref[...] += contract_last(
+        beside(grad_gate, grad_up), beside(gate_weight, up_weight)
     )
     few_ref[...] += jnp.where(
         place == 0, contract_last(grad_gate, b_tile), contract_last(grad_up, b_tile)
@@ -1601,26 +1667,38 @@
         pl.ds(pl.multiple_of((step % per_quarter) * tile, tile), tile),
     ] = dot(few_down_turned_ref[...], act)
 
-    @pl.when(step == pl.num_programs(0) - 1)
+    out_copies = [
+        pltpu.make_async_copy(source, target, out_sems.at[index])
+        for index, (source, target) in enumerate(
+            (
+                (out_ref, out_any),
+                (out_ref.at[out_ref.shape[0] - swap_rows :, :], tail_any),
+                (grad_res_ref, grad_res_any),
+            )
+        )
+    ]
+
+    @pl.when(step == steps - 1)
     def _():
         grads_out = e_ref[...]
         inner_down = only(inner_down_ref[...] * mask, 0)
         res = res_ref[...]
-        out = (res + sum_ref[...] + ADAPTER_SCALE * dot(inner_down, b_do_ref[...])).astype(
-            jnp.bfloat16
-        )
-        out_ref[...] = out
-        tail_ref[...] = out[out.shape[0] - tail_ref.shape[0] :]
+        out_ref[...] = (
+            res + sum_ref[...] + ADAPTER_SCALE * dot(inner_down, b_do_ref[...])
+        ).astype(jnp.bfloat16)
+        for copy in out_copies[:2]:
+            copy.start()
         few = jnp.where(place < 2, ADAPTER_SCALE * few_ref[...] * mask, 0.0).astype(jnp.bfloat16)
         grad_hidden = grad_hidden_ref[...] + contract_last(few, a_guo_ref[...])
         grad_res = grads_out.astype(jnp.float32) + row_norm_back(
-            res, gain_ref[...].astype(jnp.float32), grad_hidden
+            res, gains_ref[1:2, :], grad_hidden
         )
         low = grad_res.astype(jnp.bfloat16)
         grad_res_ref[...] = low
+        out_copies[2].start()
         few_out = only(ADAPTER_SCALE * contract_last(low, b_do_ref[...]) * mask, 2)
-        grad_att_ref[...] = (
-            contract_last(low, wo_ref[...]) + contract_last(few_out, a_guo_ref[...])
+        grad_att_ref[...] = contract_last(
+            beside(low, few_out), beside(wo_ref[...], a_guo_ref[...])
         ).astype(jnp.bfloat16)
         grad_a = dot(turn(few), hidden_ref[...]) + dot(turn(few_out), att_ref[...])
         inner_out = only(inner_ref[...].astype(jnp.float32), 2)
@@ -1646,6 +1724,8 @@
             grad_a_ref[...] = jnp.transpose(grad_a).astype(jnp.bfloat16)
             grad_ad_ref[...] = jnp.transpose(down_ref[...]).astype(jnp.bfloat16)
             grad_bdo_ref[...] = grad_b.astype(jnp.bfloat16)
+        for copy in out_copies:
+            copy.wait()
 
 
 def feed_forward(
@@ -1655,7 +1735,7 @@
     rows_in,
     kept,
     arrived,
-    gain,
+    gains,
     weights,
     selected,
     meta,
@@ -1665,7 +1745,7 @@
     tile = 512
     full = whole_block((rows, features))
     square = whole_block((features, features))
-    column = pl.BlockSpec((features, tile), lambda step: (0, step))
+    anywhere = pl.BlockSpec(memory_space=pl.ANY)
 
     def shape(height, length, dtype):
         return jax.ShapeDtypeStruct((height, length), dtype)
@@ -1693,27 +1773,21 @@
         in_specs=[
             pl.BlockSpec(memory_space=pltpu.SMEM),
             full,
-            full,
-            full,
-            whole_block(arrived.shape),
-            whole_block((1, features)),
+            anywhere,
+            anywhere,
+            anywhere,
+            whole_block(gains.shape),
             square,
-            column,
-            column,
-            pl.BlockSpec((tile, features), lambda step: (step, 0)),
+            anywhere,
+            anywhere,
+            anywhere,
             whole_block((features, LANES)),
             pl.BlockSpec((tile, LANES), lambda step: (step, 0)),
             pl.BlockSpec((LANES, tile), lambda step: (0, step)),
             whole_block((LANES, features)),
             whole_block(meta.shape),
         ],
-        out_specs=[
-            full,
-            whole_block(arrived.shape),
-            full,
-            full,
-            *grad_specs,
-        ],
+        out_specs=[anywhere, anywhere, anywhere, full, *grad_specs],
         out_shape=[
             shape(rows, features, jnp.bfloat16),
             shape(*arrived.shape, jnp.bfloat16),
@@ -1736,6 +1810,16 @@
             pltpu.VMEM((features, LANES), jnp.float32),
             pltpu.VMEM((features // LANES, LANES, LANES), jnp.float32),
             pltpu.VMEM((rows, features), jnp.bfloat16),
+            pltpu.VMEM((rows, features), jnp.bfloat16),
+            pltpu.VMEM(arrived.shape, jnp.bfloat16),
+            pltpu.VMEM((2, features, tile), jnp.bfloat16),
+            pltpu.VMEM((2, features, tile), jnp.bfloat16),
+            pltpu.VMEM((2, tile, features), jnp.bfloat16),
+            pltpu.VMEM((rows, features), jnp.bfloat16),
+            pltpu.VMEM((rows, features), jnp.bfloat16),
+            pltpu.SemaphoreType.DMA((3,)),
+            pltpu.SemaphoreType.DMA((2, 3)),
+            pltpu.SemaphoreType.DMA((3,)),
         ],
         compiler_params=pltpu.CompilerParams(vmem_limit_bytes=VMEM_LIMIT),
         cost_estimate=pl.CostEstimate(
@@ -1750,7 +1834,7 @@
         rows_in,
         kept,
         arrived,
-        gain[None, :],
+        gains,
         *weights,
         *selected,
         meta,
@@ -1796,17 +1880,15 @@
     head_width = q_gain.shape[0]
     half_devices = groups // 2
     segments = seq_len.shape[1]
-    chosen, back, turn_adapter, key_metas = plan(
-        groups, row_count, member[None], seq_len, seq_adapter, block_order, variate
+    chosen, back, turn_adapter, cos_table, sin_table, key_metas = plan(
+        groups, row_count, head_width, member[None], seq_len, seq_adapter, block_order, variate
     )
     meta = key_metas[0]
-    cos_table, sin_table = rope_tables(meta[:, 3], head_width)
     axes = ALL
     devices = axis_count(PACKS) * groups
     even = spreads_evenly(devices, groups, feature_width, hidden_width, adapters.shape[0])
     spread = devices if even else 0
-    q_gain_row = head_gain(q_gain)
-    k_gain_row = head_gain(k_gain)
+    gains = gain_rows(attn_gain, ffn_gain, q_gain, k_gain)
 
 
     held = (gather_half(tokens, groups), gather_half(cotangent, groups))
@@ -1840,15 +1922,13 @@
         kept_tokens,
         arrived_tokens,
         sent_grads,
-        attn_gain,
+        gains,
         (query_weight, key_weight, value_weight),
         a_qkv,
         b_qkv,
         meta,
         cos_table,
         sin_table,
-        q_gain_row,
-        k_gain_row,
         head_width,
     )
     arrived_grads = to_other_half(sent_grads, groups)
@@ -1864,7 +1944,7 @@
         my_tokens,
         kept_grads,
         arrived_grads,
-        ffn_gain,
+        gains,
         (output_weight, gate_weight, up_weight, down_weight),
         (a_guo, a_down, b_gu, b_do),
         meta,
@@ -1918,15 +1998,13 @@
         inner,
         my_tokens,
         grad_residual,
-        attn_gain,
+        gains,
         (query_weight, key_weight, value_weight),
         a_qkv,
         b_qkv,
         meta,
         cos_table,
         sin_table,
-        q_gain_row,
-        k_gain_row,
         head_width,
     )
     def bring_back(tail):
@@ -1950,15 +2028,10 @@
     )
     late_outer = lax.all_to_all(late_new, PACKS, 0, 0, tiled=True)
     late_pieces = gather_inner(late_outer, groups)
-    input_grad, own_grads = pick(
-        back, 0, row_count, bring_back(grad_tail), later=[own_grads]
-    )
-    cut_rows = early_outer.shape[1] // 2
-    early_far = [
-        lax.ppermute(early_near[:, :cut_rows], "half", swap),
-        lax.ppermute(early_half[:, cut_rows:], "near", swap),
-    ]
-    early_pieces = [[early_outer], [early_near], [early_half], early_far]
+    own_grads, early_half = hand_on(late_outer, own_grads, early_half)
+    early_far = lax.ppermute(early_half, "near", swap)
+    input_grad = pick(back, 0, row_count, bring_back(grad_tail))[0]
+    early_pieces = [[early_outer], [early_near], [early_half], [early_far]]
     early_pieces += [
         [lax.ppermute(part, "core", swap) for part in piece] for piece in early_pieces
     ]

time: 290 us -> 283 us (0.976)
  waiting for transfers between devices: 25.6 us -> 30.8 us
  Pallas kernels: 179 us -> 174 us
  local copies, waits for them, and re-layouts: 17 us -> 12.8 us
    ppermute x3, waiting for transfers between devices: 0.01 us -> 4 us  [gather_inner(): pieces = pieces + [lax.ppermute(piece, GROUP, pairs) for piece in pieces]]
    slice x2 -> x0, local copies, waits for them, and re-layouts: 3.37 us -> none  [the longest x1 1.69 us: per_device(): early_half[:, cut_rows:]]
    all_to_all x1, waiting for transfers between devices: 0.01 us -> 3.34 us  [per_device(): late_outer = lax.all_to_all(late_new, PACKS, 0, 0, tiled=True)]
    ppermute x2 -> x1, waiting for transfers between devices: 5.98 us -> 2.85 us  [per_device(): early_far = lax.ppermute(early_half, 'near', swap)]
    unnamed x54 -> x60, local copies, waits for them, and re-layouts: 9.23 us -> 11.5 us
  transfers between devices with their start and end apart: 32 -> 30, of which waited for: 8 -> 8; matrix products, arithmetic and copies ran while one was open for 5% -> 2% of each run, Pallas kernels for 56% -> 55%
where the time goes in v5:
time: 283 us; the launch traced here: 278 us
  Pallas kernels  174 us (61%)
  starting transfers between devices  55.5 us (20%)
  waiting for transfers between devices  30.8 us (11%)
  local copies, waits for them, and re-layouts  12.8 us (5%)
  other arithmetic  4.37 us (2%)
    pallas_call x1, Pallas kernels, feed_forward(): pl.pallas_call(functools.partial(feed_forward_kernel, devices), grid=(hid...  49.8 us
    pallas_call x1, Pallas kernels, attend_back(): pl.pallas_call(functools.partial(attend_back_kernel, count, segments, wid...  28.3 us
    pallas_call x4, Pallas kernels, pick(): pl.pallas_call(functools.partial(pick_kernel, [len(held) for held in held...  19.8 us
    pallas_call x1, Pallas kernels, attend(): pl.pallas_call(functools.partial(attend_kernel, count, segments, width),...  17 us
    pallas_call x1, Pallas kernels, project_heads_back(): pl.pallas_call(functools.partial(project_heads_back_kernel, count, width,...  15.4 us
    all_to_all x1, starting transfers between devices, per_device(): early = lax.all_to_all(forward_grads[0], axes, 0, 0, tiled=True)  14.5 us
    unnamed x60, local copies, waits for them, and re-layouts  11.5 us
    ppermute x4, waiting for transfers between devices, to_other_half(): lax.ppermute(array, GROUP, [(i, (i + half) % groups) for i in range(group...  9.76 us
  transfers between devices with their start and end apart: 30, of which 8 were waited for; matrix products, arithmetic and copies ran while one was open for 2% of the time, Pallas kernels for 55%

profile of v5, /device:TPU:0, one launch (start us, length us, event | category | flops | bytes accessed | tf_op | source)
XLA Modules:
  0.0 278.4 jit_solution(970667656049362955)
XLA Ops:
  1.2 5.7 %plan.1 = (bf16[768,1024]{1,0:T(8,128)(2,1)}, bf16[512,1536]{1,0:T(8,128)(2,1)}, s32[2]{0:T(128)}, f32[512,128]{1,0:T(8,128)}, f32[512,128]{1,0:T(8,128)}, /*index=5*/s32[512,128]{1,0:T(8,128)}, s32[512,128]{1,0:T(8,128)}) custom-call(s32[1]{0:T(128)} %bitcast.member_ref, s32[1,3]{1,0:T(1,128)} %length_ref.1, s32[1,3]{1,0:T(1,128)} %adapter_ref.1, ...), custom_call_target="tpu_custom_call" | custom-call | flops 2147483648 | bytes 2097152 | tf_op jit(solution)/shard_map/plan/pallas_call | solution.py:470
  8.3 4.2 %pick.5 = (bf16[256,1024]{1,0:T(8,128)(2,1)}, bf16[256,1024]{1,0:T(8,128)(2,1)}) custom-call(bf16[768,1024]{1,0:T(8,128)(2,1)} %get-tuple-element.62.chosen_ref, bf16[512,1024]{1,0:T(8,128)(2,1)} %refs_0_.3, bf16[512,1024]{1,0:T(8,128)(2,1)} %copy-done.12, bf16[512,1024]{1,0:T(8,128)(2,1)} %refs_2_.3, bf16[512,1024]{1,0:T(8,128)(2,1)} %copy-done.13), custom_call_target="tpu_custom_call" | custom-call | flops 1073741824 | bytes 4194304 | tf_op jit(solution)/shard_map/pick/pallas_call | solution.py:517
  12.5 2.9 %collective-permute-start.2 = (bf16[256,1024]{1,0:T(8,128)(2,1)}, bf16[256,1024]{1,0:T(8,128)(2,1)S(1)}, u32[]{:S(2)}, u32[]{:S(2)}) collective-permute-start(bf16[256,1024]{1,0:T(8,128)(2,1)} %get-tuple-element.64.refs_2_), channel_id=1, source_target_pairs={{0,2},{1,3},{2,0},{3,1},{4,6},{5,7},{6,4},{7,5},{8,10},{9,11},{10,... | collective-permute-start | bytes 1572872 | tf_op jit(solution)/shard_map/ppermute | solution.py:561
  16.1 6.7 %select.25 = (bf16[1024,128]{1,0:T(8,128)(2,1)}, bf16[1024,128]{1,0:T(8,128)(2,1)}, bf16[4096,128]{1,0:T(8,128)(2,1)}, bf16[128,1024]{1,0:T(8,128)(2,1)}, bf16[1...) custom-call(s32[2]{0:T(128)} %get-tuple-element.61.turn_ref, ...), custom_call_target="tpu_custom_call" | custom-call | flops 2147483648 | bytes 12058624 | tf_op jit(solution)/shard_map/select/pallas_call | solution.py:1047
  22.8 5.6 %pick.4 = (bf16[512,1024]{1,0:T(8,128)(2,1)}, bf16[512,1024]{1,0:T(8,128)(2,1)}) custom-call(bf16[768,1024]{1,0:T(8,128)(2,1)} %get-tuple-element.62.chosen_ref, bf16[512,1024]{1,0:T(8,128)(2,1)} %refs_0_.3, bf16[512,1024]{1,0:T(8,128)(2,1)} %copy-done.12, bf16[512,1024]{1,0:T(8,128)(2,1)} %refs_2_.3, bf16[512,1024]{1,0:T(8,128)(2,1)} %copy-done.13), custom_call_target="tpu_custom_call" | custom-call | flops 2147483648 | bytes 8388608 | tf_op jit(solution)/shard_map/pick/pallas_call | solution.py:517
  29.1 8.7 %project_key_value.1 = (bf16[512,1024]{1,0:T(8,128)(2,1)}, bf16[512,1024]{1,0:T(8,128)(2,1)}, bf16[512,128]{1,0:T(8,128)(2,1)}, bf16[512,1024]{1,0:T(8,128)(2,1)...) custom-call(bf16[512,1024]{1,0:T(8,128)(2,1)} %get-tuple-element.63., ...), custom_call_target="tpu_custom_call", output_to_operand_aliasing={{6}: (10, {})} | custom-call | flops 3221225472 | bytes 11534336 | tf_op jit(solution)/shard_map/project_key_value/pallas_call | solution.py:1216
  39.5 5.5 %all-to-all-start.1 = ((bf16[32,48,128]{2,1,0:T(8,128)(2,1)}), bf16[32,48,128]{2,1,0:T(8,128)(2,1)S(1)}, u32[]{:S(2)}, u32[]{:S(2)}) async-start(bf16[32,48,128]{2,1,0:T(8,128)(2,1)} %get-tuple-element.98), calls=%async_computation.1 | async-start | bytes 786432 | tf_op jit(solution)/shard_map/all_to_all | solution.py:1909
  45.0 5.9 %project_query.1 = (bf16[512,1024]{1,0:T(8,128)(2,1)}, bf16[512,1024]{1,0:T(8,128)(2,1)}) custom-call(bf16[512,1024]{1,0:T(8,128)(2,1)} %get-tuple-element.71.normed_ref.refs_6_, bf16[512,128]{1,0:T(8,128)(2,1)} %get-tuple-element.72.inner_ref.refs_7_, bf16[1024,1024]{1,0:T(8,128)(2,1)} %refs_11_.1, bf16[128,1024]{1,0:T(8,128)(2,1)} %get-tuple-element.66.b_ref.refs_15_, ...), custom_call_target="tpu_custom_call" | custom-call | flops 1610612736 | bytes 6291456 | tf_op jit(solution)/shard_map/project_query/pallas_call | solution.py:1253
  52.3 17.0 %attend.1 = (bf16[512,1024]{1,0:T(8,128)(2,1)}, f32[512,1024]{1,0:T(8,128)}) custom-call(f32[2,16]{1,0:T(2,128)} %bias_ref.3, bf16[512,1024]{1,0:T(8,128)(2,1)} %get-tuple-element.73.query_ref, s32[512,128]{1,0:T(8,128)} %get-tuple-element.67.meta_ref.qmeta_ref.refs_4_.refs_16_, bf16[512,1024]{1,0:T(8,128)(2,1)} %get-tuple-element.74.refs_0_, ...), custom_call_target="tpu_custom_call" | custom-call | flops 2147483648 | bytes 6291456 | tf_op jit(solution)/shard_map/attend/pallas_call | solution.py:142
  70.1 49.8 %feed_forward.1 = (bf16[512,1024]{1,0:T(8,128)(2,1)}, bf16[256,1024]{1,0:T(8,128)(2,1)}, bf16[512,1024]{1,0:T(8,128)(2,1)}, bf16[512,1024]{1,0:T(8,128)(2,1)}, bf16[32,144,128]{2,1,0:T(8,128)(2,1)}) custom-call(s32[2]{0:T(128)} %get-tuple-element.61.turn_ref, bf16[512,1024]{1,0:T(8,128)(2,1)} %get-tuple-element.77.att_ref.attended_ref, ...), custom_call_target="tpu_custom_call" | custom-call | flops 30064771072 | bytes 41943040 | tf_op jit(solution)/shard_map/feed_forward/pallas_call | solution.py:1770
  119.9 14.5 %all-to-all-start = ((bf16[32,144,128]{2,1,0:T(8,128)(2,1)}), bf16[32,144,128]{2,1,0:T(8,128)(2,1)S(1)}, u32[]{:S(2)}, u32[]{:S(2)}) async-start(bf16[32,144,128]{2,1,0:T(8,128)(2,1)} %get-tuple-element.97), calls=%async_computation | async-start | bytes 2359296 | tf_op jit(solution)/shard_map/all_to_all | solution.py:1972
  134.4 28.3 %attend_back.1 = (bf16[512,1024]{1,0:T(8,128)(2,1)}, bf16[512,1024]{1,0:T(8,128)(2,1)}, bf16[512,1024]{1,0:T(8,128)(2,1)}, bf16[512,1024]{1,0:T(8,128)(2,1)}, bf16[512,1024]{1,0:T(8,128)(2,1)}) custom-call(f32[2,16]{1,0:T(2,128)} %bias_ref.3, bf16[512,1024]{1,0:T(8,128)(2,1)} %get-tuple-element.73.query_ref, ...), custom_call_target="tpu_custom_call" | custom-call | flops 5368709120 | bytes 10485760 | tf_op jit(solution)/shard_map/attend_back/pallas_call | solution.py:269
  166.0 4.1 %settle_early.1 = (bf16[544,128]{1,0:T(8,128)(2,1)}, bf16[4,544,128]{2,1,0:T(8,128)(2,1)}, f32[192,128]{1,0:T(8,128)}, f32[192,128]{1,0:T(8,128)}, s32[1,1024]{1,0:T(1,128)}, /*index=5*/s32[1,512]{1,0:T(1,128)}) custom-call(bf16[32,144,128]{2,1,0:T(8,128)(2,1)} %copy-done.1, bf16[32,48,128]{2,1,0:T(8,128)(2,1)} %copy-done.9, ...), custom_call_target="tpu_custom_call" | custom-call | flops 536870912 | bytes 2359296 | tf_op jit(solution)/shard_map/settle_early/pallas_call | solution.py:761
  170.1 4.6 %all-to-all-start.3 = ((bf16[4,544,128]{2,1,0:T(8,128)(2,1)}), bf16[4,544,128]{2,1,0:T(8,128)(2,1)S(1)}, u32[]{:S(2)}, u32[]{:S(2)}) async-start(bf16[4,544,128]{2,1,0:T(8,128)(2,1)} %get-tuple-element.100.refs_19_), calls=%async_computation.3 | async-start | bytes 1114112 | tf_op jit(solution)/shard_map/all_to_all | solution.py:1976
  174.7 2.8 collective-permute-done.7.refs_2_.refs_20_
  178.6 15.4 %project_heads_back.1 = (bf16[512,1024]{1,0:T(8,128)(2,1)}, bf16[256,1024]{1,0:T(8,128)(2,1)}, bf16[32,64,128]{2,1,0:T(8,128)(2,1)}) custom-call(bf16[512,1024]{1,0:T(8,128)(2,1)} %get-tuple-element.89.refs_0_.gq_ref, bf16[512,1024]{1,0:T(8,128)(2,1)} %get-tuple-element.90.refs_0_, bf16[512,1024]{1,0:T(8,128)(2,1)} %copy-done.11, ...), custom_call_target="tpu_custom_call" | custom-call | flops 4294967296 | bytes 22020096 | tf_op jit(solution)/shard_map/project_heads_back/pallas_call | solution.py:1432
  194.1 5.7 %all-to-all-start.2 = ((bf16[32,64,128]{2,1,0:T(8,128)(2,1)}), bf16[32,64,128]{2,1,0:T(8,128)(2,1)S(1)}, u32[]{:S(2)}, u32[]{:S(2)}) async-start(bf16[32,64,128]{2,1,0:T(8,128)(2,1)} %get-tuple-element.104), calls=%async_computation.2 | async-start | bytes 1048576 | tf_op jit(solution)/shard_map/all_to_all | solution.py:2024
  204.5 5.0 %pick.6.refs_2_ = bf16[512,1024]{1,0:T(8,128)(2,1)} custom-call(bf16[512,1536]{1,0:T(8,128)(2,1)} %get-tuple-element.60.chosen_ref, bf16[512,1024]{1,0:T(8,128)(2,1)} %get-tuple-element.85.refs_0_, bf16[512,1024]{1,0:T(8,128)(2,1)} %copy-done.24, bf16[256,1024]{1,0:T(8,128)(2,1)} %copy-done.17, bf16[256,1024]{1,0:T(8,128)(2,1)} %copy-done.29), custom_call_target="tpu_custom_call" | custom-call | flops 1610612736 | bytes 4194304 | tf_op jit(solution)/shard_map/pick/pallas_call | solution.py:517
  209.5 5.9 %all-to-all-done.2.arrived_ref = bf16[32,64,128]{2,1,0:T(8,128)(2,1)S(1)} async-done(((bf16[32,64,128]{2,1,0:T(8,128)(2,1)}), bf16[32,64,128]{2,1,0:T(8,128)(2,1)S(1)}, u32[]{:S(2)}, u32[]{:S(2)}) %all-to-all-start.2) | async-done | bytes 524320 | tf_op jit(solution)/shard_map/all_to_all | solution.py:2024
  215.4 4.8 %collective-permute-done.12.refs_3_.refs_1_ = bf16[4,544,128]{2,1,0:T(8,128)(2,1)S(1)} collective-permute-done((bf16[4,544,128]{2,1,0:T(8,128)(2,1)S(1)}, bf16[4,544,128]{2,1,0:T(8,128)(2,1)S(1)}, u32[]{:S(2)}, u32[]{:S(2)}) %collective-permute-start.12) | collective-permute-done | bytes 557088 | tf_op jit(solution)/shard_map/ppermute | solution.py:1978
  221.3 2.9 %settle_late.1 = (bf16[32,24,128]{2,1,0:T(8,128)(2,1)}, bf16[8,192,128]{2,1,0:T(8,128)(2,1)}, bf16[256,1024]{1,0:T(8,128)(2,1)}) custom-call(s32[1,1024]{1,0:T(1,128)} %get-tuple-element.102.tall_ref, s32[1,512]{1,0:T(1,128)} %get-tuple-element.103.square_ref, bf16[32,64,128]{2,1,0:T(8,128)(2,1)} %copy-done.7, ...), custom_call_target="tpu_custom_call", output_to_operand_aliasing={{2}: (7, {})} | custom-call | flops 536870912 | bytes 1048576 | tf_op jit(solution)/shard_map/settle_late/pallas_call | solution.py:810
  225.7 4.8 %all-to-all-start.4 = ((bf16[8,192,128]{2,1,0:T(8,128)(2,1)}), bf16[8,192,128]{2,1,0:T(8,128)(2,1)S(1)}, u32[]{:S(2)}, u32[]{:S(2)}) async-start(bf16[8,192,128]{2,1,0:T(8,128)(2,1)} %get-tuple-element.110), calls=%async_computation.4 | async-start | bytes 786432 | tf_op jit(solution)/shard_map/all_to_all | solution.py:2029
  231.0 7.0 %collective-permute-done.14.refs_2_ = bf16[256,1024]{1,0:T(8,128)(2,1)} collective-permute-done((bf16[256,1024]{1,0:T(8,128)(2,1)}, bf16[256,1024]{1,0:T(8,128)(2,1)}, u32[]{:S(2)}, u32[]{:S(2)}) %collective-permute-start.14) | collective-permute-done | bytes 524320 | tf_op jit(solution)/shard_map/ppermute | solution.py:561
  239.4 3.3 %all-to-all-done.4.refs_0_ = bf16[8,192,128]{2,1,0:T(8,128)(2,1)S(1)} async-done(((bf16[8,192,128]{2,1,0:T(8,128)(2,1)}), bf16[8,192,128]{2,1,0:T(8,128)(2,1)S(1)}, u32[]{:S(2)}, u32[]{:S(2)}) %all-to-all-start.4) | async-done | bytes 393248 | tf_op jit(solution)/shard_map/all_to_all | solution.py:2029
  243.5 3.5 %all-to-all-start.5 = ((bf16[32,24,128]{2,1,0:T(8,128)(2,1)}), bf16[32,24,128]{2,1,0:T(8,128)(2,1)S(1)}, u32[]{:S(2)}, u32[]{:S(2)}) async-start(bf16[32,24,128]{2,1,0:T(8,128)(2,1)} %get-tuple-element.112), calls=%async_computation.5 | async-start | bytes 393216 | tf_op jit(solution)/shard_map/all_to_all | solution.py:1845
  247.0 1.8 collective-permute-start.19
  251.8 5.0 %pick.7.refs_8_ = bf16[512,1024]{1,0:T(8,128)(2,1)} custom-call(bf16[512,1536]{1,0:T(8,128)(2,1)} %get-tuple-element.60.chosen_ref, bf16[512,1024]{1,0:T(8,128)(2,1)} %get-tuple-element.101.refs_0_, bf16[512,1024]{1,0:T(8,128)(2,1)} %collective-permute-done.11.refs_1_, bf16[256,1024]{1,0:T(8,128)(2,1)} %collective-permute-done.14.refs_2_, ...), custom_call_target="tpu_custom_call" | custom-call | flops 1610612736 | bytes 4194304 | tf_op jit(solution)/shard_map/pick/pallas_call | solution.py:517
  257.1 4.0 %collective-permute-done.16.refs_9_.refs_1_ = bf16[8,192,128]{2,1,0:T(8,128)(2,1)S(1)} collective-permute-done((bf16[8,192,128]{2,1,0:T(8,128)(2,1)}, bf16[8,192,128]{2,1,0:T(8,128)(2,1)S(1)}, u32[]{:S(2)}, u32[]{:S(2)}) %collective-permute-start.16) | collective-permute-done | bytes 393248 | tf_op jit(solution)/shard_map/ppermute | solution.py:834
  261.2 2.8 %collective-permute-done.19.refs_3_ = bf16[4,544,128]{2,1,0:T(8,128)(2,1)S(1)} collective-permute-done((bf16[4,544,128]{2,1,0:T(8,128)(2,1)}, bf16[4,544,128]{2,1,0:T(8,128)(2,1)S(1)}, u32[]{:S(2)}, u32[]{:S(2)}) %collective-permute-start.19) | collective-permute-done | bytes 557088 | tf_op jit(solution)/shard_map/ppermute | solution.py:2032
  264.0 2.3 fusion.2
  267.1 6.0 %assemble.2.refs_4_ = bf16[23552,128]{1,0:T(8,128)(2,1)} custom-call(bf16[512,512]{1,0:T(8,128)(2,1)} %fusion.1.order_ref, bf16[4,544,128]{2,1,0:T(8,128)(2,1)} %copy-done.4, bf16[4,544,128]{2,1,0:T(8,128)(2,1)} %copy-done.5, bf16[4,544,128]{2,1,0:T(8,128)(2,1)} %get-tuple-element.113.refs_2_, bf16[4,544,128]{2,1,0:T(8,128)(2,1)} %copy-done.15, ...), custom_call_target="tpu_custom_call" | custom-call | flops 2281701376 | bytes 8912896 | tf_op jit(solution)/shard_map/assemble/pallas_call | solution.py:924
  274.8 3.4 %assemble.3 = bf16[23552,128]{1,0:T(8,128)(2,1)} custom-call(bf16[512,512]{1,0:T(8,128)(2,1)} %fusion.order_ref, bf16[8,192,128]{2,1,0:T(8,128)(2,1)} %copy-done.2, bf16[8,192,128]{2,1,0:T(8,128)(2,1)} %copy-done.8, bf16[8,192,128]{2,1,0:T(8,128)(2,1)} %copy-done.18, bf16[8,192,128]{2,1,0:T(8,128)(2,1)} %copy-done.19, ...), custom_call_target="tpu_custom_call", output_to_operand_aliasing={{}: (5, {})} | custom-call | flops 805306368 | bytes 3145728 | tf_op jit(solution)/shard_map/assemble/pallas_call | solution.py:924
  (127 shorter events, 27.1 us)
Async XLA Ops:
  0.6 6.3 %collective-permute-start = (bf16[512,1024]{1,0:T(8,128)(2,1)}, bf16[512,1024]{1,0:T(8,128)(2,1)S(1)}, u32[]{:S(2)}, u32[]{:S(2)}) collective-permute-start(bf16[512,1024]{1,0:T(8,128)(2,1)} %refs_0_.3), channel_id=1, source_target_pairs={{1,0},{0,1},{3,2},{2,3},{5,4},{4,5},{7,6},{6,7},{9,8},{8,9},{11,10... | collective-permute-start | bytes 3145736 | tf_op jit(solution)/shard_map/ppermute | solution.py:552
  1.2 5.8 %collective-permute-start.1 = (bf16[512,1024]{1,0:T(8,128)(2,1)}, bf16[512,1024]{1,0:T(8,128)(2,1)S(1)}, u32[]{:S(2)}, u32[]{:S(2)}) collective-permute-start(bf16[512,1024]{1,0:T(8,128)(2,1)} %refs_2_.3), channel_id=1, source_target_pairs={{1,0},{0,1},{3,2},{2,3},{5,4},{4,5},{7,6},{6,7},{9,8},{8,9},{11,10... | collective-permute-start | bytes 3145736 | tf_op jit(solution)/shard_map/ppermute | solution.py:552
  12.5 15.9 %collective-permute-start.2 = (bf16[256,1024]{1,0:T(8,128)(2,1)}, bf16[256,1024]{1,0:T(8,128)(2,1)S(1)}, u32[]{:S(2)}, u32[]{:S(2)}) collective-permute-start(bf16[256,1024]{1,0:T(8,128)(2,1)} %get-tuple-element.64.refs_2_), channel_id=1, source_target_pairs={{0,2},{1,3},{2,0},{3,1},{4,6},{5,7},{6,4},{7,5},{8,10},{9,11},{10,... | collective-permute-start | bytes 1572872 | tf_op jit(solution)/shard_map/ppermute | solution.py:561
  37.8 13.1 %collective-permute-start.3 = (bf16[512,1024]{1,0:T(8,128)(2,1)}, bf16[512,1024]{1,0:T(8,128)(2,1)S(1)}, u32[]{:S(2)}, u32[]{:S(2)}) collective-permute-start(bf16[512,1024]{1,0:T(8,128)(2,1)} %get-tuple-element.74.refs_0_), channel_id=1, source_target_pairs={{1,0},{0,1},{3,2},{2,3},{5,4},{4,5},{7,6},{6,7},{9,8},{8,9},{11,10... | collective-permute-start | bytes 3145736 | tf_op jit(solution)/shard_map/ppermute | solution.py:552
  37.8 13.1 %collective-permute-start.4 = (bf16[512,1024]{1,0:T(8,128)(2,1)}, bf16[512,1024]{1,0:T(8,128)(2,1)S(1)}, u32[]{:S(2)}, u32[]{:S(2)}) collective-permute-start(bf16[512,1024]{1,0:T(8,128)(2,1)} %get-tuple-element.75.refs_2_), channel_id=1, source_target_pairs={{1,0},{0,1},{3,2},{2,3},{5,4},{4,5},{7,6},{6,7},{9,8},{8,9},{11,10... | collective-permute-start | bytes 3145736 | tf_op jit(solution)/shard_map/ppermute | solution.py:552
  38.3 31.0 %collective-permute-start.5 = (bf16[256,1024]{1,0:T(8,128)(2,1)}, bf16[256,1024]{1,0:T(8,128)(2,1)S(1)}, u32[]{:S(2)}, u32[]{:S(2)}) collective-permute-start(bf16[256,1024]{1,0:T(8,128)(2,1)} %get-tuple-element.80), channel_id=1, source_target_pairs={{0,2},{1,3},{2,0},{3,1},{4,6},{5,7},{6,4},{7,5},{8,10},{9,11},{10,... | collective-permute-start | bytes 1572872 | tf_op jit(solution)/shard_map/ppermute | solution.py:561
  39.5 80.4 %all-to-all-start.1 = ((bf16[32,48,128]{2,1,0:T(8,128)(2,1)}), bf16[32,48,128]{2,1,0:T(8,128)(2,1)S(1)}, u32[]{:S(2)}, u32[]{:S(2)}) async-start(bf16[32,48,128]{2,1,0:T(8,128)(2,1)} %get-tuple-element.98), calls=%async_computation.1 | async-start | bytes 786432 | tf_op jit(solution)/shard_map/all_to_all | solution.py:1909
  119.9 42.8 %copy-start.9 = (bf16[32,48,128]{2,1,0:T(8,128)(2,1)}, bf16[32,48,128]{2,1,0:T(8,128)(2,1)S(1)}, u32[]{:S(2)}) copy-start(bf16[32,48,128]{2,1,0:T(8,128)(2,1)S(1)} %all-to-all-done.1.moments_ref) | copy-start | bytes 1179652
  119.9 45.1 %all-to-all-start = ((bf16[32,144,128]{2,1,0:T(8,128)(2,1)}), bf16[32,144,128]{2,1,0:T(8,128)(2,1)S(1)}, u32[]{:S(2)}, u32[]{:S(2)}) async-start(bf16[32,144,128]{2,1,0:T(8,128)(2,1)} %get-tuple-element.97), calls=%async_computation | async-start | bytes 2359296 | tf_op jit(solution)/shard_map/all_to_all | solution.py:1972
  162.7 14.8 %collective-permute-start.9 = (bf16[512,1024]{1,0:T(8,128)(2,1)}, bf16[512,1024]{1,0:T(8,128)(2,1)S(1)}, u32[]{:S(2)}, u32[]{:S(2)}) collective-permute-start(bf16[512,1024]{1,0:T(8,128)(2,1)} %get-tuple-element.91), channel_id=1, source_target_pairs={{1,0},{0,1},{3,2},{2,3},{5,4},{4,5},{7,6},{6,7},{9,8},{8,9},{11,10... | collective-permute-start | bytes 3145736 | tf_op jit(solution)/shard_map/ppermute | solution.py:552
  162.9 14.6 %collective-permute-start.10 = (bf16[512,1024]{1,0:T(8,128)(2,1)}, bf16[512,1024]{1,0:T(8,128)(2,1)}, u32[]{:S(2)}, u32[]{:S(2)}) collective-permute-start(bf16[512,1024]{1,0:T(8,128)(2,1)} %get-tuple-element.93), channel_id=1, source_target_pairs={{1,0},{0,1},{3,2},{2,3},{5,4},{4,5},{7,6},{6,7},{9,8},{8,9},{11,10... | collective-permute-start | bytes 3145736 | tf_op jit(solution)/shard_map/ppermute | solution.py:552
  163.3 14.2 %collective-permute-start.7 = (bf16[256,1024]{1,0:T(8,128)(2,1)}, bf16[256,1024]{1,0:T(8,128)(2,1)S(1)}, u32[]{:S(2)}, u32[]{:S(2)}) collective-permute-start(bf16[256,1024]{1,0:T(8,128)(2,1)} %get-tuple-element.86), channel_id=1, source_target_pairs={{0,2},{1,3},{2,0},{3,1},{4,6},{5,7},{6,4},{7,5},{8,10},{9,11},{10,... | collective-permute-start | bytes 1572872 | tf_op jit(solution)/shard_map/ppermute | solution.py:561
  170.1 24.0 %all-to-all-start.3 = ((bf16[4,544,128]{2,1,0:T(8,128)(2,1)}), bf16[4,544,128]{2,1,0:T(8,128)(2,1)S(1)}, u32[]{:S(2)}, u32[]{:S(2)}) async-start(bf16[4,544,128]{2,1,0:T(8,128)(2,1)} %get-tuple-element.100.refs_19_), calls=%async_computation.3 | async-start | bytes 1114112 | tf_op jit(solution)/shard_map/all_to_all | solution.py:1976
  174.7 28.7 %collective-permute-start.6 = (bf16[512,1024]{1,0:T(8,128)(2,1)}, bf16[512,1024]{1,0:T(8,128)(2,1)S(1)}, u32[]{:S(2)}, u32[]{:S(2)}) collective-permute-start(bf16[512,1024]{1,0:T(8,128)(2,1)} %get-tuple-element.85.refs_0_), channel_id=1, source_target_pairs={{1,0},{0,1},{3,2},{2,3},{5,4},{4,5},{7,6},{6,7},{9,8},{8,9},{11,10... | collective-permute-start | bytes 3145736 | tf_op jit(solution)/shard_map/ppermute | solution.py:552
  194.1 44.8 %copy-start.4 = (bf16[4,544,128]{2,1,0:T(8,128)(2,1)}, bf16[4,544,128]{2,1,0:T(8,128)(2,1)S(1)}, u32[]{:S(2)}) copy-start(bf16[4,544,128]{2,1,0:T(8,128)(2,1)S(1)} %all-to-all-done.3.refs_0_) | copy-start | bytes 1671172
  194.1 21.3 %all-to-all-start.2 = ((bf16[32,64,128]{2,1,0:T(8,128)(2,1)}), bf16[32,64,128]{2,1,0:T(8,128)(2,1)S(1)}, u32[]{:S(2)}, u32[]{:S(2)}) async-start(bf16[32,64,128]{2,1,0:T(8,128)(2,1)} %get-tuple-element.104), calls=%async_computation.2 | async-start | bytes 1048576 | tf_op jit(solution)/shard_map/all_to_all | solution.py:2024
  199.8 3.6 %collective-permute-start.8 = (bf16[256,1024]{1,0:T(8,128)(2,1)}, bf16[256,1024]{1,0:T(8,128)(2,1)S(1)}, u32[]{:S(2)}, u32[]{:S(2)}) collective-permute-start(bf16[256,1024]{1,0:T(8,128)(2,1)} %copy-done.17), channel_id=1, source_target_pairs={{1,0},{0,1},{3,2},{2,3},{5,4},{4,5},{7,6},{6,7},{9,8},{8,9},{11,10... | collective-permute-start | bytes 1572872 | tf_op jit(solution)/shard_map/ppermute | solution.py:552
  200.2 20.1 %collective-permute-start.12 = (bf16[4,544,128]{2,1,0:T(8,128)(2,1)S(1)}, bf16[4,544,128]{2,1,0:T(8,128)(2,1)S(1)}, u32[]{:S(2)}, u32[]{:S(2)}) collective-permute-start(bf16[4,544,128]{2,1,0:T(8,128)(2,1)S(1)} %all-to-all-done.3.refs_0_), channel_id=1, source_target_pairs={{0,4},{4,0},{1,5},{5,1},{2,6},{6,2},{3,7},{7,3},{8,12},{12,8},{9,1... | collective-permute-start | bytes 1671176 | tf_op jit(solution)/shard_map/ppermute | solution.py:1978
  201.8 18.5 %collective-permute-start.13 = (bf16[4,544,128]{2,1,0:T(8,128)(2,1)S(1)}, bf16[4,544,128]{2,1,0:T(8,128)(2,1)S(1)}, u32[]{:S(2)}, u32[]{:S(2)}) collective-permute-start(bf16[4,544,128]{2,1,0:T(8,128)(2,1)S(1)} %all-to-all-done.3.refs_0_), channel_id=1, source_target_pairs={{0,2},{2,0},{1,3},{3,1},{4,6},{6,4},{5,7},{7,5},{8,10},{10,8},{9,1... | collective-permute-start | bytes 1671176 | tf_op jit(solution)/shard_map/ppermute | solution.py:1979
  224.2 13.8 %collective-permute-start.14 = (bf16[256,1024]{1,0:T(8,128)(2,1)}, bf16[256,1024]{1,0:T(8,128)(2,1)}, u32[]{:S(2)}, u32[]{:S(2)}) collective-permute-start(bf16[256,1024]{1,0:T(8,128)(2,1)} %get-tuple-element.109), channel_id=1, source_target_pairs={{0,2},{1,3},{2,0},{3,1},{4,6},{5,7},{6,4},{7,5},{8,10},{9,11},{10,... | collective-permute-start | bytes 1572872 | tf_op jit(solution)/shard_map/ppermute | solution.py:561
  225.6 25.6 %collective-permute-start.11 = (bf16[512,1024]{1,0:T(8,128)(2,1)}, bf16[512,1024]{1,0:T(8,128)(2,1)}, u32[]{:S(2)}, u32[]{:S(2)}) collective-permute-start(bf16[512,1024]{1,0:T(8,128)(2,1)} %get-tuple-element.101.refs_0_), channel_id=1, source_target_pairs={{1,0},{0,1},{3,2},{2,3},{5,4},{4,5},{7,6},{6,7},{9,8},{8,9},{11,10... | collective-permute-start | bytes 3145736 | tf_op jit(solution)/shard_map/ppermute | solution.py:552
  225.7 17.1 %all-to-all-start.4 = ((bf16[8,192,128]{2,1,0:T(8,128)(2,1)}), bf16[8,192,128]{2,1,0:T(8,128)(2,1)S(1)}, u32[]{:S(2)}, u32[]{:S(2)}) async-start(bf16[8,192,128]{2,1,0:T(8,128)(2,1)} %get-tuple-element.110), calls=%async_computation.4 | async-start | bytes 786432 | tf_op jit(solution)/shard_map/all_to_all | solution.py:2029
  238.0 13.4 %collective-permute-start.15 = (bf16[256,1024]{1,0:T(8,128)(2,1)}, bf16[256,1024]{1,0:T(8,128)(2,1)}, u32[]{:S(2)}, u32[]{:S(2)}) collective-permute-start(bf16[256,1024]{1,0:T(8,128)(2,1)} %collective-permute-done.14.refs_2_), channel_id=1, source_target_pairs={{1,0},{0,1},{3,2},{2,3},{5,4},{4,5},{7,6},{6,7},{9,8},{8,9},{11,10... | collective-permute-start | bytes 1572872 | tf_op jit(solution)/shard_map/ppermute | solution.py:552
  238.9 18.1 %collective-permute-start.20 = (bf16[4,544,128]{2,1,0:T(8,128)(2,1)S(1)}, bf16[4,544,128]{2,1,0:T(8,128)(2,1)S(1)}, u32[]{:S(2)}, u32[]{:S(2)}) collective-permute-start(bf16[4,544,128]{2,1,0:T(8,128)(2,1)S(1)} %all-to-all-done.3.refs_0_), channel_id=1, source_target_pairs={{0,1},{1,0},{2,3},{3,2},{4,5},{5,4},{6,7},{7,6},{8,9},{9,8},{10,11... | collective-permute-start | bytes 1671176 | tf_op jit(solution)/shard_map/ppermute | solution.py:2036
  243.5 13.3 %all-to-all-start.5 = ((bf16[32,24,128]{2,1,0:T(8,128)(2,1)}), bf16[32,24,128]{2,1,0:T(8,128)(2,1)S(1)}, u32[]{:S(2)}, u32[]{:S(2)}) async-start(bf16[32,24,128]{2,1,0:T(8,128)(2,1)} %get-tuple-element.112), calls=%async_computation.5 | async-start | bytes 393216 | tf_op jit(solution)/shard_map/all_to_all | solution.py:1845
  247.0 17.0 %collective-permute-start.19 = (bf16[4,544,128]{2,1,0:T(8,128)(2,1)}, bf16[4,544,128]{2,1,0:T(8,128)(2,1)S(1)}, u32[]{:S(2)}, u32[]{:S(2)}) collective-permute-start(bf16[4,544,128]{2,1,0:T(8,128)(2,1)} %get-tuple-element.113.refs_2_), channel_id=1, source_target_pairs={{0,4},{4,0},{1,5},{5,1},{2,6},{6,2},{3,7},{7,3},{8,12},{12,8},{9,1... | collective-permute-start | bytes 1671176 | tf_op jit(solution)/shard_map/ppermute | solution.py:2032
  248.8 12.3 %collective-permute-start.16 = (bf16[8,192,128]{2,1,0:T(8,128)(2,1)}, bf16[8,192,128]{2,1,0:T(8,128)(2,1)S(1)}, u32[]{:S(2)}, u32[]{:S(2)}) collective-permute-start(bf16[8,192,128]{2,1,0:T(8,128)(2,1)} %copy-done.2), channel_id=1, source_target_pairs={{0,2},{1,3},{2,0},{3,1},{4,6},{5,7},{6,4},{7,5},{8,10},{9,11},{10,... | collective-permute-start | bytes 1179656 | tf_op jit(solution)/shard_map/ppermute | solution.py:834
  251.3 15.0 %collective-permute-start.21 = (bf16[4,544,128]{2,1,0:T(8,128)(2,1)S(1)}, bf16[4,544,128]{2,1,0:T(8,128)(2,1)}, u32[]{:S(2)}, u32[]{:S(2)}) collective-permute-start(bf16[4,544,128]{2,1,0:T(8,128)(2,1)S(1)} %copy-done.6), channel_id=1, source_target_pairs={{0,1},{1,0},{2,3},{3,2},{4,5},{5,4},{6,7},{7,6},{8,9},{9,8},{10,11... | collective-permute-start | bytes 1671176 | tf_op jit(solution)/shard_map/ppermute | solution.py:2036
  251.3 14.9 %collective-permute-start.22 = (bf16[4,544,128]{2,1,0:T(8,128)(2,1)}, bf16[4,544,128]{2,1,0:T(8,128)(2,1)}, u32[]{:S(2)}, u32[]{:S(2)}) collective-permute-start(bf16[4,544,128]{2,1,0:T(8,128)(2,1)} %get-tuple-element.113.refs_2_), channel_id=1, source_target_pairs={{0,1},{1,0},{2,3},{3,2},{4,5},{5,4},{6,7},{7,6},{8,9},{9,8},{10,11... | collective-permute-start | bytes 1671176 | tf_op jit(solution)/shard_map/ppermute | solution.py:2036
  257.0 16.2 %collective-permute-start.17 = (bf16[8,192,128]{2,1,0:T(8,128)(2,1)S(1)}, bf16[8,192,128]{2,1,0:T(8,128)(2,1)S(1)}, u32[]{:S(2)}, u32[]{:S(2)}) collective-permute-start(bf16[8,192,128]{2,1,0:T(8,128)(2,1)S(1)} %copy-done.3), channel_id=1, source_target_pairs={{0,1},{1,0},{2,3},{3,2},{4,5},{5,4},{6,7},{7,6},{8,9},{9,8},{10,11... | collective-permute-start | bytes 1179656 | tf_op jit(solution)/shard_map/ppermute | solution.py:834
  261.1 12.1 %collective-permute-start.18 = (bf16[8,192,128]{2,1,0:T(8,128)(2,1)S(1)}, bf16[8,192,128]{2,1,0:T(8,128)(2,1)S(1)}, u32[]{:S(2)}, u32[]{:S(2)}) collective-permute-start(bf16[8,192,128]{2,1,0:T(8,128)(2,1)S(1)} %collective-permute-done.16.refs_9_.refs_1_), channel_id=1, source_target_pairs={{0,1},{1,0},{2,3},{3,2},{4,5},{5,4},{6,7},{7,6},{8,9},{9,8},{10,11... | collective-permute-start | bytes 1179656 | tf_op jit(solution)/shard_map/ppermute | solution.py:834
  264.0 2.3 collective-permute-start.23
  (28 other events, 115.4 us)
